TPU v7x, 32 devices: a whole 2x2x4 slice. The times are simulated.
32 devices in a mesh: func: 16 (over z, y, x), rep: 2 (over core).
Axes of the slice: x: 2, y: 2, z: 4, core: 2. Of those that a mesh axis runs over, the one named last changes fastest.
Arguments:
- orbitals: bfloat16 [1536, 32, 1024], P('func', 'rep'), may hold values from -6 to 6
- centres: int32 [1536, 3], P('func'), may hold values from 0 to 463, as said below
- potential: float32 [512, 128, 128], P('func'), may hold values from -6 to 6
- kernel: bfloat16 [2, 9216, 128], P('rep', 'func'), may hold values from -0.15625 to 0.15625
- kernel_cols: int32 [12, 12], replicated, may hold values from 0 to 11, as said below
- hamiltonian: bfloat16 [2, 9216, 128], P('rep', 'func'), may hold values from -0.15625 to 0.15625
- intersection_cols: int32 [12, 12], replicated, may hold values from 0 to 11, as said below
Outputs:
- gradient: bfloat16 [1536, 32, 1024], P('func', 'rep')
Inputs may be any that keep to these rules, and one draw needn't show every extreme that they name: centres[f, 0] = 32 * g + o with 0 <= g <= 14 and 0 <= o < 16; centres[f, 1] and centres[f, 2] lie in 0 to 127. In each aligned block of 96 rows, at most 14 rows share the same g, and in some such block of every draw exactly 14 do. Every draw has a row with g = 14, o = 15, centres[f, 1] = 127 and centres[f, 2] = 0. `kernel_cols`: each row names 12 distinct column blocks, the first being the row's own block. `intersection_cols`: each row names 12 distinct column blocks, the first being the row's own block.
All inputs are finite; a program needn't handle non-finite values.
Results may differ from a plain program's by a relative error of at most 0.006.
Values may be sent and summed in bfloat16 or wider, within the bound.
No kernel may reach another device: no remote copies, remote signals or barrier semaphores. Data moves between devices by JAX's collectives and lax.ppermute only.
A program may use at most 256 MiB of HBM per device.

v0:
```python
import jax
import jax.numpy as jnp
from jax import lax
from jax.sharding import PartitionSpec as P

BOX = 32
BLK = 128
NNZB = 12
NB = 12


COEFF_CENTRE = -2.5
COEFF_NEAR = 4.0 / 3.0
COEFF_FAR = -1.0 / 12.0
INV_SPACING = 0.25


def with_halo(shard, sides, width):
    for axis, dim in sides:
        devices, length = (lax.axis_size(axis), shard.shape[dim])
        up = [(i, (i + 1) % devices) for i in range(devices - 1)]
        down = [(j, i) for i, j in up]
        last = lax.slice_in_dim(shard, length - width, length, axis=dim)
        first = lax.slice_in_dim(shard, 0, width, axis=dim)
        before = lax.ppermute(last, axis, up)
        after = lax.ppermute(first, axis, down)
        shard = jnp.concatenate([before, shard, after], axis=dim)
    return shard


def passed_along(block, axis, distance):
    devices = range(lax.axis_size(axis))
    route = [(i - distance, i) for i in devices if i - distance in devices]
    return lax.ppermute(block, axis, route)


def planar_shift(value_entries, offset, edge):
    width = value_entries.shape[-1]
    padded = jnp.pad(value_entries, ((0, 0), (0, 0), (2 * edge, 2 * edge)))
    return lax.slice_in_dim(padded, 2 * edge + offset, 2 * edge + offset + width, axis=2)


def kinetic_term(extended, planes, edge):
    value_entries = extended.astype(jnp.float32)
    centre = value_entries[:, 2 : 2 + planes]
    total = 3.0 * COEFF_CENTRE * centre
    total = total + COEFF_NEAR * (
        value_entries[:, 1 : 1 + planes] + value_entries[:, 3 : 3 + planes]
    )
    total = total + COEFF_FAR * (value_entries[:, 0:planes] + value_entries[:, 4 : 4 + planes])
    column = jnp.arange(edge * edge, dtype=jnp.int32) % edge
    for distance, weight in ((1, COEFF_NEAR), (2, COEFF_FAR)):
        across = planar_shift(centre, distance * edge, edge) + planar_shift(
            centre, -distance * edge, edge
        )
        upward = jnp.where(column + distance < edge, planar_shift(centre, distance, edge), 0.0)
        downward = jnp.where(column - distance >= 0, planar_shift(centre, -distance, edge), 0.0)
        total = total + weight * (across + upward + downward)
    return -0.5 * INV_SPACING * total


def apply_blocks(blocks, cols, rows):
    count = blocks.shape[0]
    width = rows.shape[1]
    grouped_rows = rows.reshape(-1, BLK, width)[cols]
    product = jnp.einsum("ikab,ikbp->iap", blocks, grouped_rows, preferred_element_type=jnp.float32)
    return product.reshape(count * BLK, width)


def shards(orbitals, centres, potential, kernel, kernel_cols, hamiltonian, intersection_cols):
    rep_index = lax.axis_index("rep")
    n_func = lax.axis_size("func")
    owned, planes, flat = orbitals.shape
    edge = BOX
    capacity = 2 * ((owned + n_func - 2) // (n_func - 1))
    slots = n_func * capacity
    extended = with_halo(orbitals, (("rep", 1),), 2)
    kinetic_energy_part = kinetic_term(extended, planes, edge).reshape(owned, planes * flat)
    upper_planes = passed_along(potential[:planes], "func", -1)
    local_pot = jnp.concatenate([potential, upper_planes], axis=0)
    local_pot = jnp.concatenate([local_pot, local_pot[:, : edge - 1]], axis=1)
    local_pot = jnp.concatenate([local_pot, local_pot[:, :, : edge - 1]], axis=2)
    regions = centres[:, 0] // edge
    start_plane = centres[:, 0] % edge + planes * rep_index
    positions = jnp.arange(owned, dtype=jnp.int32)
    earlier = (regions[:, None] == regions[None, :]) & (positions[None, :] < positions[:, None])
    rank_within = jnp.sum(earlier.astype(jnp.int32), axis=1)
    slot_of = regions * capacity + rank_within
    placing = slot_of[None, :] == jnp.arange(slots, dtype=jnp.int32)[:, None]
    phi_flat = orbitals.reshape(owned, planes * flat)
    details = jnp.stack([start_plane, centres[:, 1], centres[:, 2]], axis=1)
    send_meta = jnp.dot(placing.astype(jnp.int32), details)
    send_rows = jnp.dot(
        placing.astype(jnp.bfloat16), phi_flat, preferred_element_type=jnp.float32
    ).astype(jnp.bfloat16)
    pieces = lax.all_to_all(
        send_rows.reshape(n_func, capacity, planes, flat),
        "func",
        split_axis=0,
        concat_axis=0,
        tiled=True,
    )
    meta = lax.all_to_all(
        send_meta.reshape(n_func, capacity, 3), "func", split_axis=0, concat_axis=0, tiled=True
    )
    senders = meta.shape[0]
    count = meta.shape[1]
    flat_meta = meta.reshape(senders * count, 3)

    def window(entry):
        cut = lax.dynamic_slice(local_pot, (entry[0], entry[1], entry[2]), (planes, edge, edge))
        return cut.reshape(planes, edge * edge)

    window_list = jax.vmap(window)(flat_meta).reshape(senders, count, planes, edge * edge)
    returned = (window_list * pieces.astype(jnp.float32)).astype(jnp.bfloat16)
    back_rows = lax.all_to_all(returned, "func", split_axis=0, concat_axis=0, tiled=True)
    potential_part = back_rows.reshape(slots, planes * flat)[slot_of]
    hphi = (kinetic_energy_part + potential_part.astype(jnp.float32)).astype(jnp.bfloat16)
    phi_pts, hphi_pts = (
        lax.all_to_all(phi_flat, "func", split_axis=1, concat_axis=0, tiled=True),
        lax.all_to_all(hphi, "func", split_axis=1, concat_axis=0, tiled=True),
    )
    complete_kernel_matrix, full_h = (
        lax.all_gather(kernel, "func", axis=1, tiled=True),
        lax.all_gather(hamiltonian, "func", axis=1, tiled=True),
    )
    complete_kernel_matrix, full_h = (
        lax.all_gather(complete_kernel_matrix, "rep", axis=0, tiled=True),
        lax.all_gather(full_h, "rep", axis=0, tiled=True),
    )
    k_blocks = complete_kernel_matrix.reshape(NB, NNZB, BLK, BLK)
    h_blocks = full_h.reshape(NB, NNZB, BLK, BLK)
    kphi = apply_blocks(k_blocks, kernel_cols, phi_pts).astype(jnp.bfloat16)
    ydiff = (hphi_pts.astype(jnp.float32) - apply_blocks(h_blocks, intersection_cols, kphi)).astype(
        jnp.bfloat16
    )
    gradient = apply_blocks(k_blocks, kernel_cols, ydiff).astype(jnp.bfloat16)
    owned_grad = lax.all_to_all(gradient, "func", split_axis=0, concat_axis=1, tiled=True)
    return owned_grad.reshape(owned, planes, flat)


def solution(mesh):
    placed = (
        P("func", "rep", None),
        P("func", None),
        P("func", None, None),
        P("rep", "func", None),
        P(),
        P("rep", "func", None),
        P(),
    )
    return jax.shard_map(
        shards, mesh=mesh, in_specs=placed, out_specs=P("func", "rep", None), check_vma=False
    )
```

profile of v0, /device:TPU:0, one launch (start us, length us, event | category | flops | bytes accessed | tf_op | source)
XLA Modules:
  0.0 1635.1 jit_solution(6162973071339348050)
XLA Ops:
  14.7 10.4 all-to-all-start
  29.0 5.0 convolution_convert_fusion
  34.2 11.3 copy.58
  45.5 7.2 all-to-all-start.1
  57.7 1000.7 %while.1 = (s32[]{:T(128)}, f32[48,159,159]{2,1,0:T(8,128)}, s32[224,3]{0,1:T(4,128)S(1)}, f32[224,16,32,32]{3,2,1,0:T(8,128)}, s32[]{:T(128)}) while((s32[]{:T(128)}, f32[48,159,159]{2,1,0:T(8,128)}, s32[224,3]{0,1:T(4,128)S(1)}, f32[224,16,32,32]{3,2,1,0:T(8,128)}, s32[]{:T(128)}) %tuple.26), condition=%wide.while_cond, body=%wide.while_body.sunk | while | flops 2 | bytes 526449 | solution.py:111
  98.5 3.9 bitcast_dynamic-update-slice_fusion.2
  143.1 3.9 bitcast_dynamic-update-slice_fusion.2
  187.8 3.9 bitcast_dynamic-update-slice_fusion.2
  205.7 3.9 bitcast_dynamic-update-slice_fusion.2
  228.1 3.9 bitcast_dynamic-update-slice_fusion.2
  330.8 3.9 bitcast_dynamic-update-slice_fusion.2
  384.4 3.9 bitcast_dynamic-update-slice_fusion.2
  429.0 3.9 bitcast_dynamic-update-slice_fusion.2
  455.9 3.9 bitcast_dynamic-update-slice_fusion.2
  473.7 3.9 bitcast_dynamic-update-slice_fusion.2
  478.2 3.9 bitcast_dynamic-update-slice_fusion.2
  491.7 3.9 bitcast_dynamic-update-slice_fusion.2
  514.0 3.9 bitcast_dynamic-update-slice_fusion.2
  523.0 3.9 bitcast_dynamic-update-slice_fusion.2
  692.6 3.9 bitcast_dynamic-update-slice_fusion.2
  706.0 3.9 bitcast_dynamic-update-slice_fusion.2
  732.8 3.9 bitcast_dynamic-update-slice_fusion.2
  741.8 3.9 bitcast_dynamic-update-slice_fusion.2
  808.8 3.9 bitcast_dynamic-update-slice_fusion.2
  884.8 3.9 bitcast_dynamic-update-slice_fusion.2
  898.2 3.9 bitcast_dynamic-update-slice_fusion.2
  1018.7 3.9 bitcast_dynamic-update-slice_fusion.2
  1027.7 3.9 bitcast_dynamic-update-slice_fusion.2
  1058.4 44.6 %reshape.98 = f32[16,14,16,1024]{3,2,1,0:T(8,128)} reshape(f32[224,16,32,32]{3,2,1,0:T(8,128)} %get-tuple-element.12) | data formatting | bytes 29360128 | tf_op jit(solution)/shard_map/reshape;vmap()/reshape | solution.py:114
  1103.0 11.0 multiply_convert_fusion
  1113.9 7.3 all-to-all-start.2
  1126.1 138.6 %all-to-all-done.2 = bf16[16,14,16,1024]{3,2,1,0:T(8,128)(2,1)} async-done(((bf16[16,14,16,1024]{3,2,1,0:T(8,128)(2,1)}), bf16[16,14,16,1024]{3,2,1,0:T(8,128)(2,1)}, u32[]{:S(2)}, u32[]{:S(2)}) %all-to-all-start.2) | async-done | bytes 7340064 | tf_op jit(solution)/shard_map/all_to_all | solution.py:116
  1264.7 47.7 %all-to-all-start.4 = ((bf16[96,16,1024]{2,0,1:T(8,128)(2,1)}), bf16[96,16,1024]{2,0,1:T(8,128)(2,1)S(1)}, u32[]{:S(2)}, u32[]{:S(2)}) async-start(bf16[96,16,1024]{2,0,1:T(8,128)(2,1)} %copy.40), calls=%async_computation.4 | async-start | bytes 6291456 | tf_op jit(solution)/shard_map/all_to_all | solution.py:120
  1327.8 11.6 copy.59
  1339.4 22.7 %gather_fusion = bf16[96,16384]{1,0:T(8,128)(2,1)} fusion(bf16[224,16384]{1,0:T(8,128)(2,1)} %bitcast.90, s32[1024]{0:T(1024)S(1)} %pad_clamp_fusion.2), kind=kCustom, calls=%fused_computation | custom fusion | bytes 6291840 | tf_op jit(solution)/shard_map/gather | solution.py:117
  1362.1 5.2 convert_element_type.85
  1367.3 40.0 %fusion.9 = bf16[96,16,1024]{2,0,1:T(8,128)(2,1)} fusion(f32[96,16,1024]{2,0,1:T(8,128)} %slice.120, f32[12,16,8,1024]{3,2,1,0:T(8,128)} %bitcast.94, f32[96,20,1024]{2,0,1:T(8,128)} %copy-done, pred[1024]{0:T(1024)(128)(4,1)S(1)} %get-tuple-element.31, pred[1024]{0:T(1024)(128)(4,1)S(1)} %get-tuple-element.32, pred[1024]{0:T(1024)(128)(4,1)S(1)} %get-tuple-element.33, ...), kind=kLoop, calls=%fused_computation.26 | loop fusion | flops 37748736 | bytes 40898560 | tf_op jit(solution)/shard_map/convert_element_type | solution.py:118
  1407.3 7.0 all-to-all-start.3
  1415.1 15.8 gather_fusion.1
  1430.9 17.6 %fusion.23 = bf16[12,128,1024]{1,2,0:T(8,128)(2,1)S(1)} fusion(bf16[12,12,128,1024]{3,2,1,0:T(8,128)(2,1)} %bitcast.88, bf16[12,12,128,128]{3,2,1,0:T(8,128)(2,1)} %bitcast.95), kind=kOutput, calls=%fused_computation.46 | convolution fusion | flops 4833411072 | bytes 45613056 | tf_op jit(solution)/shard_map/ikab,ikbp->iap/dot_general | solution.py:66
  1448.5 14.3 gather_fusion.2
  1462.8 12.8 all-to-all-done.3
  1475.6 5.2 convert_element_type.87
  1480.8 6.6 copy.48
  1487.4 18.8 %fusion.22 = bf16[12,128,1024]{1,2,0:T(8,128)(2,1)S(1)} fusion(f32[12,128,1024]{1,2,0:T(8,128)} %copy.48, bf16[12,12,128,1024]{2,3,1,0:T(8,128)(2,1)} %bitcast.87, bf16[12,12,128,128]{3,2,1,0:T(8,128)(2,1)} %bitcast.101), kind=kOutput, calls=%fused_computation.42 | convolution fusion | flops 4834983936 | bytes 51904512 | tf_op jit(solution)/shard_map/ikab,ikbp->iap/dot_general | solution.py:66
  1506.2 14.3 gather_fusion.3
  1520.6 18.2 %bitcast_convert_fusion = bf16[12,1024,128]{1,2,0:T(8,128)(2,1)S(1)} fusion(bf16[12,12,128,1024]{2,3,1,0:T(8,128)(2,1)} %bitcast.89, bf16[12,12,128,128]{3,2,1,0:T(8,128)(2,1)} %bitcast.96), kind=kOutput, calls=%fused_computation.43 | convolution fusion | flops 4833411072 | bytes 45613056 | tf_op jit(solution)/shard_map/ikab,ikbp->iap/dot_general | solution.py:66
  1538.8 86.2 %all_to_all.51 = bf16[16,96,1024]{2,1,0:T(8,128)(2,1)S(1)} all-to-all(bf16[16,96,1024]{2,1,0:T(8,128)(2,1)S(1)} %bitcast.97), channel_id=1, replica_groups=mesh['func'=16,'rep'=2] {'func'}, dimensions={0} | all-to-all | bytes 6291456 | tf_op jit(solution)/shard_map/all_to_all | solution.py:138
  (715 shorter events, 952.7 us)
Async XLA Ops:
  8.8 44.1 %collective-permute-start.2 = (f32[16,128,128]{2,1,0:T(8,128)}, f32[16,128,128]{2,1,0:T(8,128)}, u32[]{:S(2)}, u32[]{:S(2)}) collective-permute-start(f32[16,128,128]{2,1,0:T(8,128)} %slice.87), channel_id=1, source_target_pairs={{2,0},{4,2},{6,4},{8,6},{10,8},{12,10},{14,12},{16,14},{18,16},{20... | collective-permute-start | bytes 3145736 | tf_op jit(solution)/shard_map/ppermute | solution.py:34
  14.7 30.8 %all-to-all-start = ((s32[16,14,3]{1,2,0:T(4,128)}), s32[16,14,3]{1,2,0:T(4,128)S(1)}, u32[]{:S(2)}, u32[]{:S(2)}) async-start(s32[16,14,3]{1,2,0:T(4,128)} %copy.43), calls=%async_computation | async-start | bytes 65536 | tf_op jit(solution)/shard_map/all_to_all | solution.py:103
  29.0 5.0 copy-start.2
  45.5 1057.5 %all-to-all-start.1 = ((bf16[16,14,16,1024]{3,2,1,0:T(8,128)(2,1)}), bf16[16,14,16,1024]{3,2,1,0:T(8,128)(2,1)}, u32[]{:S(2)}, u32[]{:S(2)}) async-start(bf16[16,14,16,1024]{3,2,1,0:T(8,128)(2,1)} %bitcast.92), calls=%async_computation.1 | async-start | bytes 14680064 | tf_op jit(solution)/shard_map/all_to_all | solution.py:96
  1113.9 8.8 copy-start.1
  1113.9 150.8 %all-to-all-start.2 = ((bf16[16,14,16,1024]{3,2,1,0:T(8,128)(2,1)}), bf16[16,14,16,1024]{3,2,1,0:T(8,128)(2,1)}, u32[]{:S(2)}, u32[]{:S(2)}) async-start(bf16[16,14,16,1024]{3,2,1,0:T(8,128)(2,1)} %multiply_convert_fusion), calls=%async_computation.2 | async-start | bytes 14680064 | tf_op jit(solution)/shard_map/all_to_all | solution.py:116
  1121.3 191.2 %all-gather.5.cloned.1.call-start = ((), (), s32[]{:S(2)}) async-start(), calls=%async_computation.6 | async-start | bytes 2506752 | tf_op jit(solution)/shard_map/all_gather | solution.py:124
  1122.0 292.4 %all-gather.9.cloned.1.call-start = ((), (), s32[]{:S(2)}) async-start(), calls=%async_computation.8 | async-start | bytes 2506752 | tf_op jit(solution)/shard_map/all_gather | solution.py:125
  1264.7 142.6 %all-to-all-start.4 = ((bf16[96,16,1024]{2,0,1:T(8,128)(2,1)}), bf16[96,16,1024]{2,0,1:T(8,128)(2,1)S(1)}, u32[]{:S(2)}, u32[]{:S(2)}) async-start(bf16[96,16,1024]{2,0,1:T(8,128)(2,1)} %copy.40), calls=%async_computation.4 | async-start | bytes 6291456 | tf_op jit(solution)/shard_map/all_to_all | solution.py:120
  1312.4 118.5 %all-gather.7.cloned.1.call-start = ((), (), s32[]{:S(2)}) async-start(), calls=%async_computation.7 | async-start | bytes 7077888 | tf_op jit(solution)/shard_map/all_gather | solution.py:128
  1314.3 2.7 collective-permute-start
  1315.7 3.6 collective-permute-start.1
  1321.5 3.1 copy-start
  1407.3 7.6 copy-start.3
  1407.3 7.7 copy-start.4
  1407.3 68.2 %all-to-all-start.3 = ((bf16[96,16,1024]{2,0,1:T(8,128)(2,1)}), bf16[96,16,1024]{2,0,1:T(8,128)(2,1)}, u32[]{:S(2)}, u32[]{:S(2)}) async-start(bf16[96,16,1024]{2,0,1:T(8,128)(2,1)} %fusion.9), calls=%async_computation.3 | async-start | bytes 6291456 | tf_op jit(solution)/shard_map/all_to_all | solution.py:121
  1414.3 73.1 %all-gather.11.cloned.1.call-start = ((), (), s32[]{:S(2)}) async-start(), calls=%async_computation.9 | async-start | bytes 7077888 | tf_op jit(solution)/shard_map/all_gather | solution.py:129
Sparse Core Ops, SparseCore 0:
  1124.9 159.9 all-gather.4
  1287.7 95.4 all-gather.8
  1384.8 16.5 all-gather.6
  1416.4 15.6 all-gather.10
where the time goes:
time: 1660 us; the launch traced here: 1640 us
  local copies, waits for them, and re-layouts  1170 us (70%)
  waiting for transfers between devices  156 us (9%)
  blocking collectives  86.2 us (5%)
  starting transfers between devices  83.7 us (5%)
  other arithmetic  70 us (4%)
  matrix products  59.8 us (4%)
    gather x672, local copies, waits for them, and re-layouts  1000 us
    all_to_all x1, waiting for transfers between devices, shards(): lax.all_to_all(returned, 'func', split_axis=0, concat_axis=0, tiled=True)  139 us
    all_to_all x1, blocking collectives, shards(): lax.all_to_all(gradient, 'func', split_axis=0, concat_axis=1, tiled=True)  86.2 us
    dot_general x3, matrix products, apply_blocks(): jnp.einsum('ikab,ikbp->iap', blocks, grouped_rows, preferred_element_type...  54.6 us
    all_to_all x1, starting transfers between devices, shards(): lax.all_to_all(phi_flat, 'func', split_axis=1, concat_axis=0, tiled=True)  47.7 us
    reshape x1, local copies, waits for them, and re-layouts, shards(): jax.vmap(window)(flat_meta).reshape(senders, count, planes, edge * edge)  44.6 us
    gather x3, local copies, waits for them, and re-layouts, apply_blocks(): grouped_rows = rows.reshape(-1, BLK, width)[cols]  44.4 us
    convert_element_type x1, other arithmetic, shards(): (kinetic_energy_part + potential_part.astype(jnp.float32)).astype(jnp.bfl...  40 us
  transfers between devices with their start and end apart: 12, of which 3 were waited for; matrix products, arithmetic and copies ran while one was open for 75% of the time, Pallas kernels for 0%

commit v1 on v0

v1 whole, which is shorter than its diff:
```python
import jax
import jax.numpy as jnp
from jax import lax
from jax.experimental import pallas as pl
from jax.experimental.pallas import tpu as pltpu
from jax.sharding import PartitionSpec as P

BOX = 32
BLK = 128
NNZB = 12
NB = 12
NF = NB * BLK
LANES = 128
ROWS = 16
GROUP = 16
COLS = 256
VMEM = 56 * 1024 * 1024

CENTRE = 90.0
NEAR = -16.0
FAR = 1.0
SCALE = 1.0 / 96.0


def planar_band():
    row = lax.broadcasted_iota(jnp.int32, (2 * COLS, COLS), 0) - LANES
    col = lax.broadcasted_iota(jnp.int32, (2 * COLS, COLS), 1)
    across = jnp.abs((row + LANES) // BOX - (col + LANES) // BOX)
    along = jnp.abs((row + LANES) % BOX - (col + LANES) % BOX)
    band = jnp.zeros((2 * COLS, COLS), jnp.float32)
    for one, other in ((across, along), (along, across)):
        band = jnp.where((one == 0) & (other == 1), NEAR, band)
        band = jnp.where((one == 0) & (other == 2), FAR, band)
    band = jnp.where((across == 0) & (along == 0), CENTRE, band)
    return band.astype(jnp.bfloat16)


def hphi_kernel(
    info, phi, halo, band, pot, out, buf, rows, win, sems
):
    planes, group, flat = phi.shape
    step = pl.program_id(0)
    total = pl.num_programs(0) * group
    x_blocks = pot.shape[2]
    span = 3 * ROWS
    flag = info[0, 3].astype(jnp.float32)

    def copies(index, slot):
        z = info[index, 0]
        first = info[index, 1] // ROWS
        out_list = []
        for k in range(3):
            block = lax.rem(first + k, 2 * x_blocks)
            out_list.append(
                pltpu.make_async_copy(
                    pot.at[block // x_blocks, pl.ds(z, planes), lax.rem(block, x_blocks)],
                    buf.at[slot, k],
                    sems.at[slot, k],
                )
            )
        return out_list

    @pl.when(step == 0)
    def _():
        for copy in copies(0, 0):
            copy.start()

    lane = lax.broadcasted_iota(jnp.int32, (8, LANES), 1)

    def one_function(f, carry):
        index = step * group + f
        slot = lax.rem(index, 2)

        @pl.when(index + 1 < total)
        def _():
            for copy in copies(index + 1, 1 - slot):
                copy.start()

        for copy in copies(index, slot):
            copy.wait()
        for z in range(planes):
            for k in range(3):
                rows[pl.ds(z * span + k * ROWS, ROWS), :] = buf[slot, k, z].astype(jnp.float32)
        shift_x = lax.rem(info[index, 1], ROWS)
        shift_y = info[index, 2]
        for z in range(planes):
            value = None
            for b in range(4):
                part = rows[pl.ds(z * span + b + shift_x, 8, stride=4), :]
                part = pltpu.roll(part, lax.rem(b * BOX + LANES - shift_y, LANES), axis=1)
                value = part if value is None else jnp.where(lane >= b * BOX, part, value)
            win[pl.ds(z * group + f, 8, stride=planes * group), :] = value
        return carry

    lax.fori_loop(0, group, one_function, 0)

    pieces = flat // COLS
    for c in range(pieces):
        low = max(0, c * COLS - LANES)
        high = min(flat, c * COLS + COLS + LANES)
        cols = slice(c * COLS, (c + 1) * COLS)
        left = phi[:, :, low:high].reshape(planes * group, high - low)
        base = low - (c * COLS - LANES)
        planar = jnp.dot(
            left, band[base : base + high - low, :], preferred_element_type=jnp.float32
        )
        level = [phi[z, :, cols].astype(jnp.float32) for z in range(planes)]
        other = [halo[h, :, cols].astype(jnp.float32) for h in range(2)]
        below = [h * flag for h in other]
        above = [h * (1.0 - flag) for h in other]
        level = below + level + above
        for z in range(planes):
            kin = planar[z * group : (z + 1) * group]
            kin = kin + NEAR * (level[z + 1] + level[z + 3]) + FAR * (level[z] + level[z + 4])
            w = jnp.concatenate(
                [
                    win[pl.ds((a * planes + z) * group, group), :]
                    for a in range(c * COLS // LANES, (c + 1) * COLS // LANES)
                ],
                axis=1,
            )
            vphi = (w * level[z + 2]).astype(jnp.bfloat16).astype(jnp.float32)
            out[z, :, cols] = (SCALE * kin + vphi).astype(jnp.bfloat16)


def make_hphi(info, phi, halo, band, pot):
    planes, owned, flat = phi.shape
    x_blocks = pot.shape[2]
    span = 3 * ROWS
    grid_spec = pltpu.PrefetchScalarGridSpec(
        num_scalar_prefetch=1,
        grid=(owned // GROUP,),
        in_specs=[
            pl.BlockSpec((planes, GROUP, flat), lambda i, s: (0, i, 0)),
            pl.BlockSpec((2, GROUP, flat), lambda i, s: (0, i, 0)),
            pl.BlockSpec(band.shape, lambda i, s: (0, 0)),
            pl.BlockSpec(memory_space=pl.ANY),
        ],
        out_specs=pl.BlockSpec((planes, GROUP, flat), lambda i, s: (0, i, 0)),
        scratch_shapes=[
            pltpu.VMEM((2, 3, planes, ROWS, LANES), jnp.bfloat16),
            pltpu.VMEM((planes * span, LANES), jnp.float32),
            pltpu.VMEM((flat // LANES * planes * GROUP, LANES), jnp.float32),
            pltpu.SemaphoreType.DMA((2, 3)),
        ],
    )
    return pl.pallas_call(
        hphi_kernel,
        out_shape=jax.ShapeDtypeStruct((planes, owned, flat), jnp.bfloat16),
        grid_spec=grid_spec,
        compiler_params=pltpu.CompilerParams(vmem_limit_bytes=VMEM),
        name="hphi",
        cost_estimate=pl.CostEstimate(
            flops=4 * planes * owned * flat * COLS, bytes_accessed=30 << 20, transcendentals=0
        ),
    )(info, phi, halo, band, pot)


def dense_rows(cols, blocks, dense):
    def one_block(n, carry):
        i = n // NNZB
        col = cols[i, lax.rem(n, NNZB)]
        dense[pl.ds(pl.multiple_of(i * BLK, BLK), BLK), pl.ds(pl.multiple_of(col * BLK, BLK), BLK)] = (
            blocks[pl.ds(pl.multiple_of(n * BLK, BLK), BLK), :]
        )
        return carry

    lax.fori_loop(0, NB * NNZB, one_block, 0)


def first_kernel(k_cols, h_cols, k_blocks, h_blocks, phi, dense_k, product, dense_h):
    @pl.when(pl.program_id(0) == 0)
    def _():
        dense_rows(k_cols, k_blocks, dense_k)
        dense_rows(h_cols, h_blocks, dense_h)

    kphi = jnp.dot(dense_k[...], phi[...], preferred_element_type=jnp.float32)
    product[...] = jnp.dot(
        dense_h[...], kphi.astype(jnp.bfloat16), preferred_element_type=jnp.float32
    )


def first_products(k_cols, h_cols, k_blocks, h_blocks, phi):
    width = phi.shape[1]
    tile = min(COLS, width)
    whole = pl.BlockSpec(k_blocks.shape, lambda i, a, b: (0, 0), pipeline_mode=pl.Buffered(1))
    grid_spec = pltpu.PrefetchScalarGridSpec(
        num_scalar_prefetch=2,
        grid=(width // tile,),
        in_specs=[whole, whole, pl.BlockSpec((NF, tile), lambda i, a, b: (0, i))],
        out_specs=[
            pl.BlockSpec((NF, NF), lambda i, a, b: (0, 0)),
            pl.BlockSpec((NF, tile), lambda i, a, b: (0, i)),
        ],
        scratch_shapes=[pltpu.VMEM((NF, NF), jnp.bfloat16)],
    )
    return pl.pallas_call(
        first_kernel,
        out_shape=[
            jax.ShapeDtypeStruct((NF, NF), jnp.bfloat16),
            jax.ShapeDtypeStruct((NF, width), jnp.float32),
        ],
        grid_spec=grid_spec,
        compiler_params=pltpu.CompilerParams(vmem_limit_bytes=VMEM),
        name="products",
        cost_estimate=pl.CostEstimate(
            flops=4 * NF * NF * width, bytes_accessed=24 << 20, transcendentals=0
        ),
    )(k_cols, h_cols, k_blocks, h_blocks, phi)


def last_kernel(dense_k, hphi, product, out):
    ydiff = (hphi[...].astype(jnp.float32) - product[...]).astype(jnp.bfloat16)
    out[...] = jnp.dot(dense_k[...], ydiff, preferred_element_type=jnp.float32).astype(jnp.bfloat16)


def last_product(dense_k, hphi, product):
    width = hphi.shape[1]
    tile = min(COLS, width)
    columns = pl.BlockSpec((NF, tile), lambda i: (0, i))
    return pl.pallas_call(
        last_kernel,
        out_shape=jax.ShapeDtypeStruct((NF, width), jnp.bfloat16),
        grid=(width // tile,),
        in_specs=[pl.BlockSpec((NF, NF), lambda i: (0, 0)), columns, columns],
        out_specs=columns,
        compiler_params=pltpu.CompilerParams(vmem_limit_bytes=VMEM),
        name="gradient",
        cost_estimate=pl.CostEstimate(
            flops=2 * NF * NF * width, bytes_accessed=17 << 20, transcendentals=0
        ),
    )(dense_k, hphi, product)


def shards(orbitals, centres, potential, kernel, kernel_cols, hamiltonian, intersection_cols):
    rep = lax.axis_index("rep")
    n_func = lax.axis_size("func")
    n_rep = lax.axis_size("rep")
    owned, planes, flat = orbitals.shape
    z_planes, x_size, y_size = potential.shape
    shares = n_func // planes
    width = flat // shares

    def exchange(rows):
        return lax.all_to_all(rows, "func", split_axis=0, concat_axis=0, tiled=True)

    def to_points(plane_rows):
        cut = plane_rows.reshape(planes, owned, shares, width).transpose(0, 2, 1, 3)
        return exchange(cut.reshape(n_func, owned, width)).reshape(n_func * owned, width)

    half = lax.dynamic_slice_in_dim(potential, rep * (x_size // n_rep), x_size // n_rep, axis=1)
    half = half.astype(jnp.bfloat16).reshape(z_planes, x_size // n_rep // ROWS, ROWS, y_size)
    pot = lax.all_gather(half, ("rep", "func"), axis=0, tiled=True)
    pot = pot.reshape(n_rep, n_func * z_planes, x_size // n_rep // ROWS, ROWS, y_size)

    phi_planes = orbitals.transpose(1, 0, 2)
    edge = jnp.where(rep == 0, phi_planes[planes - 2 :], phi_planes[:2])
    halo = lax.ppermute(edge, "rep", [(0, 1), (1, 0)])
    flag = jnp.full((owned, 1), rep, jnp.int32)
    info = jnp.concatenate(
        [centres[:, :1] + planes * rep, centres[:, 1:], flag], axis=1
    ).astype(jnp.int32)

    phi_pts = to_points(phi_planes)
    k_blocks = lax.all_gather(kernel, ("rep", "func"), axis=1, tiled=True).reshape(-1, BLK)
    h_blocks = lax.all_gather(hamiltonian, ("rep", "func"), axis=1, tiled=True).reshape(-1, BLK)

    extra = -owned % GROUP
    padded = [
        jnp.pad(info, ((0, extra), (0, 0))),
        jnp.pad(phi_planes, ((0, 0), (0, extra), (0, 0))),
        jnp.pad(halo, ((0, 0), (0, extra), (0, 0))),
    ]
    hphi = make_hphi(*padded, planar_band(), pot)[:, :owned]
    dense_k, product = first_products(kernel_cols, intersection_cols, k_blocks, h_blocks, phi_pts)
    hphi_pts = to_points(hphi)
    gradient = last_product(dense_k, hphi_pts, product)
    back = exchange(gradient.reshape(n_func, owned, width))
    back = back.reshape(planes, shares, owned, width).transpose(2, 0, 1, 3)
    return back.reshape(owned, planes, flat)


def solution(mesh):
    placed = (
        P("func", "rep", None),
        P("func", None),
        P("func", None, None),
        P("rep", "func", None),
        P(),
        P("rep", "func", None),
        P(),
    )
    return jax.shard_map(
        shards, mesh=mesh, in_specs=placed, out_specs=P("func", "rep", None), check_vma=False
    )
```

time: 1660 us -> 477 us (0.29); the launches traced: 1640 us -> 474 us
  local copies, waits for them, and re-layouts: 1170 us -> 12 us
  Pallas kernels: 0 us -> 105 us
  waiting for transfers between devices: 156 us -> 252 us
  starting transfers between devices: 83.7 us -> 13.1 us
  other arithmetic: 70 us -> 2.81 us
  matrix products: 59.8 us -> 0 us
    gather x676 -> x0, local copies, waits for them, and re-layouts: 1070 us -> none
    all_gather x4 -> x3, waiting for transfers between devices: 0.04 us -> 251 us  [the longest x1 154 us: shards(): pot = lax.all_gather(half, ('rep', 'func'), axis=0, tiled=True)]
    all_to_all x5 -> x2, waiting for transfers between devices: 151 us -> 0.01 us  [exchange(): return lax.all_to_all(rows, 'func', split_axis=0, concat_axis=0, tiled=True)]
    pallas_call x0 -> x3, Pallas kernels: none -> 105 us  [the longest x1 62.6 us: make_hphi(): pl.pallas_call(hphi_kernel, out_shape=jax.ShapeDtypeStruct((planes, owned...]
    all_to_all x5 -> x2, starting transfers between devices: 79.6 us -> 13 us  [exchange(): return lax.all_to_all(rows, 'func', split_axis=0, concat_axis=0, tiled=True)]
    convert_element_type x5 -> x1, other arithmetic: 63.6 us -> 1.55 us  [planar_band(): return band.astype(jnp.bfloat16)]
    dot_general x5 -> x0, matrix products: 59.8 us -> none  [the longest x3 54.6 us: apply_blocks(): jnp.einsum('ikab,ikbp->iap', blocks, grouped_rows, preferred_element_type...]
    reshape x4 -> x1, local copies, waits for them, and re-layouts: 45.4 us -> 3.39 us  [shards(): return back.reshape(owned, planes, flat)]
  transfers between devices with their start and end apart: 12 -> 6, of which waited for: 3 -> 2; matrix products, arithmetic and copies ran while one was open for 75% -> 2% of each run, Pallas kernels for 0% -> 20%
where the time goes in v1:
time: 477 us; the launch traced here: 474 us
  waiting for transfers between devices  252 us (53%)
  Pallas kernels  105 us (22%)
  blocking collectives  76 us (16%)
  between operations  13.2 us (3%)
  starting transfers between devices  13.1 us (3%)
  local copies, waits for them, and re-layouts  12 us (3%)
    all_gather x1, waiting for transfers between devices, shards(): pot = lax.all_gather(half, ('rep', 'func'), axis=0, tiled=True)  154 us
    all_gather x1, waiting for transfers between devices, shards(): lax.all_gather(hamiltonian, ('rep', 'func'), axis=1, tiled=True)  96.7 us
    all_to_all x1, blocking collectives, exchange(): return lax.all_to_all(rows, 'func', split_axis=0, concat_axis=0, tiled=True)  76 us
    pallas_call x1, Pallas kernels, make_hphi(): pl.pallas_call(hphi_kernel, out_shape=jax.ShapeDtypeStruct((planes, owned...  62.6 us
    pallas_call x1, Pallas kernels, first_products(): pl.pallas_call(first_kernel, out_shape=[jax.ShapeDtypeStruct((NF, NF), jn...  31.9 us
    all_to_all x2, starting transfers between devices, exchange(): return lax.all_to_all(rows, 'func', split_axis=0, concat_axis=0, tiled=True)  13 us
    pallas_call x1, Pallas kernels, last_product(): pl.pallas_call(last_kernel, out_shape=jax.ShapeDtypeStruct((NF, width), j...  10.3 us
  transfers between devices with their start and end apart: 6, of which 2 were waited for; matrix products, arithmetic and copies ran while one was open for 2% of the time, Pallas kernels for 20%

profile of v1, /device:TPU:0, one launch (start us, length us, event | category | flops | bytes accessed | tf_op | source)
XLA Modules:
  0.0 473.9 jit_solution(17530069190486098578)
XLA Ops:
  6.5 0.0 copy-start
  6.5 0.0 all-gather.8.cloned.1.call-start
  6.5 1.6 copy-done
  8.1 0.9 dynamic-slice_convert_fusion
  9.1 0.0 all-gather.8.cloned.1.call-update
  9.1 0.0 all-gather.4.cloned.1.call-start
  9.1 0.7 all-gather.4.cloned.1.call-update
  9.8 5.3 %copy.17 = bf16[96,16,1024]{2,0,1:T(8,128)(2,1)} copy(bf16[96,16,1024]{2,1,0:T(8,128)(2,1)} %param.7) | data formatting | bytes 6291456 | tf_op args[0]
  15.1 0.0 copy-start.2
  15.1 8.5 %all-to-all-start = ((bf16[16,96,1024]{2,1,0:T(8,128)(2,1)}), bf16[16,96,1024]{2,1,0:T(8,128)(2,1)}, u32[]{:S(2)}, u32[]{:S(2)}) async-start(bf16[16,96,1024]{2,1,0:T(8,128)(2,1)} %bitcast.16), calls=%async_computation | async-start | bytes 6291456 | tf_op jit(solution)/shard_map/all_to_all | solution.py:245
  23.6 0.0 all-gather.6.cloned.1.call-start
  23.7 0.7 all-gather.6.cloned.1.call-update
  24.4 1.2 slice_select_fusion
  25.5 0.1 collective-permute-start
  25.6 0.1 pad.2.clone
  25.7 0.0 copy-done.2
  25.7 0.1 add_add_fusion
  25.8 0.7 copy.14.info
  26.5 1.5 select_convert_fusion.band
  28.1 0.0 collective-permute-done.halo
  28.1 0.0 copy-start.1
  28.1 153.8 %all-gather.8.cloned.1.call-done = bf16[1024,4,16,128]{3,2,1,0:T(8,128)(2,1)} async-done(((bf16[32,4,16,128]{3,2,1,0:T(8,128)(2,1)}), bf16[1024,4,16,128]{3,2,1,0:T(8,128)(2,1)}) %all-gather.8.cloned.1.call-update) | async-done | bytes 16777232 | tf_op jit(solution)/shard_map/all_gather | solution.py:253
  181.8 0.0 copy-done.1
  181.8 62.6 %hphi.1 = bf16[16,96,1024]{2,1,0:T(8,128)(2,1)} custom-call(s32[96,4]{1,0:T(8,128)} %copy.14.info, bf16[16,96,1024]{2,1,0:T(8,128)(2,1)} %bitcast.18, bf16[2,96,1024]{2,1,0:T(8,128)(2,1)} %copy-done.1, bf16[512,256]{1,0:T(8,128)(2,1)} %select_convert_fusion.band, bf16[2,512,4,16,128]{4,3,2,1,0:T(8,128)(2,1)} %bitcast.19), custom_call_target="tpu_custom_call" | custom-call | flops 1610612736 | bytes 31457280 | tf_op jit(solution)/shard_map/hphi/pallas_call | solution.py:147
  244.5 0.0 all-to-all-done
  244.5 4.5 all-to-all-start.1
  249.0 0.0 all-gather.4.cloned.1.call-done
  249.0 96.7 %all-gather.6.cloned.1.call-done = bf16[1,18432,128]{2,1,0:T(8,128)(2,1)} async-done(((bf16[1,576,128]{2,1,0:T(8,128)(2,1)}), bf16[1,18432,128]{2,1,0:T(8,128)(2,1)}) %all-gather.6.cloned.1.call-update) | async-done | bytes 4718608 | tf_op jit(solution)/shard_map/all_gather | solution.py:266
  345.8 31.9 %products.1 = (bf16[1536,1536]{1,0:T(8,128)(2,1)}, f32[1536,1024]{1,0:T(8,128)}) custom-call(s32[12,12]{1,0:T(8,128)} %k_cols.1, s32[12,12]{1,0:T(8,128)} %h_cols.1, bf16[18432,128]{1,0:T(8,128)(2,1)} %bitcast.23, bf16[18432,128]{1,0:T(8,128)(2,1)} %bitcast.24, bf16[1536,1024]{1,0:T(8,128)(2,1)} %bitcast.3.phi), custom_call_target="tpu_custom_call" | custom-call | flops 9663676416 | bytes 25165824 | tf_op jit(solution)/shard_map/products/pallas_call | solution.py:197
  377.6 0.0 all-to-all-done.1
  377.7 10.3 %gradient.1 = bf16[1536,1024]{1,0:T(8,128)(2,1)} custom-call(bf16[1536,1536]{1,0:T(8,128)(2,1)} %get-tuple-element.7.dense_k, bf16[1536,1024]{1,0:T(8,128)(2,1)} %bitcast.6.hphi, f32[1536,1024]{1,0:T(8,128)} %get-tuple-element.8.product), custom_call_target="tpu_custom_call" | custom-call | flops 4831838208 | bytes 17825792 | tf_op jit(solution)/shard_map/gradient/pallas_call | solution.py:221
  388.0 76.0 %all_to_all.15 = bf16[16,96,1024]{2,1,0:T(8,128)(2,1)S(1)} all-to-all(bf16[16,96,1024]{2,1,0:T(8,128)(2,1)} %bitcast.21), channel_id=1, replica_groups=mesh['func'=16,'rep'=2] {'func'}, dimensions={0} | all-to-all | bytes 6291456 | tf_op jit(solution)/shard_map/all_to_all | solution.py:245
  463.9 3.4 copy.15
  (8 shorter events, 0.0 us)
Async XLA Ops:
  6.5 1.6 copy-start
  6.5 175.3 %all-gather.8.cloned.1.call-start = ((), (), s32[]{:S(2)}) async-start(), calls=%async_computation.5 | async-start | bytes 17301504 | tf_op jit(solution)/shard_map/all_gather | solution.py:253
  9.1 239.9 %all-gather.4.cloned.1.call-start = ((), (), s32[]{:S(2)}) async-start(), calls=%async_computation.3 | async-start | bytes 4866048 | tf_op jit(solution)/shard_map/all_gather | solution.py:265
  15.1 10.6 %copy-start.2 = (s32[96,3]{0,1:T(4,128)S(1)}, s32[96,3]{0,1:T(4,128)}, u32[]{:S(2)}) copy-start(s32[96,3]{0,1:T(4,128)} %param.8) | copy-start | bytes 3460
  15.1 229.4 %all-to-all-start = ((bf16[16,96,1024]{2,1,0:T(8,128)(2,1)}), bf16[16,96,1024]{2,1,0:T(8,128)(2,1)}, u32[]{:S(2)}, u32[]{:S(2)}) async-start(bf16[16,96,1024]{2,1,0:T(8,128)(2,1)} %bitcast.16), calls=%async_computation | async-start | bytes 6291456 | tf_op jit(solution)/shard_map/all_to_all | solution.py:245
  23.6 322.1 %all-gather.6.cloned.1.call-start = ((), (), s32[]{:S(2)}) async-start(), calls=%async_computation.4 | async-start | bytes 4866048 | tf_op jit(solution)/shard_map/all_gather | solution.py:266
  25.5 2.6 collective-permute-start
  28.1 153.8 %copy-start.1 = (bf16[2,96,1024]{2,1,0:T(8,128)(2,1)}, bf16[2,96,1024]{2,1,0:T(8,128)(2,1)S(1)}, u32[]{:S(2)}) copy-start(bf16[2,96,1024]{2,1,0:T(8,128)(2,1)S(1)} %collective-permute-done.halo) | copy-start | bytes 1179652
  244.5 133.1 %all-to-all-start.1 = ((bf16[16,96,1024]{2,1,0:T(8,128)(2,1)}), bf16[16,96,1024]{2,1,0:T(8,128)(2,1)}, u32[]{:S(2)}, u32[]{:S(2)}) async-start(bf16[16,96,1024]{2,1,0:T(8,128)(2,1)} %hphi.1), calls=%async_computation.1 | async-start | bytes 6291456 | tf_op jit(solution)/shard_map/all_to_all | solution.py:245
Sparse Core Ops, SparseCore 0:
  10.3 171.4 all-gather.7
  184.7 61.7 all-gather.3
  249.4 96.3 all-gather.5

commit v2 on v1

--- a/solution.py
+++ b/solution.py
@@ -15,6 +15,8 @@
 GROUP = 16
 COLS = 256
 VMEM = 56 * 1024 * 1024
+SLOTS = 8
+PIECES = 2
 
 CENTRE = 90.0
 NEAR = -16.0
@@ -41,7 +43,7 @@
     planes, group, flat = phi.shape
     step = pl.program_id(0)
     total = pl.num_programs(0) * group
-    x_blocks = pot.shape[2]
+    x_blocks = pot.shape[1]
     span = 3 * ROWS
     flag = info[0, 3].astype(jnp.float32)
 
@@ -53,7 +55,7 @@
             block = lax.rem(first + k, 2 * x_blocks)
             out_list.append(
                 pltpu.make_async_copy(
-                    pot.at[block // x_blocks, pl.ds(z, planes), lax.rem(block, x_blocks)],
+                    pot.at[block // x_blocks, lax.rem(block, x_blocks), pl.ds(z, planes)],
                     buf.at[slot, k],
                     sems.at[slot, k],
                 )
@@ -62,18 +64,20 @@
 
     @pl.when(step == 0)
     def _():
-        for copy in copies(0, 0):
-            copy.start()
+        for early in range(SLOTS - 1):
+            for copy in copies(early, early):
+                copy.start()
 
     lane = lax.broadcasted_iota(jnp.int32, (8, LANES), 1)
 
     def one_function(f, carry):
         index = step * group + f
-        slot = lax.rem(index, 2)
-
-        @pl.when(index + 1 < total)
+        slot = lax.rem(index, SLOTS)
+        ahead = index + SLOTS - 1
+
+        @pl.when(ahead < total)
         def _():
-            for copy in copies(index + 1, 1 - slot):
+            for copy in copies(ahead, lax.rem(ahead, SLOTS)):
                 copy.start()
 
         for copy in copies(index, slot):
@@ -125,7 +129,6 @@
 
 def make_hphi(info, phi, halo, band, pot):
     planes, owned, flat = phi.shape
-    x_blocks = pot.shape[2]
     span = 3 * ROWS
     grid_spec = pltpu.PrefetchScalarGridSpec(
         num_scalar_prefetch=1,
@@ -138,10 +141,10 @@
         ],
         out_specs=pl.BlockSpec((planes, GROUP, flat), lambda i, s: (0, i, 0)),
         scratch_shapes=[
-            pltpu.VMEM((2, 3, planes, ROWS, LANES), jnp.bfloat16),
+            pltpu.VMEM((SLOTS, 3, planes, ROWS, LANES), jnp.bfloat16),
             pltpu.VMEM((planes * span, LANES), jnp.float32),
             pltpu.VMEM((flat // LANES * planes * GROUP, LANES), jnp.float32),
-            pltpu.SemaphoreType.DMA((2, 3)),
+            pltpu.SemaphoreType.DMA((SLOTS, 3)),
         ],
     )
     return pl.pallas_call(
@@ -232,6 +235,48 @@
     )(dense_k, hphi, product)
 
 
+SIDES = (4, 2, 2)
+
+
+def place_of():
+    me = lax.axis_index("func")
+    return me // 4, (me // 2) % 2, me % 2
+
+
+def along_z(part):
+    z = place_of()[0]
+    n = lax.axis_size("func")
+    held = [part]
+    for k in range(1, 4):
+        held.append(lax.ppermute(part, "func", [(i, (i + 4 * k) % n) for i in range(n)]))
+
+    def at(level):
+        taken = held[0]
+        for k in range(1, 4):
+            taken = jnp.where((z - level) % 4 == k, held[k], taken)
+        return taken
+
+    return jnp.stack([at(level) for level in range(4)])
+
+
+def swapped(block, bit):
+    n = lax.axis_size("func")
+    return lax.ppermute(block, "func", [(i, i ^ bit) for i in range(n)])
+
+
+def other_core(block):
+    return lax.ppermute(block, "rep", [(0, 1), (1, 0)])
+
+
+def put(whole, piece, blocks, core):
+    _, y, x = place_of()
+    for block, (to_y, to_x) in zip(blocks, ((y, x), (y, 1 - x), (1 - y, x), (1 - y, 1 - x))):
+        rest = whole.ndim - 5
+        start = (core, piece, 0, to_y, to_x) + (0,) * rest
+        whole = lax.dynamic_update_slice(whole, block, start)
+    return whole
+
+
 def shards(orbitals, centres, potential, kernel, kernel_cols, hamiltonian, intersection_cols):
     rep = lax.axis_index("rep")
     n_func = lax.axis_size("func")
@@ -240,20 +285,19 @@
     z_planes, x_size, y_size = potential.shape
     shares = n_func // planes
     width = flat // shares
+    x_blocks = x_size // n_rep // ROWS
 
     def exchange(rows):
         return lax.all_to_all(rows, "func", split_axis=0, concat_axis=0, tiled=True)
 
-    def to_points(plane_rows):
-        cut = plane_rows.reshape(planes, owned, shares, width).transpose(0, 2, 1, 3)
-        return exchange(cut.reshape(n_func, owned, width)).reshape(n_func * owned, width)
+    def cut(plane_rows):
+        pieces = plane_rows.reshape(planes, owned, shares, width).transpose(0, 2, 1, 3)
+        return pieces.reshape(n_func, owned, width)
 
     half = lax.dynamic_slice_in_dim(potential, rep * (x_size // n_rep), x_size // n_rep, axis=1)
-    half = half.astype(jnp.bfloat16).reshape(z_planes, x_size // n_rep // ROWS, ROWS, y_size)
-    pot = lax.all_gather(half, ("rep", "func"), axis=0, tiled=True)
-    pot = pot.reshape(n_rep, n_func * z_planes, x_size // n_rep // ROWS, ROWS, y_size)
-
+    half = half.astype(jnp.bfloat16).reshape(z_planes, x_blocks, ROWS, y_size).transpose(1, 0, 2, 3)
     phi_planes = orbitals.transpose(1, 0, 2)
+    phi_cut = cut(phi_planes)
     edge = jnp.where(rep == 0, phi_planes[planes - 2 :], phi_planes[:2])
     halo = lax.ppermute(edge, "rep", [(0, 1), (1, 0)])
     flag = jnp.full((owned, 1), rep, jnp.int32)
@@ -261,9 +305,43 @@
         [centres[:, :1] + planes * rep, centres[:, 1:], flag], axis=1
     ).astype(jnp.int32)
 
-    phi_pts = to_points(phi_planes)
-    k_blocks = lax.all_gather(kernel, ("rep", "func"), axis=1, tiled=True).reshape(-1, BLK)
-    h_blocks = lax.all_gather(hamiltonian, ("rep", "func"), axis=1, tiled=True).reshape(-1, BLK)
+    if n_func == 16:
+        per = x_blocks // PIECES
+        lines = [along_z(half[p * per : (p + 1) * per]) for p in range(PIECES)]
+        lines, phi_cut = lax.optimization_barrier((lines, phi_cut))
+        phi_pts = exchange(phi_cut)
+        near = [swapped(lines[p], 1 + p) for p in range(PIECES)]
+        far = [(swapped(lines[p], 2 - p), swapped(near[p], 2 - p)) for p in range(PIECES)]
+        pot = jnp.zeros((n_rep, x_blocks) + SIDES + (z_planes, ROWS, y_size), jnp.bfloat16)
+        for p in range(PIECES):
+            blocks = [lines[p], near[p], *far[p]] if p == 0 else [lines[p], far[p][0], near[p], far[p][1]]
+            for core, group in ((rep, blocks), (1 - rep, [other_core(b) for b in blocks])):
+                laid = [b.transpose(1, 0, 2, 3, 4)[None, :, :, None, None] for b in group]
+                pot = put(pot, per * p, laid, core)
+        pot = pot.reshape(n_rep, x_blocks, n_func * z_planes, ROWS, y_size)
+
+        near, kernel, hamiltonian = lax.optimization_barrier((near, kernel, hamiltonian))
+        gathered = []
+        for p, stored in enumerate((kernel, hamiltonian)):
+            line = along_z(stored[0])
+            close = swapped(line, 1 + p)
+            rest = (swapped(line, 2 - p), swapped(close, 2 - p))
+            blocks = [line, close, *rest] if p == 0 else [line, rest[0], close, rest[1]]
+            whole = jnp.zeros((n_rep, 1) + SIDES + stored.shape[1:], jnp.bfloat16)
+            for core, group in ((rep, blocks), (1 - rep, [other_core(b) for b in blocks])):
+                whole = put(whole, 0, [b[None, None, :, None, None] for b in group], core)
+            gathered.append(whole.reshape(-1, BLK))
+        k_blocks, h_blocks = gathered
+    else:
+        pot = lax.all_gather(half, ("rep", "func"), axis=0, tiled=False)
+        pot = pot.reshape(n_rep, n_func, x_blocks, z_planes, ROWS, y_size)
+        pot = pot.transpose(0, 2, 1, 3, 4, 5)
+        pot = pot.reshape(n_rep, x_blocks, n_func * z_planes, ROWS, y_size)
+        phi_pts = exchange(phi_cut)
+        k_blocks, h_blocks = (
+            lax.all_gather(stored, ("rep", "func"), axis=1, tiled=True).reshape(-1, BLK)
+            for stored in (kernel, hamiltonian)
+        )
 
     extra = -owned % GROUP
     padded = [
@@ -272,8 +350,9 @@
         jnp.pad(halo, ((0, 0), (0, extra), (0, 0))),
     ]
     hphi = make_hphi(*padded, planar_band(), pot)[:, :owned]
+    phi_pts = phi_pts.reshape(n_func * owned, width)
     dense_k, product = first_products(kernel_cols, intersection_cols, k_blocks, h_blocks, phi_pts)
-    hphi_pts = to_points(hphi)
+    hphi_pts = exchange(cut(hphi)).reshape(n_func * owned, width)
     gradient = last_product(dense_k, hphi_pts, product)
     back = exchange(gradient.reshape(n_func, owned, width))
     back = back.reshape(planes, shares, owned, width).transpose(2, 0, 1, 3)

time: 477 us -> 490 us (1.027)
  starting transfers between devices: 13.1 us -> 94.8 us
  waiting for transfers between devices: 252 us -> 196 us
  Pallas kernels: 105 us -> 71.7 us
  local copies, waits for them, and re-layouts: 12 us -> 44.8 us
  between operations: 13.2 us -> 0.4 us
    all_gather x3 -> x0, waiting for transfers between devices: 251 us -> none  [the longest x1 154 us: shards(): pot = lax.all_gather(half, ('rep', 'func'), axis=0, tiled=True)]
    ppermute x0 -> x40, waiting for transfers between devices: none -> 196 us  [the longest x12 111 us: swapped(): return lax.ppermute(block, 'func', [(i, i ^ bit) for i in range(n)])]
    ppermute x0 -> x40, starting transfers between devices: none -> 79.6 us  [the longest x12 53.6 us: along_z(): lax.ppermute(part, 'func', [(i, (i + 4 * k) % n) for i in range(n)])]
    pallas_call x1, Pallas kernels: 62.6 us -> 29.5 us  [make_hphi(): pl.pallas_call(hphi_kernel, out_shape=jax.ShapeDtypeStruct((planes, owned...]
    dynamic_update_slice x0 -> x30, local copies, waits for them, and re-layouts: none -> 21.2 us  [put(): whole = lax.dynamic_update_slice(whole, block, start)]
    broadcast_in_dim x0 -> x1, local copies, waits for them, and re-layouts: none -> 6.22 us  [shards(): jnp.zeros((n_rep, x_blocks) + SIDES + (z_planes, ROWS, y_size), jnp.bfloa...]
    unnamed x7 -> x17, local copies, waits for them, and re-layouts: 6.88 us -> 11 us
  transfers between devices with their start and end apart: 6 -> 43, of which waited for: 2 -> 17; matrix products, arithmetic and copies ran while one was open for 2% -> 8% of each run, Pallas kernels for 20% -> 13%
where the time goes in v2:
time: 490 us; the launch traced here: 489 us
  waiting for transfers between devices  196 us (40%)
  starting transfers between devices  94.8 us (19%)
  blocking collectives  78.1 us (16%)
  Pallas kernels  71.7 us (15%)
  local copies, waits for them, and re-layouts  44.8 us (9%)
    ppermute x12, waiting for transfers between devices, swapped(): return lax.ppermute(block, 'func', [(i, i ^ bit) for i in range(n)])  111 us
    ppermute x12, waiting for transfers between devices, along_z(): lax.ppermute(part, 'func', [(i, (i + 4 * k) % n) for i in range(n)])  83 us
    all_to_all x1, blocking collectives, exchange(): return lax.all_to_all(rows, 'func', split_axis=0, concat_axis=0, tiled=True)  78.1 us
    ppermute x12, starting transfers between devices, along_z(): lax.ppermute(part, 'func', [(i, (i + 4 * k) % n) for i in range(n)])  53.6 us
    pallas_call x1, Pallas kernels, first_products(): pl.pallas_call(first_kernel, out_shape=[jax.ShapeDtypeStruct((NF, NF), jn...  31.9 us
    pallas_call x1, Pallas kernels, make_hphi(): pl.pallas_call(hphi_kernel, out_shape=jax.ShapeDtypeStruct((planes, owned...  29.5 us
    ppermute x12, starting transfers between devices, swapped(): return lax.ppermute(block, 'func', [(i, i ^ bit) for i in range(n)])  23.2 us
    dynamic_update_slice x30, local copies, waits for them, and re-layouts, put(): whole = lax.dynamic_update_slice(whole, block, start)  21.2 us
  transfers between devices with their start and end apart: 43, of which 17 were waited for; matrix products, arithmetic and copies ran while one was open for 8% of the time, Pallas kernels for 13%

profile of v2, /device:TPU:0, one launch (start us, length us, event | category | flops | bytes accessed | tf_op | source)
XLA Modules:
  0.0 489.3 jit_solution(12768919486103387422)
XLA Ops:
  0.0 1.6 copy-done
  1.8 5.1 %collective-permute-start.3 = (bf16[2,32,16,128]{3,2,1,0:T(8,128)(2,1)S(1)}, bf16[2,32,16,128]{3,2,1,0:T(8,128)(2,1)S(1)}, u32[]{:S(2)}, u32[]{:S(2)}) collective-permute-start(bf16[2,32,16,128]{3,2,1,0:T(8,128)(2,1)S(1)} %get-tuple-element.35), channel_id=1, source_target_pairs={{0,24},{2,26},{4,28},{6,30},{8,0},{10,2},{12,4},{14,6},{16,8},{18,... | collective-permute-start | bytes 786440 | tf_op jit(solution)/shard_map/ppermute | solution.py:251
  7.9 2.8 collective-permute-start
  11.8 5.3 %copy.96 = bf16[96,16,1024]{2,0,1:T(8,128)(2,1)} copy(bf16[96,16,1024]{2,1,0:T(8,128)(2,1)} %param.7) | data formatting | bytes 6291456 | tf_op args[0]
  17.2 7.0 %collective-permute-start.2 = (bf16[2,32,16,128]{3,2,1,0:T(8,128)(2,1)S(1)}, bf16[2,32,16,128]{3,2,1,0:T(8,128)(2,1)S(1)}, u32[]{:S(2)}, u32[]{:S(2)}) collective-permute-start(bf16[2,32,16,128]{3,2,1,0:T(8,128)(2,1)S(1)} %get-tuple-element.36), channel_id=1, source_target_pairs={{0,8},{2,10},{4,12},{6,14},{8,16},{10,18},{12,20},{14,22},{16,24},... | collective-permute-start | bytes 786440 | tf_op jit(solution)/shard_map/ppermute | solution.py:251
  24.2 7.3 %collective-permute-done.4 = bf16[2,32,16,128]{3,2,1,0:T(8,128)(2,1)S(1)} collective-permute-done((bf16[2,32,16,128]{3,2,1,0:T(8,128)(2,1)S(1)}, bf16[2,32,16,128]{3,2,1,0:T(8,128)(2,1)S(1)}, u32[]{:S(2)}, u32[]{:S(2)}) %collective-permute-start.4) | collective-permute-done | bytes 262176 | tf_op jit(solution)/shard_map/ppermute | solution.py:251
  31.8 19.9 %collective-permute-done.1 = bf16[2,32,16,128]{3,2,1,0:T(8,128)(2,1)S(1)} collective-permute-done((bf16[2,32,16,128]{3,2,1,0:T(8,128)(2,1)S(1)}, bf16[2,32,16,128]{3,2,1,0:T(8,128)(2,1)S(1)}, u32[]{:S(2)}, u32[]{:S(2)}) %collective-permute-start.1) | collective-permute-done | bytes 262176 | tf_op jit(solution)/shard_map/ppermute | solution.py:251
  51.9 1.6 collective-permute-start.6
  53.5 5.2 %all-to-all-start = ((bf16[16,96,1024]{2,1,0:T(8,128)(2,1)}), bf16[16,96,1024]{2,1,0:T(8,128)(2,1)}, u32[]{:S(2)}, u32[]{:S(2)}) async-start(bf16[16,96,1024]{2,1,0:T(8,128)(2,1)} %bitcast.215.phi), calls=%async_computation | async-start | bytes 6291456 | tf_op jit(solution)/shard_map/all_to_all | solution.py:291
  59.5 1.9 collective-permute-start.29
  62.9 15.3 %collective-permute-done.6 = bf16[4,2,32,16,128]{4,3,2,1,0:T(8,128)(2,1)} collective-permute-done((bf16[4,2,32,16,128]{4,3,2,1,0:T(8,128)(2,1)S(1)}, bf16[4,2,32,16,128]{4,3,2,1,0:T(8,128)(2,1)}, u32[]{:S(2)}, u32[]{:S(2)}) %collective-permute-start.6) | collective-permute-done | bytes 1048608 | tf_op jit(solution)/shard_map/ppermute | solution.py:264
  78.2 2.5 collective-permute-start.30
  80.8 1.5 select_convert_fusion.band
  82.3 6.2 %broadcast_in_dim.138 = bf16[2,4,4,2,2,32,16,128]{7,6,5,4,3,2,1,0:T(8,128)(2,1)} broadcast(bf16[]{:T(256)} %constant.257.clone.1), dimensions={} | broadcast | bytes 16777218 | tf_op jit(solution)/shard_map/broadcast_in_dim | solution.py:315
  89.7 24.4 %collective-permute-done.29 = bf16[4,2,32,16,128]{4,3,2,1,0:T(8,128)(2,1)S(1)} collective-permute-done((bf16[4,2,32,16,128]{4,3,2,1,0:T(8,128)(2,1)S(1)}, bf16[4,2,32,16,128]{4,3,2,1,0:T(8,128)(2,1)S(1)}, u32[]{:S(2)}, u32[]{:S(2)}) %collective-permute-start.29) | collective-permute-done | bytes 1048608 | tf_op jit(solution)/shard_map/ppermute | solution.py:264
  114.1 2.4 copy_dynamic-update-slice_fusion.6
  117.7 3.9 collective-permute-start.35
  121.6 18.2 %collective-permute-done.7 = bf16[4,2,32,16,128]{4,3,2,0,1:T(8,128)(2,1)S(1)} collective-permute-done((bf16[4,2,32,16,128]{4,3,2,0,1:T(8,128)(2,1)S(1)}, bf16[4,2,32,16,128]{4,3,2,0,1:T(8,128)(2,1)S(1)}, u32[]{:S(2)}, u32[]{:S(2)}) %collective-permute-start.7) | collective-permute-done | bytes 1048608 | tf_op jit(solution)/shard_map/ppermute | solution.py:264
  139.8 1.5 collective-permute-start.36
  141.2 19.9 %collective-permute-done.30 = bf16[4,2,32,16,128]{4,3,2,1,0:T(8,128)(2,1)S(1)} collective-permute-done((bf16[4,2,32,16,128]{4,3,2,1,0:T(8,128)(2,1)}, bf16[4,2,32,16,128]{4,3,2,1,0:T(8,128)(2,1)S(1)}, u32[]{:S(2)}, u32[]{:S(2)}) %collective-permute-start.30) | collective-permute-done | bytes 1048608 | tf_op jit(solution)/shard_map/ppermute | solution.py:264
  171.9 1.2 bitcast_dynamic-update-slice_fusion.5
  177.8 1.3 bitcast_dynamic-update-slice_fusion
  179.9 29.5 %hphi.1 = bf16[16,96,1024]{2,1,0:T(8,128)(2,1)} custom-call(s32[96,4]{1,0:T(8,128)} %copy.84.info, bf16[16,96,1024]{2,1,0:T(8,128)(2,1)} %bitcast.215.phi, bf16[2,96,1024]{2,1,0:T(8,128)(2,1)} %copy-done.4, bf16[512,256]{1,0:T(8,128)(2,1)} %select_convert_fusion.band, bf16[2,4,512,16,128]{4,3,2,1,0:T(8,128)(2,1)} %bitcast.98.pot), custom_call_target="tpu_custom_call" | custom-call | flops 1610612736 | bytes 31457280 | tf_op jit(solution)/shard_map/hphi/pallas_call | solution.py:150
  209.4 9.4 %all-to-all-start.1 = ((bf16[16,96,1024]{2,1,0:T(8,128)(2,1)}), bf16[16,96,1024]{2,1,0:T(8,128)(2,1)}, u32[]{:S(2)}, u32[]{:S(2)}) async-start(bf16[16,96,1024]{2,1,0:T(8,128)(2,1)} %hphi.1), calls=%async_computation.1 | async-start | bytes 6291456 | tf_op jit(solution)/shard_map/all_to_all | solution.py:291
  218.9 3.7 collective-permute-start.18
  223.7 2.4 collective-permute-start.10
  226.1 1.5 collective-permute-start.8
  227.6 47.5 %collective-permute-done.18 = bf16[576,128]{1,0:T(8,128)(2,1)S(1)} collective-permute-done((bf16[576,128]{1,0:T(8,128)(2,1)S(1)}, bf16[576,128]{1,0:T(8,128)(2,1)S(1)}, u32[]{:S(2)}, u32[]{:S(2)}) %collective-permute-start.18) | collective-permute-done | bytes 147488 | tf_op jit(solution)/shard_map/ppermute | solution.py:251
  275.1 27.9 %collective-permute-start.9 = (bf16[576,128]{1,0:T(8,128)(2,1)S(1)}, bf16[576,128]{1,0:T(8,128)(2,1)S(1)}, u32[]{:S(2)}, u32[]{:S(2)}) collective-permute-start(bf16[576,128]{1,0:T(8,128)(2,1)S(1)} %bitcast.230), channel_id=1, source_target_pairs={{0,16},{2,18},{4,20},{6,22},{8,24},{10,26},{12,28},{14,30},{16,0},... | collective-permute-start | bytes 442376 | tf_op jit(solution)/shard_map/ppermute | solution.py:251
  302.9 6.8 %collective-permute-done.19 = bf16[576,128]{1,0:T(8,128)(2,1)S(1)} collective-permute-done((bf16[576,128]{1,0:T(8,128)(2,1)S(1)}, bf16[576,128]{1,0:T(8,128)(2,1)S(1)}, u32[]{:S(2)}, u32[]{:S(2)}) %collective-permute-start.19) | collective-permute-done | bytes 147488 | tf_op jit(solution)/shard_map/ppermute | solution.py:251
  309.9 2.2 collective-permute-start.21
  312.1 1.3 collective-permute-start.22
  313.4 1.6 collective-permute-done.9
  315.2 2.2 collective-permute-start.11
  317.4 1.3 collective-permute-start.12
  321.0 2.6 collective-permute-done.21
  323.6 1.5 collective-permute-done.22
  325.1 1.5 collective-permute-start.23
  326.8 9.5 %collective-permute-done.11 = bf16[4,576,128]{2,1,0:T(8,128)(2,1)S(1)} collective-permute-done((bf16[4,576,128]{2,1,0:T(8,128)(2,1)S(1)}, bf16[4,576,128]{2,1,0:T(8,128)(2,1)S(1)}, u32[]{:S(2)}, u32[]{:S(2)}) %collective-permute-start.11) | collective-permute-done | bytes 589856 | tf_op jit(solution)/shard_map/ppermute | solution.py:264
  337.0 8.8 %collective-permute-done.23 = bf16[4,576,128]{2,1,0:T(8,128)(2,1)S(1)} collective-permute-done((bf16[4,576,128]{2,1,0:T(8,128)(2,1)S(1)}, bf16[4,576,128]{2,1,0:T(8,128)(2,1)S(1)}, u32[]{:S(2)}, u32[]{:S(2)}) %collective-permute-start.23) | collective-permute-done | bytes 589856 | tf_op jit(solution)/shard_map/ppermute | solution.py:264
  345.8 3.0 collective-permute-start.13
  349.7 9.6 %collective-permute-done.13 = bf16[4,576,128]{2,1,0:T(8,128)(2,1)S(1)} collective-permute-done((bf16[4,576,128]{2,1,0:T(8,128)(2,1)S(1)}, bf16[4,576,128]{2,1,0:T(8,128)(2,1)S(1)}, u32[]{:S(2)}, u32[]{:S(2)}) %collective-permute-start.13) | collective-permute-done | bytes 589856 | tf_op jit(solution)/shard_map/ppermute | solution.py:264
  362.2 1.3 copy-done.3
  363.5 2.1 copy-done.2
  365.6 31.9 %products.1 = (bf16[1536,1536]{1,0:T(8,128)(2,1)}, f32[1536,1024]{1,0:T(8,128)}) custom-call(s32[12,12]{1,0:T(8,128)} %k_cols.1, s32[12,12]{1,0:T(8,128)} %h_cols.1, bf16[18432,128]{1,0:T(8,128)(2,1)} %bitcast.221, bf16[18432,128]{1,0:T(8,128)(2,1)} %bitcast.222, bf16[1536,1024]{1,0:T(8,128)(2,1)} %bitcast.58.phi), custom_call_target="tpu_custom_call" | custom-call | flops 9663676416 | bytes 25165824 | tf_op jit(solution)/shard_map/products/pallas_call | solution.py:200
  397.5 10.3 %gradient.1 = bf16[1536,1024]{1,0:T(8,128)(2,1)} custom-call(bf16[1536,1536]{1,0:T(8,128)(2,1)} %get-tuple-element.17.dense_k, bf16[1536,1024]{1,0:T(8,128)(2,1)} %bitcast.99.hphi, f32[1536,1024]{1,0:T(8,128)} %get-tuple-element.18.product), custom_call_target="tpu_custom_call" | custom-call | flops 4831838208 | bytes 17825792 | tf_op jit(solution)/shard_map/gradient/pallas_call | solution.py:224
  407.8 78.1 %all_to_all.15 = bf16[16,96,1024]{2,1,0:T(8,128)(2,1)S(1)} all-to-all(bf16[16,96,1024]{2,1,0:T(8,128)(2,1)} %bitcast.223), channel_id=1, replica_groups=mesh['func'=16,'rep'=2] {'func'}, dimensions={0} | all-to-all | bytes 6291456 | tf_op jit(solution)/shard_map/all_to_all | solution.py:291
  485.9 3.4 copy.85
  (119 shorter events, 32.1 us)
Async XLA Ops:
  1.6 15.6 %copy-start.7 = (s32[96,3]{0,1:T(4,128)S(1)}, s32[96,3]{0,1:T(4,128)}, u32[]{:S(2)}) copy-start(s32[96,3]{0,1:T(4,128)} %param.8) | copy-start | bytes 3460
  1.8 15.4 %collective-permute-start.3 = (bf16[2,32,16,128]{3,2,1,0:T(8,128)(2,1)S(1)}, bf16[2,32,16,128]{3,2,1,0:T(8,128)(2,1)S(1)}, u32[]{:S(2)}, u32[]{:S(2)}) collective-permute-start(bf16[2,32,16,128]{3,2,1,0:T(8,128)(2,1)S(1)} %get-tuple-element.35), channel_id=1, source_target_pairs={{0,24},{2,26},{4,28},{6,30},{8,0},{10,2},{12,4},{14,6},{16,8},{18,... | collective-permute-start | bytes 786440 | tf_op jit(solution)/shard_map/ppermute | solution.py:251
  6.9 24.6 %collective-permute-start.4 = (bf16[2,32,16,128]{3,2,1,0:T(8,128)(2,1)S(1)}, bf16[2,32,16,128]{3,2,1,0:T(8,128)(2,1)S(1)}, u32[]{:S(2)}, u32[]{:S(2)}) collective-permute-start(bf16[2,32,16,128]{3,2,1,0:T(8,128)(2,1)S(1)} %get-tuple-element.35), channel_id=1, source_target_pairs={{0,16},{2,18},{4,20},{6,22},{8,24},{10,26},{12,28},{14,30},{16,0},... | collective-permute-start | bytes 786440 | tf_op jit(solution)/shard_map/ppermute | solution.py:251
  6.9 24.6 %collective-permute-start.5 = (bf16[2,32,16,128]{3,2,1,0:T(8,128)(2,1)S(1)}, bf16[2,32,16,128]{3,2,1,0:T(8,128)(2,1)S(1)}, u32[]{:S(2)}, u32[]{:S(2)}) collective-permute-start(bf16[2,32,16,128]{3,2,1,0:T(8,128)(2,1)S(1)} %get-tuple-element.35), channel_id=1, source_target_pairs={{0,8},{2,10},{4,12},{6,14},{8,16},{10,18},{12,20},{14,22},{16,24},... | collective-permute-start | bytes 786440 | tf_op jit(solution)/shard_map/ppermute | solution.py:251
  7.9 23.9 %collective-permute-start = (bf16[2,32,16,128]{3,2,1,0:T(8,128)(2,1)S(1)}, bf16[2,32,16,128]{3,2,1,0:T(8,128)(2,1)S(1)}, u32[]{:S(2)}, u32[]{:S(2)}) collective-permute-start(bf16[2,32,16,128]{3,2,1,0:T(8,128)(2,1)S(1)} %get-tuple-element.36), channel_id=1, source_target_pairs={{0,24},{2,26},{4,28},{6,30},{8,0},{10,2},{12,4},{14,6},{16,8},{18,... | collective-permute-start | bytes 786440 | tf_op jit(solution)/shard_map/ppermute | solution.py:251
  10.7 41.0 %collective-permute-start.1 = (bf16[2,32,16,128]{3,2,1,0:T(8,128)(2,1)S(1)}, bf16[2,32,16,128]{3,2,1,0:T(8,128)(2,1)S(1)}, u32[]{:S(2)}, u32[]{:S(2)}) collective-permute-start(bf16[2,32,16,128]{3,2,1,0:T(8,128)(2,1)S(1)} %get-tuple-element.36), channel_id=1, source_target_pairs={{0,16},{2,18},{4,20},{6,22},{8,24},{10,26},{12,28},{14,30},{16,0},... | collective-permute-start | bytes 786440 | tf_op jit(solution)/shard_map/ppermute | solution.py:251
  17.2 34.5 %collective-permute-start.2 = (bf16[2,32,16,128]{3,2,1,0:T(8,128)(2,1)S(1)}, bf16[2,32,16,128]{3,2,1,0:T(8,128)(2,1)S(1)}, u32[]{:S(2)}, u32[]{:S(2)}) collective-permute-start(bf16[2,32,16,128]{3,2,1,0:T(8,128)(2,1)S(1)} %get-tuple-element.36), channel_id=1, source_target_pairs={{0,8},{2,10},{4,12},{6,14},{8,16},{10,18},{12,20},{14,22},{16,24},... | collective-permute-start | bytes 786440 | tf_op jit(solution)/shard_map/ppermute | solution.py:251
  51.9 26.3 %collective-permute-start.6 = (bf16[4,2,32,16,128]{4,3,2,1,0:T(8,128)(2,1)S(1)}, bf16[4,2,32,16,128]{4,3,2,1,0:T(8,128)(2,1)}, u32[]{:S(2)}, u32[]{:S(2)}) collective-permute-start(bf16[4,2,32,16,128]{4,3,2,1,0:T(8,128)(2,1)S(1)} %pad_maximum_fusion), channel_id=1, source_target_pairs={{0,2},{2,0},{4,6},{6,4},{8,10},{10,8},{12,14},{14,12},{16,18},{18,... | collective-permute-start | bytes 3145736 | tf_op jit(solution)/shard_map/ppermute | solution.py:264
  53.5 155.9 %all-to-all-start = ((bf16[16,96,1024]{2,1,0:T(8,128)(2,1)}), bf16[16,96,1024]{2,1,0:T(8,128)(2,1)}, u32[]{:S(2)}, u32[]{:S(2)}) async-start(bf16[16,96,1024]{2,1,0:T(8,128)(2,1)} %bitcast.215.phi), calls=%async_computation | async-start | bytes 6291456 | tf_op jit(solution)/shard_map/all_to_all | solution.py:291
  59.5 54.6 %collective-permute-start.29 = (bf16[4,2,32,16,128]{4,3,2,1,0:T(8,128)(2,1)S(1)}, bf16[4,2,32,16,128]{4,3,2,1,0:T(8,128)(2,1)S(1)}, u32[]{:S(2)}, u32[]{:S(2)}) collective-permute-start(bf16[4,2,32,16,128]{4,3,2,1,0:T(8,128)(2,1)S(1)} %pad_maximum_fusion), channel_id=1, source_target_pairs={{0,4},{2,6},{4,0},{6,2},{8,12},{10,14},{12,8},{14,10},{16,20},{18,... | collective-permute-start | bytes 3145736 | tf_op jit(solution)/shard_map/ppermute | solution.py:264
  62.7 55.0 %collective-permute-start.31 = (bf16[4,2,32,16,128]{4,3,2,1,0:T(8,128)(2,1)S(1)}, bf16[4,2,32,16,128]{4,3,2,1,0:T(8,128)(2,1)S(1)}, u32[]{:S(2)}, u32[]{:S(2)}) collective-permute-start(bf16[4,2,32,16,128]{4,3,2,1,0:T(8,128)(2,1)S(1)} %pad_maximum_fusion), channel_id=1, source_target_pairs={{0,1},{1,0},{2,3},{3,2},{4,5},{5,4},{6,7},{7,6},{8,9},{9,8},{10,11... | collective-permute-start | bytes 3145736 | tf_op jit(solution)/shard_map/ppermute | solution.py:268
  62.7 77.0 %collective-permute-start.7 = (bf16[4,2,32,16,128]{4,3,2,0,1:T(8,128)(2,1)S(1)}, bf16[4,2,32,16,128]{4,3,2,0,1:T(8,128)(2,1)S(1)}, u32[]{:S(2)}, u32[]{:S(2)}) collective-permute-start(bf16[4,2,32,16,128]{4,3,2,0,1:T(8,128)(2,1)S(1)} %pad_maximum_fusion.1), channel_id=1, source_target_pairs={{0,4},{2,6},{4,0},{6,2},{8,12},{10,14},{12,8},{14,10},{16,20},{18,... | collective-permute-start | bytes 3145736 | tf_op jit(solution)/shard_map/ppermute | solution.py:264
  78.2 82.9 %collective-permute-start.30 = (bf16[4,2,32,16,128]{4,3,2,1,0:T(8,128)(2,1)}, bf16[4,2,32,16,128]{4,3,2,1,0:T(8,128)(2,1)S(1)}, u32[]{:S(2)}, u32[]{:S(2)}) collective-permute-start(bf16[4,2,32,16,128]{4,3,2,1,0:T(8,128)(2,1)} %collective-permute-done.6), channel_id=1, source_target_pairs={{0,4},{2,6},{4,0},{6,2},{8,12},{10,14},{12,8},{14,10},{16,20},{18,... | collective-permute-start | bytes 3145736 | tf_op jit(solution)/shard_map/ppermute | solution.py:264
  89.7 73.8 %collective-permute-start.32 = (bf16[4,2,32,16,128]{4,3,2,1,0:T(8,128)(2,1)}, bf16[4,2,32,16,128]{4,3,2,1,0:T(8,128)(2,1)S(1)}, u32[]{:S(2)}, u32[]{:S(2)}) collective-permute-start(bf16[4,2,32,16,128]{4,3,2,1,0:T(8,128)(2,1)} %collective-permute-done.6), channel_id=1, source_target_pairs={{0,1},{1,0},{2,3},{3,2},{4,5},{5,4},{6,7},{7,6},{8,9},{9,8},{10,11... | collective-permute-start | bytes 3145736 | tf_op jit(solution)/shard_map/ppermute | solution.py:268
  114.1 51.1 %collective-permute-start.33 = (bf16[4,2,32,16,128]{4,3,2,1,0:T(8,128)(2,1)S(1)}, bf16[4,2,32,16,128]{4,3,2,1,0:T(8,128)(2,1)S(1)}, u32[]{:S(2)}, u32[]{:S(2)}) collective-permute-start(bf16[4,2,32,16,128]{4,3,2,1,0:T(8,128)(2,1)S(1)} %collective-permute-done.29), channel_id=1, source_target_pairs={{0,1},{1,0},{2,3},{3,2},{4,5},{5,4},{6,7},{7,6},{8,9},{9,8},{10,11... | collective-permute-start | bytes 3145736 | tf_op jit(solution)/shard_map/ppermute | solution.py:268
  117.7 48.7 %collective-permute-start.35 = (bf16[4,2,32,16,128]{4,3,2,0,1:T(8,128)(2,1)S(1)}, bf16[4,2,32,16,128]{4,3,2,0,1:T(8,128)(2,1)S(1)}, u32[]{:S(2)}, u32[]{:S(2)}) collective-permute-start(bf16[4,2,32,16,128]{4,3,2,0,1:T(8,128)(2,1)S(1)} %pad_maximum_fusion.1), channel_id=1, source_target_pairs={{0,2},{2,0},{4,6},{6,4},{8,10},{10,8},{12,14},{14,12},{16,18},{18,... | collective-permute-start | bytes 3145736 | tf_op jit(solution)/shard_map/ppermute | solution.py:264
  139.8 28.1 %collective-permute-start.36 = (bf16[4,2,32,16,128]{4,3,2,0,1:T(8,128)(2,1)S(1)}, bf16[4,2,32,16,128]{4,3,2,0,1:T(8,128)(2,1)S(1)}, u32[]{:S(2)}, u32[]{:S(2)}) collective-permute-start(bf16[4,2,32,16,128]{4,3,2,0,1:T(8,128)(2,1)S(1)} %collective-permute-done.7), channel_id=1, source_target_pairs={{0,2},{2,0},{4,6},{6,4},{8,10},{10,8},{12,14},{14,12},{16,18},{18,... | collective-permute-start | bytes 3145736 | tf_op jit(solution)/shard_map/ppermute | solution.py:264
  161.2 6.7 %collective-permute-start.34 = (bf16[4,2,32,16,128]{4,3,2,1,0:T(8,128)(2,1)S(1)}, bf16[4,2,32,16,128]{4,3,2,1,0:T(8,128)(2,1)S(1)}, u32[]{:S(2)}, u32[]{:S(2)}) collective-permute-start(bf16[4,2,32,16,128]{4,3,2,1,0:T(8,128)(2,1)S(1)} %collective-permute-done.30), channel_id=1, source_target_pairs={{0,1},{1,0},{2,3},{3,2},{4,5},{5,4},{6,7},{7,6},{8,9},{9,8},{10,11... | collective-permute-start | bytes 3145736 | tf_op jit(solution)/shard_map/ppermute | solution.py:268
  163.5 15.6 %collective-permute-start.28 = (bf16[2,96,1024]{2,1,0:T(8,128)(2,1)S(1)}, bf16[2,96,1024]{2,1,0:T(8,128)(2,1)S(1)}, u32[]{:S(2)}, u32[]{:S(2)}) collective-permute-start(bf16[2,96,1024]{2,1,0:T(8,128)(2,1)S(1)} %slice_select_fusion), channel_id=1, source_target_pairs={{0,1},{1,0},{2,3},{3,2},{4,5},{5,4},{6,7},{7,6},{8,9},{9,8},{10,11... | collective-permute-start | bytes 1179656 | tf_op jit(solution)/shard_map/ppermute | solution.py:302
  165.2 9.1 %collective-permute-start.37 = (bf16[4,2,32,16,128]{4,3,2,0,1:T(8,128)(2,1)S(1)}, bf16[4,2,32,16,128]{4,3,2,0,1:T(8,128)(2,1)S(1)}, u32[]{:S(2)}, u32[]{:S(2)}) collective-permute-start(bf16[4,2,32,16,128]{4,3,2,0,1:T(8,128)(2,1)S(1)} %pad_maximum_fusion.1), channel_id=1, source_target_pairs={{0,1},{1,0},{2,3},{3,2},{4,5},{5,4},{6,7},{7,6},{8,9},{9,8},{10,11... | collective-permute-start | bytes 3145736 | tf_op jit(solution)/shard_map/ppermute | solution.py:268
  166.3 10.3 %collective-permute-start.39 = (bf16[4,2,32,16,128]{4,3,2,0,1:T(8,128)(2,1)S(1)}, bf16[4,2,32,16,128]{4,3,2,0,1:T(8,128)(2,1)S(1)}, u32[]{:S(2)}, u32[]{:S(2)}) collective-permute-start(bf16[4,2,32,16,128]{4,3,2,0,1:T(8,128)(2,1)S(1)} %collective-permute-done.7), channel_id=1, source_target_pairs={{0,1},{1,0},{2,3},{3,2},{4,5},{5,4},{6,7},{7,6},{8,9},{9,8},{10,11... | collective-permute-start | bytes 3145736 | tf_op jit(solution)/shard_map/ppermute | solution.py:268
  167.9 7.6 %collective-permute-start.38 = (bf16[4,2,32,16,128]{4,3,2,0,1:T(8,128)(2,1)S(1)}, bf16[4,2,32,16,128]{4,3,2,0,1:T(8,128)(2,1)S(1)}, u32[]{:S(2)}, u32[]{:S(2)}) collective-permute-start(bf16[4,2,32,16,128]{4,3,2,0,1:T(8,128)(2,1)S(1)} %collective-permute-done.35), channel_id=1, source_target_pairs={{0,1},{1,0},{2,3},{3,2},{4,5},{5,4},{6,7},{7,6},{8,9},{9,8},{10,11... | collective-permute-start | bytes 3145736 | tf_op jit(solution)/shard_map/ppermute | solution.py:268
  167.9 10.0 %collective-permute-start.40 = (bf16[4,2,32,16,128]{4,3,2,0,1:T(8,128)(2,1)S(1)}, bf16[4,2,32,16,128]{4,3,2,0,1:T(8,128)(2,1)S(1)}, u32[]{:S(2)}, u32[]{:S(2)}) collective-permute-start(bf16[4,2,32,16,128]{4,3,2,0,1:T(8,128)(2,1)S(1)} %collective-permute-done.36), channel_id=1, source_target_pairs={{0,1},{1,0},{2,3},{3,2},{4,5},{5,4},{6,7},{7,6},{8,9},{9,8},{10,11... | collective-permute-start | bytes 3145736 | tf_op jit(solution)/shard_map/ppermute | solution.py:268
  209.4 9.5 %copy-start.5 = (bf16[1,576,128]{2,1,0:T(8,128)(2,1)S(1)}, bf16[1,576,128]{2,1,0:T(8,128)(2,1)}, u32[]{:S(2)}) copy-start(bf16[1,576,128]{2,1,0:T(8,128)(2,1)} %param.12) | copy-start | bytes 442372
  209.4 14.3 %copy-start.6 = (bf16[1,576,128]{2,1,0:T(8,128)(2,1)S(1)}, bf16[1,576,128]{2,1,0:T(8,128)(2,1)}, u32[]{:S(2)}) copy-start(bf16[1,576,128]{2,1,0:T(8,128)(2,1)} %param.10) | copy-start | bytes 442372
  209.4 188.1 %all-to-all-start.1 = ((bf16[16,96,1024]{2,1,0:T(8,128)(2,1)}), bf16[16,96,1024]{2,1,0:T(8,128)(2,1)}, u32[]{:S(2)}, u32[]{:S(2)}) async-start(bf16[16,96,1024]{2,1,0:T(8,128)(2,1)} %hphi.1), calls=%async_computation.1 | async-start | bytes 6291456 | tf_op jit(solution)/shard_map/all_to_all | solution.py:291
  218.9 56.2 %collective-permute-start.18 = (bf16[576,128]{1,0:T(8,128)(2,1)S(1)}, bf16[576,128]{1,0:T(8,128)(2,1)S(1)}, u32[]{:S(2)}, u32[]{:S(2)}) collective-permute-start(bf16[576,128]{1,0:T(8,128)(2,1)S(1)} %bitcast.225), channel_id=1, source_target_pairs={{0,24},{2,26},{4,28},{6,30},{8,0},{10,2},{12,4},{14,6},{16,8},{18,... | collective-permute-start | bytes 442376 | tf_op jit(solution)/shard_map/ppermute | solution.py:251
  222.6 87.1 %collective-permute-start.19 = (bf16[576,128]{1,0:T(8,128)(2,1)S(1)}, bf16[576,128]{1,0:T(8,128)(2,1)S(1)}, u32[]{:S(2)}, u32[]{:S(2)}) collective-permute-start(bf16[576,128]{1,0:T(8,128)(2,1)S(1)} %bitcast.226), channel_id=1, source_target_pairs={{0,16},{2,18},{4,20},{6,22},{8,24},{10,26},{12,28},{14,30},{16,0},... | collective-permute-start | bytes 442376 | tf_op jit(solution)/shard_map/ppermute | solution.py:251
  222.9 86.8 %collective-permute-start.20 = (bf16[576,128]{1,0:T(8,128)(2,1)S(1)}, bf16[576,128]{1,0:T(8,128)(2,1)S(1)}, u32[]{:S(2)}, u32[]{:S(2)}) collective-permute-start(bf16[576,128]{1,0:T(8,128)(2,1)S(1)} %bitcast.227), channel_id=1, source_target_pairs={{0,8},{2,10},{4,12},{6,14},{8,16},{10,18},{12,20},{14,22},{16,24},... | collective-permute-start | bytes 442376 | tf_op jit(solution)/shard_map/ppermute | solution.py:251
  223.7 89.7 %collective-permute-start.10 = (bf16[576,128]{1,0:T(8,128)(2,1)S(1)}, bf16[576,128]{1,0:T(8,128)(2,1)S(1)}, u32[]{:S(2)}, u32[]{:S(2)}) collective-permute-start(bf16[576,128]{1,0:T(8,128)(2,1)S(1)} %bitcast.228), channel_id=1, source_target_pairs={{0,8},{2,10},{4,12},{6,14},{8,16},{10,18},{12,20},{14,22},{16,24},... | collective-permute-start | bytes 442376 | tf_op jit(solution)/shard_map/ppermute | solution.py:251
  226.1 87.3 %collective-permute-start.8 = (bf16[576,128]{1,0:T(8,128)(2,1)S(1)}, bf16[576,128]{1,0:T(8,128)(2,1)S(1)}, u32[]{:S(2)}, u32[]{:S(2)}) collective-permute-start(bf16[576,128]{1,0:T(8,128)(2,1)S(1)} %bitcast.229), channel_id=1, source_target_pairs={{0,24},{2,26},{4,28},{6,30},{8,0},{10,2},{12,4},{14,6},{16,8},{18,... | collective-permute-start | bytes 442376 | tf_op jit(solution)/shard_map/ppermute | solution.py:251
  275.1 39.9 %collective-permute-start.9 = (bf16[576,128]{1,0:T(8,128)(2,1)S(1)}, bf16[576,128]{1,0:T(8,128)(2,1)S(1)}, u32[]{:S(2)}, u32[]{:S(2)}) collective-permute-start(bf16[576,128]{1,0:T(8,128)(2,1)S(1)} %bitcast.230), channel_id=1, source_target_pairs={{0,16},{2,18},{4,20},{6,22},{8,24},{10,26},{12,28},{14,30},{16,0},... | collective-permute-start | bytes 442376 | tf_op jit(solution)/shard_map/ppermute | solution.py:251
  309.9 13.7 %collective-permute-start.21 = (bf16[4,576,128]{2,1,0:T(8,128)(2,1)S(1)}, bf16[4,576,128]{2,1,0:T(8,128)(2,1)S(1)}, u32[]{:S(2)}, u32[]{:S(2)}) collective-permute-start(bf16[4,576,128]{2,1,0:T(8,128)(2,1)S(1)} %pad_maximum_fusion.3), channel_id=1, source_target_pairs={{0,2},{2,0},{4,6},{6,4},{8,10},{10,8},{12,14},{14,12},{16,18},{18,... | collective-permute-start | bytes 1769480 | tf_op jit(solution)/shard_map/ppermute | solution.py:264
  312.1 13.0 %collective-permute-start.22 = (bf16[4,576,128]{2,1,0:T(8,128)(2,1)S(1)}, bf16[4,576,128]{2,1,0:T(8,128)(2,1)S(1)}, u32[]{:S(2)}, u32[]{:S(2)}) collective-permute-start(bf16[4,576,128]{2,1,0:T(8,128)(2,1)S(1)} %pad_maximum_fusion.3), channel_id=1, source_target_pairs={{0,4},{2,6},{4,0},{6,2},{8,12},{10,14},{12,8},{14,10},{16,20},{18,... | collective-permute-start | bytes 1769480 | tf_op jit(solution)/shard_map/ppermute | solution.py:264
  313.4 35.5 %collective-permute-start.24 = (bf16[4,576,128]{2,1,0:T(8,128)(2,1)S(1)}, bf16[4,576,128]{2,1,0:T(8,128)(2,1)S(1)}, u32[]{:S(2)}, u32[]{:S(2)}) collective-permute-start(bf16[4,576,128]{2,1,0:T(8,128)(2,1)S(1)} %pad_maximum_fusion.3), channel_id=1, source_target_pairs={{0,1},{1,0},{2,3},{3,2},{4,5},{5,4},{6,7},{7,6},{8,9},{9,8},{10,11... | collective-permute-start | bytes 1769480 | tf_op jit(solution)/shard_map/ppermute | solution.py:268
  315.2 21.1 %collective-permute-start.11 = (bf16[4,576,128]{2,1,0:T(8,128)(2,1)S(1)}, bf16[4,576,128]{2,1,0:T(8,128)(2,1)S(1)}, u32[]{:S(2)}, u32[]{:S(2)}) collective-permute-start(bf16[4,576,128]{2,1,0:T(8,128)(2,1)S(1)} %pad_maximum_fusion.2), channel_id=1, source_target_pairs={{0,2},{2,0},{4,6},{6,4},{8,10},{10,8},{12,14},{14,12},{16,18},{18,... | collective-permute-start | bytes 1769480 | tf_op jit(solution)/shard_map/ppermute | solution.py:264
  317.4 18.9 %collective-permute-start.12 = (bf16[4,576,128]{2,1,0:T(8,128)(2,1)S(1)}, bf16[4,576,128]{2,1,0:T(8,128)(2,1)S(1)}, u32[]{:S(2)}, u32[]{:S(2)}) collective-permute-start(bf16[4,576,128]{2,1,0:T(8,128)(2,1)S(1)} %pad_maximum_fusion.2), channel_id=1, source_target_pairs={{0,4},{2,6},{4,0},{6,2},{8,12},{10,14},{12,8},{14,10},{16,20},{18,... | collective-permute-start | bytes 1769480 | tf_op jit(solution)/shard_map/ppermute | solution.py:264
  323.6 36.4 %collective-permute-start.14 = (bf16[4,576,128]{2,1,0:T(8,128)(2,1)S(1)}, bf16[4,576,128]{2,1,0:T(8,128)(2,1)S(1)}, u32[]{:S(2)}, u32[]{:S(2)}) collective-permute-start(bf16[4,576,128]{2,1,0:T(8,128)(2,1)S(1)} %pad_maximum_fusion.2), channel_id=1, source_target_pairs={{0,1},{1,0},{2,3},{3,2},{4,5},{5,4},{6,7},{7,6},{8,9},{9,8},{10,11... | collective-permute-start | bytes 1769480 | tf_op jit(solution)/shard_map/ppermute | solution.py:268
  325.1 20.7 %collective-permute-start.23 = (bf16[4,576,128]{2,1,0:T(8,128)(2,1)S(1)}, bf16[4,576,128]{2,1,0:T(8,128)(2,1)S(1)}, u32[]{:S(2)}, u32[]{:S(2)}) collective-permute-start(bf16[4,576,128]{2,1,0:T(8,128)(2,1)S(1)} %collective-permute-done.22), channel_id=1, source_target_pairs={{0,2},{2,0},{4,6},{6,4},{8,10},{10,8},{12,14},{14,12},{16,18},{18,... | collective-permute-start | bytes 1769480 | tf_op jit(solution)/shard_map/ppermute | solution.py:264
  336.2 12.8 %collective-permute-start.25 = (bf16[4,576,128]{2,1,0:T(8,128)(2,1)S(1)}, bf16[4,576,128]{2,1,0:T(8,128)(2,1)S(1)}, u32[]{:S(2)}, u32[]{:S(2)}) collective-permute-start(bf16[4,576,128]{2,1,0:T(8,128)(2,1)S(1)} %collective-permute-done.21), channel_id=1, source_target_pairs={{0,1},{1,0},{2,3},{3,2},{4,5},{5,4},{6,7},{7,6},{8,9},{9,8},{10,11... | collective-permute-start | bytes 1769480 | tf_op jit(solution)/shard_map/ppermute | solution.py:268
  336.3 23.0 %collective-permute-start.26 = (bf16[4,576,128]{2,1,0:T(8,128)(2,1)S(1)}, bf16[4,576,128]{2,1,0:T(8,128)(2,1)S(1)}, u32[]{:S(2)}, u32[]{:S(2)}) collective-permute-start(bf16[4,576,128]{2,1,0:T(8,128)(2,1)S(1)} %collective-permute-done.22), channel_id=1, source_target_pairs={{0,1},{1,0},{2,3},{3,2},{4,5},{5,4},{6,7},{7,6},{8,9},{9,8},{10,11... | collective-permute-start | bytes 1769480 | tf_op jit(solution)/shard_map/ppermute | solution.py:268
  345.8 13.5 %collective-permute-start.13 = (bf16[4,576,128]{2,1,0:T(8,128)(2,1)S(1)}, bf16[4,576,128]{2,1,0:T(8,128)(2,1)S(1)}, u32[]{:S(2)}, u32[]{:S(2)}) collective-permute-start(bf16[4,576,128]{2,1,0:T(8,128)(2,1)S(1)} %collective-permute-done.11), channel_id=1, source_target_pairs={{0,4},{2,6},{4,0},{6,2},{8,12},{10,14},{12,8},{14,10},{16,20},{18,... | collective-permute-start | bytes 1769480 | tf_op jit(solution)/shard_map/ppermute | solution.py:264
  348.9 11.3 %collective-permute-start.15 = (bf16[4,576,128]{2,1,0:T(8,128)(2,1)S(1)}, bf16[4,576,128]{2,1,0:T(8,128)(2,1)S(1)}, u32[]{:S(2)}, u32[]{:S(2)}) collective-permute-start(bf16[4,576,128]{2,1,0:T(8,128)(2,1)S(1)} %collective-permute-done.11), channel_id=1, source_target_pairs={{0,1},{1,0},{2,3},{3,2},{4,5},{5,4},{6,7},{7,6},{8,9},{9,8},{10,11... | collective-permute-start | bytes 1769480 | tf_op jit(solution)/shard_map/ppermute | solution.py:268
  349.0 11.2 %collective-permute-start.16 = (bf16[4,576,128]{2,1,0:T(8,128)(2,1)S(1)}, bf16[4,576,128]{2,1,0:T(8,128)(2,1)S(1)}, u32[]{:S(2)}, u32[]{:S(2)}) collective-permute-start(bf16[4,576,128]{2,1,0:T(8,128)(2,1)S(1)} %collective-permute-done.12), channel_id=1, source_target_pairs={{0,1},{1,0},{2,3},{3,2},{4,5},{5,4},{6,7},{7,6},{8,9},{9,8},{10,11... | collective-permute-start | bytes 1769480 | tf_op jit(solution)/shard_map/ppermute | solution.py:268
  359.3 2.0 collective-permute-start.27
  359.4 2.8 collective-permute-start.17
  361.4 2.1 copy-start.3
  407.8 81.5 %copy-start.1 = (f32[32,128,128]{2,1,0:T(8,128)S(1)}, f32[32,128,128]{2,1,0:T(8,128)}, u32[]{:S(2)}) copy-start(f32[32,128,128]{2,1,0:T(8,128)} %param.9) | copy-start | bytes 6291460
  (3 other events, 4.5 us)

commit v3 on v2

--- a/solution.py
+++ b/solution.py
@@ -1,3 +1,5 @@
+import functools
+
 import jax
 import jax.numpy as jnp
 from jax import lax
@@ -24,6 +26,21 @@
 SCALE = 1.0 / 96.0
 
 
+SIDES = (4, 2, 2)
+
+
+def block_places(here, blocks, pieces=PIECES):
+    rep, y, x = (here[k] for k in range(3))
+    places = []
+    for n, block in enumerate(blocks):
+        core = rep if n < len(blocks) // 2 else 1 - rep
+        piece = n // 4 % pieces
+        to_y = y if n % 4 < 2 else 1 - y
+        to_x = x if n % 2 == 0 else 1 - x
+        places.append((block, core, piece, to_y * SIDES[2] + to_x))
+    return places
+
+
 def planar_band():
     row = lax.broadcasted_iota(jnp.int32, (2 * COLS, COLS), 0) - LANES
     col = lax.broadcasted_iota(jnp.int32, (2 * COLS, COLS), 1)
@@ -37,15 +54,17 @@
     return band.astype(jnp.bfloat16)
 
 
-def hphi_kernel(
-    info, phi, halo, band, pot, out, buf, rows, win, sems
-):
+def hphi_kernel(info, here, phi, halo, band, *refs, resident):
     planes, group, flat = phi.shape
     step = pl.program_id(0)
     total = pl.num_programs(0) * group
+    span = 3 * ROWS
+    flag = here[0].astype(jnp.float32)
+    if resident:
+        blocks, (out, pot, rows, win, sems) = refs[:-5], refs[-5:]
+    else:
+        pot, out, buf, rows, win, sems = refs
     x_blocks = pot.shape[1]
-    span = 3 * ROWS
-    flag = info[0, 3].astype(jnp.float32)
 
     def copies(index, slot):
         z = info[index, 0]
@@ -64,27 +83,54 @@
 
     @pl.when(step == 0)
     def _():
-        for early in range(SLOTS - 1):
-            for copy in copies(early, early):
+        if resident:
+            started = []
+            for n, (block, core, piece, column) in enumerate(block_places(here, blocks)):
+                per, depth = block.shape[1:3]
+                for z in range(SIDES[0]):
+                    target = pl.multiple_of((z * SIDES[1] * SIDES[2] + column) * depth, depth)
+                    started.append(
+                        pltpu.make_async_copy(
+                            block.at[z],
+                            pot.at[core, pl.ds(piece * per, per), pl.ds(target, depth)],
+                            sems.at[n, z],
+                        )
+                    )
+            for copy in started:
                 copy.start()
+            for copy in started:
+                copy.wait()
+        else:
+            for early in range(SLOTS - 1):
+                for copy in copies(early, early):
+                    copy.start()
 
     lane = lax.broadcasted_iota(jnp.int32, (8, LANES), 1)
 
     def one_function(f, carry):
         index = step * group + f
-        slot = lax.rem(index, SLOTS)
-        ahead = index + SLOTS - 1
-
-        @pl.when(ahead < total)
-        def _():
-            for copy in copies(ahead, lax.rem(ahead, SLOTS)):
-                copy.start()
-
-        for copy in copies(index, slot):
-            copy.wait()
-        for z in range(planes):
+        if resident:
+            z0 = info[index, 0]
+            first = info[index, 1] // ROWS
             for k in range(3):
-                rows[pl.ds(z * span + k * ROWS, ROWS), :] = buf[slot, k, z].astype(jnp.float32)
+                block = lax.rem(first + k, 2 * x_blocks)
+                source = pot.at[block // x_blocks, lax.rem(block, x_blocks)]
+                for z in range(planes):
+                    rows[pl.ds(z * span + k * ROWS, ROWS), :] = source[z0 + z].astype(jnp.float32)
+        else:
+            slot = lax.rem(index, SLOTS)
+            ahead = index + SLOTS - 1
+
+            @pl.when(ahead < total)
+            def _():
+                for copy in copies(ahead, lax.rem(ahead, SLOTS)):
+                    copy.start()
+
+            for copy in copies(index, slot):
+                copy.wait()
+            for z in range(planes):
+                for k in range(3):
+                    rows[pl.ds(z * span + k * ROWS, ROWS), :] = buf[slot, k, z].astype(jnp.float32)
         shift_x = lax.rem(info[index, 1], ROWS)
         shift_y = info[index, 2]
         for z in range(planes):
@@ -127,36 +173,44 @@
             out[z, :, cols] = (SCALE * kin + vphi).astype(jnp.bfloat16)
 
 
-def make_hphi(info, phi, halo, band, pot):
+def make_hphi(info, here, phi, halo, band, blocks, resident):
     planes, owned, flat = phi.shape
     span = 3 * ROWS
+    if resident:
+        per, depth = blocks[0].shape[1:3]
+        size = (2, PIECES * per, SIDES[0] * SIDES[1] * SIDES[2] * depth, ROWS, LANES)
+        taken = pltpu.VMEM(size, jnp.bfloat16)
+        sems = pltpu.SemaphoreType.DMA((len(blocks), SIDES[0]))
+    else:
+        taken = pltpu.VMEM((SLOTS, 3, planes, ROWS, LANES), jnp.bfloat16)
+        sems = pltpu.SemaphoreType.DMA((SLOTS, 3))
     grid_spec = pltpu.PrefetchScalarGridSpec(
-        num_scalar_prefetch=1,
+        num_scalar_prefetch=2,
         grid=(owned // GROUP,),
         in_specs=[
-            pl.BlockSpec((planes, GROUP, flat), lambda i, s: (0, i, 0)),
-            pl.BlockSpec((2, GROUP, flat), lambda i, s: (0, i, 0)),
-            pl.BlockSpec(band.shape, lambda i, s: (0, 0)),
-            pl.BlockSpec(memory_space=pl.ANY),
-        ],
-        out_specs=pl.BlockSpec((planes, GROUP, flat), lambda i, s: (0, i, 0)),
+            pl.BlockSpec((planes, GROUP, flat), lambda i, s, t: (0, i, 0)),
+            pl.BlockSpec((2, GROUP, flat), lambda i, s, t: (0, i, 0)),
+            pl.BlockSpec(band.shape, lambda i, s, t: (0, 0)),
+        ]
+        + [pl.BlockSpec(memory_space=pl.ANY)] * len(blocks),
+        out_specs=pl.BlockSpec((planes, GROUP, flat), lambda i, s, t: (0, i, 0)),
         scratch_shapes=[
-            pltpu.VMEM((SLOTS, 3, planes, ROWS, LANES), jnp.bfloat16),
+            taken,
             pltpu.VMEM((planes * span, LANES), jnp.float32),
             pltpu.VMEM((flat // LANES * planes * GROUP, LANES), jnp.float32),
-            pltpu.SemaphoreType.DMA((SLOTS, 3)),
+            sems,
         ],
     )
     return pl.pallas_call(
-        hphi_kernel,
+        functools.partial(hphi_kernel, resident=resident),
         out_shape=jax.ShapeDtypeStruct((planes, owned, flat), jnp.bfloat16),
         grid_spec=grid_spec,
         compiler_params=pltpu.CompilerParams(vmem_limit_bytes=VMEM),
         name="hphi",
         cost_estimate=pl.CostEstimate(
-            flops=4 * planes * owned * flat * COLS, bytes_accessed=30 << 20, transcendentals=0
+            flops=8 * planes * owned * flat * flat, bytes_accessed=60 << 20, transcendentals=0
         ),
-    )(info, phi, halo, band, pot)
+    )(info, here, phi, halo, band, *blocks)
 
 
 def dense_rows(cols, blocks, dense):
@@ -168,14 +222,44 @@
         )
         return carry
 
-    lax.fori_loop(0, NB * NNZB, one_block, 0)
-
-
-def first_kernel(k_cols, h_cols, k_blocks, h_blocks, phi, dense_k, product, dense_h):
+    lax.fori_loop(0, NB * NNZB, one_block, 0, unroll=4)
+
+
+def first_kernel(here, k_cols, h_cols, *refs):
+    phi, dense_k, product, dense_h, k_blocks, h_blocks, sems = refs[-7:]
+    half = (len(refs) - 7) // 2
+    depth = refs[0].shape[-2]
+
+    def copies(which):
+        stored = refs[which * half : (which + 1) * half]
+        target = (k_blocks, h_blocks)[which]
+        if half == 1:
+            return [pltpu.make_async_copy(stored[0], target, sems.at[which, 0, 0])]
+        out_list = []
+        columns = SIDES[1] * SIDES[2]
+        for n, (block, core, _, column) in enumerate(block_places(here, stored, 1)):
+            for z in range(SIDES[0]):
+                row = ((core * SIDES[0] + z) * columns + column) * depth
+                out_list.append(
+                    pltpu.make_async_copy(
+                        block.at[z],
+                        target.at[pl.ds(pl.multiple_of(row, depth), depth)],
+                        sems.at[which, n, z],
+                    )
+                )
+        return out_list
+
     @pl.when(pl.program_id(0) == 0)
     def _():
-        dense_rows(k_cols, k_blocks, dense_k)
-        dense_rows(h_cols, h_blocks, dense_h)
+        for which in range(2):
+            for copy in copies(which):
+                copy.start()
+        for which, (cols, blocks, dense) in enumerate(
+            ((k_cols, k_blocks, dense_k), (h_cols, h_blocks, dense_h))
+        ):
+            for copy in copies(which):
+                copy.wait()
+            dense_rows(cols, blocks, dense)
 
     kphi = jnp.dot(dense_k[...], phi[...], preferred_element_type=jnp.float32)
     product[...] = jnp.dot(
@@ -183,19 +267,25 @@
     )
 
 
-def first_products(k_cols, h_cols, k_blocks, h_blocks, phi):
+def first_products(here, k_cols, h_cols, k_parts, h_parts, phi):
     width = phi.shape[1]
     tile = min(COLS, width)
-    whole = pl.BlockSpec(k_blocks.shape, lambda i, a, b: (0, 0), pipeline_mode=pl.Buffered(1))
+    stored = pltpu.VMEM((NB * NNZB * BLK, BLK), jnp.bfloat16)
     grid_spec = pltpu.PrefetchScalarGridSpec(
-        num_scalar_prefetch=2,
+        num_scalar_prefetch=3,
         grid=(width // tile,),
-        in_specs=[whole, whole, pl.BlockSpec((NF, tile), lambda i, a, b: (0, i))],
+        in_specs=[pl.BlockSpec(memory_space=pl.ANY)] * (2 * len(k_parts))
+        + [pl.BlockSpec((NF, tile), lambda i, *s: (0, i))],
         out_specs=[
-            pl.BlockSpec((NF, NF), lambda i, a, b: (0, 0)),
-            pl.BlockSpec((NF, tile), lambda i, a, b: (0, i)),
+            pl.BlockSpec((NF, NF), lambda i, *s: (0, 0)),
+            pl.BlockSpec((NF, tile), lambda i, *s: (0, i)),
         ],
-        scratch_shapes=[pltpu.VMEM((NF, NF), jnp.bfloat16)],
+        scratch_shapes=[
+            pltpu.VMEM((NF, NF), jnp.bfloat16),
+            stored,
+            stored,
+            pltpu.SemaphoreType.DMA((2, len(k_parts), SIDES[0])),
+        ],
     )
     return pl.pallas_call(
         first_kernel,
@@ -209,7 +299,7 @@
         cost_estimate=pl.CostEstimate(
             flops=4 * NF * NF * width, bytes_accessed=24 << 20, transcendentals=0
         ),
-    )(k_cols, h_cols, k_blocks, h_blocks, phi)
+    )(here, k_cols, h_cols, *k_parts, *h_parts, phi)
 
 
 def last_kernel(dense_k, hphi, product, out):
@@ -235,9 +325,6 @@
     )(dense_k, hphi, product)
 
 
-SIDES = (4, 2, 2)
-
-
 def place_of():
     me = lax.axis_index("func")
     return me // 4, (me // 2) % 2, me % 2
@@ -264,17 +351,16 @@
     return lax.ppermute(block, "func", [(i, i ^ bit) for i in range(n)])
 
 
+def ordered(lines, near, far, first=0):
+    blocks = []
+    for p, (line, close, (apart, corner)) in enumerate(zip(lines, near, far)):
+        middle = [close, apart] if (p + first) % 2 == 0 else [apart, close]
+        blocks += [line, *middle, corner]
+    return blocks
+
+
 def other_core(block):
     return lax.ppermute(block, "rep", [(0, 1), (1, 0)])
-
-
-def put(whole, piece, blocks, core):
-    _, y, x = place_of()
-    for block, (to_y, to_x) in zip(blocks, ((y, x), (y, 1 - x), (1 - y, x), (1 - y, 1 - x))):
-        rest = whole.ndim - 5
-        start = (core, piece, 0, to_y, to_x) + (0,) * rest
-        whole = lax.dynamic_update_slice(whole, block, start)
-    return whole
 
 
 def shards(orbitals, centres, potential, kernel, kernel_cols, hamiltonian, intersection_cols):
@@ -300,46 +386,33 @@
     phi_cut = cut(phi_planes)
     edge = jnp.where(rep == 0, phi_planes[planes - 2 :], phi_planes[:2])
     halo = lax.ppermute(edge, "rep", [(0, 1), (1, 0)])
-    flag = jnp.full((owned, 1), rep, jnp.int32)
-    info = jnp.concatenate(
-        [centres[:, :1] + planes * rep, centres[:, 1:], flag], axis=1
-    ).astype(jnp.int32)
-
-    if n_func == 16:
+    info = jnp.concatenate([centres[:, :1] + planes * rep, centres[:, 1:]], axis=1)
+    info = info.astype(jnp.int32)
+
+    resident = n_func == SIDES[0] * SIDES[1] * SIDES[2]
+    if resident:
+        _, y, x = place_of()
+        here = jnp.stack([rep, y, x]).astype(jnp.int32)
         per = x_blocks // PIECES
         lines = [along_z(half[p * per : (p + 1) * per]) for p in range(PIECES)]
-        lines, phi_cut = lax.optimization_barrier((lines, phi_cut))
+        lines, kernel, hamiltonian = lax.optimization_barrier((lines, kernel, hamiltonian))
+        near = [swapped(lines[p], 1 + p) for p in range(PIECES)]
+        matrix_lines = [along_z(stored[0]) for stored in (kernel, hamiltonian)]
+        far = [(swapped(lines[p], 2 - p), swapped(near[p], 2 - p)) for p in range(PIECES)]
+        pot = ordered(lines, near, far)
+        pot, matrix_lines, phi_cut = lax.optimization_barrier((pot, matrix_lines, phi_cut))
+        pot = pot + [other_core(block) for block in pot]
         phi_pts = exchange(phi_cut)
-        near = [swapped(lines[p], 1 + p) for p in range(PIECES)]
-        far = [(swapped(lines[p], 2 - p), swapped(near[p], 2 - p)) for p in range(PIECES)]
-        pot = jnp.zeros((n_rep, x_blocks) + SIDES + (z_planes, ROWS, y_size), jnp.bfloat16)
-        for p in range(PIECES):
-            blocks = [lines[p], near[p], *far[p]] if p == 0 else [lines[p], far[p][0], near[p], far[p][1]]
-            for core, group in ((rep, blocks), (1 - rep, [other_core(b) for b in blocks])):
-                laid = [b.transpose(1, 0, 2, 3, 4)[None, :, :, None, None] for b in group]
-                pot = put(pot, per * p, laid, core)
-        pot = pot.reshape(n_rep, x_blocks, n_func * z_planes, ROWS, y_size)
-
-        near, kernel, hamiltonian = lax.optimization_barrier((near, kernel, hamiltonian))
-        gathered = []
-        for p, stored in enumerate((kernel, hamiltonian)):
-            line = along_z(stored[0])
-            close = swapped(line, 1 + p)
-            rest = (swapped(line, 2 - p), swapped(close, 2 - p))
-            blocks = [line, close, *rest] if p == 0 else [line, rest[0], close, rest[1]]
-            whole = jnp.zeros((n_rep, 1) + SIDES + stored.shape[1:], jnp.bfloat16)
-            for core, group in ((rep, blocks), (1 - rep, [other_core(b) for b in blocks])):
-                whole = put(whole, 0, [b[None, None, :, None, None] for b in group], core)
-            gathered.append(whole.reshape(-1, BLK))
-        k_blocks, h_blocks = gathered
+        matrix_near = [swapped(matrix_lines[p], 1 + p) for p in range(2)]
     else:
+        here = jnp.stack([rep, rep, rep]).astype(jnp.int32)
         pot = lax.all_gather(half, ("rep", "func"), axis=0, tiled=False)
         pot = pot.reshape(n_rep, n_func, x_blocks, z_planes, ROWS, y_size)
         pot = pot.transpose(0, 2, 1, 3, 4, 5)
-        pot = pot.reshape(n_rep, x_blocks, n_func * z_planes, ROWS, y_size)
+        pot = [pot.reshape(n_rep, x_blocks, n_func * z_planes, ROWS, y_size)]
         phi_pts = exchange(phi_cut)
-        k_blocks, h_blocks = (
-            lax.all_gather(stored, ("rep", "func"), axis=1, tiled=True).reshape(-1, BLK)
+        k_parts, h_parts = (
+            [lax.all_gather(stored, ("rep", "func"), axis=1, tiled=True).reshape(-1, BLK)]
             for stored in (kernel, hamiltonian)
         )
 
@@ -349,9 +422,23 @@
         jnp.pad(phi_planes, ((0, 0), (0, extra), (0, 0))),
         jnp.pad(halo, ((0, 0), (0, extra), (0, 0))),
     ]
-    hphi = make_hphi(*padded, planar_band(), pot)[:, :owned]
+    info, phi_planes, halo = padded
+    hphi = make_hphi(info, here, phi_planes, halo, planar_band(), pot, resident)[:, :owned]
+    if resident:
+        hphi, matrix_near = lax.optimization_barrier((hphi, matrix_near))
+        matrix_far = [
+            (swapped(matrix_lines[p], 2 - p), swapped(matrix_near[p], 2 - p)) for p in range(2)
+        ]
+        k_parts, h_parts = (
+            ordered(matrix_lines[p : p + 1], matrix_near[p : p + 1], matrix_far[p : p + 1], p)
+            for p in range(2)
+        )
+        k_parts = k_parts + [other_core(block) for block in k_parts]
+        h_parts = h_parts + [other_core(block) for block in h_parts]
     phi_pts = phi_pts.reshape(n_func * owned, width)
-    dense_k, product = first_products(kernel_cols, intersection_cols, k_blocks, h_blocks, phi_pts)
+    dense_k, product = first_products(
+        here, kernel_cols, intersection_cols, k_parts, h_parts, phi_pts
+    )
     hphi_pts = exchange(cut(hphi)).reshape(n_func * owned, width)
     gradient = last_product(dense_k, hphi_pts, product)
     back = exchange(gradient.reshape(n_func, owned, width))

time: 490 us -> 402 us (0.82)
  waiting for transfers between devices: 196 us -> 155 us
  local copies, waits for them, and re-layouts: 44.8 us -> 14.5 us
  starting transfers between devices: 94.8 us -> 68.7 us
  blocking collectives: 78.1 us -> 83.7 us
    ppermute x12, waiting for transfers between devices: 83 us -> 47.8 us  [along_z(): lax.ppermute(part, 'func', [(i, (i + 4 * k) % n) for i in range(n)])]
    ppermute x12, starting transfers between devices: 53.6 us -> 30.3 us  [along_z(): lax.ppermute(part, 'func', [(i, (i + 4 * k) % n) for i in range(n)])]
    ppermute x12, waiting for transfers between devices: 111 us -> 88.6 us  [swapped(): return lax.ppermute(block, 'func', [(i, i ^ bit) for i in range(n)])]
    dynamic_update_slice x30 -> x0, local copies, waits for them, and re-layouts: 21.2 us -> none  [put(): whole = lax.dynamic_update_slice(whole, block, start)]
    all_to_all x2, waiting for transfers between devices: 0.01 us -> 11.8 us  [exchange(): return lax.all_to_all(rows, 'func', split_axis=0, concat_axis=0, tiled=True)]
    ppermute x12, starting transfers between devices: 23.2 us -> 15.4 us  [swapped(): return lax.ppermute(block, 'func', [(i, i ^ bit) for i in range(n)])]
    broadcast_in_dim x1 -> x0, local copies, waits for them, and re-layouts: 6.22 us -> none  [shards(): jnp.zeros((n_rep, x_blocks) + SIDES + (z_planes, ROWS, y_size), jnp.bfloa...]
    all_to_all x1, blocking collectives: 78.1 us -> 83.7 us  [exchange(): return lax.all_to_all(rows, 'func', split_axis=0, concat_axis=0, tiled=True)]
  transfers between devices with their start and end apart: 43 -> 43, of which waited for: 17 -> 20; matrix products, arithmetic and copies ran while one was open for 8% -> 2% of each run, Pallas kernels for 13% -> 16%
where the time goes in v3:
time: 402 us; the launch traced here: 401 us
  waiting for transfers between devices  155 us (39%)
  blocking collectives  83.7 us (21%)
  Pallas kernels  73 us (18%)
  starting transfers between devices  68.7 us (17%)
  local copies, waits for them, and re-layouts  14.5 us (4%)
  other arithmetic  5.86 us (1%)
    ppermute x12, waiting for transfers between devices, swapped(): return lax.ppermute(block, 'func', [(i, i ^ bit) for i in range(n)])  88.6 us
    all_to_all x1, blocking collectives, exchange(): return lax.all_to_all(rows, 'func', split_axis=0, concat_axis=0, tiled=True)  83.7 us
    ppermute x12, waiting for transfers between devices, along_z(): lax.ppermute(part, 'func', [(i, (i + 4 * k) % n) for i in range(n)])  47.8 us
    pallas_call x1, Pallas kernels, make_hphi(): pl.pallas_call(functools.partial(hphi_kernel, resident=resident), out_sha...  32.9 us
    ppermute x12, starting transfers between devices, along_z(): lax.ppermute(part, 'func', [(i, (i + 4 * k) % n) for i in range(n)])  30.3 us
    pallas_call x1, Pallas kernels, first_products(): pl.pallas_call(first_kernel, out_shape=[jax.ShapeDtypeStruct((NF, NF), jn...  29.9 us
    all_to_all x2, starting transfers between devices, exchange(): return lax.all_to_all(rows, 'func', split_axis=0, concat_axis=0, tiled=True)  19.6 us
    ppermute x12, starting transfers between devices, swapped(): return lax.ppermute(block, 'func', [(i, i ^ bit) for i in range(n)])  15.4 us
  transfers between devices with their start and end apart: 43, of which 20 were waited for; matrix products, arithmetic and copies ran while one was open for 2% of the time, Pallas kernels for 16%

profile of v3, /device:TPU:0, one launch (start us, length us, event | category | flops | bytes accessed | tf_op | source)
XLA Modules:
  0.0 400.9 jit_solution(13288504797453863978)
XLA Ops:
  0.0 1.6 copy-done
  1.8 5.1 %collective-permute-start.3 = (bf16[2,32,16,128]{3,2,1,0:T(8,128)(2,1)S(1)}, bf16[2,32,16,128]{3,2,1,0:T(8,128)(2,1)S(1)}, u32[]{:S(2)}, u32[]{:S(2)}) collective-permute-start(bf16[2,32,16,128]{3,2,1,0:T(8,128)(2,1)S(1)} %get-tuple-element.61), channel_id=1, source_target_pairs={{0,24},{2,26},{4,28},{6,30},{8,0},{10,2},{12,4},{14,6},{16,8},{18,... | collective-permute-start | bytes 786440 | tf_op jit(solution)/shard_map/ppermute | solution.py:338
  6.9 1.0 collective-permute-start.5
  7.9 2.8 collective-permute-start
  10.7 1.1 collective-permute-start.1
  11.8 1.8 collective-permute-done.3
  13.6 10.6 %collective-permute-start.2 = (bf16[2,32,16,128]{3,2,1,0:T(8,128)(2,1)S(1)}, bf16[2,32,16,128]{3,2,1,0:T(8,128)(2,1)S(1)}, u32[]{:S(2)}, u32[]{:S(2)}) collective-permute-start(bf16[2,32,16,128]{3,2,1,0:T(8,128)(2,1)S(1)} %get-tuple-element.62), channel_id=1, source_target_pairs={{0,8},{2,10},{4,12},{6,14},{8,16},{10,18},{12,20},{14,22},{16,24},... | collective-permute-start | bytes 786440 | tf_op jit(solution)/shard_map/ppermute | solution.py:338
  24.2 7.3 %collective-permute-done.4 = bf16[2,32,16,128]{3,2,1,0:T(8,128)(2,1)S(1)} collective-permute-done((bf16[2,32,16,128]{3,2,1,0:T(8,128)(2,1)S(1)}, bf16[2,32,16,128]{3,2,1,0:T(8,128)(2,1)S(1)}, u32[]{:S(2)}, u32[]{:S(2)}) %collective-permute-start.4) | collective-permute-done | bytes 262176 | tf_op jit(solution)/shard_map/ppermute | solution.py:338
  31.7 20.0 %collective-permute-done.1 = bf16[2,32,16,128]{3,2,1,0:T(8,128)(2,1)S(1)} collective-permute-done((bf16[2,32,16,128]{3,2,1,0:T(8,128)(2,1)S(1)}, bf16[2,32,16,128]{3,2,1,0:T(8,128)(2,1)S(1)}, u32[]{:S(2)}, u32[]{:S(2)}) %collective-permute-start.1) | collective-permute-done | bytes 262176 | tf_op jit(solution)/shard_map/ppermute | solution.py:338
  52.1 1.6 collective-permute-start.10
  53.7 1.5 collective-permute-start.6
  55.2 2.8 collective-permute-start.16
  58.0 2.0 collective-permute-start.17
  60.0 1.8 collective-permute-done.15
  61.8 2.0 collective-permute-start.12
  63.8 8.0 %collective-permute-done.16 = bf16[576,128]{1,0:T(8,128)(2,1)S(1)} collective-permute-done((bf16[576,128]{1,0:T(8,128)(2,1)S(1)}, bf16[576,128]{1,0:T(8,128)(2,1)S(1)}, u32[]{:S(2)}, u32[]{:S(2)}) %collective-permute-start.16) | collective-permute-done | bytes 147488 | tf_op jit(solution)/shard_map/ppermute | solution.py:338
  72.8 5.4 %collective-permute-done.10.refs_6_ = bf16[4,2,32,16,128]{4,3,2,1,0:T(8,128)(2,1)S(1)} collective-permute-done((bf16[4,2,32,16,128]{4,3,2,1,0:T(8,128)(2,1)S(1)}, bf16[4,2,32,16,128]{4,3,2,1,0:T(8,128)(2,1)S(1)}, u32[]{:S(2)}, u32[]{:S(2)}) %collective-permute-start.10) | collective-permute-done | bytes 1048608 | tf_op jit(solution)/shard_map/ppermute | solution.py:351
  78.2 1.5 collective-permute-start.11
  79.8 1.5 collective-permute-start.8
  81.3 2.8 collective-permute-start.13
  84.1 3.4 copy.25
  87.5 3.0 collective-permute-done.13
  91.4 6.0 %collective-permute-done.14 = bf16[576,128]{1,0:T(8,128)(2,1)S(1)} collective-permute-done((bf16[576,128]{1,0:T(8,128)(2,1)S(1)}, bf16[576,128]{1,0:T(8,128)(2,1)S(1)}, u32[]{:S(2)}, u32[]{:S(2)}) %collective-permute-start.14) | collective-permute-done | bytes 147488 | tf_op jit(solution)/shard_map/ppermute | solution.py:338
  98.4 2.3 collective-permute-done.7.refs_2_
  100.7 1.5 collective-permute-done.9.refs_5_
  102.2 20.1 %collective-permute-done.11.refs_7_ = bf16[4,2,32,16,128]{4,3,2,1,0:T(8,128)(2,1)S(1)} collective-permute-done((bf16[4,2,32,16,128]{4,3,2,1,0:T(8,128)(2,1)S(1)}, bf16[4,2,32,16,128]{4,3,2,1,0:T(8,128)(2,1)S(1)}, u32[]{:S(2)}, u32[]{:S(2)}) %collective-permute-start.11) | collective-permute-done | bytes 1048608 | tf_op jit(solution)/shard_map/ppermute | solution.py:351
  124.3 5.5 %all-to-all-start = ((bf16[16,96,1024]{2,1,0:T(8,128)(2,1)}), bf16[16,96,1024]{2,1,0:T(8,128)(2,1)S(1)}, u32[]{:S(2)}, u32[]{:S(2)}) async-start(bf16[16,96,1024]{2,1,0:T(8,128)(2,1)} %bitcast.58.phi), calls=%async_computation | async-start | bytes 6291456 | tf_op jit(solution)/shard_map/all_to_all | solution.py:377
  130.5 1.2 slice_select_fusion
  132.3 3.0 collective-permute-done.18.halo
  138.0 1.6 select_convert_fusion.band
  139.6 1.9 collective-permute-start.27
  141.5 1.5 collective-permute-start.28
  143.0 1.0 collective-permute-done.26.refs_15_
  144.0 32.9 %hphi.1 = bf16[16,96,1024]{2,1,0:T(8,128)(2,1)} custom-call(s32[96,3]{1,0:T(8,128)} %copy.21.info, s32[3]{0:T(128)} %pad_add_fusion.1.here, bf16[16,96,1024]{2,1,0:T(8,128)(2,1)} %bitcast.58.phi, bf16[2,96,1024]{2,1,0:T(8,128)(2,1)} %collective-permute-done.18.halo, bf16[512,256]{1,0:T(8,128)(2,1)} %select_convert_fusion.band, ...), custom_call_target="tpu_custom_call" | custom-call | flops 12884901888 | bytes 62914560 | tf_op jit(solution)/shard_map/hphi/pallas_call | solution.py:204
  177.7 11.8 %all-to-all-done = bf16[16,96,1024]{2,1,0:T(8,128)(2,1)S(1)} async-done(((bf16[16,96,1024]{2,1,0:T(8,128)(2,1)}), bf16[16,96,1024]{2,1,0:T(8,128)(2,1)S(1)}, u32[]{:S(2)}, u32[]{:S(2)}) %all-to-all-start) | async-done | bytes 3145760 | tf_op jit(solution)/shard_map/all_to_all | solution.py:377
  189.5 1.7 copy-done.3
  191.2 14.1 %all-to-all-start.1 = ((bf16[16,96,1024]{2,1,0:T(8,128)(2,1)}), bf16[16,96,1024]{2,1,0:T(8,128)(2,1)}, u32[]{:S(2)}, u32[]{:S(2)}) async-start(bf16[16,96,1024]{2,1,0:T(8,128)(2,1)} %hphi.1), calls=%async_computation.1 | async-start | bytes 6291456 | tf_op jit(solution)/shard_map/all_to_all | solution.py:377
  205.2 1.9 collective-permute-start.29
  207.2 1.5 collective-permute-start.35
  209.2 35.4 %collective-permute-done.29.refs_2_ = bf16[4,576,128]{2,1,0:T(8,128)(2,1)S(1)} collective-permute-done((bf16[4,576,128]{2,1,0:T(8,128)(2,1)}, bf16[4,576,128]{2,1,0:T(8,128)(2,1)S(1)}, u32[]{:S(2)}, u32[]{:S(2)}) %collective-permute-start.29) | collective-permute-done | bytes 589856 | tf_op jit(solution)/shard_map/ppermute | solution.py:351
  244.6 1.5 collective-permute-start.36
  246.9 22.1 %collective-permute-done.30.refs_3_ = bf16[4,576,128]{2,1,0:T(8,128)(2,1)S(1)} collective-permute-done((bf16[4,576,128]{2,1,0:T(8,128)(2,1)}, bf16[4,576,128]{2,1,0:T(8,128)(2,1)S(1)}, u32[]{:S(2)}, u32[]{:S(2)}) %collective-permute-start.30) | collective-permute-done | bytes 589856 | tf_op jit(solution)/shard_map/ppermute | solution.py:351
  269.0 1.8 collective-permute-done.36.refs_11_
  271.0 1.8 collective-permute-done.40.refs_15_
  273.5 29.9 %products.1 = (bf16[1536,1536]{1,0:T(8,128)(2,1)}, f32[1536,1024]{1,0:T(8,128)}) custom-call(s32[3]{0:T(128)} %pad_add_fusion.1.here, s32[12,12]{1,0:T(8,128)} %k_cols.1, s32[12,12]{1,0:T(8,128)} %h_cols.1, bf16[4,576,128]{2,1,0:T(8,128)(2,1)} %pad_maximum_fusion.2.refs_0_, bf16[4,576,128]{2,1,0:T(8,128)(2,1)} %copy-done.15, ...), custom_call_target="tpu_custom_call" | custom-call | flops 9663676416 | bytes 25165824 | tf_op jit(solution)/shard_map/products/pallas_call | solution.py:290
  303.4 10.3 %gradient.1 = bf16[1536,1024]{1,0:T(8,128)(2,1)} custom-call(bf16[1536,1536]{1,0:T(8,128)(2,1)} %get-tuple-element.42.dense_k, bf16[1536,1024]{1,0:T(8,128)(2,1)} %bitcast.25.hphi, f32[1536,1024]{1,0:T(8,128)} %get-tuple-element.44.product), custom_call_target="tpu_custom_call" | custom-call | flops 4831838208 | bytes 17825792 | tf_op jit(solution)/shard_map/gradient/pallas_call | solution.py:314
  313.7 83.7 %all_to_all.15 = bf16[16,96,1024]{2,1,0:T(8,128)(2,1)S(1)} all-to-all(bf16[16,96,1024]{2,1,0:T(8,128)(2,1)} %bitcast.65), channel_id=1, replica_groups=mesh['func'=16,'rep'=2] {'func'}, dimensions={0} | all-to-all | bytes 6291456 | tf_op jit(solution)/shard_map/all_to_all | solution.py:377
  397.5 3.4 copy.22
  (123 shorter events, 12.7 us)
Async XLA Ops:
  1.8 11.9 %collective-permute-start.3 = (bf16[2,32,16,128]{3,2,1,0:T(8,128)(2,1)S(1)}, bf16[2,32,16,128]{3,2,1,0:T(8,128)(2,1)S(1)}, u32[]{:S(2)}, u32[]{:S(2)}) collective-permute-start(bf16[2,32,16,128]{3,2,1,0:T(8,128)(2,1)S(1)} %get-tuple-element.61), channel_id=1, source_target_pairs={{0,24},{2,26},{4,28},{6,30},{8,0},{10,2},{12,4},{14,6},{16,8},{18,... | collective-permute-start | bytes 786440 | tf_op jit(solution)/shard_map/ppermute | solution.py:338
  6.9 24.6 %collective-permute-start.4 = (bf16[2,32,16,128]{3,2,1,0:T(8,128)(2,1)S(1)}, bf16[2,32,16,128]{3,2,1,0:T(8,128)(2,1)S(1)}, u32[]{:S(2)}, u32[]{:S(2)}) collective-permute-start(bf16[2,32,16,128]{3,2,1,0:T(8,128)(2,1)S(1)} %get-tuple-element.61), channel_id=1, source_target_pairs={{0,16},{2,18},{4,20},{6,22},{8,24},{10,26},{12,28},{14,30},{16,0},... | collective-permute-start | bytes 786440 | tf_op jit(solution)/shard_map/ppermute | solution.py:338
  6.9 24.6 %collective-permute-start.5 = (bf16[2,32,16,128]{3,2,1,0:T(8,128)(2,1)S(1)}, bf16[2,32,16,128]{3,2,1,0:T(8,128)(2,1)S(1)}, u32[]{:S(2)}, u32[]{:S(2)}) collective-permute-start(bf16[2,32,16,128]{3,2,1,0:T(8,128)(2,1)S(1)} %get-tuple-element.61), channel_id=1, source_target_pairs={{0,8},{2,10},{4,12},{6,14},{8,16},{10,18},{12,20},{14,22},{16,24},... | collective-permute-start | bytes 786440 | tf_op jit(solution)/shard_map/ppermute | solution.py:338
  7.9 23.8 %collective-permute-start = (bf16[2,32,16,128]{3,2,1,0:T(8,128)(2,1)S(1)}, bf16[2,32,16,128]{3,2,1,0:T(8,128)(2,1)S(1)}, u32[]{:S(2)}, u32[]{:S(2)}) collective-permute-start(bf16[2,32,16,128]{3,2,1,0:T(8,128)(2,1)S(1)} %get-tuple-element.62), channel_id=1, source_target_pairs={{0,24},{2,26},{4,28},{6,30},{8,0},{10,2},{12,4},{14,6},{16,8},{18,... | collective-permute-start | bytes 786440 | tf_op jit(solution)/shard_map/ppermute | solution.py:338
  10.7 41.0 %collective-permute-start.1 = (bf16[2,32,16,128]{3,2,1,0:T(8,128)(2,1)S(1)}, bf16[2,32,16,128]{3,2,1,0:T(8,128)(2,1)S(1)}, u32[]{:S(2)}, u32[]{:S(2)}) collective-permute-start(bf16[2,32,16,128]{3,2,1,0:T(8,128)(2,1)S(1)} %get-tuple-element.62), channel_id=1, source_target_pairs={{0,16},{2,18},{4,20},{6,22},{8,24},{10,26},{12,28},{14,30},{16,0},... | collective-permute-start | bytes 786440 | tf_op jit(solution)/shard_map/ppermute | solution.py:338
  13.6 38.0 %collective-permute-start.2 = (bf16[2,32,16,128]{3,2,1,0:T(8,128)(2,1)S(1)}, bf16[2,32,16,128]{3,2,1,0:T(8,128)(2,1)S(1)}, u32[]{:S(2)}, u32[]{:S(2)}) collective-permute-start(bf16[2,32,16,128]{3,2,1,0:T(8,128)(2,1)S(1)} %get-tuple-element.62), channel_id=1, source_target_pairs={{0,8},{2,10},{4,12},{6,14},{8,16},{10,18},{12,20},{14,22},{16,24},... | collective-permute-start | bytes 786440 | tf_op jit(solution)/shard_map/ppermute | solution.py:338
  31.6 30.2 %copy-start.7 = (bf16[1,576,128]{2,1,0:T(8,128)(2,1)S(1)}, bf16[1,576,128]{2,1,0:T(8,128)(2,1)}, u32[]{:S(2)}) copy-start(bf16[1,576,128]{2,1,0:T(8,128)(2,1)} %param.10) | copy-start | bytes 442372
  31.6 52.5 %copy-start.2 = (bf16[96,16,1024]{2,1,0:T(8,128)(2,1)S(1)}, bf16[96,16,1024]{2,1,0:T(8,128)(2,1)}, u32[]{:S(2)}) copy-start(bf16[96,16,1024]{2,1,0:T(8,128)(2,1)} %param.7) | copy-start | bytes 9437188
  52.1 35.4 %copy-start.4 = (bf16[4,2,32,16,128]{4,3,2,1,0:T(8,128)(2,1)}, bf16[4,2,32,16,128]{4,3,2,1,0:T(8,128)(2,1)S(1)}, u32[]{:S(2)}) copy-start(bf16[4,2,32,16,128]{4,3,2,1,0:T(8,128)(2,1)S(1)} %get-tuple-element.30.refs_0_) | copy-start | bytes 3145732
  52.1 48.6 %copy-start.5 = (bf16[4,2,32,16,128]{4,3,2,1,0:T(8,128)(2,1)}, bf16[4,2,32,16,128]{4,3,2,1,0:T(8,128)(2,1)S(1)}, u32[]{:S(2)}) copy-start(bf16[4,2,32,16,128]{4,3,2,1,0:T(8,128)(2,1)S(1)} %get-tuple-element.34.refs_4_) | copy-start | bytes 3145732
  52.1 26.2 %collective-permute-start.10 = (bf16[4,2,32,16,128]{4,3,2,1,0:T(8,128)(2,1)S(1)}, bf16[4,2,32,16,128]{4,3,2,1,0:T(8,128)(2,1)S(1)}, u32[]{:S(2)}, u32[]{:S(2)}) collective-permute-start(bf16[4,2,32,16,128]{4,3,2,1,0:T(8,128)(2,1)S(1)} %get-tuple-element.34.refs_4_), channel_id=1, source_target_pairs={{0,4},{2,6},{4,0},{6,2},{8,12},{10,14},{12,8},{14,10},{16,20},{18,... | collective-permute-start | bytes 3145736 | tf_op jit(solution)/shard_map/ppermute | solution.py:351
  53.7 26.1 %collective-permute-start.6 = (bf16[4,2,32,16,128]{4,3,2,1,0:T(8,128)(2,1)S(1)}, bf16[4,2,32,16,128]{4,3,2,1,0:T(8,128)(2,1)S(1)}, u32[]{:S(2)}, u32[]{:S(2)}) collective-permute-start(bf16[4,2,32,16,128]{4,3,2,1,0:T(8,128)(2,1)S(1)} %get-tuple-element.30.refs_0_), channel_id=1, source_target_pairs={{0,2},{2,0},{4,6},{6,4},{8,10},{10,8},{12,14},{14,12},{16,18},{18,... | collective-permute-start | bytes 3145736 | tf_op jit(solution)/shard_map/ppermute | solution.py:351
  55.2 6.7 %collective-permute-start.15 = (bf16[576,128]{1,0:T(8,128)(2,1)S(1)}, bf16[576,128]{1,0:T(8,128)(2,1)S(1)}, u32[]{:S(2)}, u32[]{:S(2)}) collective-permute-start(bf16[576,128]{1,0:T(8,128)(2,1)S(1)} %bitcast.67), channel_id=1, source_target_pairs={{0,24},{2,26},{4,28},{6,30},{8,0},{10,2},{12,4},{14,6},{16,8},{18,... | collective-permute-start | bytes 442376 | tf_op jit(solution)/shard_map/ppermute | solution.py:338
  55.2 16.6 %collective-permute-start.16 = (bf16[576,128]{1,0:T(8,128)(2,1)S(1)}, bf16[576,128]{1,0:T(8,128)(2,1)S(1)}, u32[]{:S(2)}, u32[]{:S(2)}) collective-permute-start(bf16[576,128]{1,0:T(8,128)(2,1)S(1)} %bitcast.68), channel_id=1, source_target_pairs={{0,16},{2,18},{4,20},{6,22},{8,24},{10,26},{12,28},{14,30},{16,0},... | collective-permute-start | bytes 442376 | tf_op jit(solution)/shard_map/ppermute | solution.py:338
  58.0 14.3 %collective-permute-start.17 = (bf16[576,128]{1,0:T(8,128)(2,1)S(1)}, bf16[576,128]{1,0:T(8,128)(2,1)S(1)}, u32[]{:S(2)}, u32[]{:S(2)}) collective-permute-start(bf16[576,128]{1,0:T(8,128)(2,1)S(1)} %bitcast.69), channel_id=1, source_target_pairs={{0,8},{2,10},{4,12},{6,14},{8,16},{10,18},{12,20},{14,22},{16,24},... | collective-permute-start | bytes 442376 | tf_op jit(solution)/shard_map/ppermute | solution.py:338
  61.8 19.4 %collective-permute-start.12 = (bf16[576,128]{1,0:T(8,128)(2,1)S(1)}, bf16[576,128]{1,0:T(8,128)(2,1)S(1)}, u32[]{:S(2)}, u32[]{:S(2)}) collective-permute-start(bf16[576,128]{1,0:T(8,128)(2,1)S(1)} %bitcast.70), channel_id=1, source_target_pairs={{0,24},{2,26},{4,28},{6,30},{8,0},{10,2},{12,4},{14,6},{16,8},{18,... | collective-permute-start | bytes 442376 | tf_op jit(solution)/shard_map/ppermute | solution.py:338
  71.8 28.9 %collective-permute-start.7 = (bf16[4,2,32,16,128]{4,3,2,1,0:T(8,128)(2,1)S(1)}, bf16[4,2,32,16,128]{4,3,2,1,0:T(8,128)(2,1)S(1)}, u32[]{:S(2)}, u32[]{:S(2)}) collective-permute-start(bf16[4,2,32,16,128]{4,3,2,1,0:T(8,128)(2,1)S(1)} %get-tuple-element.30.refs_0_), channel_id=1, source_target_pairs={{0,4},{2,6},{4,0},{6,2},{8,12},{10,14},{12,8},{14,10},{16,20},{18,... | collective-permute-start | bytes 3145736 | tf_op jit(solution)/shard_map/ppermute | solution.py:351
  72.3 29.9 %collective-permute-start.9 = (bf16[4,2,32,16,128]{4,3,2,1,0:T(8,128)(2,1)S(1)}, bf16[4,2,32,16,128]{4,3,2,1,0:T(8,128)(2,1)S(1)}, u32[]{:S(2)}, u32[]{:S(2)}) collective-permute-start(bf16[4,2,32,16,128]{4,3,2,1,0:T(8,128)(2,1)S(1)} %get-tuple-element.34.refs_4_), channel_id=1, source_target_pairs={{0,2},{2,0},{4,6},{6,4},{8,10},{10,8},{12,14},{14,12},{16,18},{18,... | collective-permute-start | bytes 3145736 | tf_op jit(solution)/shard_map/ppermute | solution.py:351
  78.2 44.1 %collective-permute-start.11 = (bf16[4,2,32,16,128]{4,3,2,1,0:T(8,128)(2,1)S(1)}, bf16[4,2,32,16,128]{4,3,2,1,0:T(8,128)(2,1)S(1)}, u32[]{:S(2)}, u32[]{:S(2)}) collective-permute-start(bf16[4,2,32,16,128]{4,3,2,1,0:T(8,128)(2,1)S(1)} %collective-permute-done.10.refs_6_), channel_id=1, source_target_pairs={{0,2},{2,0},{4,6},{6,4},{8,10},{10,8},{12,14},{14,12},{16,18},{18,... | collective-permute-start | bytes 3145736 | tf_op jit(solution)/shard_map/ppermute | solution.py:351
  79.8 42.6 %collective-permute-start.8 = (bf16[4,2,32,16,128]{4,3,2,1,0:T(8,128)(2,1)S(1)}, bf16[4,2,32,16,128]{4,3,2,1,0:T(8,128)(2,1)S(1)}, u32[]{:S(2)}, u32[]{:S(2)}) collective-permute-start(bf16[4,2,32,16,128]{4,3,2,1,0:T(8,128)(2,1)S(1)} %collective-permute-done.6.refs_1_), channel_id=1, source_target_pairs={{0,4},{2,6},{4,0},{6,2},{8,12},{10,14},{12,8},{14,10},{16,20},{18,... | collective-permute-start | bytes 3145736 | tf_op jit(solution)/shard_map/ppermute | solution.py:351
  81.3 9.2 %collective-permute-start.13 = (bf16[576,128]{1,0:T(8,128)(2,1)S(1)}, bf16[576,128]{1,0:T(8,128)(2,1)S(1)}, u32[]{:S(2)}, u32[]{:S(2)}) collective-permute-start(bf16[576,128]{1,0:T(8,128)(2,1)S(1)} %bitcast.71), channel_id=1, source_target_pairs={{0,16},{2,18},{4,20},{6,22},{8,24},{10,26},{12,28},{14,30},{16,0},... | collective-permute-start | bytes 442376 | tf_op jit(solution)/shard_map/ppermute | solution.py:338
  90.5 6.9 %collective-permute-start.14 = (bf16[576,128]{1,0:T(8,128)(2,1)S(1)}, bf16[576,128]{1,0:T(8,128)(2,1)S(1)}, u32[]{:S(2)}, u32[]{:S(2)}) collective-permute-start(bf16[576,128]{1,0:T(8,128)(2,1)S(1)} %bitcast.72), channel_id=1, source_target_pairs={{0,8},{2,10},{4,12},{6,14},{8,16},{10,18},{12,20},{14,22},{16,24},... | collective-permute-start | bytes 442376 | tf_op jit(solution)/shard_map/ppermute | solution.py:338
  124.3 65.2 %all-to-all-start = ((bf16[16,96,1024]{2,1,0:T(8,128)(2,1)}), bf16[16,96,1024]{2,1,0:T(8,128)(2,1)S(1)}, u32[]{:S(2)}, u32[]{:S(2)}) async-start(bf16[16,96,1024]{2,1,0:T(8,128)(2,1)} %bitcast.58.phi), calls=%async_computation | async-start | bytes 6291456 | tf_op jit(solution)/shard_map/all_to_all | solution.py:377
  129.9 5.6 %collective-permute-start.19 = (bf16[4,2,32,16,128]{4,3,2,1,0:T(8,128)(2,1)}, bf16[4,2,32,16,128]{4,3,2,1,0:T(8,128)(2,1)}, u32[]{:S(2)}, u32[]{:S(2)}) collective-permute-start(bf16[4,2,32,16,128]{4,3,2,1,0:T(8,128)(2,1)} %copy-done.4), channel_id=1, source_target_pairs={{0,1},{1,0},{2,3},{3,2},{4,5},{5,4},{6,7},{7,6},{8,9},{9,8},{10,11... | collective-permute-start | bytes 3145736 | tf_op jit(solution)/shard_map/ppermute | solution.py:363
  129.9 5.9 %collective-permute-start.20 = (bf16[4,2,32,16,128]{4,3,2,1,0:T(8,128)(2,1)}, bf16[4,2,32,16,128]{4,3,2,1,0:T(8,128)(2,1)}, u32[]{:S(2)}, u32[]{:S(2)}) collective-permute-start(bf16[4,2,32,16,128]{4,3,2,1,0:T(8,128)(2,1)} %copy-done.10), channel_id=1, source_target_pairs={{0,1},{1,0},{2,3},{3,2},{4,5},{5,4},{6,7},{7,6},{8,9},{9,8},{10,11... | collective-permute-start | bytes 3145736 | tf_op jit(solution)/shard_map/ppermute | solution.py:363
  130.4 6.1 %collective-permute-start.21 = (bf16[4,2,32,16,128]{4,3,2,1,0:T(8,128)(2,1)}, bf16[4,2,32,16,128]{4,3,2,1,0:T(8,128)(2,1)}, u32[]{:S(2)}, u32[]{:S(2)}) collective-permute-start(bf16[4,2,32,16,128]{4,3,2,1,0:T(8,128)(2,1)} %copy-done.11), channel_id=1, source_target_pairs={{0,1},{1,0},{2,3},{3,2},{4,5},{5,4},{6,7},{7,6},{8,9},{9,8},{10,11... | collective-permute-start | bytes 3145736 | tf_op jit(solution)/shard_map/ppermute | solution.py:363
  131.7 3.7 collective-permute-start.18
  132.2 7.4 %collective-permute-start.22 = (bf16[4,2,32,16,128]{4,3,2,1,0:T(8,128)(2,1)}, bf16[4,2,32,16,128]{4,3,2,1,0:T(8,128)(2,1)}, u32[]{:S(2)}, u32[]{:S(2)}) collective-permute-start(bf16[4,2,32,16,128]{4,3,2,1,0:T(8,128)(2,1)} %copy-done.14), channel_id=1, source_target_pairs={{0,1},{1,0},{2,3},{3,2},{4,5},{5,4},{6,7},{7,6},{8,9},{9,8},{10,11... | collective-permute-start | bytes 3145736 | tf_op jit(solution)/shard_map/ppermute | solution.py:363
  135.3 6.1 %collective-permute-start.23 = (bf16[4,2,32,16,128]{4,3,2,1,0:T(8,128)(2,1)}, bf16[4,2,32,16,128]{4,3,2,1,0:T(8,128)(2,1)}, u32[]{:S(2)}, u32[]{:S(2)}) collective-permute-start(bf16[4,2,32,16,128]{4,3,2,1,0:T(8,128)(2,1)} %copy-done.5), channel_id=1, source_target_pairs={{0,1},{1,0},{2,3},{3,2},{4,5},{5,4},{6,7},{7,6},{8,9},{9,8},{10,11... | collective-permute-start | bytes 3145736 | tf_op jit(solution)/shard_map/ppermute | solution.py:363
  135.5 7.5 %collective-permute-start.24 = (bf16[4,2,32,16,128]{4,3,2,1,0:T(8,128)(2,1)}, bf16[4,2,32,16,128]{4,3,2,1,0:T(8,128)(2,1)}, u32[]{:S(2)}, u32[]{:S(2)}) collective-permute-start(bf16[4,2,32,16,128]{4,3,2,1,0:T(8,128)(2,1)} %copy-done.12), channel_id=1, source_target_pairs={{0,1},{1,0},{2,3},{3,2},{4,5},{5,4},{6,7},{7,6},{8,9},{9,8},{10,11... | collective-permute-start | bytes 3145736 | tf_op jit(solution)/shard_map/ppermute | solution.py:363
  135.9 7.1 %collective-permute-start.25 = (bf16[4,2,32,16,128]{4,3,2,1,0:T(8,128)(2,1)}, bf16[4,2,32,16,128]{4,3,2,1,0:T(8,128)(2,1)}, u32[]{:S(2)}, u32[]{:S(2)}) collective-permute-start(bf16[4,2,32,16,128]{4,3,2,1,0:T(8,128)(2,1)} %copy-done.9), channel_id=1, source_target_pairs={{0,1},{1,0},{2,3},{3,2},{4,5},{5,4},{6,7},{7,6},{8,9},{9,8},{10,11... | collective-permute-start | bytes 3145736 | tf_op jit(solution)/shard_map/ppermute | solution.py:363
  136.5 7.5 %collective-permute-start.26 = (bf16[4,2,32,16,128]{4,3,2,1,0:T(8,128)(2,1)}, bf16[4,2,32,16,128]{4,3,2,1,0:T(8,128)(2,1)}, u32[]{:S(2)}, u32[]{:S(2)}) collective-permute-start(bf16[4,2,32,16,128]{4,3,2,1,0:T(8,128)(2,1)} %copy-done.13), channel_id=1, source_target_pairs={{0,1},{1,0},{2,3},{3,2},{4,5},{5,4},{6,7},{7,6},{8,9},{9,8},{10,11... | collective-permute-start | bytes 3145736 | tf_op jit(solution)/shard_map/ppermute | solution.py:363
  139.6 37.2 %collective-permute-start.27 = (bf16[4,576,128]{2,1,0:T(8,128)(2,1)}, bf16[4,576,128]{2,1,0:T(8,128)(2,1)S(1)}, u32[]{:S(2)}, u32[]{:S(2)}) collective-permute-start(bf16[4,576,128]{2,1,0:T(8,128)(2,1)} %pad_maximum_fusion.2.refs_0_), channel_id=1, source_target_pairs={{0,2},{2,0},{4,6},{6,4},{8,10},{10,8},{12,14},{14,12},{16,18},{18,... | collective-permute-start | bytes 1769480 | tf_op jit(solution)/shard_map/ppermute | solution.py:351
  141.5 36.2 %collective-permute-start.28 = (bf16[4,576,128]{2,1,0:T(8,128)(2,1)}, bf16[4,576,128]{2,1,0:T(8,128)(2,1)}, u32[]{:S(2)}, u32[]{:S(2)}) collective-permute-start(bf16[4,576,128]{2,1,0:T(8,128)(2,1)} %pad_maximum_fusion.3.refs_8_), channel_id=1, source_target_pairs={{0,4},{2,6},{4,0},{6,2},{8,12},{10,14},{12,8},{14,10},{16,20},{18,... | collective-permute-start | bytes 1769480 | tf_op jit(solution)/shard_map/ppermute | solution.py:351
  191.2 112.2 %all-to-all-start.1 = ((bf16[16,96,1024]{2,1,0:T(8,128)(2,1)}), bf16[16,96,1024]{2,1,0:T(8,128)(2,1)}, u32[]{:S(2)}, u32[]{:S(2)}) async-start(bf16[16,96,1024]{2,1,0:T(8,128)(2,1)} %hphi.1), calls=%async_computation.1 | async-start | bytes 6291456 | tf_op jit(solution)/shard_map/all_to_all | solution.py:377
  205.2 39.3 %collective-permute-start.29 = (bf16[4,576,128]{2,1,0:T(8,128)(2,1)}, bf16[4,576,128]{2,1,0:T(8,128)(2,1)S(1)}, u32[]{:S(2)}, u32[]{:S(2)}) collective-permute-start(bf16[4,576,128]{2,1,0:T(8,128)(2,1)} %pad_maximum_fusion.2.refs_0_), channel_id=1, source_target_pairs={{0,4},{2,6},{4,0},{6,2},{8,12},{10,14},{12,8},{14,10},{16,20},{18,... | collective-permute-start | bytes 1769480 | tf_op jit(solution)/shard_map/ppermute | solution.py:351
  207.2 37.4 %collective-permute-start.35 = (bf16[4,576,128]{2,1,0:T(8,128)(2,1)}, bf16[4,576,128]{2,1,0:T(8,128)(2,1)S(1)}, u32[]{:S(2)}, u32[]{:S(2)}) collective-permute-start(bf16[4,576,128]{2,1,0:T(8,128)(2,1)} %pad_maximum_fusion.3.refs_8_), channel_id=1, source_target_pairs={{0,2},{2,0},{4,6},{6,4},{8,10},{10,8},{12,14},{14,12},{16,18},{18,... | collective-permute-start | bytes 1769480 | tf_op jit(solution)/shard_map/ppermute | solution.py:351
  208.6 37.5 %collective-permute-start.31 = (bf16[4,576,128]{2,1,0:T(8,128)(2,1)}, bf16[4,576,128]{2,1,0:T(8,128)(2,1)S(1)}, u32[]{:S(2)}, u32[]{:S(2)}) collective-permute-start(bf16[4,576,128]{2,1,0:T(8,128)(2,1)} %pad_maximum_fusion.2.refs_0_), channel_id=1, source_target_pairs={{0,1},{1,0},{2,3},{3,2},{4,5},{5,4},{6,7},{7,6},{8,9},{9,8},{10,11... | collective-permute-start | bytes 1769480 | tf_op jit(solution)/shard_map/ppermute | solution.py:363
  208.6 37.7 %collective-permute-start.37 = (bf16[4,576,128]{2,1,0:T(8,128)(2,1)}, bf16[4,576,128]{2,1,0:T(8,128)(2,1)S(1)}, u32[]{:S(2)}, u32[]{:S(2)}) collective-permute-start(bf16[4,576,128]{2,1,0:T(8,128)(2,1)} %pad_maximum_fusion.3.refs_8_), channel_id=1, source_target_pairs={{0,1},{1,0},{2,3},{3,2},{4,5},{5,4},{6,7},{7,6},{8,9},{9,8},{10,11... | collective-permute-start | bytes 1769480 | tf_op jit(solution)/shard_map/ppermute | solution.py:363
  244.6 28.2 %copy-start.16 = (bf16[4,576,128]{2,1,0:T(8,128)(2,1)}, bf16[4,576,128]{2,1,0:T(8,128)(2,1)S(1)}, u32[]{:S(2)}) copy-start(bf16[4,576,128]{2,1,0:T(8,128)(2,1)S(1)} %collective-permute-done.29.refs_2_) | copy-start | bytes 1769476
  244.6 2.1 collective-permute-start.33
  244.6 24.4 %collective-permute-start.30 = (bf16[4,576,128]{2,1,0:T(8,128)(2,1)}, bf16[4,576,128]{2,1,0:T(8,128)(2,1)S(1)}, u32[]{:S(2)}, u32[]{:S(2)}) collective-permute-start(bf16[4,576,128]{2,1,0:T(8,128)(2,1)} %copy-done.15), channel_id=1, source_target_pairs={{0,4},{2,6},{4,0},{6,2},{8,12},{10,14},{12,8},{14,10},{16,20},{18,... | collective-permute-start | bytes 1769480 | tf_op jit(solution)/shard_map/ppermute | solution.py:351
  244.6 26.1 %collective-permute-start.36 = (bf16[4,576,128]{2,1,0:T(8,128)(2,1)}, bf16[4,576,128]{2,1,0:T(8,128)(2,1)S(1)}, u32[]{:S(2)}, u32[]{:S(2)}) collective-permute-start(bf16[4,576,128]{2,1,0:T(8,128)(2,1)} %collective-permute-done.28.refs_10_), channel_id=1, source_target_pairs={{0,2},{2,0},{4,6},{6,4},{8,10},{10,8},{12,14},{14,12},{16,18},{18,... | collective-permute-start | bytes 1769480 | tf_op jit(solution)/shard_map/ppermute | solution.py:351
  246.1 24.7 %collective-permute-start.38 = (bf16[4,576,128]{2,1,0:T(8,128)(2,1)S(1)}, bf16[4,576,128]{2,1,0:T(8,128)(2,1)S(1)}, u32[]{:S(2)}, u32[]{:S(2)}) collective-permute-start(bf16[4,576,128]{2,1,0:T(8,128)(2,1)S(1)} %collective-permute-done.35.refs_9_), channel_id=1, source_target_pairs={{0,1},{1,0},{2,3},{3,2},{4,5},{5,4},{6,7},{7,6},{8,9},{9,8},{10,11... | collective-permute-start | bytes 1769480 | tf_op jit(solution)/shard_map/ppermute | solution.py:363
  246.3 24.4 %collective-permute-start.32 = (bf16[4,576,128]{2,1,0:T(8,128)(2,1)}, bf16[4,576,128]{2,1,0:T(8,128)(2,1)S(1)}, u32[]{:S(2)}, u32[]{:S(2)}) collective-permute-start(bf16[4,576,128]{2,1,0:T(8,128)(2,1)} %copy-done.15), channel_id=1, source_target_pairs={{0,1},{1,0},{2,3},{3,2},{4,5},{5,4},{6,7},{7,6},{8,9},{9,8},{10,11... | collective-permute-start | bytes 1769480 | tf_op jit(solution)/shard_map/ppermute | solution.py:363
  246.7 24.2 %collective-permute-start.39 = (bf16[4,576,128]{2,1,0:T(8,128)(2,1)}, bf16[4,576,128]{2,1,0:T(8,128)(2,1)S(1)}, u32[]{:S(2)}, u32[]{:S(2)}) collective-permute-start(bf16[4,576,128]{2,1,0:T(8,128)(2,1)} %collective-permute-done.28.refs_10_), channel_id=1, source_target_pairs={{0,1},{1,0},{2,3},{3,2},{4,5},{5,4},{6,7},{7,6},{8,9},{9,8},{10,11... | collective-permute-start | bytes 1769480 | tf_op jit(solution)/shard_map/ppermute | solution.py:363
  268.9 2.0 collective-permute-start.34
  270.7 2.0 collective-permute-start.40
  (23 other events, 221.3 us)

commit v4 on v3

--- a/solution.py
+++ b/solution.py
@@ -29,12 +29,12 @@
 SIDES = (4, 2, 2)
 
 
-def block_places(here, blocks, pieces=PIECES):
+def block_places(here, blocks):
     rep, y, x = (here[k] for k in range(3))
     places = []
     for n, block in enumerate(blocks):
         core = rep if n < len(blocks) // 2 else 1 - rep
-        piece = n // 4 % pieces
+        piece = n // 4 % PIECES
         to_y = y if n % 4 < 2 else 1 - y
         to_x = x if n % 2 == 0 else 1 - x
         places.append((block, core, piece, to_y * SIDES[2] + to_x))
@@ -225,26 +225,29 @@
     lax.fori_loop(0, NB * NNZB, one_block, 0, unroll=4)
 
 
-def first_kernel(here, k_cols, h_cols, *refs):
+def first_kernel(here, k_cols, h_cols, *refs, resident):
     phi, dense_k, product, dense_h, k_blocks, h_blocks, sems = refs[-7:]
-    half = (len(refs) - 7) // 2
-    depth = refs[0].shape[-2]
+    parts = refs[:-7]
 
     def copies(which):
-        stored = refs[which * half : (which + 1) * half]
         target = (k_blocks, h_blocks)[which]
-        if half == 1:
-            return [pltpu.make_async_copy(stored[0], target, sems.at[which, 0, 0])]
+        if not resident:
+            return [pltpu.make_async_copy(parts[which], target, sems.at[which, 0, 0])]
+        depth = parts[0].shape[-2]
+        rep, y, x, z = (here[k] for k in range(4))
         out_list = []
-        columns = SIDES[1] * SIDES[2]
-        for n, (block, core, _, column) in enumerate(block_places(here, stored, 1)):
-            for z in range(SIDES[0]):
-                row = ((core * SIDES[0] + z) * columns + column) * depth
+        for n, part in enumerate(parts):
+            core = rep if n < SIDES[0] else 1 - rep
+            level = lax.rem(z + SIDES[0] - n % SIDES[0], SIDES[0])
+            for c in range(SIDES[1] * SIDES[2]):
+                to_y = y if c < 2 else 1 - y
+                to_x = x if c % 2 == 0 else 1 - x
+                row = (((core * SIDES[0] + level) * SIDES[1] + to_y) * SIDES[2] + to_x) * depth
                 out_list.append(
                     pltpu.make_async_copy(
-                        block.at[z],
+                        part.at[which, c],
                         target.at[pl.ds(pl.multiple_of(row, depth), depth)],
-                        sems.at[which, n, z],
+                        sems.at[which, n, c],
                     )
                 )
         return out_list
@@ -267,14 +270,14 @@
     )
 
 
-def first_products(here, k_cols, h_cols, k_parts, h_parts, phi):
+def first_products(here, k_cols, h_cols, parts, phi, resident):
     width = phi.shape[1]
     tile = min(COLS, width)
     stored = pltpu.VMEM((NB * NNZB * BLK, BLK), jnp.bfloat16)
     grid_spec = pltpu.PrefetchScalarGridSpec(
         num_scalar_prefetch=3,
         grid=(width // tile,),
-        in_specs=[pl.BlockSpec(memory_space=pl.ANY)] * (2 * len(k_parts))
+        in_specs=[pl.BlockSpec(memory_space=pl.ANY)] * len(parts)
         + [pl.BlockSpec((NF, tile), lambda i, *s: (0, i))],
         out_specs=[
             pl.BlockSpec((NF, NF), lambda i, *s: (0, 0)),
@@ -284,11 +287,11 @@
             pltpu.VMEM((NF, NF), jnp.bfloat16),
             stored,
             stored,
-            pltpu.SemaphoreType.DMA((2, len(k_parts), SIDES[0])),
+            pltpu.SemaphoreType.DMA((2, len(parts), SIDES[1] * SIDES[2])),
         ],
     )
     return pl.pallas_call(
-        first_kernel,
+        functools.partial(first_kernel, resident=resident),
         out_shape=[
             jax.ShapeDtypeStruct((NF, NF), jnp.bfloat16),
             jax.ShapeDtypeStruct((NF, width), jnp.float32),
@@ -299,7 +302,7 @@
         cost_estimate=pl.CostEstimate(
             flops=4 * NF * NF * width, bytes_accessed=24 << 20, transcendentals=0
         ),
-    )(here, k_cols, h_cols, *k_parts, *h_parts, phi)
+    )(here, k_cols, h_cols, *parts, phi)
 
 
 def last_kernel(dense_k, hphi, product, out):
@@ -351,10 +354,20 @@
     return lax.ppermute(block, "func", [(i, i ^ bit) for i in range(n)])
 
 
-def ordered(lines, near, far, first=0):
+def onward(block, step, up):
+    n = lax.axis_size("func")
+    plane = n // SIDES[0]
+    if up:
+        route = [(i, i + plane) for i in range(plane * (step - 1), n - plane)]
+    else:
+        route = [(i, i - plane) for i in range(plane, n - plane * (step - 1))]
+    return lax.ppermute(block, "func", route)
+
+
+def ordered(lines, near, far):
     blocks = []
     for p, (line, close, (apart, corner)) in enumerate(zip(lines, near, far)):
-        middle = [close, apart] if (p + first) % 2 == 0 else [apart, close]
+        middle = [close, apart] if p % 2 == 0 else [apart, close]
         blocks += [line, *middle, corner]
     return blocks
 
@@ -388,33 +401,49 @@
     halo = lax.ppermute(edge, "rep", [(0, 1), (1, 0)])
     info = jnp.concatenate([centres[:, :1] + planes * rep, centres[:, 1:]], axis=1)
     info = info.astype(jnp.int32)
+    band = planar_band()
 
     resident = n_func == SIDES[0] * SIDES[1] * SIDES[2]
     if resident:
-        _, y, x = place_of()
-        here = jnp.stack([rep, y, x]).astype(jnp.int32)
+        level, y, x = place_of()
+        here = jnp.stack([rep, y, x, level]).astype(jnp.int32)
         per = x_blocks // PIECES
+        stored = [kernel[0], hamiltonian[0]]
         lines = [along_z(half[p * per : (p + 1) * per]) for p in range(PIECES)]
-        lines, kernel, hamiltonian = lax.optimization_barrier((lines, kernel, hamiltonian))
+        close = [swapped(stored[p], 1 + p) for p in range(2)]
+        apart = [(swapped(stored[p], 2 - p), swapped(close[p], 2 - p)) for p in range(2)]
+        around = ordered(stored, close, apart)
+        around = jnp.stack([jnp.stack(around[:4]), jnp.stack(around[4:])])
+        lines, around, halo, band, info, phi_cut = lax.optimization_barrier(
+            (lines, around, halo, band, info, phi_cut)
+        )
         near = [swapped(lines[p], 1 + p) for p in range(PIECES)]
-        matrix_lines = [along_z(stored[0]) for stored in (kernel, hamiltonian)]
+        ups, downs = [onward(around, 1, True)], [onward(around, 1, False)]
+        lines_too = [other_core(block) for block in lines]
+        near, ups, downs = lax.optimization_barrier((near, ups, downs))
         far = [(swapped(lines[p], 2 - p), swapped(near[p], 2 - p)) for p in range(PIECES)]
-        pot = ordered(lines, near, far)
-        pot, matrix_lines, phi_cut = lax.optimization_barrier((pot, matrix_lines, phi_cut))
-        pot = pot + [other_core(block) for block in pot]
+        ups.append(onward(ups[0], 2, True))
+        downs.append(onward(downs[0], 2, False))
+        near_too = [other_core(block) for block in near]
+        far, ups, downs, phi_cut, lines_too, near_too = lax.optimization_barrier(
+            (far, ups, downs, phi_cut, lines_too, near_too)
+        )
         phi_pts = exchange(phi_cut)
-        matrix_near = [swapped(matrix_lines[p], 1 + p) for p in range(2)]
+        ups.append(onward(ups[1], 3, True))
+        downs.append(onward(downs[1], 3, False))
+        far_too = [tuple(other_core(block) for block in pair) for pair in far]
+        pot = ordered(lines, near, far) + ordered(lines_too, near_too, far_too)
     else:
-        here = jnp.stack([rep, rep, rep]).astype(jnp.int32)
+        here = jnp.stack([rep, rep, rep, rep]).astype(jnp.int32)
         pot = lax.all_gather(half, ("rep", "func"), axis=0, tiled=False)
         pot = pot.reshape(n_rep, n_func, x_blocks, z_planes, ROWS, y_size)
         pot = pot.transpose(0, 2, 1, 3, 4, 5)
         pot = [pot.reshape(n_rep, x_blocks, n_func * z_planes, ROWS, y_size)]
         phi_pts = exchange(phi_cut)
-        k_parts, h_parts = (
-            [lax.all_gather(stored, ("rep", "func"), axis=1, tiled=True).reshape(-1, BLK)]
+        parts = [
+            lax.all_gather(stored, ("rep", "func"), axis=1, tiled=True).reshape(-1, BLK)
             for stored in (kernel, hamiltonian)
-        )
+        ]
 
     extra = -owned % GROUP
     padded = [
@@ -423,21 +452,16 @@
         jnp.pad(halo, ((0, 0), (0, extra), (0, 0))),
     ]
     info, phi_planes, halo = padded
-    hphi = make_hphi(info, here, phi_planes, halo, planar_band(), pot, resident)[:, :owned]
+    hphi = make_hphi(info, here, phi_planes, halo, band, pot, resident)[:, :owned]
     if resident:
-        hphi, matrix_near = lax.optimization_barrier((hphi, matrix_near))
-        matrix_far = [
-            (swapped(matrix_lines[p], 2 - p), swapped(matrix_near[p], 2 - p)) for p in range(2)
-        ]
-        k_parts, h_parts = (
-            ordered(matrix_lines[p : p + 1], matrix_near[p : p + 1], matrix_far[p : p + 1], p)
-            for p in range(2)
-        )
-        k_parts = k_parts + [other_core(block) for block in k_parts]
-        h_parts = h_parts + [other_core(block) for block in h_parts]
+        hphi, ups, downs = lax.optimization_barrier((hphi, ups, downs))
+        parts = [around]
+        for k in range(1, SIDES[0]):
+            parts.append(jnp.where(level >= k, ups[k - 1], downs[SIDES[0] - 1 - k]))
+        parts = parts + [other_core(part) for part in parts]
     phi_pts = phi_pts.reshape(n_func * owned, width)
     dense_k, product = first_products(
-        here, kernel_cols, intersection_cols, k_parts, h_parts, phi_pts
+        here, kernel_cols, intersection_cols, parts, phi_pts, resident
     )
     hphi_pts = exchange(cut(hphi)).reshape(n_func * owned, width)
     gradient = last_product(dense_k, hphi_pts, product)

time: 402 us -> 397 us (0.988)
  starting transfers between devices: 68.7 us -> 60.2 us
    ppermute x0 -> x6, waiting for transfers between devices: none -> 37.5 us  [onward(): return lax.ppermute(block, 'func', route)]
    ppermute x12 -> x6, waiting for transfers between devices: 47.8 us -> 17.8 us  [along_z(): lax.ppermute(part, 'func', [(i, (i + 4 * k) % n) for i in range(n)])]
    ppermute x12 -> x6, starting transfers between devices: 30.3 us -> 14.3 us  [along_z(): lax.ppermute(part, 'func', [(i, (i + 4 * k) % n) for i in range(n)])]
    ppermute x12, waiting for transfers between devices: 88.6 us -> 73.9 us  [swapped(): return lax.ppermute(block, 'func', [(i, i ^ bit) for i in range(n)])]
    all_to_all x2, waiting for transfers between devices: 11.8 us -> 20.9 us  [exchange(): return lax.all_to_all(rows, 'func', split_axis=0, concat_axis=0, tiled=True)]
    ppermute x0 -> x6, starting transfers between devices: none -> 7.67 us  [onward(): return lax.ppermute(block, 'func', route)]
    select_n x0 -> x3, other arithmetic: none -> 4.31 us  [shards(): parts.append(jnp.where(level >= k, ups[k - 1], downs[SIDES[0] - 1 - k]))]
  transfers between devices with their start and end apart: 43 -> 39, of which waited for: 20 -> 16; matrix products, arithmetic and copies ran while one was open for 2% -> 4% of each run, Pallas kernels for 16% -> 16%
where the time goes in v4:
time: 397 us
  waiting for transfers between devices  155 us (39%)
  blocking collectives  84.7 us (21%)
  Pallas kernels  73.1 us (18%)
  starting transfers between devices  60.2 us (15%)
  local copies, waits for them, and re-layouts  14.9 us (4%)
  other arithmetic  8.57 us (2%)
    all_to_all x1, blocking collectives, exchange(): return lax.all_to_all(rows, 'func', split_axis=0, concat_axis=0, tiled=True)  84.7 us
    ppermute x12, waiting for transfers between devices, swapped(): return lax.ppermute(block, 'func', [(i, i ^ bit) for i in range(n)])  73.9 us
    ppermute x6, waiting for transfers between devices, onward(): return lax.ppermute(block, 'func', route)  37.5 us
    pallas_call x1, Pallas kernels, make_hphi(): pl.pallas_call(functools.partial(hphi_kernel, resident=resident), out_sha...  32.9 us
    pallas_call x1, Pallas kernels, first_products(): pl.pallas_call(functools.partial(first_kernel, resident=resident), out_sh...  29.9 us
    all_to_all x2, waiting for transfers between devices, exchange(): return lax.all_to_all(rows, 'func', split_axis=0, concat_axis=0, tiled=True)  20.9 us
    all_to_all x2, starting transfers between devices, exchange(): return lax.all_to_all(rows, 'func', split_axis=0, concat_axis=0, tiled=True)  18.1 us
    ppermute x6, waiting for transfers between devices, along_z(): lax.ppermute(part, 'func', [(i, (i + 4 * k) % n) for i in range(n)])  17.8 us
  transfers between devices with their start and end apart: 39, of which 16 were waited for; matrix products, arithmetic and copies ran while one was open for 4% of the time, Pallas kernels for 16%

profile of v4, /device:TPU:0, one launch (start us, length us, event | category | flops | bytes accessed | tf_op | source)
XLA Modules:
  0.0 396.6 jit_solution(626328257107053399)
XLA Ops:
  0.0 1.6 copy-done
  1.8 5.1 %collective-permute-start.3 = (bf16[2,32,16,128]{3,2,1,0:T(8,128)(2,1)S(1)}, bf16[2,32,16,128]{3,2,1,0:T(8,128)(2,1)S(1)}, u32[]{:S(2)}, u32[]{:S(2)}) collective-permute-start(bf16[2,32,16,128]{3,2,1,0:T(8,128)(2,1)S(1)} %get-tuple-element.79), channel_id=1, source_target_pairs={{0,24},{2,26},{4,28},{6,30},{8,0},{10,2},{12,4},{14,6},{16,8},{18,... | collective-permute-start | bytes 786440 | tf_op jit(solution)/shard_map/ppermute | solution.py:341
  6.9 1.0 collective-permute-start.5
  7.9 2.8 collective-permute-start
  10.7 1.1 collective-permute-start.1
  11.9 1.6 select_convert_fusion.band
  13.5 5.3 %copy.25 = bf16[96,16,1024]{2,0,1:T(8,128)(2,1)} copy(bf16[96,16,1024]{2,1,0:T(8,128)(2,1)} %param.7) | data formatting | bytes 6291456 | tf_op args[0]
  18.8 1.2 slice_select_fusion
  20.0 4.2 %collective-permute-start.2 = (bf16[2,32,16,128]{3,2,1,0:T(8,128)(2,1)S(1)}, bf16[2,32,16,128]{3,2,1,0:T(8,128)(2,1)S(1)}, u32[]{:S(2)}, u32[]{:S(2)}) collective-permute-start(bf16[2,32,16,128]{3,2,1,0:T(8,128)(2,1)S(1)} %get-tuple-element.80), channel_id=1, source_target_pairs={{0,8},{2,10},{4,12},{6,14},{8,16},{10,18},{12,20},{14,22},{16,24},... | collective-permute-start | bytes 786440 | tf_op jit(solution)/shard_map/ppermute | solution.py:341
  24.2 7.3 %collective-permute-done.4 = bf16[2,32,16,128]{3,2,1,0:T(8,128)(2,1)S(1)} collective-permute-done((bf16[2,32,16,128]{3,2,1,0:T(8,128)(2,1)S(1)}, bf16[2,32,16,128]{3,2,1,0:T(8,128)(2,1)S(1)}, u32[]{:S(2)}, u32[]{:S(2)}) %collective-permute-start.4) | collective-permute-done | bytes 262176 | tf_op jit(solution)/shard_map/ppermute | solution.py:341
  31.5 1.5 collective-permute-start.6
  33.0 1.5 collective-permute-start.10
  34.6 2.7 collective-permute-done.6
  37.3 1.5 collective-permute-start.7
  38.9 2.3 collective-permute-start.9
  41.2 10.5 %collective-permute-done.1 = bf16[2,32,16,128]{3,2,1,0:T(8,128)(2,1)S(1)} collective-permute-done((bf16[2,32,16,128]{3,2,1,0:T(8,128)(2,1)S(1)}, bf16[2,32,16,128]{3,2,1,0:T(8,128)(2,1)S(1)}, u32[]{:S(2)}, u32[]{:S(2)}) %collective-permute-start.1) | collective-permute-done | bytes 262176 | tf_op jit(solution)/shard_map/ppermute | solution.py:341
  51.7 1.5 collective-permute-start.8
  53.2 1.5 collective-permute-start.11
  55.1 1.7 collective-permute-done.8
  56.9 1.4 collective-permute-done.11
  58.6 1.4 collective-permute-start.15
  60.0 1.3 collective-permute-start.16
  61.3 1.6 collective-permute-start.13
  62.8 1.5 collective-permute-start.14
  64.8 19.8 %collective-permute-done.13.refs_1_ = bf16[4,2,32,16,128]{4,3,2,1,0:T(8,128)(2,1)S(1)} collective-permute-done((bf16[4,2,32,16,128]{4,3,2,1,0:T(8,128)(2,1)S(1)}, bf16[4,2,32,16,128]{4,3,2,1,0:T(8,128)(2,1)S(1)}, u32[]{:S(2)}, u32[]{:S(2)}) %collective-permute-start.13) | collective-permute-done | bytes 1048608 | tf_op jit(solution)/shard_map/ppermute | solution.py:354
  84.6 1.5 collective-permute-start.19
  86.1 2.8 collective-permute-done.14.refs_6_
  89.4 1.5 collective-permute-start.18
  91.0 20.5 %collective-permute-done.17.refs_2_ = bf16[4,2,32,16,128]{4,3,2,1,0:T(8,128)(2,1)} collective-permute-done((bf16[4,2,32,16,128]{4,3,2,1,0:T(8,128)(2,1)S(1)}, bf16[4,2,32,16,128]{4,3,2,1,0:T(8,128)(2,1)}, u32[]{:S(2)}, u32[]{:S(2)}) %collective-permute-start.17) | collective-permute-done | bytes 1048608 | tf_op jit(solution)/shard_map/ppermute | solution.py:354
  112.2 1.3 collective-permute-start.22
  114.3 16.1 %collective-permute-done.18.refs_3_ = bf16[4,2,32,16,128]{4,3,2,1,0:T(8,128)(2,1)S(1)} collective-permute-done((bf16[4,2,32,16,128]{4,3,2,1,0:T(8,128)(2,1)S(1)}, bf16[4,2,32,16,128]{4,3,2,1,0:T(8,128)(2,1)S(1)}, u32[]{:S(2)}, u32[]{:S(2)}) %collective-permute-start.18) | collective-permute-done | bytes 1048608 | tf_op jit(solution)/shard_map/ppermute | solution.py:354
  130.3 8.9 %collective-permute-done.20.refs_7_ = bf16[4,2,32,16,128]{4,3,2,1,0:T(8,128)(2,1)S(1)} collective-permute-done((bf16[4,2,32,16,128]{4,3,2,1,0:T(8,128)(2,1)S(1)}, bf16[4,2,32,16,128]{4,3,2,1,0:T(8,128)(2,1)S(1)}, u32[]{:S(2)}, u32[]{:S(2)}) %collective-permute-start.20) | collective-permute-done | bytes 1048608 | tf_op jit(solution)/shard_map/ppermute | solution.py:354
  142.0 11.7 %all-to-all-start = ((bf16[16,96,1024]{2,1,0:T(8,128)(2,1)}), bf16[16,96,1024]{2,1,0:T(8,128)(2,1)}, u32[]{:S(2)}, u32[]{:S(2)}) async-start(bf16[16,96,1024]{2,1,0:T(8,128)(2,1)} %bitcast.45.phi), calls=%async_computation | async-start | bytes 6291456 | tf_op jit(solution)/shard_map/all_to_all | solution.py:390
  156.1 1.7 collective-permute-start.31
  157.8 1.3 collective-permute-start.32
  159.8 1.5 collective-permute-done.30.refs_15_
  161.3 32.9 %hphi.1 = bf16[16,96,1024]{2,1,0:T(8,128)(2,1)} custom-call(s32[96,3]{1,0:T(8,128)} %copy.21.info, s32[4]{0:T(128)} %pad_add_fusion.1.here, bf16[16,96,1024]{2,1,0:T(8,128)(2,1)} %bitcast.45.phi, bf16[2,96,1024]{2,1,0:T(8,128)(2,1)} %copy-done.27, bf16[512,256]{1,0:T(8,128)(2,1)} %select_convert_fusion.band, bf16[4,2,32,16,128]{4,3,2,1,0:T(8,128)(2,1)} %copy-done.9, ...), custom_call_target="tpu_custom_call" | custom-call | flops 12884901888 | bytes 62914560 | tf_op jit(solution)/shard_map/hphi/pallas_call | solution.py:204
  194.2 37.5 %collective-permute-done.32 = bf16[2,4,576,128]{3,2,1,0:T(8,128)(2,1)} collective-permute-done((bf16[2,4,576,128]{3,2,1,0:T(8,128)(2,1)}, bf16[2,4,576,128]{3,2,1,0:T(8,128)(2,1)}, u32[]{:S(2)}, u32[]{:S(2)}) %collective-permute-start.32) | collective-permute-done | bytes 1179680 | tf_op jit(solution)/shard_map/ppermute | solution.py:364
  231.7 6.4 %all-to-all-start.1 = ((bf16[16,96,1024]{2,1,0:T(8,128)(2,1)}), bf16[16,96,1024]{2,1,0:T(8,128)(2,1)}, u32[]{:S(2)}, u32[]{:S(2)}) async-start(bf16[16,96,1024]{2,1,0:T(8,128)(2,1)} %hphi.1), calls=%async_computation.1 | async-start | bytes 6291456 | tf_op jit(solution)/shard_map/all_to_all | solution.py:390
  238.2 1.5 broadcast_select_fusion.refs_3_
  240.2 1.4 broadcast_select_fusion.1.refs_2_
  242.0 1.4 broadcast_select_fusion.2.refs_1_
  244.5 1.8 collective-permute-done.34.refs_5_
  247.4 29.9 %products.1 = (bf16[1536,1536]{1,0:T(8,128)(2,1)}, f32[1536,1024]{1,0:T(8,128)}) custom-call(s32[4]{0:T(128)} %pad_add_fusion.1.here, s32[12,12]{1,0:T(8,128)} %k_cols.1, s32[12,12]{1,0:T(8,128)} %h_cols.1, bf16[2,4,576,128]{3,2,1,0:T(8,128)(2,1)} %copy-done.2, bf16[2,4,576,128]{3,2,1,0:T(8,128)(2,1)} %copy-done.8, bf16[2,4,576,128]{3,2,1,0:T(8,128)(2,1)} %copy-done.7, ...), custom_call_target="tpu_custom_call" | custom-call | flops 9663676416 | bytes 25165824 | tf_op jit(solution)/shard_map/products/pallas_call | solution.py:293
  277.2 20.9 %all-to-all-done.1 = bf16[16,96,1024]{2,1,0:T(8,128)(2,1)} async-done(((bf16[16,96,1024]{2,1,0:T(8,128)(2,1)}), bf16[16,96,1024]{2,1,0:T(8,128)(2,1)}, u32[]{:S(2)}, u32[]{:S(2)}) %all-to-all-start.1) | async-done | bytes 3145760 | tf_op jit(solution)/shard_map/all_to_all | solution.py:390
  298.1 10.3 %gradient.1 = bf16[1536,1024]{1,0:T(8,128)(2,1)} custom-call(bf16[1536,1536]{1,0:T(8,128)(2,1)} %get-tuple-element.68.dense_k, bf16[1536,1024]{1,0:T(8,128)(2,1)} %bitcast.26.hphi, f32[1536,1024]{1,0:T(8,128)} %get-tuple-element.70.product), custom_call_target="tpu_custom_call" | custom-call | flops 4831838208 | bytes 17825792 | tf_op jit(solution)/shard_map/gradient/pallas_call | solution.py:317
  308.4 84.7 %all_to_all.15 = bf16[16,96,1024]{2,1,0:T(8,128)(2,1)S(1)} all-to-all(bf16[16,96,1024]{2,1,0:T(8,128)(2,1)} %bitcast.51), channel_id=1, replica_groups=mesh['func'=16,'rep'=2] {'func'}, dimensions={0} | all-to-all | bytes 6291456 | tf_op jit(solution)/shard_map/all_to_all | solution.py:390
  393.2 3.4 copy.22
  (117 shorter events, 12.3 us)
Async XLA Ops:
  1.8 18.2 %collective-permute-start.3 = (bf16[2,32,16,128]{3,2,1,0:T(8,128)(2,1)S(1)}, bf16[2,32,16,128]{3,2,1,0:T(8,128)(2,1)S(1)}, u32[]{:S(2)}, u32[]{:S(2)}) collective-permute-start(bf16[2,32,16,128]{3,2,1,0:T(8,128)(2,1)S(1)} %get-tuple-element.79), channel_id=1, source_target_pairs={{0,24},{2,26},{4,28},{6,30},{8,0},{10,2},{12,4},{14,6},{16,8},{18,... | collective-permute-start | bytes 786440 | tf_op jit(solution)/shard_map/ppermute | solution.py:341
  6.9 24.6 %collective-permute-start.4 = (bf16[2,32,16,128]{3,2,1,0:T(8,128)(2,1)S(1)}, bf16[2,32,16,128]{3,2,1,0:T(8,128)(2,1)S(1)}, u32[]{:S(2)}, u32[]{:S(2)}) collective-permute-start(bf16[2,32,16,128]{3,2,1,0:T(8,128)(2,1)S(1)} %get-tuple-element.79), channel_id=1, source_target_pairs={{0,16},{2,18},{4,20},{6,22},{8,24},{10,26},{12,28},{14,30},{16,0},... | collective-permute-start | bytes 786440 | tf_op jit(solution)/shard_map/ppermute | solution.py:341
  6.9 26.1 %collective-permute-start.5 = (bf16[2,32,16,128]{3,2,1,0:T(8,128)(2,1)S(1)}, bf16[2,32,16,128]{3,2,1,0:T(8,128)(2,1)S(1)}, u32[]{:S(2)}, u32[]{:S(2)}) collective-permute-start(bf16[2,32,16,128]{3,2,1,0:T(8,128)(2,1)S(1)} %get-tuple-element.79), channel_id=1, source_target_pairs={{0,8},{2,10},{4,12},{6,14},{8,16},{10,18},{12,20},{14,22},{16,24},... | collective-permute-start | bytes 786440 | tf_op jit(solution)/shard_map/ppermute | solution.py:341
  7.9 33.3 %collective-permute-start = (bf16[2,32,16,128]{3,2,1,0:T(8,128)(2,1)S(1)}, bf16[2,32,16,128]{3,2,1,0:T(8,128)(2,1)S(1)}, u32[]{:S(2)}, u32[]{:S(2)}) collective-permute-start(bf16[2,32,16,128]{3,2,1,0:T(8,128)(2,1)S(1)} %get-tuple-element.80), channel_id=1, source_target_pairs={{0,24},{2,26},{4,28},{6,30},{8,0},{10,2},{12,4},{14,6},{16,8},{18,... | collective-permute-start | bytes 786440 | tf_op jit(solution)/shard_map/ppermute | solution.py:341
  10.7 41.0 %collective-permute-start.1 = (bf16[2,32,16,128]{3,2,1,0:T(8,128)(2,1)S(1)}, bf16[2,32,16,128]{3,2,1,0:T(8,128)(2,1)S(1)}, u32[]{:S(2)}, u32[]{:S(2)}) collective-permute-start(bf16[2,32,16,128]{3,2,1,0:T(8,128)(2,1)S(1)} %get-tuple-element.80), channel_id=1, source_target_pairs={{0,16},{2,18},{4,20},{6,22},{8,24},{10,26},{12,28},{14,30},{16,0},... | collective-permute-start | bytes 786440 | tf_op jit(solution)/shard_map/ppermute | solution.py:341
  20.0 33.2 %collective-permute-start.2 = (bf16[2,32,16,128]{3,2,1,0:T(8,128)(2,1)S(1)}, bf16[2,32,16,128]{3,2,1,0:T(8,128)(2,1)S(1)}, u32[]{:S(2)}, u32[]{:S(2)}) collective-permute-start(bf16[2,32,16,128]{3,2,1,0:T(8,128)(2,1)S(1)} %get-tuple-element.80), channel_id=1, source_target_pairs={{0,8},{2,10},{4,12},{6,14},{8,16},{10,18},{12,20},{14,22},{16,24},... | collective-permute-start | bytes 786440 | tf_op jit(solution)/shard_map/ppermute | solution.py:341
  31.5 5.8 %collective-permute-start.6 = (bf16[576,128]{1,0:T(8,128)(2,1)S(1)}, bf16[576,128]{1,0:T(8,128)(2,1)S(1)}, u32[]{:S(2)}, u32[]{:S(2)}) collective-permute-start(bf16[576,128]{1,0:T(8,128)(2,1)S(1)} %bitcast.53), channel_id=1, source_target_pairs={{0,2},{2,0},{4,6},{6,4},{8,10},{10,8},{12,14},{14,12},{16,18},{18,... | collective-permute-start | bytes 442376 | tf_op jit(solution)/shard_map/ppermute | solution.py:354
  33.0 5.9 %collective-permute-start.10 = (bf16[576,128]{1,0:T(8,128)(2,1)S(1)}, bf16[576,128]{1,0:T(8,128)(2,1)S(1)}, u32[]{:S(2)}, u32[]{:S(2)}) collective-permute-start(bf16[576,128]{1,0:T(8,128)(2,1)S(1)} %bitcast.55), channel_id=1, source_target_pairs={{0,4},{2,6},{4,0},{6,2},{8,12},{10,14},{12,8},{14,10},{16,20},{18,... | collective-permute-start | bytes 442376 | tf_op jit(solution)/shard_map/ppermute | solution.py:354
  37.3 17.8 %collective-permute-start.7 = (bf16[576,128]{1,0:T(8,128)(2,1)S(1)}, bf16[576,128]{1,0:T(8,128)(2,1)S(1)}, u32[]{:S(2)}, u32[]{:S(2)}) collective-permute-start(bf16[576,128]{1,0:T(8,128)(2,1)S(1)} %bitcast.54), channel_id=1, source_target_pairs={{0,4},{2,6},{4,0},{6,2},{8,12},{10,14},{12,8},{14,10},{16,20},{18,... | collective-permute-start | bytes 442376 | tf_op jit(solution)/shard_map/ppermute | solution.py:354
  38.9 18.0 %collective-permute-start.9 = (bf16[576,128]{1,0:T(8,128)(2,1)S(1)}, bf16[576,128]{1,0:T(8,128)(2,1)S(1)}, u32[]{:S(2)}, u32[]{:S(2)}) collective-permute-start(bf16[576,128]{1,0:T(8,128)(2,1)S(1)} %bitcast.56), channel_id=1, source_target_pairs={{0,2},{2,0},{4,6},{6,4},{8,10},{10,8},{12,14},{14,12},{16,18},{18,... | collective-permute-start | bytes 442376 | tf_op jit(solution)/shard_map/ppermute | solution.py:354
  41.2 17.4 %collective-permute-start.12 = (bf16[2,96,1024]{2,1,0:T(8,128)(2,1)S(1)}, bf16[2,96,1024]{2,1,0:T(8,128)(2,1)S(1)}, u32[]{:S(2)}, u32[]{:S(2)}) collective-permute-start(bf16[2,96,1024]{2,1,0:T(8,128)(2,1)S(1)} %slice_select_fusion), channel_id=1, source_target_pairs={{0,1},{1,0},{2,3},{3,2},{4,5},{5,4},{6,7},{7,6},{8,9},{9,8},{10,11... | collective-permute-start | bytes 1179656 | tf_op jit(solution)/shard_map/ppermute | solution.py:401
  51.7 5.1 %collective-permute-start.8 = (bf16[576,128]{1,0:T(8,128)(2,1)S(1)}, bf16[576,128]{1,0:T(8,128)(2,1)S(1)}, u32[]{:S(2)}, u32[]{:S(2)}) collective-permute-start(bf16[576,128]{1,0:T(8,128)(2,1)S(1)} %collective-permute-done.6), channel_id=1, source_target_pairs={{0,4},{2,6},{4,0},{6,2},{8,12},{10,14},{12,8},{14,10},{16,20},{18,... | collective-permute-start | bytes 442376 | tf_op jit(solution)/shard_map/ppermute | solution.py:354
  53.2 5.1 %collective-permute-start.11 = (bf16[576,128]{1,0:T(8,128)(2,1)S(1)}, bf16[576,128]{1,0:T(8,128)(2,1)S(1)}, u32[]{:S(2)}, u32[]{:S(2)}) collective-permute-start(bf16[576,128]{1,0:T(8,128)(2,1)S(1)} %collective-permute-done.10), channel_id=1, source_target_pairs={{0,2},{2,0},{4,6},{6,4},{8,10},{10,8},{12,14},{14,12},{16,18},{18,... | collective-permute-start | bytes 442376 | tf_op jit(solution)/shard_map/ppermute | solution.py:354
  55.1 33.8 %copy-start.9 = (bf16[4,2,32,16,128]{4,3,2,1,0:T(8,128)(2,1)}, bf16[4,2,32,16,128]{4,3,2,1,0:T(8,128)(2,1)S(1)}, u32[]{:S(2)}) copy-start(bf16[4,2,32,16,128]{4,3,2,1,0:T(8,128)(2,1)S(1)} %get-tuple-element.42.refs_0_) | copy-start | bytes 3145732
  55.1 33.8 %copy-start.10 = (bf16[4,2,32,16,128]{4,3,2,1,0:T(8,128)(2,1)}, bf16[4,2,32,16,128]{4,3,2,1,0:T(8,128)(2,1)S(1)}, u32[]{:S(2)}) copy-start(bf16[4,2,32,16,128]{4,3,2,1,0:T(8,128)(2,1)S(1)} %get-tuple-element.43.refs_4_) | copy-start | bytes 3145732
  58.5 179.6 %copy-start.2 = (bf16[2,4,576,128]{3,2,1,0:T(8,128)(2,1)}, bf16[2,4,576,128]{3,2,1,0:T(8,128)(2,1)S(1)}, u32[]{:S(2)}) copy-start(bf16[2,4,576,128]{3,2,1,0:T(8,128)(2,1)S(1)} %pad_maximum_fusion.refs_0_) | copy-start | bytes 3538948
  58.5 80.7 %copy-start.27 = (bf16[2,96,1024]{2,1,0:T(8,128)(2,1)}, bf16[2,96,1024]{2,1,0:T(8,128)(2,1)S(1)}, u32[]{:S(2)}) copy-start(bf16[2,96,1024]{2,1,0:T(8,128)(2,1)S(1)} %collective-permute-done.12.halo) | copy-start | bytes 1179652
  58.6 30.4 %collective-permute-start.15 = (bf16[2,4,576,128]{3,2,1,0:T(8,128)(2,1)S(1)}, bf16[2,4,576,128]{3,2,1,0:T(8,128)(2,1)S(1)}, u32[]{:S(2)}, u32[]{:S(2)}) collective-permute-start(bf16[2,4,576,128]{3,2,1,0:T(8,128)(2,1)S(1)} %pad_maximum_fusion.refs_0_), channel_id=1, source_target_pairs={{0,8},{2,10},{4,12},{6,14},{8,16},{10,18},{12,20},{14,22},{16,24},... | collective-permute-start | bytes 3538952 | tf_op jit(solution)/shard_map/ppermute | solution.py:364
  60.0 29.5 %collective-permute-start.16 = (bf16[2,4,576,128]{3,2,1,0:T(8,128)(2,1)S(1)}, bf16[2,4,576,128]{3,2,1,0:T(8,128)(2,1)S(1)}, u32[]{:S(2)}, u32[]{:S(2)}) collective-permute-start(bf16[2,4,576,128]{3,2,1,0:T(8,128)(2,1)S(1)} %pad_maximum_fusion.refs_0_), channel_id=1, source_target_pairs={{8,0},{10,2},{12,4},{14,6},{16,8},{18,10},{20,12},{22,14},{24,16},... | collective-permute-start | bytes 3538952 | tf_op jit(solution)/shard_map/ppermute | solution.py:364
  61.3 23.4 %collective-permute-start.13 = (bf16[4,2,32,16,128]{4,3,2,1,0:T(8,128)(2,1)S(1)}, bf16[4,2,32,16,128]{4,3,2,1,0:T(8,128)(2,1)S(1)}, u32[]{:S(2)}, u32[]{:S(2)}) collective-permute-start(bf16[4,2,32,16,128]{4,3,2,1,0:T(8,128)(2,1)S(1)} %get-tuple-element.42.refs_0_), channel_id=1, source_target_pairs={{0,2},{2,0},{4,6},{6,4},{8,10},{10,8},{12,14},{14,12},{16,18},{18,... | collective-permute-start | bytes 3145736 | tf_op jit(solution)/shard_map/ppermute | solution.py:354
  62.8 26.1 %collective-permute-start.14 = (bf16[4,2,32,16,128]{4,3,2,1,0:T(8,128)(2,1)S(1)}, bf16[4,2,32,16,128]{4,3,2,1,0:T(8,128)(2,1)S(1)}, u32[]{:S(2)}, u32[]{:S(2)}) collective-permute-start(bf16[4,2,32,16,128]{4,3,2,1,0:T(8,128)(2,1)S(1)} %get-tuple-element.43.refs_4_), channel_id=1, source_target_pairs={{0,4},{2,6},{4,0},{6,2},{8,12},{10,14},{12,8},{14,10},{16,20},{18,... | collective-permute-start | bytes 3145736 | tf_op jit(solution)/shard_map/ppermute | solution.py:354
  64.3 47.2 %collective-permute-start.17 = (bf16[4,2,32,16,128]{4,3,2,1,0:T(8,128)(2,1)S(1)}, bf16[4,2,32,16,128]{4,3,2,1,0:T(8,128)(2,1)}, u32[]{:S(2)}, u32[]{:S(2)}) collective-permute-start(bf16[4,2,32,16,128]{4,3,2,1,0:T(8,128)(2,1)S(1)} %get-tuple-element.42.refs_0_), channel_id=1, source_target_pairs={{0,4},{2,6},{4,0},{6,2},{8,12},{10,14},{12,8},{14,10},{16,20},{18,... | collective-permute-start | bytes 3145736 | tf_op jit(solution)/shard_map/ppermute | solution.py:354
  84.6 54.6 %copy-start.18 = (bf16[4,2,32,16,128]{4,3,2,1,0:T(8,128)(2,1)}, bf16[4,2,32,16,128]{4,3,2,1,0:T(8,128)(2,1)S(1)}, u32[]{:S(2)}) copy-start(bf16[4,2,32,16,128]{4,3,2,1,0:T(8,128)(2,1)S(1)} %collective-permute-done.13.refs_1_) | copy-start | bytes 3145732
  84.6 27.6 %collective-permute-start.19 = (bf16[4,2,32,16,128]{4,3,2,1,0:T(8,128)(2,1)S(1)}, bf16[4,2,32,16,128]{4,3,2,1,0:T(8,128)(2,1)S(1)}, u32[]{:S(2)}, u32[]{:S(2)}) collective-permute-start(bf16[4,2,32,16,128]{4,3,2,1,0:T(8,128)(2,1)S(1)} %get-tuple-element.43.refs_4_), channel_id=1, source_target_pairs={{0,2},{2,0},{4,6},{6,4},{8,10},{10,8},{12,14},{14,12},{16,18},{18,... | collective-permute-start | bytes 3145736 | tf_op jit(solution)/shard_map/ppermute | solution.py:354
  88.9 50.4 %copy-start.19 = (bf16[4,2,32,16,128]{4,3,2,1,0:T(8,128)(2,1)}, bf16[4,2,32,16,128]{4,3,2,1,0:T(8,128)(2,1)S(1)}, u32[]{:S(2)}) copy-start(bf16[4,2,32,16,128]{4,3,2,1,0:T(8,128)(2,1)S(1)} %collective-permute-done.14.refs_6_) | copy-start | bytes 3145732
  88.9 24.6 %collective-permute-start.23 = (bf16[4,2,32,16,128]{4,3,2,1,0:T(8,128)(2,1)S(1)}, bf16[4,2,32,16,128]{4,3,2,1,0:T(8,128)(2,1)S(1)}, u32[]{:S(2)}, u32[]{:S(2)}) collective-permute-start(bf16[4,2,32,16,128]{4,3,2,1,0:T(8,128)(2,1)S(1)} %get-tuple-element.42.refs_0_), channel_id=1, source_target_pairs={{0,1},{1,0},{2,3},{3,2},{4,5},{5,4},{6,7},{7,6},{8,9},{9,8},{10,11... | collective-permute-start | bytes 3145736 | tf_op jit(solution)/shard_map/ppermute | solution.py:376
  88.9 24.7 %collective-permute-start.24 = (bf16[4,2,32,16,128]{4,3,2,1,0:T(8,128)(2,1)S(1)}, bf16[4,2,32,16,128]{4,3,2,1,0:T(8,128)(2,1)S(1)}, u32[]{:S(2)}, u32[]{:S(2)}) collective-permute-start(bf16[4,2,32,16,128]{4,3,2,1,0:T(8,128)(2,1)S(1)} %get-tuple-element.43.refs_4_), channel_id=1, source_target_pairs={{0,1},{1,0},{2,3},{3,2},{4,5},{5,4},{6,7},{7,6},{8,9},{9,8},{10,11... | collective-permute-start | bytes 3145736 | tf_op jit(solution)/shard_map/ppermute | solution.py:376
  89.4 49.9 %copy-start.3 = (bf16[2,4,576,128]{3,2,1,0:T(8,128)(2,1)}, bf16[2,4,576,128]{3,2,1,0:T(8,128)(2,1)S(1)}, u32[]{:S(2)}) copy-start(bf16[2,4,576,128]{3,2,1,0:T(8,128)(2,1)S(1)} %collective-permute-done.16) | copy-start | bytes 3538948
  89.4 40.9 %collective-permute-start.18 = (bf16[4,2,32,16,128]{4,3,2,1,0:T(8,128)(2,1)S(1)}, bf16[4,2,32,16,128]{4,3,2,1,0:T(8,128)(2,1)S(1)}, u32[]{:S(2)}, u32[]{:S(2)}) collective-permute-start(bf16[4,2,32,16,128]{4,3,2,1,0:T(8,128)(2,1)S(1)} %collective-permute-done.13.refs_1_), channel_id=1, source_target_pairs={{0,4},{2,6},{4,0},{6,2},{8,12},{10,14},{12,8},{14,10},{16,20},{18,... | collective-permute-start | bytes 3145736 | tf_op jit(solution)/shard_map/ppermute | solution.py:354
  111.5 27.8 %collective-permute-start.21 = (bf16[2,4,576,128]{3,2,1,0:T(8,128)(2,1)S(1)}, bf16[2,4,576,128]{3,2,1,0:T(8,128)(2,1)S(1)}, u32[]{:S(2)}, u32[]{:S(2)}) collective-permute-start(bf16[2,4,576,128]{3,2,1,0:T(8,128)(2,1)S(1)} %collective-permute-done.15), channel_id=1, source_target_pairs={{8,16},{10,18},{12,20},{14,22},{16,24},{18,26},{20,28},{22,30},{9,... | collective-permute-start | bytes 3538952 | tf_op jit(solution)/shard_map/ppermute | solution.py:364
  112.2 27.1 %copy-start.20 = (bf16[4,2,32,16,128]{4,3,2,1,0:T(8,128)(2,1)}, bf16[4,2,32,16,128]{4,3,2,1,0:T(8,128)(2,1)S(1)}, u32[]{:S(2)}) copy-start(bf16[4,2,32,16,128]{4,3,2,1,0:T(8,128)(2,1)S(1)} %collective-permute-done.19.refs_5_) | copy-start | bytes 3145732
  112.2 29.7 %collective-permute-start.22 = (bf16[2,4,576,128]{3,2,1,0:T(8,128)(2,1)S(1)}, bf16[2,4,576,128]{3,2,1,0:T(8,128)(2,1)}, u32[]{:S(2)}, u32[]{:S(2)}) collective-permute-start(bf16[2,4,576,128]{3,2,1,0:T(8,128)(2,1)S(1)} %collective-permute-done.16), channel_id=1, source_target_pairs={{8,0},{10,2},{12,4},{14,6},{16,8},{18,10},{20,12},{22,14},{9,1},{1... | collective-permute-start | bytes 3538952 | tf_op jit(solution)/shard_map/ppermute | solution.py:364
  113.5 25.8 %copy-start.21 = (bf16[4,2,32,16,128]{4,3,2,1,0:T(8,128)(2,1)}, bf16[4,2,32,16,128]{4,3,2,1,0:T(8,128)(2,1)S(1)}, u32[]{:S(2)}) copy-start(bf16[4,2,32,16,128]{4,3,2,1,0:T(8,128)(2,1)S(1)} %collective-permute-done.23.refs_8_) | copy-start | bytes 3145732
  113.6 25.7 %collective-permute-start.25 = (bf16[4,2,32,16,128]{4,3,2,1,0:T(8,128)(2,1)S(1)}, bf16[4,2,32,16,128]{4,3,2,1,0:T(8,128)(2,1)S(1)}, u32[]{:S(2)}, u32[]{:S(2)}) collective-permute-start(bf16[4,2,32,16,128]{4,3,2,1,0:T(8,128)(2,1)S(1)} %collective-permute-done.13.refs_1_), channel_id=1, source_target_pairs={{0,1},{1,0},{2,3},{3,2},{4,5},{5,4},{6,7},{7,6},{8,9},{9,8},{10,11... | collective-permute-start | bytes 3145736 | tf_op jit(solution)/shard_map/ppermute | solution.py:376
  113.7 25.6 %collective-permute-start.20 = (bf16[4,2,32,16,128]{4,3,2,1,0:T(8,128)(2,1)S(1)}, bf16[4,2,32,16,128]{4,3,2,1,0:T(8,128)(2,1)S(1)}, u32[]{:S(2)}, u32[]{:S(2)}) collective-permute-start(bf16[4,2,32,16,128]{4,3,2,1,0:T(8,128)(2,1)S(1)} %collective-permute-done.14.refs_6_), channel_id=1, source_target_pairs={{0,2},{2,0},{4,6},{6,4},{8,10},{10,8},{12,14},{14,12},{16,18},{18,... | collective-permute-start | bytes 3145736 | tf_op jit(solution)/shard_map/ppermute | solution.py:354
  130.3 8.9 %collective-permute-start.26 = (bf16[4,2,32,16,128]{4,3,2,1,0:T(8,128)(2,1)S(1)}, bf16[4,2,32,16,128]{4,3,2,1,0:T(8,128)(2,1)S(1)}, u32[]{:S(2)}, u32[]{:S(2)}) collective-permute-start(bf16[4,2,32,16,128]{4,3,2,1,0:T(8,128)(2,1)S(1)} %collective-permute-done.14.refs_6_), channel_id=1, source_target_pairs={{0,1},{1,0},{2,3},{3,2},{4,5},{5,4},{6,7},{7,6},{8,9},{9,8},{10,11... | collective-permute-start | bytes 3145736 | tf_op jit(solution)/shard_map/ppermute | solution.py:376
  142.0 89.7 %all-to-all-start = ((bf16[16,96,1024]{2,1,0:T(8,128)(2,1)}), bf16[16,96,1024]{2,1,0:T(8,128)(2,1)}, u32[]{:S(2)}, u32[]{:S(2)}) async-start(bf16[16,96,1024]{2,1,0:T(8,128)(2,1)} %bitcast.45.phi), calls=%async_computation | async-start | bytes 6291456 | tf_op jit(solution)/shard_map/all_to_all | solution.py:390
  153.7 4.2 %collective-permute-start.27 = (bf16[4,2,32,16,128]{4,3,2,1,0:T(8,128)(2,1)}, bf16[4,2,32,16,128]{4,3,2,1,0:T(8,128)(2,1)}, u32[]{:S(2)}, u32[]{:S(2)}) collective-permute-start(bf16[4,2,32,16,128]{4,3,2,1,0:T(8,128)(2,1)} %collective-permute-done.17.refs_2_), channel_id=1, source_target_pairs={{0,1},{1,0},{2,3},{3,2},{4,5},{5,4},{6,7},{7,6},{8,9},{9,8},{10,11... | collective-permute-start | bytes 3145736 | tf_op jit(solution)/shard_map/ppermute | solution.py:376
  153.8 5.4 %collective-permute-start.28 = (bf16[4,2,32,16,128]{4,3,2,1,0:T(8,128)(2,1)}, bf16[4,2,32,16,128]{4,3,2,1,0:T(8,128)(2,1)}, u32[]{:S(2)}, u32[]{:S(2)}) collective-permute-start(bf16[4,2,32,16,128]{4,3,2,1,0:T(8,128)(2,1)} %copy-done.23), channel_id=1, source_target_pairs={{0,1},{1,0},{2,3},{3,2},{4,5},{5,4},{6,7},{7,6},{8,9},{9,8},{10,11... | collective-permute-start | bytes 3145736 | tf_op jit(solution)/shard_map/ppermute | solution.py:376
  154.3 5.5 %collective-permute-start.29 = (bf16[4,2,32,16,128]{4,3,2,1,0:T(8,128)(2,1)}, bf16[4,2,32,16,128]{4,3,2,1,0:T(8,128)(2,1)}, u32[]{:S(2)}, u32[]{:S(2)}) collective-permute-start(bf16[4,2,32,16,128]{4,3,2,1,0:T(8,128)(2,1)} %copy-done.20), channel_id=1, source_target_pairs={{0,1},{1,0},{2,3},{3,2},{4,5},{5,4},{6,7},{7,6},{8,9},{9,8},{10,11... | collective-permute-start | bytes 3145736 | tf_op jit(solution)/shard_map/ppermute | solution.py:376
  154.3 6.9 %collective-permute-start.30 = (bf16[4,2,32,16,128]{4,3,2,1,0:T(8,128)(2,1)}, bf16[4,2,32,16,128]{4,3,2,1,0:T(8,128)(2,1)}, u32[]{:S(2)}, u32[]{:S(2)}) collective-permute-start(bf16[4,2,32,16,128]{4,3,2,1,0:T(8,128)(2,1)} %copy-done.25), channel_id=1, source_target_pairs={{0,1},{1,0},{2,3},{3,2},{4,5},{5,4},{6,7},{7,6},{8,9},{9,8},{10,11... | collective-permute-start | bytes 3145736 | tf_op jit(solution)/shard_map/ppermute | solution.py:376
  156.1 38.0 %collective-permute-start.31 = (bf16[2,4,576,128]{3,2,1,0:T(8,128)(2,1)}, bf16[2,4,576,128]{3,2,1,0:T(8,128)(2,1)}, u32[]{:S(2)}, u32[]{:S(2)}) collective-permute-start(bf16[2,4,576,128]{3,2,1,0:T(8,128)(2,1)} %copy-done.4), channel_id=1, source_target_pairs={{16,24},{18,26},{20,28},{22,30},{17,25},{19,27},{21,29},{23,31}} | collective-permute-start | bytes 3538952 | tf_op jit(solution)/shard_map/ppermute | solution.py:364
  157.8 73.8 %collective-permute-start.32 = (bf16[2,4,576,128]{3,2,1,0:T(8,128)(2,1)}, bf16[2,4,576,128]{3,2,1,0:T(8,128)(2,1)}, u32[]{:S(2)}, u32[]{:S(2)}) collective-permute-start(bf16[2,4,576,128]{3,2,1,0:T(8,128)(2,1)} %collective-permute-done.22), channel_id=1, source_target_pairs={{8,0},{10,2},{12,4},{14,6},{9,1},{11,3},{13,5},{15,7}} | collective-permute-start | bytes 3538952 | tf_op jit(solution)/shard_map/ppermute | solution.py:364
  231.7 66.5 %all-to-all-start.1 = ((bf16[16,96,1024]{2,1,0:T(8,128)(2,1)}), bf16[16,96,1024]{2,1,0:T(8,128)(2,1)}, u32[]{:S(2)}, u32[]{:S(2)}) async-start(bf16[16,96,1024]{2,1,0:T(8,128)(2,1)} %hphi.1), calls=%async_computation.1 | async-start | bytes 6291456 | tf_op jit(solution)/shard_map/all_to_all | solution.py:390
  238.1 5.8 %collective-permute-start.33 = (bf16[2,4,576,128]{3,2,1,0:T(8,128)(2,1)S(1)}, bf16[2,4,576,128]{3,2,1,0:T(8,128)(2,1)S(1)}, u32[]{:S(2)}, u32[]{:S(2)}) collective-permute-start(bf16[2,4,576,128]{3,2,1,0:T(8,128)(2,1)S(1)} %pad_maximum_fusion.refs_0_), channel_id=1, source_target_pairs={{0,1},{1,0},{2,3},{3,2},{4,5},{5,4},{6,7},{7,6},{8,9},{9,8},{10,11... | collective-permute-start | bytes 3538952 | tf_op jit(solution)/shard_map/ppermute | solution.py:376
  239.7 4.2 %collective-permute-start.36 = (bf16[2,4,576,128]{3,2,1,0:T(8,128)(2,1)S(1)}, bf16[2,4,576,128]{3,2,1,0:T(8,128)(2,1)S(1)}, u32[]{:S(2)}, u32[]{:S(2)}) collective-permute-start(bf16[2,4,576,128]{3,2,1,0:T(8,128)(2,1)S(1)} %broadcast_select_fusion.refs_3_), channel_id=1, source_target_pairs={{0,1},{1,0},{2,3},{3,2},{4,5},{5,4},{6,7},{7,6},{8,9},{9,8},{10,11... | collective-permute-start | bytes 3538952 | tf_op jit(solution)/shard_map/ppermute | solution.py:376
  241.6 2.9 collective-permute-start.35
  243.4 2.9 collective-permute-start.34
  (19 other events, 98.4 us)

commit v5 on v4

--- a/solution.py
+++ b/solution.py
@@ -228,15 +228,30 @@
 def first_kernel(here, k_cols, h_cols, *refs, resident):
     phi, dense_k, product, dense_h, k_blocks, h_blocks, sems = refs[-7:]
     parts = refs[:-7]
+    last = 2 * SIDES[0]
 
     def copies(which):
         target = (k_blocks, h_blocks)[which]
         if not resident:
             return [pltpu.make_async_copy(parts[which], target, sems.at[which, 0, 0])]
-        depth = parts[0].shape[-2]
+        out_list = []
+        if which == 0:
+            columns = SIDES[1] * SIDES[2]
+            for n, (part, core, piece, column) in enumerate(block_places(here, parts[:-last])):
+                depth = part.shape[-2]
+                for z in range(SIDES[0]):
+                    row = (((core * SIDES[0] + z) * columns + column) * PIECES + piece) * depth
+                    out_list.append(
+                        pltpu.make_async_copy(
+                            part.at[z],
+                            target.at[pl.ds(pl.multiple_of(row, depth), depth)],
+                            sems.at[which, n, z],
+                        )
+                    )
+            return out_list
+        depth = parts[-1].shape[-2]
         rep, y, x, z = (here[k] for k in range(4))
-        out_list = []
-        for n, part in enumerate(parts):
+        for n, part in enumerate(parts[-last:]):
             core = rep if n < SIDES[0] else 1 - rep
             level = lax.rem(z + SIDES[0] - n % SIDES[0], SIDES[0])
             for c in range(SIDES[1] * SIDES[2]):
@@ -245,7 +260,7 @@
                 row = (((core * SIDES[0] + level) * SIDES[1] + to_y) * SIDES[2] + to_x) * depth
                 out_list.append(
                     pltpu.make_async_copy(
-                        part.at[which, c],
+                        part.at[c],
                         target.at[pl.ds(pl.multiple_of(row, depth), depth)],
                         sems.at[which, n, c],
                     )
@@ -408,31 +423,38 @@
         level, y, x = place_of()
         here = jnp.stack([rep, y, x, level]).astype(jnp.int32)
         per = x_blocks // PIECES
-        stored = [kernel[0], hamiltonian[0]]
         lines = [along_z(half[p * per : (p + 1) * per]) for p in range(PIECES)]
-        close = [swapped(stored[p], 1 + p) for p in range(2)]
-        apart = [(swapped(stored[p], 2 - p), swapped(close[p], 2 - p)) for p in range(2)]
-        around = ordered(stored, close, apart)
-        around = jnp.stack([jnp.stack(around[:4]), jnp.stack(around[4:])])
-        lines, around, halo, band, info, phi_cut = lax.optimization_barrier(
-            (lines, around, halo, band, info, phi_cut)
+        h_own = hamiltonian[0]
+        h_near, h_apart = swapped(h_own, 1), swapped(h_own, 2)
+        around = jnp.stack([h_own, h_near, h_apart, swapped(h_near, 2)])
+        lines, around, kernel, halo, band, info, phi_cut = lax.optimization_barrier(
+            (lines, around, kernel, halo, band, info, phi_cut)
         )
         near = [swapped(lines[p], 1 + p) for p in range(PIECES)]
         ups, downs = [onward(around, 1, True)], [onward(around, 1, False)]
+        k_line = along_z(kernel[0])
         lines_too = [other_core(block) for block in lines]
-        near, ups, downs = lax.optimization_barrier((near, ups, downs))
+        near, ups, downs, k_line = lax.optimization_barrier((near, ups, downs, k_line))
         far = [(swapped(lines[p], 2 - p), swapped(near[p], 2 - p)) for p in range(PIECES)]
         ups.append(onward(ups[0], 2, True))
         downs.append(onward(downs[0], 2, False))
+        rows_of = k_line.shape[1] // PIECES
+        k_lines = [k_line[:, p * rows_of : (p + 1) * rows_of] for p in range(PIECES)]
+        k_near = [swapped(k_lines[p], 1 + p) for p in range(PIECES)]
         near_too = [other_core(block) for block in near]
-        far, ups, downs, phi_cut, lines_too, near_too = lax.optimization_barrier(
-            (far, ups, downs, phi_cut, lines_too, near_too)
-        )
-        phi_pts = exchange(phi_cut)
         ups.append(onward(ups[1], 3, True))
         downs.append(onward(downs[1], 3, False))
         far_too = [tuple(other_core(block) for block in pair) for pair in far]
+        far, ups, downs, k_near, phi_cut, lines_too, near_too = lax.optimization_barrier(
+            (far, ups, downs, k_near, phi_cut, lines_too, near_too)
+        )
+        phi_pts = exchange(phi_cut)
+        k_far = [(swapped(k_lines[p], 2 - p), swapped(k_near[p], 2 - p)) for p in range(PIECES)]
         pot = ordered(lines, near, far) + ordered(lines_too, near_too, far_too)
+        h_parts = [around]
+        for k in range(1, SIDES[0]):
+            h_parts.append(jnp.where(level >= k, ups[k - 1], downs[SIDES[0] - 1 - k]))
+        h_parts = h_parts + [other_core(part) for part in h_parts]
     else:
         here = jnp.stack([rep, rep, rep, rep]).astype(jnp.int32)
         pot = lax.all_gather(half, ("rep", "func"), axis=0, tiled=False)
@@ -454,11 +476,9 @@
     info, phi_planes, halo = padded
     hphi = make_hphi(info, here, phi_planes, halo, band, pot, resident)[:, :owned]
     if resident:
-        hphi, ups, downs = lax.optimization_barrier((hphi, ups, downs))
-        parts = [around]
-        for k in range(1, SIDES[0]):
-            parts.append(jnp.where(level >= k, ups[k - 1], downs[SIDES[0] - 1 - k]))
-        parts = parts + [other_core(part) for part in parts]
+        hphi, k_far = lax.optimization_barrier((hphi, k_far))
+        k_parts = ordered(k_lines, k_near, k_far)
+        parts = k_parts + [other_core(part) for part in k_parts] + h_parts
     phi_pts = phi_pts.reshape(n_func * owned, width)
     dense_k, product = first_products(
         here, kernel_cols, intersection_cols, parts, phi_pts, resident

time: 397 us -> 420 us (1.058)
  starting transfers between devices: 60.2 us -> 79.5 us
    ppermute x6, waiting for transfers between devices: 37.5 us -> 0.02 us  [onward(): return lax.ppermute(block, 'func', route)]
    ppermute x6 -> x9, waiting for transfers between devices: 17.8 us -> 36 us  [along_z(): lax.ppermute(part, 'func', [(i, (i + 4 * k) % n) for i in range(n)])]
    ppermute x6 -> x9, starting transfers between devices: 14.3 us -> 28.1 us  [along_z(): lax.ppermute(part, 'func', [(i, (i + 4 * k) % n) for i in range(n)])]
    all_to_all x2, waiting for transfers between devices: 20.9 us -> 32.7 us  [exchange(): return lax.all_to_all(rows, 'func', split_axis=0, concat_axis=0, tiled=True)]
    ppermute x12 -> x15, waiting for transfers between devices: 73.9 us -> 84.5 us  [swapped(): return lax.ppermute(block, 'func', [(i, i ^ bit) for i in range(n)])]
    ppermute x12 -> x15, starting transfers between devices: 17.1 us -> 19.2 us  [swapped(): return lax.ppermute(block, 'func', [(i, i ^ bit) for i in range(n)])]
    unnamed x57 -> x95, local copies, waits for them, and re-layouts: 10.6 us -> 12.4 us
  transfers between devices with their start and end apart: 39 -> 53, of which waited for: 16 -> 21; matrix products, arithmetic and copies ran while one was open for 4% -> 3% of each run, Pallas kernels for 16% -> 15%
where the time goes in v5:
time: 420 us; the launch traced here: 419 us
  waiting for transfers between devices  157 us (37%)
  blocking collectives  84.5 us (20%)
  starting transfers between devices  79.5 us (19%)
  Pallas kernels  74.3 us (18%)
  local copies, waits for them, and re-layouts  16.7 us (4%)
  other arithmetic  6.25 us (1%)
    ppermute x15, waiting for transfers between devices, swapped(): return lax.ppermute(block, 'func', [(i, i ^ bit) for i in range(n)])  84.5 us
    all_to_all x1, blocking collectives, exchange(): return lax.all_to_all(rows, 'func', split_axis=0, concat_axis=0, tiled=True)  84.5 us
    ppermute x9, waiting for transfers between devices, along_z(): lax.ppermute(part, 'func', [(i, (i + 4 * k) % n) for i in range(n)])  36 us
    pallas_call x1, Pallas kernels, make_hphi(): pl.pallas_call(functools.partial(hphi_kernel, resident=resident), out_sha...  33 us
    all_to_all x2, waiting for transfers between devices, exchange(): return lax.all_to_all(rows, 'func', split_axis=0, concat_axis=0, tiled=True)  32.7 us
    pallas_call x1, Pallas kernels, first_products(): pl.pallas_call(functools.partial(first_kernel, resident=resident), out_sh...  31 us
    ppermute x9, starting transfers between devices, along_z(): lax.ppermute(part, 'func', [(i, (i + 4 * k) % n) for i in range(n)])  28.1 us
    all_to_all x2, starting transfers between devices, exchange(): return lax.all_to_all(rows, 'func', split_axis=0, concat_axis=0, tiled=True)  19.3 us
  transfers between devices with their start and end apart: 53, of which 21 were waited for; matrix products, arithmetic and copies ran while one was open for 3% of the time, Pallas kernels for 15%

profile of v5, /device:TPU:0, one launch (start us, length us, event | category | flops | bytes accessed | tf_op | source)
XLA Modules:
  0.0 418.8 jit_solution(15830338401617416182)
XLA Ops:
  0.0 1.6 copy-done
  1.8 5.1 %collective-permute-start.3 = (bf16[2,32,16,128]{3,2,1,0:T(8,128)(2,1)S(1)}, bf16[2,32,16,128]{3,2,1,0:T(8,128)(2,1)S(1)}, u32[]{:S(2)}, u32[]{:S(2)}) collective-permute-start(bf16[2,32,16,128]{3,2,1,0:T(8,128)(2,1)S(1)} %get-tuple-element.93), channel_id=1, source_target_pairs={{0,24},{2,26},{4,28},{6,30},{8,0},{10,2},{12,4},{14,6},{16,8},{18,... | collective-permute-start | bytes 786440 | tf_op jit(solution)/shard_map/ppermute | solution.py:356
  6.9 1.0 collective-permute-start.5
  7.9 2.8 collective-permute-start
  10.7 1.1 collective-permute-start.1
  11.9 1.6 select_convert_fusion.band
  13.5 5.3 %copy.25 = bf16[96,16,1024]{2,0,1:T(8,128)(2,1)} copy(bf16[96,16,1024]{2,1,0:T(8,128)(2,1)} %param.7) | data formatting | bytes 6291456 | tf_op args[0]
  18.8 1.2 slice_select_fusion
  20.0 4.2 %collective-permute-start.2 = (bf16[2,32,16,128]{3,2,1,0:T(8,128)(2,1)S(1)}, bf16[2,32,16,128]{3,2,1,0:T(8,128)(2,1)S(1)}, u32[]{:S(2)}, u32[]{:S(2)}) collective-permute-start(bf16[2,32,16,128]{3,2,1,0:T(8,128)(2,1)S(1)} %get-tuple-element.94), channel_id=1, source_target_pairs={{0,8},{2,10},{4,12},{6,14},{8,16},{10,18},{12,20},{14,22},{16,24},... | collective-permute-start | bytes 786440 | tf_op jit(solution)/shard_map/ppermute | solution.py:356
  24.2 7.3 %collective-permute-done.4 = bf16[2,32,16,128]{3,2,1,0:T(8,128)(2,1)S(1)} collective-permute-done((bf16[2,32,16,128]{3,2,1,0:T(8,128)(2,1)S(1)}, bf16[2,32,16,128]{3,2,1,0:T(8,128)(2,1)S(1)}, u32[]{:S(2)}, u32[]{:S(2)}) %collective-permute-start.4) | collective-permute-done | bytes 262176 | tf_op jit(solution)/shard_map/ppermute | solution.py:356
  31.5 1.5 collective-permute-start.6
  33.0 1.5 collective-permute-start.7
  34.6 2.0 collective-permute-done.6
  36.6 1.5 collective-permute-start.8
  38.2 13.5 %collective-permute-done.1 = bf16[2,32,16,128]{3,2,1,0:T(8,128)(2,1)S(1)} collective-permute-done((bf16[2,32,16,128]{3,2,1,0:T(8,128)(2,1)S(1)}, bf16[2,32,16,128]{3,2,1,0:T(8,128)(2,1)S(1)}, u32[]{:S(2)}, u32[]{:S(2)}) %collective-permute-start.1) | collective-permute-done | bytes 262176 | tf_op jit(solution)/shard_map/ppermute | solution.py:356
  52.2 1.6 collective-permute-start.10
  53.8 2.9 collective-permute-start.12
  56.6 1.3 collective-permute-start.13
  58.0 4.1 collective-permute-start.14
  62.6 14.1 %collective-permute-done.14 = bf16[576,128]{1,0:T(8,128)(2,1)S(1)} collective-permute-done((bf16[576,128]{1,0:T(8,128)(2,1)S(1)}, bf16[576,128]{1,0:T(8,128)(2,1)S(1)}, u32[]{:S(2)}, u32[]{:S(2)}) %collective-permute-start.14) | collective-permute-done | bytes 147488 | tf_op jit(solution)/shard_map/ppermute | solution.py:356
  76.7 9.2 %collective-permute-start.16 = (bf16[576,128]{1,0:T(8,128)(2,1)S(1)}, bf16[576,128]{1,0:T(8,128)(2,1)S(1)}, u32[]{:S(2)}, u32[]{:S(2)}) collective-permute-start(bf16[576,128]{1,0:T(8,128)(2,1)S(1)} %bitcast.62), channel_id=1, source_target_pairs={{0,8},{2,10},{4,12},{6,14},{8,16},{10,18},{12,20},{14,22},{16,24},... | collective-permute-start | bytes 442376 | tf_op jit(solution)/shard_map/ppermute | solution.py:356
  86.0 1.0 collective-permute-done.15
  87.0 1.5 collective-permute-start.11
  88.6 1.5 collective-permute-start.17
  91.4 21.7 %collective-permute-done.11.refs_6_ = bf16[4,2,32,16,128]{4,3,2,1,0:T(8,128)(2,1)S(1)} collective-permute-done((bf16[4,2,32,16,128]{4,3,2,1,0:T(8,128)(2,1)S(1)}, bf16[4,2,32,16,128]{4,3,2,1,0:T(8,128)(2,1)S(1)}, u32[]{:S(2)}, u32[]{:S(2)}) %collective-permute-start.11) | collective-permute-done | bytes 1048608 | tf_op jit(solution)/shard_map/ppermute | solution.py:369
  113.8 19.0 %collective-permute-done.17.refs_2_ = bf16[4,2,32,16,128]{4,3,2,1,0:T(8,128)(2,1)S(1)} collective-permute-done((bf16[4,2,32,16,128]{4,3,2,1,0:T(8,128)(2,1)S(1)}, bf16[4,2,32,16,128]{4,3,2,1,0:T(8,128)(2,1)S(1)}, u32[]{:S(2)}, u32[]{:S(2)}) %collective-permute-start.17) | collective-permute-done | bytes 1048608 | tf_op jit(solution)/shard_map/ppermute | solution.py:369
  132.8 1.5 collective-permute-start.18
  135.5 1.3 collective-permute-start.23
  136.8 4.3 %collective-permute-done.25.refs_1_ = bf16[4,288,128]{2,1,0:T(8,128)(2,1)S(1)} collective-permute-done((bf16[4,288,128]{2,1,0:T(8,128)(2,1)S(1)}, bf16[4,288,128]{2,1,0:T(8,128)(2,1)S(1)}, u32[]{:S(2)}, u32[]{:S(2)}) %collective-permute-start.25) | collective-permute-done | bytes 294944 | tf_op jit(solution)/shard_map/ppermute | solution.py:369
  141.2 19.6 %collective-permute-done.26.refs_6_ = bf16[4,288,128]{2,1,0:T(8,128)(2,1)S(1)} collective-permute-done((bf16[4,288,128]{2,1,0:T(8,128)(2,1)S(1)}, bf16[4,288,128]{2,1,0:T(8,128)(2,1)S(1)}, u32[]{:S(2)}, u32[]{:S(2)}) %collective-permute-start.26) | collective-permute-done | bytes 294944 | tf_op jit(solution)/shard_map/ppermute | solution.py:369
  162.3 1.3 collective-permute-start.24
  163.6 17.9 %collective-permute-done.20.refs_7_ = bf16[4,2,32,16,128]{4,3,2,1,0:T(8,128)(2,1)S(1)} collective-permute-done((bf16[4,2,32,16,128]{4,3,2,1,0:T(8,128)(2,1)S(1)}, bf16[4,2,32,16,128]{4,3,2,1,0:T(8,128)(2,1)S(1)}, u32[]{:S(2)}, u32[]{:S(2)}) %collective-permute-start.20) | collective-permute-done | bytes 1048608 | tf_op jit(solution)/shard_map/ppermute | solution.py:369
  181.6 0.9 copy-done.29
  184.0 4.5 %all-to-all-start = ((bf16[16,96,1024]{2,1,0:T(8,128)(2,1)}), bf16[16,96,1024]{2,1,0:T(8,128)(2,1)}, u32[]{:S(2)}, u32[]{:S(2)}) async-start(bf16[16,96,1024]{2,1,0:T(8,128)(2,1)} %bitcast.50.phi), calls=%async_computation | async-start | bytes 6291456 | tf_op jit(solution)/shard_map/all_to_all | solution.py:405
  191.0 1.7 collective-permute-start.35
  192.7 1.5 collective-permute-start.37
  194.5 1.7 collective-permute-start.36
  196.2 1.5 collective-permute-start.38
  197.7 33.0 %hphi.1 = bf16[16,96,1024]{2,1,0:T(8,128)(2,1)} custom-call(s32[96,3]{1,0:T(8,128)} %copy.21.info, s32[4]{0:T(128)} %pad_add_fusion.1.here, bf16[16,96,1024]{2,1,0:T(8,128)(2,1)} %bitcast.50.phi, bf16[2,96,1024]{2,1,0:T(8,128)(2,1)} %copy-done.35, bf16[512,256]{1,0:T(8,128)(2,1)} %select_convert_fusion.band, bf16[4,2,32,16,128]{4,3,2,1,0:T(8,128)(2,1)} %copy-done.2, ...), custom_call_target="tpu_custom_call" | custom-call | flops 12884901888 | bytes 62914560 | tf_op jit(solution)/shard_map/hphi/pallas_call | solution.py:204
  232.8 13.3 %all-to-all-done = bf16[16,96,1024]{2,1,0:T(8,128)(2,1)} async-done(((bf16[16,96,1024]{2,1,0:T(8,128)(2,1)}), bf16[16,96,1024]{2,1,0:T(8,128)(2,1)}, u32[]{:S(2)}, u32[]{:S(2)}) %all-to-all-start) | async-done | bytes 3145760 | tf_op jit(solution)/shard_map/all_to_all | solution.py:405
  246.1 14.8 %all-to-all-start.1 = ((bf16[16,96,1024]{2,1,0:T(8,128)(2,1)}), bf16[16,96,1024]{2,1,0:T(8,128)(2,1)}, u32[]{:S(2)}, u32[]{:S(2)}) async-start(bf16[16,96,1024]{2,1,0:T(8,128)(2,1)} %hphi.1), calls=%async_computation.1 | async-start | bytes 6291456 | tf_op jit(solution)/shard_map/all_to_all | solution.py:405
  261.6 0.9 broadcast_select_fusion.refs_19_
  264.4 1.1 broadcast_select_fusion.2.refs_17_
  270.2 31.0 %products.1 = (bf16[1536,1536]{1,0:T(8,128)(2,1)}, f32[1536,1024]{1,0:T(8,128)}) custom-call(s32[4]{0:T(128)} %pad_add_fusion.1.here, s32[12,12]{1,0:T(8,128)} %k_cols.1, s32[12,12]{1,0:T(8,128)} %h_cols.1, bf16[4,288,128]{2,1,0:T(8,128)(2,1)} %copy-done.17, bf16[4,288,128]{2,1,0:T(8,128)(2,1)} %copy-done.36, bf16[4,288,128]{2,1,0:T(8,128)(2,1)} %copy-done.38, ...), custom_call_target="tpu_custom_call" | custom-call | flops 9663676416 | bytes 25165824 | tf_op jit(solution)/shard_map/products/pallas_call | solution.py:308
  301.2 19.5 %all-to-all-done.1 = bf16[16,96,1024]{2,1,0:T(8,128)(2,1)} async-done(((bf16[16,96,1024]{2,1,0:T(8,128)(2,1)}), bf16[16,96,1024]{2,1,0:T(8,128)(2,1)}, u32[]{:S(2)}, u32[]{:S(2)}) %all-to-all-start.1) | async-done | bytes 3145760 | tf_op jit(solution)/shard_map/all_to_all | solution.py:405
  320.7 10.3 %gradient.1 = bf16[1536,1024]{1,0:T(8,128)(2,1)} custom-call(bf16[1536,1536]{1,0:T(8,128)(2,1)} %get-tuple-element.76.dense_k, bf16[1536,1024]{1,0:T(8,128)(2,1)} %bitcast.25.hphi, f32[1536,1024]{1,0:T(8,128)} %get-tuple-element.78.product), custom_call_target="tpu_custom_call" | custom-call | flops 4831838208 | bytes 17825792 | tf_op jit(solution)/shard_map/gradient/pallas_call | solution.py:332
  331.0 84.5 %all_to_all.15 = bf16[16,96,1024]{2,1,0:T(8,128)(2,1)S(1)} all-to-all(bf16[16,96,1024]{2,1,0:T(8,128)(2,1)} %bitcast.56), channel_id=1, replica_groups=mesh['func'=16,'rep'=2] {'func'}, dimensions={0} | all-to-all | bytes 6291456 | tf_op jit(solution)/shard_map/all_to_all | solution.py:405
  415.5 3.4 copy.22
  (184 shorter events, 19.7 us)
Async XLA Ops:
  1.8 18.2 %collective-permute-start.3 = (bf16[2,32,16,128]{3,2,1,0:T(8,128)(2,1)S(1)}, bf16[2,32,16,128]{3,2,1,0:T(8,128)(2,1)S(1)}, u32[]{:S(2)}, u32[]{:S(2)}) collective-permute-start(bf16[2,32,16,128]{3,2,1,0:T(8,128)(2,1)S(1)} %get-tuple-element.93), channel_id=1, source_target_pairs={{0,24},{2,26},{4,28},{6,30},{8,0},{10,2},{12,4},{14,6},{16,8},{18,... | collective-permute-start | bytes 786440 | tf_op jit(solution)/shard_map/ppermute | solution.py:356
  6.9 24.6 %collective-permute-start.4 = (bf16[2,32,16,128]{3,2,1,0:T(8,128)(2,1)S(1)}, bf16[2,32,16,128]{3,2,1,0:T(8,128)(2,1)S(1)}, u32[]{:S(2)}, u32[]{:S(2)}) collective-permute-start(bf16[2,32,16,128]{3,2,1,0:T(8,128)(2,1)S(1)} %get-tuple-element.93), channel_id=1, source_target_pairs={{0,16},{2,18},{4,20},{6,22},{8,24},{10,26},{12,28},{14,30},{16,0},... | collective-permute-start | bytes 786440 | tf_op jit(solution)/shard_map/ppermute | solution.py:356
  6.9 26.1 %collective-permute-start.5 = (bf16[2,32,16,128]{3,2,1,0:T(8,128)(2,1)S(1)}, bf16[2,32,16,128]{3,2,1,0:T(8,128)(2,1)S(1)}, u32[]{:S(2)}, u32[]{:S(2)}) collective-permute-start(bf16[2,32,16,128]{3,2,1,0:T(8,128)(2,1)S(1)} %get-tuple-element.93), channel_id=1, source_target_pairs={{0,8},{2,10},{4,12},{6,14},{8,16},{10,18},{12,20},{14,22},{16,24},... | collective-permute-start | bytes 786440 | tf_op jit(solution)/shard_map/ppermute | solution.py:356
  7.9 28.8 %collective-permute-start = (bf16[2,32,16,128]{3,2,1,0:T(8,128)(2,1)S(1)}, bf16[2,32,16,128]{3,2,1,0:T(8,128)(2,1)S(1)}, u32[]{:S(2)}, u32[]{:S(2)}) collective-permute-start(bf16[2,32,16,128]{3,2,1,0:T(8,128)(2,1)S(1)} %get-tuple-element.94), channel_id=1, source_target_pairs={{0,24},{2,26},{4,28},{6,30},{8,0},{10,2},{12,4},{14,6},{16,8},{18,... | collective-permute-start | bytes 786440 | tf_op jit(solution)/shard_map/ppermute | solution.py:356
  10.7 41.0 %collective-permute-start.1 = (bf16[2,32,16,128]{3,2,1,0:T(8,128)(2,1)S(1)}, bf16[2,32,16,128]{3,2,1,0:T(8,128)(2,1)S(1)}, u32[]{:S(2)}, u32[]{:S(2)}) collective-permute-start(bf16[2,32,16,128]{3,2,1,0:T(8,128)(2,1)S(1)} %get-tuple-element.94), channel_id=1, source_target_pairs={{0,16},{2,18},{4,20},{6,22},{8,24},{10,26},{12,28},{14,30},{16,0},... | collective-permute-start | bytes 786440 | tf_op jit(solution)/shard_map/ppermute | solution.py:356
  20.0 31.6 %collective-permute-start.2 = (bf16[2,32,16,128]{3,2,1,0:T(8,128)(2,1)S(1)}, bf16[2,32,16,128]{3,2,1,0:T(8,128)(2,1)S(1)}, u32[]{:S(2)}, u32[]{:S(2)}) collective-permute-start(bf16[2,32,16,128]{3,2,1,0:T(8,128)(2,1)S(1)} %get-tuple-element.94), channel_id=1, source_target_pairs={{0,8},{2,10},{4,12},{6,14},{8,16},{10,18},{12,20},{14,22},{16,24},... | collective-permute-start | bytes 786440 | tf_op jit(solution)/shard_map/ppermute | solution.py:356
  31.5 5.1 %collective-permute-start.6 = (bf16[576,128]{1,0:T(8,128)(2,1)S(1)}, bf16[576,128]{1,0:T(8,128)(2,1)S(1)}, u32[]{:S(2)}, u32[]{:S(2)}) collective-permute-start(bf16[576,128]{1,0:T(8,128)(2,1)S(1)} %bitcast.58), channel_id=1, source_target_pairs={{0,2},{2,0},{4,6},{6,4},{8,10},{10,8},{12,14},{14,12},{16,18},{18,... | collective-permute-start | bytes 442376 | tf_op jit(solution)/shard_map/ppermute | solution.py:369
  33.0 19.1 %collective-permute-start.7 = (bf16[576,128]{1,0:T(8,128)(2,1)S(1)}, bf16[576,128]{1,0:T(8,128)(2,1)S(1)}, u32[]{:S(2)}, u32[]{:S(2)}) collective-permute-start(bf16[576,128]{1,0:T(8,128)(2,1)S(1)} %bitcast.59), channel_id=1, source_target_pairs={{0,4},{2,6},{4,0},{6,2},{8,12},{10,14},{12,8},{14,10},{16,20},{18,... | collective-permute-start | bytes 442376 | tf_op jit(solution)/shard_map/ppermute | solution.py:369
  36.6 15.6 %collective-permute-start.9 = (bf16[2,96,1024]{2,1,0:T(8,128)(2,1)S(1)}, bf16[2,96,1024]{2,1,0:T(8,128)(2,1)S(1)}, u32[]{:S(2)}, u32[]{:S(2)}) collective-permute-start(bf16[2,96,1024]{2,1,0:T(8,128)(2,1)S(1)} %slice_select_fusion), channel_id=1, source_target_pairs={{0,1},{1,0},{2,3},{3,2},{4,5},{5,4},{6,7},{7,6},{8,9},{9,8},{10,11... | collective-permute-start | bytes 1179656 | tf_op jit(solution)/shard_map/ppermute | solution.py:416
  36.6 15.5 %collective-permute-start.8 = (bf16[576,128]{1,0:T(8,128)(2,1)S(1)}, bf16[576,128]{1,0:T(8,128)(2,1)S(1)}, u32[]{:S(2)}, u32[]{:S(2)}) collective-permute-start(bf16[576,128]{1,0:T(8,128)(2,1)S(1)} %collective-permute-done.6), channel_id=1, source_target_pairs={{0,4},{2,6},{4,0},{6,2},{8,12},{10,14},{12,8},{14,10},{16,20},{18,... | collective-permute-start | bytes 442376 | tf_op jit(solution)/shard_map/ppermute | solution.py:369
  52.2 38.5 %collective-permute-start.10 = (bf16[4,2,32,16,128]{4,3,2,1,0:T(8,128)(2,1)S(1)}, bf16[4,2,32,16,128]{4,3,2,1,0:T(8,128)(2,1)S(1)}, u32[]{:S(2)}, u32[]{:S(2)}) collective-permute-start(bf16[4,2,32,16,128]{4,3,2,1,0:T(8,128)(2,1)S(1)} %get-tuple-element.42.refs_0_), channel_id=1, source_target_pairs={{0,2},{2,0},{4,6},{6,4},{8,10},{10,8},{12,14},{14,12},{16,18},{18,... | collective-permute-start | bytes 3145736 | tf_op jit(solution)/shard_map/ppermute | solution.py:369
  53.8 36.4 %collective-permute-start.12 = (bf16[4,576,128]{2,1,0:T(8,128)(2,1)S(1)}, bf16[4,576,128]{2,1,0:T(8,128)(2,1)S(1)}, u32[]{:S(2)}, u32[]{:S(2)}) collective-permute-start(bf16[4,576,128]{2,1,0:T(8,128)(2,1)S(1)} %pad_maximum_fusion.2.refs_16_), channel_id=1, source_target_pairs={{0,8},{2,10},{4,12},{6,14},{8,16},{10,18},{12,20},{14,22},{16,24},... | collective-permute-start | bytes 1769480 | tf_op jit(solution)/shard_map/ppermute | solution.py:379
  56.6 34.0 %collective-permute-start.13 = (bf16[4,576,128]{2,1,0:T(8,128)(2,1)S(1)}, bf16[4,576,128]{2,1,0:T(8,128)(2,1)S(1)}, u32[]{:S(2)}, u32[]{:S(2)}) collective-permute-start(bf16[4,576,128]{2,1,0:T(8,128)(2,1)S(1)} %pad_maximum_fusion.2.refs_16_), channel_id=1, source_target_pairs={{8,0},{10,2},{12,4},{14,6},{16,8},{18,10},{20,12},{22,14},{24,16},... | collective-permute-start | bytes 1769480 | tf_op jit(solution)/shard_map/ppermute | solution.py:379
  58.0 18.8 %collective-permute-start.14 = (bf16[576,128]{1,0:T(8,128)(2,1)S(1)}, bf16[576,128]{1,0:T(8,128)(2,1)S(1)}, u32[]{:S(2)}, u32[]{:S(2)}) collective-permute-start(bf16[576,128]{1,0:T(8,128)(2,1)S(1)} %bitcast.60), channel_id=1, source_target_pairs={{0,24},{2,26},{4,28},{6,30},{8,0},{10,2},{12,4},{14,6},{16,8},{18,... | collective-permute-start | bytes 442376 | tf_op jit(solution)/shard_map/ppermute | solution.py:356
  62.0 25.0 %collective-permute-start.15 = (bf16[576,128]{1,0:T(8,128)(2,1)S(1)}, bf16[576,128]{1,0:T(8,128)(2,1)S(1)}, u32[]{:S(2)}, u32[]{:S(2)}) collective-permute-start(bf16[576,128]{1,0:T(8,128)(2,1)S(1)} %bitcast.61), channel_id=1, source_target_pairs={{0,16},{2,18},{4,20},{6,22},{8,24},{10,26},{12,28},{14,30},{16,0},... | collective-permute-start | bytes 442376 | tf_op jit(solution)/shard_map/ppermute | solution.py:356
  76.7 11.9 %collective-permute-start.16 = (bf16[576,128]{1,0:T(8,128)(2,1)S(1)}, bf16[576,128]{1,0:T(8,128)(2,1)S(1)}, u32[]{:S(2)}, u32[]{:S(2)}) collective-permute-start(bf16[576,128]{1,0:T(8,128)(2,1)S(1)} %bitcast.62), channel_id=1, source_target_pairs={{0,8},{2,10},{4,12},{6,14},{8,16},{10,18},{12,20},{14,22},{16,24},... | collective-permute-start | bytes 442376 | tf_op jit(solution)/shard_map/ppermute | solution.py:356
  87.0 26.1 %collective-permute-start.11 = (bf16[4,2,32,16,128]{4,3,2,1,0:T(8,128)(2,1)S(1)}, bf16[4,2,32,16,128]{4,3,2,1,0:T(8,128)(2,1)S(1)}, u32[]{:S(2)}, u32[]{:S(2)}) collective-permute-start(bf16[4,2,32,16,128]{4,3,2,1,0:T(8,128)(2,1)S(1)} %get-tuple-element.43.refs_4_), channel_id=1, source_target_pairs={{0,4},{2,6},{4,0},{6,2},{8,12},{10,14},{12,8},{14,10},{16,20},{18,... | collective-permute-start | bytes 3145736 | tf_op jit(solution)/shard_map/ppermute | solution.py:369
  88.6 44.1 %collective-permute-start.17 = (bf16[4,2,32,16,128]{4,3,2,1,0:T(8,128)(2,1)S(1)}, bf16[4,2,32,16,128]{4,3,2,1,0:T(8,128)(2,1)S(1)}, u32[]{:S(2)}, u32[]{:S(2)}) collective-permute-start(bf16[4,2,32,16,128]{4,3,2,1,0:T(8,128)(2,1)S(1)} %get-tuple-element.42.refs_0_), channel_id=1, source_target_pairs={{0,4},{2,6},{4,0},{6,2},{8,12},{10,14},{12,8},{14,10},{16,20},{18,... | collective-permute-start | bytes 3145736 | tf_op jit(solution)/shard_map/ppermute | solution.py:369
  90.2 44.2 %collective-permute-start.19 = (bf16[4,2,32,16,128]{4,3,2,1,0:T(8,128)(2,1)S(1)}, bf16[4,2,32,16,128]{4,3,2,1,0:T(8,128)(2,1)S(1)}, u32[]{:S(2)}, u32[]{:S(2)}) collective-permute-start(bf16[4,2,32,16,128]{4,3,2,1,0:T(8,128)(2,1)S(1)} %get-tuple-element.43.refs_4_), channel_id=1, source_target_pairs={{0,2},{2,0},{4,6},{6,4},{8,10},{10,8},{12,14},{14,12},{16,18},{18,... | collective-permute-start | bytes 3145736 | tf_op jit(solution)/shard_map/ppermute | solution.py:369
  90.7 44.3 %collective-permute-start.27 = (bf16[4,2,32,16,128]{4,3,2,1,0:T(8,128)(2,1)S(1)}, bf16[4,2,32,16,128]{4,3,2,1,0:T(8,128)(2,1)S(1)}, u32[]{:S(2)}, u32[]{:S(2)}) collective-permute-start(bf16[4,2,32,16,128]{4,3,2,1,0:T(8,128)(2,1)S(1)} %get-tuple-element.42.refs_0_), channel_id=1, source_target_pairs={{0,1},{1,0},{2,3},{3,2},{4,5},{5,4},{6,7},{7,6},{8,9},{9,8},{10,11... | collective-permute-start | bytes 3145736 | tf_op jit(solution)/shard_map/ppermute | solution.py:391
  90.7 44.8 %collective-permute-start.28 = (bf16[4,2,32,16,128]{4,3,2,1,0:T(8,128)(2,1)S(1)}, bf16[4,2,32,16,128]{4,3,2,1,0:T(8,128)(2,1)S(1)}, u32[]{:S(2)}, u32[]{:S(2)}) collective-permute-start(bf16[4,2,32,16,128]{4,3,2,1,0:T(8,128)(2,1)S(1)} %get-tuple-element.43.refs_4_), channel_id=1, source_target_pairs={{0,1},{1,0},{2,3},{3,2},{4,5},{5,4},{6,7},{7,6},{8,9},{9,8},{10,11... | collective-permute-start | bytes 3145736 | tf_op jit(solution)/shard_map/ppermute | solution.py:391
  113.1 48.4 %collective-permute-start.21 = (bf16[4,576,128]{2,1,0:T(8,128)(2,1)S(1)}, bf16[4,576,128]{2,1,0:T(8,128)(2,1)S(1)}, u32[]{:S(2)}, u32[]{:S(2)}) collective-permute-start(bf16[4,576,128]{2,1,0:T(8,128)(2,1)S(1)} %collective-permute-done.12), channel_id=1, source_target_pairs={{8,16},{10,18},{12,20},{14,22},{16,24},{18,26},{20,28},{22,30},{9,... | collective-permute-start | bytes 1769480 | tf_op jit(solution)/shard_map/ppermute | solution.py:379
  132.8 29.5 %collective-permute-start.18 = (bf16[4,2,32,16,128]{4,3,2,1,0:T(8,128)(2,1)S(1)}, bf16[4,2,32,16,128]{4,3,2,1,0:T(8,128)(2,1)S(1)}, u32[]{:S(2)}, u32[]{:S(2)}) collective-permute-start(bf16[4,2,32,16,128]{4,3,2,1,0:T(8,128)(2,1)S(1)} %collective-permute-done.10.refs_1_), channel_id=1, source_target_pairs={{0,4},{2,6},{4,0},{6,2},{8,12},{10,14},{12,8},{14,10},{16,20},{18,... | collective-permute-start | bytes 3145736 | tf_op jit(solution)/shard_map/ppermute | solution.py:369
  134.4 6.8 %collective-permute-start.25 = (bf16[4,288,128]{2,1,0:T(8,128)(2,1)S(1)}, bf16[4,288,128]{2,1,0:T(8,128)(2,1)S(1)}, u32[]{:S(2)}, u32[]{:S(2)}) collective-permute-start(bf16[4,288,128]{2,1,0:T(8,128)(2,1)S(1)} %get-tuple-element.88.refs_0_), channel_id=1, source_target_pairs={{0,2},{2,0},{4,6},{6,4},{8,10},{10,8},{12,14},{14,12},{16,18},{18,... | collective-permute-start | bytes 884744 | tf_op jit(solution)/shard_map/ppermute | solution.py:369
  135.0 25.8 %collective-permute-start.26 = (bf16[4,288,128]{2,1,0:T(8,128)(2,1)S(1)}, bf16[4,288,128]{2,1,0:T(8,128)(2,1)S(1)}, u32[]{:S(2)}, u32[]{:S(2)}) collective-permute-start(bf16[4,288,128]{2,1,0:T(8,128)(2,1)S(1)} %get-tuple-element.87.refs_4_), channel_id=1, source_target_pairs={{0,4},{2,6},{4,0},{6,2},{8,12},{10,14},{12,8},{14,10},{16,20},{18,... | collective-permute-start | bytes 884744 | tf_op jit(solution)/shard_map/ppermute | solution.py:369
  135.5 26.0 %collective-permute-start.23 = (bf16[4,576,128]{2,1,0:T(8,128)(2,1)S(1)}, bf16[4,576,128]{2,1,0:T(8,128)(2,1)S(1)}, u32[]{:S(2)}, u32[]{:S(2)}) collective-permute-start(bf16[4,576,128]{2,1,0:T(8,128)(2,1)S(1)} %collective-permute-done.13), channel_id=1, source_target_pairs={{8,0},{10,2},{12,4},{14,6},{16,8},{18,10},{20,12},{22,14},{9,1},{1... | collective-permute-start | bytes 1769480 | tf_op jit(solution)/shard_map/ppermute | solution.py:379
  141.2 40.3 %collective-permute-start.29 = (bf16[4,2,32,16,128]{4,3,2,1,0:T(8,128)(2,1)S(1)}, bf16[4,2,32,16,128]{4,3,2,1,0:T(8,128)(2,1)S(1)}, u32[]{:S(2)}, u32[]{:S(2)}) collective-permute-start(bf16[4,2,32,16,128]{4,3,2,1,0:T(8,128)(2,1)S(1)} %collective-permute-done.10.refs_1_), channel_id=1, source_target_pairs={{0,1},{1,0},{2,3},{3,2},{4,5},{5,4},{6,7},{7,6},{8,9},{9,8},{10,11... | collective-permute-start | bytes 3145736 | tf_op jit(solution)/shard_map/ppermute | solution.py:391
  160.8 20.7 %collective-permute-start.20 = (bf16[4,2,32,16,128]{4,3,2,1,0:T(8,128)(2,1)S(1)}, bf16[4,2,32,16,128]{4,3,2,1,0:T(8,128)(2,1)S(1)}, u32[]{:S(2)}, u32[]{:S(2)}) collective-permute-start(bf16[4,2,32,16,128]{4,3,2,1,0:T(8,128)(2,1)S(1)} %collective-permute-done.11.refs_6_), channel_id=1, source_target_pairs={{0,2},{2,0},{4,6},{6,4},{8,10},{10,8},{12,14},{14,12},{16,18},{18,... | collective-permute-start | bytes 3145736 | tf_op jit(solution)/shard_map/ppermute | solution.py:369
  161.5 20.0 %collective-permute-start.30 = (bf16[4,2,32,16,128]{4,3,2,1,0:T(8,128)(2,1)S(1)}, bf16[4,2,32,16,128]{4,3,2,1,0:T(8,128)(2,1)S(1)}, u32[]{:S(2)}, u32[]{:S(2)}) collective-permute-start(bf16[4,2,32,16,128]{4,3,2,1,0:T(8,128)(2,1)S(1)} %collective-permute-done.11.refs_6_), channel_id=1, source_target_pairs={{0,1},{1,0},{2,3},{3,2},{4,5},{5,4},{6,7},{7,6},{8,9},{9,8},{10,11... | collective-permute-start | bytes 3145736 | tf_op jit(solution)/shard_map/ppermute | solution.py:391
  161.6 20.0 %collective-permute-start.22 = (bf16[4,576,128]{2,1,0:T(8,128)(2,1)S(1)}, bf16[4,576,128]{2,1,0:T(8,128)(2,1)S(1)}, u32[]{:S(2)}, u32[]{:S(2)}) collective-permute-start(bf16[4,576,128]{2,1,0:T(8,128)(2,1)S(1)} %collective-permute-done.21), channel_id=1, source_target_pairs={{16,24},{18,26},{20,28},{22,30},{17,25},{19,27},{21,29},{23,31}} | collective-permute-start | bytes 1769480 | tf_op jit(solution)/shard_map/ppermute | solution.py:379
  162.3 21.7 %collective-permute-start.24 = (bf16[4,576,128]{2,1,0:T(8,128)(2,1)S(1)}, bf16[4,576,128]{2,1,0:T(8,128)(2,1)}, u32[]{:S(2)}, u32[]{:S(2)}) collective-permute-start(bf16[4,576,128]{2,1,0:T(8,128)(2,1)S(1)} %collective-permute-done.23), channel_id=1, source_target_pairs={{8,0},{10,2},{12,4},{14,6},{9,1},{11,3},{13,5},{15,7}} | collective-permute-start | bytes 1769480 | tf_op jit(solution)/shard_map/ppermute | solution.py:379
  184.0 62.1 %all-to-all-start = ((bf16[16,96,1024]{2,1,0:T(8,128)(2,1)}), bf16[16,96,1024]{2,1,0:T(8,128)(2,1)}, u32[]{:S(2)}, u32[]{:S(2)}) async-start(bf16[16,96,1024]{2,1,0:T(8,128)(2,1)} %bitcast.50.phi), calls=%async_computation | async-start | bytes 6291456 | tf_op jit(solution)/shard_map/all_to_all | solution.py:405
  188.5 4.1 collective-permute-start.31
  188.6 5.9 %collective-permute-start.33 = (bf16[4,2,32,16,128]{4,3,2,1,0:T(8,128)(2,1)}, bf16[4,2,32,16,128]{4,3,2,1,0:T(8,128)(2,1)S(1)}, u32[]{:S(2)}, u32[]{:S(2)}) collective-permute-start(bf16[4,2,32,16,128]{4,3,2,1,0:T(8,128)(2,1)} %copy-done.24), channel_id=1, source_target_pairs={{0,1},{1,0},{2,3},{3,2},{4,5},{5,4},{6,7},{7,6},{8,9},{9,8},{10,11... | collective-permute-start | bytes 3145736 | tf_op jit(solution)/shard_map/ppermute | solution.py:391
  189.1 7.1 %collective-permute-start.32 = (bf16[4,2,32,16,128]{4,3,2,1,0:T(8,128)(2,1)}, bf16[4,2,32,16,128]{4,3,2,1,0:T(8,128)(2,1)}, u32[]{:S(2)}, u32[]{:S(2)}) collective-permute-start(bf16[4,2,32,16,128]{4,3,2,1,0:T(8,128)(2,1)} %copy-done.27), channel_id=1, source_target_pairs={{0,1},{1,0},{2,3},{3,2},{4,5},{5,4},{6,7},{7,6},{8,9},{9,8},{10,11... | collective-permute-start | bytes 3145736 | tf_op jit(solution)/shard_map/ppermute | solution.py:391
  189.2 8.5 %collective-permute-start.34 = (bf16[4,2,32,16,128]{4,3,2,1,0:T(8,128)(2,1)}, bf16[4,2,32,16,128]{4,3,2,1,0:T(8,128)(2,1)}, u32[]{:S(2)}, u32[]{:S(2)}) collective-permute-start(bf16[4,2,32,16,128]{4,3,2,1,0:T(8,128)(2,1)} %copy-done.29), channel_id=1, source_target_pairs={{0,1},{1,0},{2,3},{3,2},{4,5},{5,4},{6,7},{7,6},{8,9},{9,8},{10,11... | collective-permute-start | bytes 3145736 | tf_op jit(solution)/shard_map/ppermute | solution.py:391
  191.0 39.7 %collective-permute-start.35 = (bf16[4,288,128]{2,1,0:T(8,128)(2,1)}, bf16[4,288,128]{2,1,0:T(8,128)(2,1)S(1)}, u32[]{:S(2)}, u32[]{:S(2)}) collective-permute-start(bf16[4,288,128]{2,1,0:T(8,128)(2,1)} %copy-done.17), channel_id=1, source_target_pairs={{0,4},{2,6},{4,0},{6,2},{8,12},{10,14},{12,8},{14,10},{16,20},{18,... | collective-permute-start | bytes 884744 | tf_op jit(solution)/shard_map/ppermute | solution.py:369
  192.7 38.0 %collective-permute-start.37 = (bf16[4,288,128]{2,1,0:T(8,128)(2,1)S(1)}, bf16[4,288,128]{2,1,0:T(8,128)(2,1)S(1)}, u32[]{:S(2)}, u32[]{:S(2)}) collective-permute-start(bf16[4,288,128]{2,1,0:T(8,128)(2,1)S(1)} %get-tuple-element.87.refs_4_), channel_id=1, source_target_pairs={{0,2},{2,0},{4,6},{6,4},{8,10},{10,8},{12,14},{14,12},{16,18},{18,... | collective-permute-start | bytes 884744 | tf_op jit(solution)/shard_map/ppermute | solution.py:369
  194.5 36.9 %collective-permute-start.36 = (bf16[4,288,128]{2,1,0:T(8,128)(2,1)}, bf16[4,288,128]{2,1,0:T(8,128)(2,1)S(1)}, u32[]{:S(2)}, u32[]{:S(2)}) collective-permute-start(bf16[4,288,128]{2,1,0:T(8,128)(2,1)} %copy-done.36), channel_id=1, source_target_pairs={{0,4},{2,6},{4,0},{6,2},{8,12},{10,14},{12,8},{14,10},{16,20},{18,... | collective-permute-start | bytes 884744 | tf_op jit(solution)/shard_map/ppermute | solution.py:369
  196.2 36.7 %collective-permute-start.38 = (bf16[4,288,128]{2,1,0:T(8,128)(2,1)}, bf16[4,288,128]{2,1,0:T(8,128)(2,1)}, u32[]{:S(2)}, u32[]{:S(2)}) collective-permute-start(bf16[4,288,128]{2,1,0:T(8,128)(2,1)} %copy-done.37), channel_id=1, source_target_pairs={{0,2},{2,0},{4,6},{6,4},{8,10},{10,8},{12,14},{14,12},{16,18},{18,... | collective-permute-start | bytes 884744 | tf_op jit(solution)/shard_map/ppermute | solution.py:369
  246.1 74.6 %all-to-all-start.1 = ((bf16[16,96,1024]{2,1,0:T(8,128)(2,1)}), bf16[16,96,1024]{2,1,0:T(8,128)(2,1)}, u32[]{:S(2)}, u32[]{:S(2)}) async-start(bf16[16,96,1024]{2,1,0:T(8,128)(2,1)} %hphi.1), calls=%async_computation.1 | async-start | bytes 6291456 | tf_op jit(solution)/shard_map/all_to_all | solution.py:405
  261.1 3.2 collective-permute-start.39
  261.5 4.0 collective-permute-start.43
  262.5 4.3 %collective-permute-start.50 = (bf16[4,576,128]{2,1,0:T(8,128)(2,1)}, bf16[4,576,128]{2,1,0:T(8,128)(2,1)}, u32[]{:S(2)}, u32[]{:S(2)}) collective-permute-start(bf16[4,576,128]{2,1,0:T(8,128)(2,1)} %broadcast_select_fusion.refs_19_), channel_id=1, source_target_pairs={{0,1},{1,0},{2,3},{3,2},{4,5},{5,4},{6,7},{7,6},{8,9},{9,8},{10,11... | collective-permute-start | bytes 1769480 | tf_op jit(solution)/shard_map/ppermute | solution.py:391
  263.0 4.1 collective-permute-start.49
  263.2 2.8 collective-permute-start.40
  264.2 2.4 collective-permute-start.45
  267.1 2.3 collective-permute-start.46
  (52 other events, 1377.4 us)

commit v6 on v3

--- a/solution.py
+++ b/solution.py
@@ -330,20 +330,21 @@
     return me // 4, (me // 2) % 2, me % 2
 
 
-def along_z(part):
+def along_z(part, cuts):
     z = place_of()[0]
     n = lax.axis_size("func")
     held = [part]
     for k in range(1, 4):
         held.append(lax.ppermute(part, "func", [(i, (i + 4 * k) % n) for i in range(n)]))
-
-    def at(level):
-        taken = held[0]
+    size = part.shape[0] // cuts
+
+    def at(level, first):
+        taken = held[0][first : first + size]
         for k in range(1, 4):
-            taken = jnp.where((z - level) % 4 == k, held[k], taken)
+            taken = jnp.where((z - level) % 4 == k, held[k][first : first + size], taken)
         return taken
 
-    return jnp.stack([at(level) for level in range(4)])
+    return [jnp.stack([at(level, c * size) for level in range(4)]) for c in range(cuts)]
 
 
 def swapped(block, bit):
@@ -388,22 +389,34 @@
     halo = lax.ppermute(edge, "rep", [(0, 1), (1, 0)])
     info = jnp.concatenate([centres[:, :1] + planes * rep, centres[:, 1:]], axis=1)
     info = info.astype(jnp.int32)
+    band = planar_band()
 
     resident = n_func == SIDES[0] * SIDES[1] * SIDES[2]
     if resident:
         _, y, x = place_of()
         here = jnp.stack([rep, y, x]).astype(jnp.int32)
-        per = x_blocks // PIECES
-        lines = [along_z(half[p * per : (p + 1) * per]) for p in range(PIECES)]
-        lines, kernel, hamiltonian = lax.optimization_barrier((lines, kernel, hamiltonian))
+        lines = along_z(half, PIECES)
+        stored = jnp.concatenate([kernel[0], hamiltonian[0]])
+        lines, stored, halo, band, info, phi_cut = lax.optimization_barrier(
+            (lines, stored, halo, band, info, phi_cut)
+        )
         near = [swapped(lines[p], 1 + p) for p in range(PIECES)]
-        matrix_lines = [along_z(stored[0]) for stored in (kernel, hamiltonian)]
+        matrix_lines = along_z(stored, 2)
+        lines_too = [other_core(block) for block in lines]
+        near, matrix_lines, lines_too = lax.optimization_barrier((near, matrix_lines, lines_too))
         far = [(swapped(lines[p], 2 - p), swapped(near[p], 2 - p)) for p in range(PIECES)]
-        pot = ordered(lines, near, far)
-        pot, matrix_lines, phi_cut = lax.optimization_barrier((pot, matrix_lines, phi_cut))
-        pot = pot + [other_core(block) for block in pot]
+        near_too = [other_core(block) for block in near]
+        far_too = [tuple(other_core(block) for block in pair) for pair in far]
+        far, matrix_lines, phi_cut, near_too = lax.optimization_barrier(
+            (far, matrix_lines, phi_cut, near_too)
+        )
         phi_pts = exchange(phi_cut)
         matrix_near = [swapped(matrix_lines[p], 1 + p) for p in range(2)]
+        matrix_near, info = lax.optimization_barrier((matrix_near, info))
+        matrix_far = [
+            (swapped(matrix_lines[p], 2 - p), swapped(matrix_near[p], 2 - p)) for p in range(2)
+        ]
+        pot = ordered(lines, near, far) + ordered(lines_too, near_too, far_too)
     else:
         here = jnp.stack([rep, rep, rep]).astype(jnp.int32)
         pot = lax.all_gather(half, ("rep", "func"), axis=0, tiled=False)
@@ -423,12 +436,9 @@
         jnp.pad(halo, ((0, 0), (0, extra), (0, 0))),
     ]
     info, phi_planes, halo = padded
-    hphi = make_hphi(info, here, phi_planes, halo, planar_band(), pot, resident)[:, :owned]
+    hphi = make_hphi(info, here, phi_planes, halo, band, pot, resident)[:, :owned]
     if resident:
-        hphi, matrix_near = lax.optimization_barrier((hphi, matrix_near))
-        matrix_far = [
-            (swapped(matrix_lines[p], 2 - p), swapped(matrix_near[p], 2 - p)) for p in range(2)
-        ]
+        hphi, matrix_far = lax.optimization_barrier((hphi, matrix_far))
         k_parts, h_parts = (
             ordered(matrix_lines[p : p + 1], matrix_near[p : p + 1], matrix_far[p : p + 1], p)
             for p in range(2)

time: 402 us -> 400 us (level)
  waiting for transfers between devices: 155 us -> 172 us
  starting transfers between devices: 68.7 us -> 56.2 us
  blocking collectives: 83.7 us -> 76 us
    ppermute x12 -> x6, starting transfers between devices: 30.3 us -> 11 us  [along_z(): lax.ppermute(part, 'func', [(i, (i + 4 * k) % n) for i in range(n)])]
    ppermute x12, starting transfers between devices: 15.4 us -> 32.9 us  [swapped(): return lax.ppermute(block, 'func', [(i, i ^ bit) for i in range(n)])]
    ppermute x12, waiting for transfers between devices: 88.6 us -> 101 us  [swapped(): return lax.ppermute(block, 'func', [(i, i ^ bit) for i in range(n)])]
    all_to_all x2, starting transfers between devices: 19.6 us -> 9.41 us  [exchange(): return lax.all_to_all(rows, 'func', split_axis=0, concat_axis=0, tiled=True)]
    ppermute x12 -> x6, waiting for transfers between devices: 47.8 us -> 57.2 us  [along_z(): lax.ppermute(part, 'func', [(i, (i + 4 * k) % n) for i in range(n)])]
    all_to_all x1, blocking collectives: 83.7 us -> 76 us  [exchange(): return lax.all_to_all(rows, 'func', split_axis=0, concat_axis=0, tiled=True)]
    all_to_all x2, waiting for transfers between devices: 11.8 us -> 7.47 us  [exchange(): return lax.all_to_all(rows, 'func', split_axis=0, concat_axis=0, tiled=True)]
    unnamed x57 -> x65, local copies, waits for them, and re-layouts: 10.2 us -> 10.8 us
  transfers between devices with their start and end apart: 43 -> 37, of which waited for: 20 -> 17; matrix products, arithmetic and copies ran while one was open for 2% -> 3% of each run, Pallas kernels for 16% -> 16%
where the time goes in v6:
time: 400 us; the launch traced here: 399 us
  waiting for transfers between devices  172 us (43%)
  blocking collectives  76 us (19%)
  Pallas kernels  73.1 us (18%)
  starting transfers between devices  56.2 us (14%)
  local copies, waits for them, and re-layouts  15.1 us (4%)
  other arithmetic  6.09 us (2%)
    ppermute x12, waiting for transfers between devices, swapped(): return lax.ppermute(block, 'func', [(i, i ^ bit) for i in range(n)])  101 us
    all_to_all x1, blocking collectives, exchange(): return lax.all_to_all(rows, 'func', split_axis=0, concat_axis=0, tiled=True)  76 us
    ppermute x6, waiting for transfers between devices, along_z(): lax.ppermute(part, 'func', [(i, (i + 4 * k) % n) for i in range(n)])  57.2 us
    pallas_call x1, Pallas kernels, make_hphi(): pl.pallas_call(functools.partial(hphi_kernel, resident=resident), out_sha...  32.9 us
    ppermute x12, starting transfers between devices, swapped(): return lax.ppermute(block, 'func', [(i, i ^ bit) for i in range(n)])  32.9 us
    pallas_call x1, Pallas kernels, first_products(): pl.pallas_call(first_kernel, out_shape=[jax.ShapeDtypeStruct((NF, NF), jn...  29.8 us
    ppermute x6, starting transfers between devices, along_z(): lax.ppermute(part, 'func', [(i, (i + 4 * k) % n) for i in range(n)])  11 us
    unnamed x65, local copies, waits for them, and re-layouts  10.8 us
  transfers between devices with their start and end apart: 37, of which 17 were waited for; matrix products, arithmetic and copies ran while one was open for 3% of the time, Pallas kernels for 16%

profile of v6, /device:TPU:0, one launch (start us, length us, event | category | flops | bytes accessed | tf_op | source)
XLA Modules:
  0.0 399.3 jit_solution(13624243062945637677)
XLA Ops:
  0.0 1.6 copy-done
  1.7 5.1 %collective-permute-start = (bf16[4,32,16,128]{3,2,1,0:T(8,128)(2,1)S(1)}, bf16[4,32,16,128]{3,2,1,0:T(8,128)(2,1)S(1)}, u32[]{:S(2)}, u32[]{:S(2)}) collective-permute-start(bf16[4,32,16,128]{3,2,1,0:T(8,128)(2,1)S(1)} %bitcast.53), channel_id=1, source_target_pairs={{0,24},{2,26},{4,28},{6,30},{8,0},{10,2},{12,4},{14,6},{16,8},{18,... | collective-permute-start | bytes 1572872 | tf_op jit(solution)/shard_map/ppermute | solution.py:338
  6.8 1.0 collective-permute-start.2
  7.8 5.3 %copy.25 = bf16[96,16,1024]{2,0,1:T(8,128)(2,1)} copy(bf16[96,16,1024]{2,1,0:T(8,128)(2,1)} %param.7) | data formatting | bytes 6291456 | tf_op args[0]
  13.2 1.2 slice_select_fusion
  14.6 1.6 select_convert_fusion.band
  16.2 3.0 collective-permute-done
  19.2 32.4 %collective-permute-done.1 = bf16[4,32,16,128]{3,2,1,0:T(8,128)(2,1)S(1)} collective-permute-done((bf16[4,32,16,128]{3,2,1,0:T(8,128)(2,1)S(1)}, bf16[4,32,16,128]{3,2,1,0:T(8,128)(2,1)S(1)}, u32[]{:S(2)}, u32[]{:S(2)}) %collective-permute-start.1) | collective-permute-done | bytes 524320 | tf_op jit(solution)/shard_map/ppermute | solution.py:338
  52.3 2.9 collective-permute-start.8
  55.2 1.9 collective-permute-start.9
  57.2 1.5 collective-permute-start.5
  58.7 1.7 collective-permute-done.7
  60.4 20.1 %collective-permute-done.8 = bf16[1152,128]{1,0:T(8,128)(2,1)S(1)} collective-permute-done((bf16[1152,128]{1,0:T(8,128)(2,1)S(1)}, bf16[1152,128]{1,0:T(8,128)(2,1)S(1)}, u32[]{:S(2)}, u32[]{:S(2)}) %collective-permute-start.8) | collective-permute-done | bytes 294944 | tf_op jit(solution)/shard_map/ppermute | solution.py:338
  80.5 1.5 collective-permute-start.6
  82.0 1.5 collective-permute-start.13
  83.7 0.9 pad_maximum_fusion.3.refs_8_
  84.6 0.9 pad_maximum_fusion.2.refs_0_
  85.6 0.6 collective-permute-start.4
  86.2 20.4 %collective-permute-done.6.refs_6_ = bf16[4,2,32,16,128]{4,3,2,1,0:T(8,128)(2,1)S(1)} collective-permute-done((bf16[4,2,32,16,128]{4,3,2,1,0:T(8,128)(2,1)S(1)}, bf16[4,2,32,16,128]{4,3,2,1,0:T(8,128)(2,1)S(1)}, u32[]{:S(2)}, u32[]{:S(2)}) %collective-permute-start.6) | collective-permute-done | bytes 1048608 | tf_op jit(solution)/shard_map/ppermute | solution.py:352
  106.6 1.5 collective-permute-start.12
  108.1 1.5 collective-permute-start.14
  109.8 19.2 %collective-permute-done.4.refs_2_ = bf16[4,2,32,16,128]{4,3,2,1,0:T(8,128)(2,1)S(1)} collective-permute-done((bf16[4,2,32,16,128]{4,3,2,1,0:T(8,128)(2,1)S(1)}, bf16[4,2,32,16,128]{4,3,2,1,0:T(8,128)(2,1)S(1)}, u32[]{:S(2)}, u32[]{:S(2)}) %collective-permute-start.4) | collective-permute-done | bytes 1048608 | tf_op jit(solution)/shard_map/ppermute | solution.py:352
  129.1 20.0 %collective-permute-done.12.refs_3_ = bf16[4,2,32,16,128]{4,3,2,1,0:T(8,128)(2,1)S(1)} collective-permute-done((bf16[4,2,32,16,128]{4,3,2,1,0:T(8,128)(2,1)S(1)}, bf16[4,2,32,16,128]{4,3,2,1,0:T(8,128)(2,1)S(1)}, u32[]{:S(2)}, u32[]{:S(2)}) %collective-permute-start.12) | collective-permute-done | bytes 1048608 | tf_op jit(solution)/shard_map/ppermute | solution.py:352
  149.2 0.9 copy-done.16
  150.4 1.0 copy-done.17
  151.4 4.6 %all-to-all-start = ((bf16[16,96,1024]{2,1,0:T(8,128)(2,1)}), bf16[16,96,1024]{2,1,0:T(8,128)(2,1)}, u32[]{:S(2)}, u32[]{:S(2)}) async-start(bf16[16,96,1024]{2,1,0:T(8,128)(2,1)} %bitcast.50.phi), calls=%async_computation | async-start | bytes 6291456 | tf_op jit(solution)/shard_map/all_to_all | solution.py:378
  156.0 1.8 collective-permute-start.17
  158.9 19.2 %collective-permute-done.17.refs_1_ = bf16[4,576,128]{2,1,0:T(8,128)(2,1)S(1)} collective-permute-done((bf16[4,576,128]{2,1,0:T(8,128)(2,1)S(1)}, bf16[4,576,128]{2,1,0:T(8,128)(2,1)S(1)}, u32[]{:S(2)}, u32[]{:S(2)}) %collective-permute-start.17) | collective-permute-done | bytes 589856 | tf_op jit(solution)/shard_map/ppermute | solution.py:352
  178.1 19.0 %collective-permute-start.18 = (bf16[4,576,128]{2,1,0:T(8,128)(2,1)S(1)}, bf16[4,576,128]{2,1,0:T(8,128)(2,1)}, u32[]{:S(2)}, u32[]{:S(2)}) collective-permute-start(bf16[4,576,128]{2,1,0:T(8,128)(2,1)S(1)} %copy-done.4), channel_id=1, source_target_pairs={{0,4},{2,6},{4,0},{6,2},{8,12},{10,14},{12,8},{14,10},{16,20},{18,... | collective-permute-start | bytes 1769480 | tf_op jit(solution)/shard_map/ppermute | solution.py:352
  197.1 0.7 pad_add_fusion.1.here
  197.7 22.1 %collective-permute-done.18.refs_10_ = bf16[4,576,128]{2,1,0:T(8,128)(2,1)} collective-permute-done((bf16[4,576,128]{2,1,0:T(8,128)(2,1)S(1)}, bf16[4,576,128]{2,1,0:T(8,128)(2,1)}, u32[]{:S(2)}, u32[]{:S(2)}) %collective-permute-start.18) | collective-permute-done | bytes 589856 | tf_op jit(solution)/shard_map/ppermute | solution.py:352
  219.8 0.7 copy.21.info
  220.6 2.1 collective-permute-start.24
  222.7 2.0 collective-permute-start.26
  224.6 32.9 %hphi.1 = bf16[16,96,1024]{2,1,0:T(8,128)(2,1)} custom-call(s32[96,3]{1,0:T(8,128)} %copy.21.info, s32[3]{0:T(128)} %pad_add_fusion.1.here, bf16[16,96,1024]{2,1,0:T(8,128)(2,1)} %bitcast.50.phi, bf16[2,96,1024]{2,1,0:T(8,128)(2,1)} %copy-done.31, bf16[512,256]{1,0:T(8,128)(2,1)} %select_convert_fusion.band, bf16[4,2,32,16,128]{4,3,2,1,0:T(8,128)(2,1)} %copy-done.2, ...), custom_call_target="tpu_custom_call" | custom-call | flops 12884901888 | bytes 62914560 | tf_op jit(solution)/shard_map/hphi/pallas_call | solution.py:204
  257.6 0.8 copy-done.20
  258.5 4.8 %all-to-all-start.1 = ((bf16[16,96,1024]{2,1,0:T(8,128)(2,1)}), bf16[16,96,1024]{2,1,0:T(8,128)(2,1)}, u32[]{:S(2)}, u32[]{:S(2)}) async-start(bf16[16,96,1024]{2,1,0:T(8,128)(2,1)} %hphi.1), calls=%async_computation.1 | async-start | bytes 6291456 | tf_op jit(solution)/shard_map/all_to_all | solution.py:378
  264.4 0.9 collective-permute-done.27.refs_4_
  265.5 1.5 collective-permute-done.31.refs_12_
  267.2 1.5 collective-permute-done.28.refs_5_
  269.6 0.8 collective-permute-done.32.refs_13_
  270.4 1.1 collective-permute-done.34.refs_15_
  271.5 0.8 copy-done.30
  272.3 29.8 %products.1 = (bf16[1536,1536]{1,0:T(8,128)(2,1)}, f32[1536,1024]{1,0:T(8,128)}) custom-call(s32[3]{0:T(128)} %pad_add_fusion.1.here, s32[12,12]{1,0:T(8,128)} %k_cols.1, s32[12,12]{1,0:T(8,128)} %h_cols.1, bf16[4,576,128]{2,1,0:T(8,128)(2,1)} %pad_maximum_fusion.2.refs_0_, bf16[4,576,128]{2,1,0:T(8,128)(2,1)} %copy-done.19, ...), custom_call_target="tpu_custom_call" | custom-call | flops 9663676416 | bytes 25165824 | tf_op jit(solution)/shard_map/products/pallas_call | solution.py:290
  302.1 7.5 %all-to-all-done.1 = bf16[16,96,1024]{2,1,0:T(8,128)(2,1)} async-done(((bf16[16,96,1024]{2,1,0:T(8,128)(2,1)}), bf16[16,96,1024]{2,1,0:T(8,128)(2,1)}, u32[]{:S(2)}, u32[]{:S(2)}) %all-to-all-start.1) | async-done | bytes 3145760 | tf_op jit(solution)/shard_map/all_to_all | solution.py:378
  309.6 10.3 %gradient.1 = bf16[1536,1024]{1,0:T(8,128)(2,1)} custom-call(bf16[1536,1536]{1,0:T(8,128)(2,1)} %get-tuple-element.66.dense_k, bf16[1536,1024]{1,0:T(8,128)(2,1)} %bitcast.25.hphi, f32[1536,1024]{1,0:T(8,128)} %get-tuple-element.68.product), custom_call_target="tpu_custom_call" | custom-call | flops 4831838208 | bytes 17825792 | tf_op jit(solution)/shard_map/gradient/pallas_call | solution.py:314
  319.9 76.0 %all_to_all.15 = bf16[16,96,1024]{2,1,0:T(8,128)(2,1)S(1)} all-to-all(bf16[16,96,1024]{2,1,0:T(8,128)(2,1)} %bitcast.59), channel_id=1, replica_groups=mesh['func'=16,'rep'=2] {'func'}, dimensions={0} | all-to-all | bytes 6291456 | tf_op jit(solution)/shard_map/all_to_all | solution.py:378
  395.9 3.4 copy.22
  (121 shorter events, 5.2 us)
Async XLA Ops:
  1.7 17.5 %collective-permute-start = (bf16[4,32,16,128]{3,2,1,0:T(8,128)(2,1)S(1)}, bf16[4,32,16,128]{3,2,1,0:T(8,128)(2,1)S(1)}, u32[]{:S(2)}, u32[]{:S(2)}) collective-permute-start(bf16[4,32,16,128]{3,2,1,0:T(8,128)(2,1)S(1)} %bitcast.53), channel_id=1, source_target_pairs={{0,24},{2,26},{4,28},{6,30},{8,0},{10,2},{12,4},{14,6},{16,8},{18,... | collective-permute-start | bytes 1572872 | tf_op jit(solution)/shard_map/ppermute | solution.py:338
  6.8 44.8 %collective-permute-start.1 = (bf16[4,32,16,128]{3,2,1,0:T(8,128)(2,1)S(1)}, bf16[4,32,16,128]{3,2,1,0:T(8,128)(2,1)S(1)}, u32[]{:S(2)}, u32[]{:S(2)}) collective-permute-start(bf16[4,32,16,128]{3,2,1,0:T(8,128)(2,1)S(1)} %bitcast.54), channel_id=1, source_target_pairs={{0,16},{2,18},{4,20},{6,22},{8,24},{10,26},{12,28},{14,30},{16,0},... | collective-permute-start | bytes 1572872 | tf_op jit(solution)/shard_map/ppermute | solution.py:338
  6.8 44.8 %collective-permute-start.2 = (bf16[4,32,16,128]{3,2,1,0:T(8,128)(2,1)S(1)}, bf16[4,32,16,128]{3,2,1,0:T(8,128)(2,1)S(1)}, u32[]{:S(2)}, u32[]{:S(2)}) collective-permute-start(bf16[4,32,16,128]{3,2,1,0:T(8,128)(2,1)S(1)} %bitcast.55), channel_id=1, source_target_pairs={{0,8},{2,10},{4,12},{6,14},{8,16},{10,18},{12,20},{14,22},{16,24},... | collective-permute-start | bytes 1572872 | tf_op jit(solution)/shard_map/ppermute | solution.py:338
  14.3 37.9 %collective-permute-start.3 = (bf16[2,96,1024]{2,1,0:T(8,128)(2,1)S(1)}, bf16[2,96,1024]{2,1,0:T(8,128)(2,1)S(1)}, u32[]{:S(2)}, u32[]{:S(2)}) collective-permute-start(bf16[2,96,1024]{2,1,0:T(8,128)(2,1)S(1)} %slice_select_fusion), channel_id=1, source_target_pairs={{0,1},{1,0},{2,3},{3,2},{4,5},{5,4},{6,7},{7,6},{8,9},{9,8},{10,11... | collective-permute-start | bytes 1179656 | tf_op jit(solution)/shard_map/ppermute | solution.py:389
  52.2 33.3 %copy-start.3 = (bf16[4,2,32,16,128]{4,3,2,1,0:T(8,128)(2,1)}, bf16[4,2,32,16,128]{4,3,2,1,0:T(8,128)(2,1)S(1)}, u32[]{:S(2)}) copy-start(bf16[4,2,32,16,128]{4,3,2,1,0:T(8,128)(2,1)S(1)} %get-tuple-element.38.refs_4_) | copy-start | bytes 3145732
  52.3 33.3 %copy-start.2 = (bf16[4,2,32,16,128]{4,3,2,1,0:T(8,128)(2,1)}, bf16[4,2,32,16,128]{4,3,2,1,0:T(8,128)(2,1)S(1)}, u32[]{:S(2)}) copy-start(bf16[4,2,32,16,128]{4,3,2,1,0:T(8,128)(2,1)S(1)} %get-tuple-element.37.refs_0_) | copy-start | bytes 3145732
  52.3 33.3 %copy-start.31 = (bf16[2,96,1024]{2,1,0:T(8,128)(2,1)}, bf16[2,96,1024]{2,1,0:T(8,128)(2,1)S(1)}, u32[]{:S(2)}) copy-start(bf16[2,96,1024]{2,1,0:T(8,128)(2,1)S(1)} %collective-permute-done.3.halo) | copy-start | bytes 1179652
  52.3 8.1 %collective-permute-start.7 = (bf16[1152,128]{1,0:T(8,128)(2,1)S(1)}, bf16[1152,128]{1,0:T(8,128)(2,1)S(1)}, u32[]{:S(2)}, u32[]{:S(2)}) collective-permute-start(bf16[1152,128]{1,0:T(8,128)(2,1)S(1)} %pad_maximum_fusion.4), channel_id=1, source_target_pairs={{0,24},{2,26},{4,28},{6,30},{8,0},{10,2},{12,4},{14,6},{16,8},{18,... | collective-permute-start | bytes 884744 | tf_op jit(solution)/shard_map/ppermute | solution.py:338
  52.3 28.1 %collective-permute-start.8 = (bf16[1152,128]{1,0:T(8,128)(2,1)S(1)}, bf16[1152,128]{1,0:T(8,128)(2,1)S(1)}, u32[]{:S(2)}, u32[]{:S(2)}) collective-permute-start(bf16[1152,128]{1,0:T(8,128)(2,1)S(1)} %pad_maximum_fusion.4), channel_id=1, source_target_pairs={{0,16},{2,18},{4,20},{6,22},{8,24},{10,26},{12,28},{14,30},{16,0},... | collective-permute-start | bytes 884744 | tf_op jit(solution)/shard_map/ppermute | solution.py:338
  55.2 26.8 %collective-permute-start.9 = (bf16[1152,128]{1,0:T(8,128)(2,1)S(1)}, bf16[1152,128]{1,0:T(8,128)(2,1)S(1)}, u32[]{:S(2)}, u32[]{:S(2)}) collective-permute-start(bf16[1152,128]{1,0:T(8,128)(2,1)S(1)} %pad_maximum_fusion.4), channel_id=1, source_target_pairs={{0,8},{2,10},{4,12},{6,14},{8,16},{10,18},{12,20},{14,22},{16,24},... | collective-permute-start | bytes 884744 | tf_op jit(solution)/shard_map/ppermute | solution.py:338
  57.2 28.4 %collective-permute-start.10 = (bf16[4,2,32,16,128]{4,3,2,1,0:T(8,128)(2,1)S(1)}, bf16[4,2,32,16,128]{4,3,2,1,0:T(8,128)(2,1)S(1)}, u32[]{:S(2)}, u32[]{:S(2)}) collective-permute-start(bf16[4,2,32,16,128]{4,3,2,1,0:T(8,128)(2,1)S(1)} %get-tuple-element.37.refs_0_), channel_id=1, source_target_pairs={{0,1},{1,0},{2,3},{3,2},{4,5},{5,4},{6,7},{7,6},{8,9},{9,8},{10,11... | collective-permute-start | bytes 3145736 | tf_op jit(solution)/shard_map/ppermute | solution.py:364
  57.2 29.0 %collective-permute-start.5 = (bf16[4,2,32,16,128]{4,3,2,1,0:T(8,128)(2,1)S(1)}, bf16[4,2,32,16,128]{4,3,2,1,0:T(8,128)(2,1)S(1)}, u32[]{:S(2)}, u32[]{:S(2)}) collective-permute-start(bf16[4,2,32,16,128]{4,3,2,1,0:T(8,128)(2,1)S(1)} %get-tuple-element.37.refs_0_), channel_id=1, source_target_pairs={{0,2},{2,0},{4,6},{6,4},{8,10},{10,8},{12,14},{14,12},{16,18},{18,... | collective-permute-start | bytes 3145736 | tf_op jit(solution)/shard_map/ppermute | solution.py:352
  60.4 25.7 %collective-permute-start.11 = (bf16[4,2,32,16,128]{4,3,2,1,0:T(8,128)(2,1)S(1)}, bf16[4,2,32,16,128]{4,3,2,1,0:T(8,128)(2,1)S(1)}, u32[]{:S(2)}, u32[]{:S(2)}) collective-permute-start(bf16[4,2,32,16,128]{4,3,2,1,0:T(8,128)(2,1)S(1)} %get-tuple-element.38.refs_4_), channel_id=1, source_target_pairs={{0,1},{1,0},{2,3},{3,2},{4,5},{5,4},{6,7},{7,6},{8,9},{9,8},{10,11... | collective-permute-start | bytes 3145736 | tf_op jit(solution)/shard_map/ppermute | solution.py:364
  80.5 26.1 %collective-permute-start.6 = (bf16[4,2,32,16,128]{4,3,2,1,0:T(8,128)(2,1)S(1)}, bf16[4,2,32,16,128]{4,3,2,1,0:T(8,128)(2,1)S(1)}, u32[]{:S(2)}, u32[]{:S(2)}) collective-permute-start(bf16[4,2,32,16,128]{4,3,2,1,0:T(8,128)(2,1)S(1)} %get-tuple-element.38.refs_4_), channel_id=1, source_target_pairs={{0,4},{2,6},{4,0},{6,2},{8,12},{10,14},{12,8},{14,10},{16,20},{18,... | collective-permute-start | bytes 3145736 | tf_op jit(solution)/shard_map/ppermute | solution.py:352
  82.0 27.6 %collective-permute-start.13 = (bf16[4,2,32,16,128]{4,3,2,1,0:T(8,128)(2,1)S(1)}, bf16[4,2,32,16,128]{4,3,2,1,0:T(8,128)(2,1)S(1)}, u32[]{:S(2)}, u32[]{:S(2)}) collective-permute-start(bf16[4,2,32,16,128]{4,3,2,1,0:T(8,128)(2,1)S(1)} %get-tuple-element.38.refs_4_), channel_id=1, source_target_pairs={{0,2},{2,0},{4,6},{6,4},{8,10},{10,8},{12,14},{14,12},{16,18},{18,... | collective-permute-start | bytes 3145736 | tf_op jit(solution)/shard_map/ppermute | solution.py:352
  85.5 92.5 %copy-start.4 = (bf16[4,576,128]{2,1,0:T(8,128)(2,1)S(1)}, bf16[4,576,128]{2,1,0:T(8,128)(2,1)}, u32[]{:S(2)}) copy-start(bf16[4,576,128]{2,1,0:T(8,128)(2,1)} %pad_maximum_fusion.3.refs_8_) | copy-start | bytes 1769476
  85.6 43.5 %copy-start.9 = (bf16[4,2,32,16,128]{4,3,2,1,0:T(8,128)(2,1)}, bf16[4,2,32,16,128]{4,3,2,1,0:T(8,128)(2,1)S(1)}, u32[]{:S(2)}) copy-start(bf16[4,2,32,16,128]{4,3,2,1,0:T(8,128)(2,1)S(1)} %collective-permute-done.10.refs_8_) | copy-start | bytes 3145732
  85.6 43.5 %collective-permute-start.4 = (bf16[4,2,32,16,128]{4,3,2,1,0:T(8,128)(2,1)S(1)}, bf16[4,2,32,16,128]{4,3,2,1,0:T(8,128)(2,1)S(1)}, u32[]{:S(2)}, u32[]{:S(2)}) collective-permute-start(bf16[4,2,32,16,128]{4,3,2,1,0:T(8,128)(2,1)S(1)} %get-tuple-element.37.refs_0_), channel_id=1, source_target_pairs={{0,4},{2,6},{4,0},{6,2},{8,12},{10,14},{12,8},{14,10},{16,20},{18,... | collective-permute-start | bytes 3145736 | tf_op jit(solution)/shard_map/ppermute | solution.py:352
  86.1 63.0 %copy-start.11 = (bf16[4,2,32,16,128]{4,3,2,1,0:T(8,128)(2,1)}, bf16[4,2,32,16,128]{4,3,2,1,0:T(8,128)(2,1)S(1)}, u32[]{:S(2)}) copy-start(bf16[4,2,32,16,128]{4,3,2,1,0:T(8,128)(2,1)S(1)} %collective-permute-done.11.refs_12_) | copy-start | bytes 3145732
  86.2 63.0 %copy-start.10 = (bf16[4,2,32,16,128]{4,3,2,1,0:T(8,128)(2,1)}, bf16[4,2,32,16,128]{4,3,2,1,0:T(8,128)(2,1)S(1)}, u32[]{:S(2)}) copy-start(bf16[4,2,32,16,128]{4,3,2,1,0:T(8,128)(2,1)S(1)} %collective-permute-done.5.refs_1_) | copy-start | bytes 3145732
  106.6 42.5 %copy-start.12 = (bf16[4,2,32,16,128]{4,3,2,1,0:T(8,128)(2,1)}, bf16[4,2,32,16,128]{4,3,2,1,0:T(8,128)(2,1)S(1)}, u32[]{:S(2)}) copy-start(bf16[4,2,32,16,128]{4,3,2,1,0:T(8,128)(2,1)S(1)} %collective-permute-done.6.refs_6_) | copy-start | bytes 3145732
  106.6 42.5 %collective-permute-start.12 = (bf16[4,2,32,16,128]{4,3,2,1,0:T(8,128)(2,1)S(1)}, bf16[4,2,32,16,128]{4,3,2,1,0:T(8,128)(2,1)S(1)}, u32[]{:S(2)}, u32[]{:S(2)}) collective-permute-start(bf16[4,2,32,16,128]{4,3,2,1,0:T(8,128)(2,1)S(1)} %collective-permute-done.5.refs_1_), channel_id=1, source_target_pairs={{0,4},{2,6},{4,0},{6,2},{8,12},{10,14},{12,8},{14,10},{16,20},{18,... | collective-permute-start | bytes 3145736 | tf_op jit(solution)/shard_map/ppermute | solution.py:352
  108.1 41.0 %collective-permute-start.15 = (bf16[4,2,32,16,128]{4,3,2,1,0:T(8,128)(2,1)S(1)}, bf16[4,2,32,16,128]{4,3,2,1,0:T(8,128)(2,1)S(1)}, u32[]{:S(2)}, u32[]{:S(2)}) collective-permute-start(bf16[4,2,32,16,128]{4,3,2,1,0:T(8,128)(2,1)S(1)} %collective-permute-done.5.refs_1_), channel_id=1, source_target_pairs={{0,1},{1,0},{2,3},{3,2},{4,5},{5,4},{6,7},{7,6},{8,9},{9,8},{10,11... | collective-permute-start | bytes 3145736 | tf_op jit(solution)/shard_map/ppermute | solution.py:364
  108.1 41.0 %collective-permute-start.14 = (bf16[4,2,32,16,128]{4,3,2,1,0:T(8,128)(2,1)S(1)}, bf16[4,2,32,16,128]{4,3,2,1,0:T(8,128)(2,1)S(1)}, u32[]{:S(2)}, u32[]{:S(2)}) collective-permute-start(bf16[4,2,32,16,128]{4,3,2,1,0:T(8,128)(2,1)S(1)} %collective-permute-done.6.refs_6_), channel_id=1, source_target_pairs={{0,2},{2,0},{4,6},{6,4},{8,10},{10,8},{12,14},{14,12},{16,18},{18,... | collective-permute-start | bytes 3145736 | tf_op jit(solution)/shard_map/ppermute | solution.py:352
  109.6 39.5 %copy-start.13 = (bf16[4,2,32,16,128]{4,3,2,1,0:T(8,128)(2,1)}, bf16[4,2,32,16,128]{4,3,2,1,0:T(8,128)(2,1)S(1)}, u32[]{:S(2)}) copy-start(bf16[4,2,32,16,128]{4,3,2,1,0:T(8,128)(2,1)S(1)} %collective-permute-done.13.refs_5_) | copy-start | bytes 3145732
  109.6 46.4 %copy-start.5 = (bf16[4,576,128]{2,1,0:T(8,128)(2,1)S(1)}, bf16[4,576,128]{2,1,0:T(8,128)(2,1)}, u32[]{:S(2)}) copy-start(bf16[4,576,128]{2,1,0:T(8,128)(2,1)} %pad_maximum_fusion.2.refs_0_) | copy-start | bytes 1769476
  109.6 41.8 %collective-permute-start.16 = (bf16[4,2,32,16,128]{4,3,2,1,0:T(8,128)(2,1)S(1)}, bf16[4,2,32,16,128]{4,3,2,1,0:T(8,128)(2,1)}, u32[]{:S(2)}, u32[]{:S(2)}) collective-permute-start(bf16[4,2,32,16,128]{4,3,2,1,0:T(8,128)(2,1)S(1)} %collective-permute-done.6.refs_6_), channel_id=1, source_target_pairs={{0,1},{1,0},{2,3},{3,2},{4,5},{5,4},{6,7},{7,6},{8,9},{9,8},{10,11... | collective-permute-start | bytes 3145736 | tf_op jit(solution)/shard_map/ppermute | solution.py:364
  151.4 107.1 %all-to-all-start = ((bf16[16,96,1024]{2,1,0:T(8,128)(2,1)}), bf16[16,96,1024]{2,1,0:T(8,128)(2,1)}, u32[]{:S(2)}, u32[]{:S(2)}) async-start(bf16[16,96,1024]{2,1,0:T(8,128)(2,1)} %bitcast.50.phi), calls=%async_computation | async-start | bytes 6291456 | tf_op jit(solution)/shard_map/all_to_all | solution.py:378
  156.0 22.1 %collective-permute-start.17 = (bf16[4,576,128]{2,1,0:T(8,128)(2,1)S(1)}, bf16[4,576,128]{2,1,0:T(8,128)(2,1)S(1)}, u32[]{:S(2)}, u32[]{:S(2)}) collective-permute-start(bf16[4,576,128]{2,1,0:T(8,128)(2,1)S(1)} %copy-done.5), channel_id=1, source_target_pairs={{0,2},{2,0},{4,6},{6,4},{8,10},{10,8},{12,14},{14,12},{16,18},{18,... | collective-permute-start | bytes 1769480 | tf_op jit(solution)/shard_map/ppermute | solution.py:352
  157.8 62.7 %collective-permute-start.19 = (bf16[4,2,32,16,128]{4,3,2,1,0:T(8,128)(2,1)}, bf16[4,2,32,16,128]{4,3,2,1,0:T(8,128)(2,1)}, u32[]{:S(2)}, u32[]{:S(2)}) collective-permute-start(bf16[4,2,32,16,128]{4,3,2,1,0:T(8,128)(2,1)} %copy-done.15), channel_id=1, source_target_pairs={{0,1},{1,0},{2,3},{3,2},{4,5},{5,4},{6,7},{7,6},{8,9},{9,8},{10,11... | collective-permute-start | bytes 3145736 | tf_op jit(solution)/shard_map/ppermute | solution.py:364
  157.8 62.7 %collective-permute-start.21 = (bf16[4,2,32,16,128]{4,3,2,1,0:T(8,128)(2,1)S(1)}, bf16[4,2,32,16,128]{4,3,2,1,0:T(8,128)(2,1)}, u32[]{:S(2)}, u32[]{:S(2)}) collective-permute-start(bf16[4,2,32,16,128]{4,3,2,1,0:T(8,128)(2,1)S(1)} %copy-done.14), channel_id=1, source_target_pairs={{0,1},{1,0},{2,3},{3,2},{4,5},{5,4},{6,7},{7,6},{8,9},{9,8},{10,11... | collective-permute-start | bytes 3145736 | tf_op jit(solution)/shard_map/ppermute | solution.py:364
  158.3 64.3 %collective-permute-start.20 = (bf16[4,2,32,16,128]{4,3,2,1,0:T(8,128)(2,1)}, bf16[4,2,32,16,128]{4,3,2,1,0:T(8,128)(2,1)}, u32[]{:S(2)}, u32[]{:S(2)}) collective-permute-start(bf16[4,2,32,16,128]{4,3,2,1,0:T(8,128)(2,1)} %copy-done.16), channel_id=1, source_target_pairs={{0,1},{1,0},{2,3},{3,2},{4,5},{5,4},{6,7},{7,6},{8,9},{9,8},{10,11... | collective-permute-start | bytes 3145736 | tf_op jit(solution)/shard_map/ppermute | solution.py:364
  158.4 66.3 %collective-permute-start.22 = (bf16[4,2,32,16,128]{4,3,2,1,0:T(8,128)(2,1)}, bf16[4,2,32,16,128]{4,3,2,1,0:T(8,128)(2,1)}, u32[]{:S(2)}, u32[]{:S(2)}) collective-permute-start(bf16[4,2,32,16,128]{4,3,2,1,0:T(8,128)(2,1)} %copy-done.18), channel_id=1, source_target_pairs={{0,1},{1,0},{2,3},{3,2},{4,5},{5,4},{6,7},{7,6},{8,9},{9,8},{10,11... | collective-permute-start | bytes 3145736 | tf_op jit(solution)/shard_map/ppermute | solution.py:364
  178.1 85.8 %copy-start.19 = (bf16[4,576,128]{2,1,0:T(8,128)(2,1)}, bf16[4,576,128]{2,1,0:T(8,128)(2,1)S(1)}, u32[]{:S(2)}) copy-start(bf16[4,576,128]{2,1,0:T(8,128)(2,1)S(1)} %collective-permute-done.17.refs_1_) | copy-start | bytes 1769476
  178.1 41.8 %collective-permute-start.18 = (bf16[4,576,128]{2,1,0:T(8,128)(2,1)S(1)}, bf16[4,576,128]{2,1,0:T(8,128)(2,1)}, u32[]{:S(2)}, u32[]{:S(2)}) collective-permute-start(bf16[4,576,128]{2,1,0:T(8,128)(2,1)S(1)} %copy-done.4), channel_id=1, source_target_pairs={{0,4},{2,6},{4,0},{6,2},{8,12},{10,14},{12,8},{14,10},{16,20},{18,... | collective-permute-start | bytes 1769480 | tf_op jit(solution)/shard_map/ppermute | solution.py:352
  219.8 37.7 %collective-permute-start.23 = (bf16[4,576,128]{2,1,0:T(8,128)(2,1)S(1)}, bf16[4,576,128]{2,1,0:T(8,128)(2,1)}, u32[]{:S(2)}, u32[]{:S(2)}) collective-permute-start(bf16[4,576,128]{2,1,0:T(8,128)(2,1)S(1)} %copy-done.5), channel_id=1, source_target_pairs={{0,4},{2,6},{4,0},{6,2},{8,12},{10,14},{12,8},{14,10},{16,20},{18,... | collective-permute-start | bytes 1769480 | tf_op jit(solution)/shard_map/ppermute | solution.py:352
  220.6 37.0 %collective-permute-start.25 = (bf16[4,576,128]{2,1,0:T(8,128)(2,1)S(1)}, bf16[4,576,128]{2,1,0:T(8,128)(2,1)S(1)}, u32[]{:S(2)}, u32[]{:S(2)}) collective-permute-start(bf16[4,576,128]{2,1,0:T(8,128)(2,1)S(1)} %copy-done.4), channel_id=1, source_target_pairs={{0,2},{2,0},{4,6},{6,4},{8,10},{10,8},{12,14},{14,12},{16,18},{18,... | collective-permute-start | bytes 1769480 | tf_op jit(solution)/shard_map/ppermute | solution.py:352
  220.6 37.0 %collective-permute-start.24 = (bf16[4,576,128]{2,1,0:T(8,128)(2,1)S(1)}, bf16[4,576,128]{2,1,0:T(8,128)(2,1)S(1)}, u32[]{:S(2)}, u32[]{:S(2)}) collective-permute-start(bf16[4,576,128]{2,1,0:T(8,128)(2,1)S(1)} %collective-permute-done.17.refs_1_), channel_id=1, source_target_pairs={{0,4},{2,6},{4,0},{6,2},{8,12},{10,14},{12,8},{14,10},{16,20},{18,... | collective-permute-start | bytes 1769480 | tf_op jit(solution)/shard_map/ppermute | solution.py:352
  222.7 35.8 %collective-permute-start.26 = (bf16[4,576,128]{2,1,0:T(8,128)(2,1)}, bf16[4,576,128]{2,1,0:T(8,128)(2,1)}, u32[]{:S(2)}, u32[]{:S(2)}) collective-permute-start(bf16[4,576,128]{2,1,0:T(8,128)(2,1)} %collective-permute-done.18.refs_10_), channel_id=1, source_target_pairs={{0,2},{2,0},{4,6},{6,4},{8,10},{10,8},{12,14},{14,12},{16,18},{18,... | collective-permute-start | bytes 1769480 | tf_op jit(solution)/shard_map/ppermute | solution.py:352
  258.5 51.1 %all-to-all-start.1 = ((bf16[16,96,1024]{2,1,0:T(8,128)(2,1)}), bf16[16,96,1024]{2,1,0:T(8,128)(2,1)}, u32[]{:S(2)}, u32[]{:S(2)}) async-start(bf16[16,96,1024]{2,1,0:T(8,128)(2,1)} %hphi.1), calls=%async_computation.1 | async-start | bytes 6291456 | tf_op jit(solution)/shard_map/all_to_all | solution.py:378
  263.3 2.1 collective-permute-start.27
  263.3 3.7 collective-permute-start.31
  263.8 4.9 %collective-permute-start.28 = (bf16[4,576,128]{2,1,0:T(8,128)(2,1)S(1)}, bf16[4,576,128]{2,1,0:T(8,128)(2,1)S(1)}, u32[]{:S(2)}, u32[]{:S(2)}) collective-permute-start(bf16[4,576,128]{2,1,0:T(8,128)(2,1)S(1)} %collective-permute-done.17.refs_1_), channel_id=1, source_target_pairs={{0,1},{1,0},{2,3},{3,2},{4,5},{5,4},{6,7},{7,6},{8,9},{9,8},{10,11... | collective-permute-start | bytes 1769480 | tf_op jit(solution)/shard_map/ppermute | solution.py:364
  263.9 4.9 %collective-permute-start.33 = (bf16[4,576,128]{2,1,0:T(8,128)(2,1)}, bf16[4,576,128]{2,1,0:T(8,128)(2,1)S(1)}, u32[]{:S(2)}, u32[]{:S(2)}) collective-permute-start(bf16[4,576,128]{2,1,0:T(8,128)(2,1)} %collective-permute-done.18.refs_10_), channel_id=1, source_target_pairs={{0,1},{1,0},{2,3},{3,2},{4,5},{5,4},{6,7},{7,6},{8,9},{9,8},{10,11... | collective-permute-start | bytes 1769480 | tf_op jit(solution)/shard_map/ppermute | solution.py:364
  264.4 5.0 %collective-permute-start.29 = (bf16[4,576,128]{2,1,0:T(8,128)(2,1)}, bf16[4,576,128]{2,1,0:T(8,128)(2,1)S(1)}, u32[]{:S(2)}, u32[]{:S(2)}) collective-permute-start(bf16[4,576,128]{2,1,0:T(8,128)(2,1)} %collective-permute-done.23.refs_2_), channel_id=1, source_target_pairs={{0,1},{1,0},{2,3},{3,2},{4,5},{5,4},{6,7},{7,6},{8,9},{9,8},{10,11... | collective-permute-start | bytes 1769480 | tf_op jit(solution)/shard_map/ppermute | solution.py:364
  265.3 4.2 %collective-permute-start.30 = (bf16[4,576,128]{2,1,0:T(8,128)(2,1)S(1)}, bf16[4,576,128]{2,1,0:T(8,128)(2,1)S(1)}, u32[]{:S(2)}, u32[]{:S(2)}) collective-permute-start(bf16[4,576,128]{2,1,0:T(8,128)(2,1)S(1)} %collective-permute-done.24.refs_3_), channel_id=1, source_target_pairs={{0,1},{1,0},{2,3},{3,2},{4,5},{5,4},{6,7},{7,6},{8,9},{9,8},{10,11... | collective-permute-start | bytes 1769480 | tf_op jit(solution)/shard_map/ppermute | solution.py:364
  267.0 3.4 collective-permute-start.32
  268.7 2.7 collective-permute-start.34
  (21 other events, 96.3 us)

commit v7 on v3

--- a/solution.py
+++ b/solution.py
@@ -388,6 +388,7 @@
     halo = lax.ppermute(edge, "rep", [(0, 1), (1, 0)])
     info = jnp.concatenate([centres[:, :1] + planes * rep, centres[:, 1:]], axis=1)
     info = info.astype(jnp.int32)
+    band = planar_band()
 
     resident = n_func == SIDES[0] * SIDES[1] * SIDES[2]
     if resident:
@@ -395,15 +396,20 @@
         here = jnp.stack([rep, y, x]).astype(jnp.int32)
         per = x_blocks // PIECES
         lines = [along_z(half[p * per : (p + 1) * per]) for p in range(PIECES)]
-        lines, kernel, hamiltonian = lax.optimization_barrier((lines, kernel, hamiltonian))
+        lines, kernel, hamiltonian, halo, band, info, phi_cut = lax.optimization_barrier(
+            (lines, kernel, hamiltonian, halo, band, info, phi_cut)
+        )
         near = [swapped(lines[p], 1 + p) for p in range(PIECES)]
         matrix_lines = [along_z(stored[0]) for stored in (kernel, hamiltonian)]
         far = [(swapped(lines[p], 2 - p), swapped(near[p], 2 - p)) for p in range(PIECES)]
         pot = ordered(lines, near, far)
-        pot, matrix_lines, phi_cut = lax.optimization_barrier((pot, matrix_lines, phi_cut))
+        matrix_near = [swapped(matrix_lines[p], 1 + p) for p in range(2)]
+        pot, matrix_lines, matrix_near, phi_cut = lax.optimization_barrier((pot, matrix_lines, matrix_near, phi_cut))
+        phi_pts = exchange(phi_cut)
+        matrix_far = [
+            (swapped(matrix_lines[p], 2 - p), swapped(matrix_near[p], 2 - p)) for p in range(2)
+        ]
         pot = pot + [other_core(block) for block in pot]
-        phi_pts = exchange(phi_cut)
-        matrix_near = [swapped(matrix_lines[p], 1 + p) for p in range(2)]
     else:
         here = jnp.stack([rep, rep, rep]).astype(jnp.int32)
         pot = lax.all_gather(half, ("rep", "func"), axis=0, tiled=False)
@@ -423,12 +429,9 @@
         jnp.pad(halo, ((0, 0), (0, extra), (0, 0))),
     ]
     info, phi_planes, halo = padded
-    hphi = make_hphi(info, here, phi_planes, halo, planar_band(), pot, resident)[:, :owned]
+    hphi = make_hphi(info, here, phi_planes, halo, band, pot, resident)[:, :owned]
     if resident:
-        hphi, matrix_near = lax.optimization_barrier((hphi, matrix_near))
-        matrix_far = [
-            (swapped(matrix_lines[p], 2 - p), swapped(matrix_near[p], 2 - p)) for p in range(2)
-        ]
+        hphi, matrix_far = lax.optimization_barrier((hphi, matrix_far))
         k_parts, h_parts = (
             ordered(matrix_lines[p : p + 1], matrix_near[p : p + 1], matrix_far[p : p + 1], p)
             for p in range(2)

time: 402 us -> 377 us (0.938)
  starting transfers between devices: 68.7 us -> 47.7 us
  waiting for transfers between devices: 155 us -> 149 us
    ppermute x12, waiting for transfers between devices: 88.6 us -> 66 us  [swapped(): return lax.ppermute(block, 'func', [(i, i ^ bit) for i in range(n)])]
    all_to_all x2, waiting for transfers between devices: 11.8 us -> 21.5 us  [exchange(): return lax.all_to_all(rows, 'func', split_axis=0, concat_axis=0, tiled=True)]
    ppermute x16, waiting for transfers between devices: 3.44 us -> 12.7 us  [other_core(): return lax.ppermute(block, 'rep', [(0, 1), (1, 0)])]
    ppermute x12, starting transfers between devices: 30.3 us -> 21.1 us  [along_z(): lax.ppermute(part, 'func', [(i, (i + 4 * k) % n) for i in range(n)])]
    all_to_all x2, starting transfers between devices: 19.6 us -> 10.6 us  [exchange(): return lax.all_to_all(rows, 'func', split_axis=0, concat_axis=0, tiled=True)]
    unnamed x57 -> x71, local copies, waits for them, and re-layouts: 10.2 us -> 12.8 us
  transfers between devices with their start and end apart: 43 -> 43, of which waited for: 20 -> 21; matrix products, arithmetic and copies ran while one was open for 2% -> 3% of each run, Pallas kernels for 16% -> 17%
where the time goes in v7:
time: 377 us
  waiting for transfers between devices  149 us (40%)
  blocking collectives  84.7 us (22%)
  Pallas kernels  73.1 us (19%)
  starting transfers between devices  47.7 us (13%)
  local copies, waits for them, and re-layouts  17.1 us (5%)
  other arithmetic  4.26 us (1%)
    all_to_all x1, blocking collectives, exchange(): return lax.all_to_all(rows, 'func', split_axis=0, concat_axis=0, tiled=True)  84.7 us
    ppermute x12, waiting for transfers between devices, swapped(): return lax.ppermute(block, 'func', [(i, i ^ bit) for i in range(n)])  66 us
    ppermute x12, waiting for transfers between devices, along_z(): lax.ppermute(part, 'func', [(i, (i + 4 * k) % n) for i in range(n)])  49.1 us
    pallas_call x1, Pallas kernels, make_hphi(): pl.pallas_call(functools.partial(hphi_kernel, resident=resident), out_sha...  32.9 us
    pallas_call x1, Pallas kernels, first_products(): pl.pallas_call(first_kernel, out_shape=[jax.ShapeDtypeStruct((NF, NF), jn...  29.8 us
    all_to_all x2, waiting for transfers between devices, exchange(): return lax.all_to_all(rows, 'func', split_axis=0, concat_axis=0, tiled=True)  21.5 us
    ppermute x12, starting transfers between devices, along_z(): lax.ppermute(part, 'func', [(i, (i + 4 * k) % n) for i in range(n)])  21.1 us
    unnamed x71, local copies, waits for them, and re-layouts  12.8 us
  transfers between devices with their start and end apart: 43, of which 21 were waited for; matrix products, arithmetic and copies ran while one was open for 3% of the time, Pallas kernels for 17%

profile of v7, /device:TPU:0, one launch (start us, length us, event | category | flops | bytes accessed | tf_op | source)
XLA Modules:
  0.0 376.6 jit_solution(15376989468135580285)
XLA Ops:
  0.0 1.6 copy-done
  1.8 5.1 %collective-permute-start.3 = (bf16[2,32,16,128]{3,2,1,0:T(8,128)(2,1)S(1)}, bf16[2,32,16,128]{3,2,1,0:T(8,128)(2,1)S(1)}, u32[]{:S(2)}, u32[]{:S(2)}) collective-permute-start(bf16[2,32,16,128]{3,2,1,0:T(8,128)(2,1)S(1)} %get-tuple-element.77), channel_id=1, source_target_pairs={{0,24},{2,26},{4,28},{6,30},{8,0},{10,2},{12,4},{14,6},{16,8},{18,... | collective-permute-start | bytes 786440 | tf_op jit(solution)/shard_map/ppermute | solution.py:338
  6.9 1.0 collective-permute-start.5
  7.9 2.8 collective-permute-start
  10.7 1.1 collective-permute-start.1
  11.9 1.6 select_convert_fusion.band
  13.5 5.3 %copy.25 = bf16[96,16,1024]{2,0,1:T(8,128)(2,1)} copy(bf16[96,16,1024]{2,1,0:T(8,128)(2,1)} %param.7) | data formatting | bytes 6291456 | tf_op args[0]
  18.8 1.2 slice_select_fusion
  19.9 4.3 %collective-permute-start.2 = (bf16[2,32,16,128]{3,2,1,0:T(8,128)(2,1)S(1)}, bf16[2,32,16,128]{3,2,1,0:T(8,128)(2,1)S(1)}, u32[]{:S(2)}, u32[]{:S(2)}) collective-permute-start(bf16[2,32,16,128]{3,2,1,0:T(8,128)(2,1)S(1)} %get-tuple-element.78), channel_id=1, source_target_pairs={{0,8},{2,10},{4,12},{6,14},{8,16},{10,18},{12,20},{14,22},{16,24},... | collective-permute-start | bytes 786440 | tf_op jit(solution)/shard_map/ppermute | solution.py:338
  24.2 7.3 %collective-permute-done.4 = bf16[2,32,16,128]{3,2,1,0:T(8,128)(2,1)S(1)} collective-permute-done((bf16[2,32,16,128]{3,2,1,0:T(8,128)(2,1)S(1)}, bf16[2,32,16,128]{3,2,1,0:T(8,128)(2,1)S(1)}, u32[]{:S(2)}, u32[]{:S(2)}) %collective-permute-start.4) | collective-permute-done | bytes 262176 | tf_op jit(solution)/shard_map/ppermute | solution.py:338
  31.7 20.0 %collective-permute-done.1 = bf16[2,32,16,128]{3,2,1,0:T(8,128)(2,1)S(1)} collective-permute-done((bf16[2,32,16,128]{3,2,1,0:T(8,128)(2,1)S(1)}, bf16[2,32,16,128]{3,2,1,0:T(8,128)(2,1)S(1)}, u32[]{:S(2)}, u32[]{:S(2)}) %collective-permute-start.1) | collective-permute-done | bytes 262176 | tf_op jit(solution)/shard_map/ppermute | solution.py:338
  52.1 1.6 collective-permute-start.11
  53.7 1.5 collective-permute-start.7
  55.2 2.8 collective-permute-start.17
  58.0 2.0 collective-permute-start.18
  60.0 1.8 collective-permute-done.16
  61.8 2.0 collective-permute-start.13
  63.8 13.2 %collective-permute-done.17 = bf16[576,128]{1,0:T(8,128)(2,1)S(1)} collective-permute-done((bf16[576,128]{1,0:T(8,128)(2,1)S(1)}, bf16[576,128]{1,0:T(8,128)(2,1)S(1)}, u32[]{:S(2)}, u32[]{:S(2)}) %collective-permute-start.17) | collective-permute-done | bytes 147488 | tf_op jit(solution)/shard_map/ppermute | solution.py:338
  77.8 6.8 %collective-permute-done.14 = bf16[576,128]{1,0:T(8,128)(2,1)S(1)} collective-permute-done((bf16[576,128]{1,0:T(8,128)(2,1)S(1)}, bf16[576,128]{1,0:T(8,128)(2,1)S(1)}, u32[]{:S(2)}, u32[]{:S(2)}) %collective-permute-start.14) | collective-permute-done | bytes 147488 | tf_op jit(solution)/shard_map/ppermute | solution.py:338
  85.7 1.5 collective-permute-start.12
  87.2 1.5 collective-permute-start.9
  88.9 4.7 %collective-permute-done.20.refs_10_ = bf16[4,576,128]{2,1,0:T(8,128)(2,1)S(1)} collective-permute-done((bf16[4,576,128]{2,1,0:T(8,128)(2,1)S(1)}, bf16[4,576,128]{2,1,0:T(8,128)(2,1)S(1)}, u32[]{:S(2)}, u32[]{:S(2)}) %collective-permute-start.20) | collective-permute-done | bytes 589856 | tf_op jit(solution)/shard_map/ppermute | solution.py:351
  94.1 45.1 %collective-permute-done.19.refs_1_ = bf16[4,576,128]{2,1,0:T(8,128)(2,1)S(1)} collective-permute-done((bf16[4,576,128]{2,1,0:T(8,128)(2,1)S(1)}, bf16[4,576,128]{2,1,0:T(8,128)(2,1)S(1)}, u32[]{:S(2)}, u32[]{:S(2)}) %collective-permute-start.19) | collective-permute-done | bytes 589856 | tf_op jit(solution)/shard_map/ppermute | solution.py:351
  139.2 0.7 copy-done.20
  140.6 1.0 copy-done.15
  141.6 4.6 %all-to-all-start = ((bf16[16,96,1024]{2,1,0:T(8,128)(2,1)}), bf16[16,96,1024]{2,1,0:T(8,128)(2,1)}, u32[]{:S(2)}, u32[]{:S(2)}) async-start(bf16[16,96,1024]{2,1,0:T(8,128)(2,1)} %bitcast.58.phi), calls=%async_computation | async-start | bytes 6291456 | tf_op jit(solution)/shard_map/all_to_all | solution.py:377
  147.4 2.3 collective-permute-done.21.refs_8_
  149.7 1.0 copy-done.16
  150.8 1.1 collective-permute-done.22.refs_9_
  152.3 2.6 collective-permute-done.23.refs_10_
  156.0 0.7 copy.21.info
  156.8 1.8 collective-permute-start.29
  158.9 1.7 collective-permute-start.31
  160.9 32.9 %hphi.1 = bf16[16,96,1024]{2,1,0:T(8,128)(2,1)} custom-call(s32[96,3]{1,0:T(8,128)} %copy.21.info, s32[3]{0:T(128)} %pad_add_fusion.1.here, bf16[16,96,1024]{2,1,0:T(8,128)(2,1)} %bitcast.58.phi, bf16[2,96,1024]{2,1,0:T(8,128)(2,1)} %copy-done.34, bf16[512,256]{1,0:T(8,128)(2,1)} %select_convert_fusion.band, bf16[4,2,32,16,128]{4,3,2,1,0:T(8,128)(2,1)} %copy-done.2, ...), custom_call_target="tpu_custom_call" | custom-call | flops 12884901888 | bytes 62914560 | tf_op jit(solution)/shard_map/hphi/pallas_call | solution.py:204
  193.9 10.2 %collective-permute-done.30.refs_3_ = bf16[4,576,128]{2,1,0:T(8,128)(2,1)S(1)} collective-permute-done((bf16[4,576,128]{2,1,0:T(8,128)(2,1)}, bf16[4,576,128]{2,1,0:T(8,128)(2,1)S(1)}, u32[]{:S(2)}, u32[]{:S(2)}) %collective-permute-start.30) | collective-permute-done | bytes 589856 | tf_op jit(solution)/shard_map/ppermute | solution.py:351
  204.1 0.9 copy-done.24
  204.9 0.8 copy-done.25
  205.8 6.0 %collective-permute-done.32.refs_11_ = bf16[4,576,128]{2,1,0:T(8,128)(2,1)} collective-permute-done((bf16[4,576,128]{2,1,0:T(8,128)(2,1)}, bf16[4,576,128]{2,1,0:T(8,128)(2,1)}, u32[]{:S(2)}, u32[]{:S(2)}) %collective-permute-start.32) | collective-permute-done | bytes 589856 | tf_op jit(solution)/shard_map/ppermute | solution.py:351
  211.8 6.0 %all-to-all-start.1 = ((bf16[16,96,1024]{2,1,0:T(8,128)(2,1)}), bf16[16,96,1024]{2,1,0:T(8,128)(2,1)}, u32[]{:S(2)}, u32[]{:S(2)}) async-start(bf16[16,96,1024]{2,1,0:T(8,128)(2,1)} %hphi.1), calls=%async_computation.1 | async-start | bytes 6291456 | tf_op jit(solution)/shard_map/all_to_all | solution.py:377
  219.0 0.9 collective-permute-done.33.refs_4_
  221.7 1.5 collective-permute-done.39.refs_14_
  223.3 1.7 collective-permute-done.35.refs_6_
  225.2 0.8 collective-permute-done.40.refs_15_
  226.8 29.8 %products.1 = (bf16[1536,1536]{1,0:T(8,128)(2,1)}, f32[1536,1024]{1,0:T(8,128)}) custom-call(s32[3]{0:T(128)} %pad_add_fusion.1.here, s32[12,12]{1,0:T(8,128)} %k_cols.1, s32[12,12]{1,0:T(8,128)} %h_cols.1, bf16[4,576,128]{2,1,0:T(8,128)(2,1)} %copy-done.6, bf16[4,576,128]{2,1,0:T(8,128)(2,1)} %copy-done.20, bf16[4,576,128]{2,1,0:T(8,128)(2,1)} %copy-done.22, ...), custom_call_target="tpu_custom_call" | custom-call | flops 9663676416 | bytes 25165824 | tf_op jit(solution)/shard_map/products/pallas_call | solution.py:290
  256.6 21.5 %all-to-all-done.1 = bf16[16,96,1024]{2,1,0:T(8,128)(2,1)} async-done(((bf16[16,96,1024]{2,1,0:T(8,128)(2,1)}), bf16[16,96,1024]{2,1,0:T(8,128)(2,1)}, u32[]{:S(2)}, u32[]{:S(2)}) %all-to-all-start.1) | async-done | bytes 3145760 | tf_op jit(solution)/shard_map/all_to_all | solution.py:377
  278.1 10.3 %gradient.1 = bf16[1536,1024]{1,0:T(8,128)(2,1)} custom-call(bf16[1536,1536]{1,0:T(8,128)(2,1)} %get-tuple-element.58.dense_k, bf16[1536,1024]{1,0:T(8,128)(2,1)} %bitcast.25.hphi, f32[1536,1024]{1,0:T(8,128)} %get-tuple-element.60.product), custom_call_target="tpu_custom_call" | custom-call | flops 4831838208 | bytes 17825792 | tf_op jit(solution)/shard_map/gradient/pallas_call | solution.py:314
  288.4 84.7 %all_to_all.15 = bf16[16,96,1024]{2,1,0:T(8,128)(2,1)S(1)} all-to-all(bf16[16,96,1024]{2,1,0:T(8,128)(2,1)} %bitcast.64), channel_id=1, replica_groups=mesh['func'=16,'rep'=2] {'func'}, dimensions={0} | all-to-all | bytes 6291456 | tf_op jit(solution)/shard_map/all_to_all | solution.py:377
  373.2 3.4 copy.22
  (137 shorter events, 11.3 us)
Async XLA Ops:
  1.8 18.2 %collective-permute-start.3 = (bf16[2,32,16,128]{3,2,1,0:T(8,128)(2,1)S(1)}, bf16[2,32,16,128]{3,2,1,0:T(8,128)(2,1)S(1)}, u32[]{:S(2)}, u32[]{:S(2)}) collective-permute-start(bf16[2,32,16,128]{3,2,1,0:T(8,128)(2,1)S(1)} %get-tuple-element.77), channel_id=1, source_target_pairs={{0,24},{2,26},{4,28},{6,30},{8,0},{10,2},{12,4},{14,6},{16,8},{18,... | collective-permute-start | bytes 786440 | tf_op jit(solution)/shard_map/ppermute | solution.py:338
  6.9 24.6 %collective-permute-start.4 = (bf16[2,32,16,128]{3,2,1,0:T(8,128)(2,1)S(1)}, bf16[2,32,16,128]{3,2,1,0:T(8,128)(2,1)S(1)}, u32[]{:S(2)}, u32[]{:S(2)}) collective-permute-start(bf16[2,32,16,128]{3,2,1,0:T(8,128)(2,1)S(1)} %get-tuple-element.77), channel_id=1, source_target_pairs={{0,16},{2,18},{4,20},{6,22},{8,24},{10,26},{12,28},{14,30},{16,0},... | collective-permute-start | bytes 786440 | tf_op jit(solution)/shard_map/ppermute | solution.py:338
  6.9 24.6 %collective-permute-start.5 = (bf16[2,32,16,128]{3,2,1,0:T(8,128)(2,1)S(1)}, bf16[2,32,16,128]{3,2,1,0:T(8,128)(2,1)S(1)}, u32[]{:S(2)}, u32[]{:S(2)}) collective-permute-start(bf16[2,32,16,128]{3,2,1,0:T(8,128)(2,1)S(1)} %get-tuple-element.77), channel_id=1, source_target_pairs={{0,8},{2,10},{4,12},{6,14},{8,16},{10,18},{12,20},{14,22},{16,24},... | collective-permute-start | bytes 786440 | tf_op jit(solution)/shard_map/ppermute | solution.py:338
  7.9 23.8 %collective-permute-start = (bf16[2,32,16,128]{3,2,1,0:T(8,128)(2,1)S(1)}, bf16[2,32,16,128]{3,2,1,0:T(8,128)(2,1)S(1)}, u32[]{:S(2)}, u32[]{:S(2)}) collective-permute-start(bf16[2,32,16,128]{3,2,1,0:T(8,128)(2,1)S(1)} %get-tuple-element.78), channel_id=1, source_target_pairs={{0,24},{2,26},{4,28},{6,30},{8,0},{10,2},{12,4},{14,6},{16,8},{18,... | collective-permute-start | bytes 786440 | tf_op jit(solution)/shard_map/ppermute | solution.py:338
  10.7 41.0 %collective-permute-start.1 = (bf16[2,32,16,128]{3,2,1,0:T(8,128)(2,1)S(1)}, bf16[2,32,16,128]{3,2,1,0:T(8,128)(2,1)S(1)}, u32[]{:S(2)}, u32[]{:S(2)}) collective-permute-start(bf16[2,32,16,128]{3,2,1,0:T(8,128)(2,1)S(1)} %get-tuple-element.78), channel_id=1, source_target_pairs={{0,16},{2,18},{4,20},{6,22},{8,24},{10,26},{12,28},{14,30},{16,0},... | collective-permute-start | bytes 786440 | tf_op jit(solution)/shard_map/ppermute | solution.py:338
  19.9 31.7 %collective-permute-start.2 = (bf16[2,32,16,128]{3,2,1,0:T(8,128)(2,1)S(1)}, bf16[2,32,16,128]{3,2,1,0:T(8,128)(2,1)S(1)}, u32[]{:S(2)}, u32[]{:S(2)}) collective-permute-start(bf16[2,32,16,128]{3,2,1,0:T(8,128)(2,1)S(1)} %get-tuple-element.78), channel_id=1, source_target_pairs={{0,8},{2,10},{4,12},{6,14},{8,16},{10,18},{12,20},{14,22},{16,24},... | collective-permute-start | bytes 786440 | tf_op jit(solution)/shard_map/ppermute | solution.py:338
  31.5 20.6 %collective-permute-start.6 = (bf16[2,96,1024]{2,1,0:T(8,128)(2,1)S(1)}, bf16[2,96,1024]{2,1,0:T(8,128)(2,1)S(1)}, u32[]{:S(2)}, u32[]{:S(2)}) collective-permute-start(bf16[2,96,1024]{2,1,0:T(8,128)(2,1)S(1)} %slice_select_fusion), channel_id=1, source_target_pairs={{0,1},{1,0},{2,3},{3,2},{4,5},{5,4},{6,7},{7,6},{8,9},{9,8},{10,11... | collective-permute-start | bytes 1179656 | tf_op jit(solution)/shard_map/ppermute | solution.py:388
  52.1 87.1 %copy-start.3 = (bf16[4,2,32,16,128]{4,3,2,1,0:T(8,128)(2,1)}, bf16[4,2,32,16,128]{4,3,2,1,0:T(8,128)(2,1)S(1)}, u32[]{:S(2)}) copy-start(bf16[4,2,32,16,128]{4,3,2,1,0:T(8,128)(2,1)S(1)} %get-tuple-element.47.refs_4_) | copy-start | bytes 3145732
  52.1 94.2 %copy-start.2 = (bf16[4,2,32,16,128]{4,3,2,1,0:T(8,128)(2,1)}, bf16[4,2,32,16,128]{4,3,2,1,0:T(8,128)(2,1)S(1)}, u32[]{:S(2)}) copy-start(bf16[4,2,32,16,128]{4,3,2,1,0:T(8,128)(2,1)S(1)} %get-tuple-element.43.refs_0_) | copy-start | bytes 3145732
  52.1 89.5 %copy-start.34 = (bf16[2,96,1024]{2,1,0:T(8,128)(2,1)}, bf16[2,96,1024]{2,1,0:T(8,128)(2,1)S(1)}, u32[]{:S(2)}) copy-start(bf16[2,96,1024]{2,1,0:T(8,128)(2,1)S(1)} %collective-permute-done.6.halo) | copy-start | bytes 1179652
  52.1 33.6 %collective-permute-start.11 = (bf16[4,2,32,16,128]{4,3,2,1,0:T(8,128)(2,1)S(1)}, bf16[4,2,32,16,128]{4,3,2,1,0:T(8,128)(2,1)S(1)}, u32[]{:S(2)}, u32[]{:S(2)}) collective-permute-start(bf16[4,2,32,16,128]{4,3,2,1,0:T(8,128)(2,1)S(1)} %get-tuple-element.47.refs_4_), channel_id=1, source_target_pairs={{0,4},{2,6},{4,0},{6,2},{8,12},{10,14},{12,8},{14,10},{16,20},{18,... | collective-permute-start | bytes 3145736 | tf_op jit(solution)/shard_map/ppermute | solution.py:351
  53.7 33.5 %collective-permute-start.7 = (bf16[4,2,32,16,128]{4,3,2,1,0:T(8,128)(2,1)S(1)}, bf16[4,2,32,16,128]{4,3,2,1,0:T(8,128)(2,1)S(1)}, u32[]{:S(2)}, u32[]{:S(2)}) collective-permute-start(bf16[4,2,32,16,128]{4,3,2,1,0:T(8,128)(2,1)S(1)} %get-tuple-element.43.refs_0_), channel_id=1, source_target_pairs={{0,2},{2,0},{4,6},{6,4},{8,10},{10,8},{12,14},{14,12},{16,18},{18,... | collective-permute-start | bytes 3145736 | tf_op jit(solution)/shard_map/ppermute | solution.py:351
  55.2 6.7 %collective-permute-start.16 = (bf16[576,128]{1,0:T(8,128)(2,1)S(1)}, bf16[576,128]{1,0:T(8,128)(2,1)S(1)}, u32[]{:S(2)}, u32[]{:S(2)}) collective-permute-start(bf16[576,128]{1,0:T(8,128)(2,1)S(1)} %bitcast.66), channel_id=1, source_target_pairs={{0,24},{2,26},{4,28},{6,30},{8,0},{10,2},{12,4},{14,6},{16,8},{18,... | collective-permute-start | bytes 442376 | tf_op jit(solution)/shard_map/ppermute | solution.py:338
  55.2 21.8 %collective-permute-start.17 = (bf16[576,128]{1,0:T(8,128)(2,1)S(1)}, bf16[576,128]{1,0:T(8,128)(2,1)S(1)}, u32[]{:S(2)}, u32[]{:S(2)}) collective-permute-start(bf16[576,128]{1,0:T(8,128)(2,1)S(1)} %bitcast.67), channel_id=1, source_target_pairs={{0,16},{2,18},{4,20},{6,22},{8,24},{10,26},{12,28},{14,30},{16,0},... | collective-permute-start | bytes 442376 | tf_op jit(solution)/shard_map/ppermute | solution.py:338
  58.0 19.0 %collective-permute-start.18 = (bf16[576,128]{1,0:T(8,128)(2,1)S(1)}, bf16[576,128]{1,0:T(8,128)(2,1)S(1)}, u32[]{:S(2)}, u32[]{:S(2)}) collective-permute-start(bf16[576,128]{1,0:T(8,128)(2,1)S(1)} %bitcast.68), channel_id=1, source_target_pairs={{0,8},{2,10},{4,12},{6,14},{8,16},{10,18},{12,20},{14,22},{16,24},... | collective-permute-start | bytes 442376 | tf_op jit(solution)/shard_map/ppermute | solution.py:338
  61.8 15.4 %collective-permute-start.13 = (bf16[576,128]{1,0:T(8,128)(2,1)S(1)}, bf16[576,128]{1,0:T(8,128)(2,1)S(1)}, u32[]{:S(2)}, u32[]{:S(2)}) collective-permute-start(bf16[576,128]{1,0:T(8,128)(2,1)S(1)} %bitcast.69), channel_id=1, source_target_pairs={{0,24},{2,26},{4,28},{6,30},{8,0},{10,2},{12,4},{14,6},{16,8},{18,... | collective-permute-start | bytes 442376 | tf_op jit(solution)/shard_map/ppermute | solution.py:338
  77.0 7.6 %collective-permute-start.14 = (bf16[576,128]{1,0:T(8,128)(2,1)S(1)}, bf16[576,128]{1,0:T(8,128)(2,1)S(1)}, u32[]{:S(2)}, u32[]{:S(2)}) collective-permute-start(bf16[576,128]{1,0:T(8,128)(2,1)S(1)} %bitcast.70), channel_id=1, source_target_pairs={{0,16},{2,18},{4,20},{6,22},{8,24},{10,26},{12,28},{14,30},{16,0},... | collective-permute-start | bytes 442376 | tf_op jit(solution)/shard_map/ppermute | solution.py:338
  77.0 8.2 %collective-permute-start.15 = (bf16[576,128]{1,0:T(8,128)(2,1)S(1)}, bf16[576,128]{1,0:T(8,128)(2,1)S(1)}, u32[]{:S(2)}, u32[]{:S(2)}) collective-permute-start(bf16[576,128]{1,0:T(8,128)(2,1)S(1)} %bitcast.71), channel_id=1, source_target_pairs={{0,8},{2,10},{4,12},{6,14},{8,16},{10,18},{12,20},{14,22},{16,24},... | collective-permute-start | bytes 442376 | tf_op jit(solution)/shard_map/ppermute | solution.py:338
  77.2 141.2 %copy-start.5 = (bf16[4,576,128]{2,1,0:T(8,128)(2,1)}, bf16[4,576,128]{2,1,0:T(8,128)(2,1)S(1)}, u32[]{:S(2)}) copy-start(bf16[4,576,128]{2,1,0:T(8,128)(2,1)S(1)} %pad_maximum_fusion.3.refs_8_) | copy-start | bytes 1769476
  77.2 16.3 %collective-permute-start.20 = (bf16[4,576,128]{2,1,0:T(8,128)(2,1)S(1)}, bf16[4,576,128]{2,1,0:T(8,128)(2,1)S(1)}, u32[]{:S(2)}, u32[]{:S(2)}) collective-permute-start(bf16[4,576,128]{2,1,0:T(8,128)(2,1)S(1)} %pad_maximum_fusion.3.refs_8_), channel_id=1, source_target_pairs={{0,4},{2,6},{4,0},{6,2},{8,12},{10,14},{12,8},{14,10},{16,20},{18,... | collective-permute-start | bytes 1769480 | tf_op jit(solution)/shard_map/ppermute | solution.py:351
  84.6 54.5 %collective-permute-start.10 = (bf16[4,2,32,16,128]{4,3,2,1,0:T(8,128)(2,1)S(1)}, bf16[4,2,32,16,128]{4,3,2,1,0:T(8,128)(2,1)S(1)}, u32[]{:S(2)}, u32[]{:S(2)}) collective-permute-start(bf16[4,2,32,16,128]{4,3,2,1,0:T(8,128)(2,1)S(1)} %get-tuple-element.47.refs_4_), channel_id=1, source_target_pairs={{0,2},{2,0},{4,6},{6,4},{8,10},{10,8},{12,14},{14,12},{16,18},{18,... | collective-permute-start | bytes 3145736 | tf_op jit(solution)/shard_map/ppermute | solution.py:351
  85.2 54.0 %collective-permute-start.8 = (bf16[4,2,32,16,128]{4,3,2,1,0:T(8,128)(2,1)S(1)}, bf16[4,2,32,16,128]{4,3,2,1,0:T(8,128)(2,1)S(1)}, u32[]{:S(2)}, u32[]{:S(2)}) collective-permute-start(bf16[4,2,32,16,128]{4,3,2,1,0:T(8,128)(2,1)S(1)} %get-tuple-element.43.refs_0_), channel_id=1, source_target_pairs={{0,4},{2,6},{4,0},{6,2},{8,12},{10,14},{12,8},{14,10},{16,20},{18,... | collective-permute-start | bytes 3145736 | tf_op jit(solution)/shard_map/ppermute | solution.py:351
  85.7 53.5 %copy-start.11 = (bf16[4,2,32,16,128]{4,3,2,1,0:T(8,128)(2,1)}, bf16[4,2,32,16,128]{4,3,2,1,0:T(8,128)(2,1)S(1)}, u32[]{:S(2)}) copy-start(bf16[4,2,32,16,128]{4,3,2,1,0:T(8,128)(2,1)S(1)} %collective-permute-done.11.refs_6_) | copy-start | bytes 3145732
  85.7 53.5 %collective-permute-start.12 = (bf16[4,2,32,16,128]{4,3,2,1,0:T(8,128)(2,1)S(1)}, bf16[4,2,32,16,128]{4,3,2,1,0:T(8,128)(2,1)S(1)}, u32[]{:S(2)}, u32[]{:S(2)}) collective-permute-start(bf16[4,2,32,16,128]{4,3,2,1,0:T(8,128)(2,1)S(1)} %collective-permute-done.11.refs_6_), channel_id=1, source_target_pairs={{0,2},{2,0},{4,6},{6,4},{8,10},{10,8},{12,14},{14,12},{16,18},{18,... | collective-permute-start | bytes 3145736 | tf_op jit(solution)/shard_map/ppermute | solution.py:351
  87.2 54.5 %collective-permute-start.9 = (bf16[4,2,32,16,128]{4,3,2,1,0:T(8,128)(2,1)S(1)}, bf16[4,2,32,16,128]{4,3,2,1,0:T(8,128)(2,1)}, u32[]{:S(2)}, u32[]{:S(2)}) collective-permute-start(bf16[4,2,32,16,128]{4,3,2,1,0:T(8,128)(2,1)S(1)} %collective-permute-done.7.refs_1_), channel_id=1, source_target_pairs={{0,4},{2,6},{4,0},{6,2},{8,12},{10,14},{12,8},{14,10},{16,20},{18,... | collective-permute-start | bytes 3145736 | tf_op jit(solution)/shard_map/ppermute | solution.py:351
  93.5 45.6 %collective-permute-start.19 = (bf16[4,576,128]{2,1,0:T(8,128)(2,1)S(1)}, bf16[4,576,128]{2,1,0:T(8,128)(2,1)S(1)}, u32[]{:S(2)}, u32[]{:S(2)}) collective-permute-start(bf16[4,576,128]{2,1,0:T(8,128)(2,1)S(1)} %pad_maximum_fusion.2.refs_0_), channel_id=1, source_target_pairs={{0,2},{2,0},{4,6},{6,4},{8,10},{10,8},{12,14},{14,12},{16,18},{18,... | collective-permute-start | bytes 1769480 | tf_op jit(solution)/shard_map/ppermute | solution.py:351
  141.6 70.2 %all-to-all-start = ((bf16[16,96,1024]{2,1,0:T(8,128)(2,1)}), bf16[16,96,1024]{2,1,0:T(8,128)(2,1)}, u32[]{:S(2)}, u32[]{:S(2)}) async-start(bf16[16,96,1024]{2,1,0:T(8,128)(2,1)} %bitcast.58.phi), calls=%async_computation | async-start | bytes 6291456 | tf_op jit(solution)/shard_map/all_to_all | solution.py:377
  146.3 3.4 collective-permute-start.21
  146.3 5.6 %collective-permute-start.22 = (bf16[4,2,32,16,128]{4,3,2,1,0:T(8,128)(2,1)}, bf16[4,2,32,16,128]{4,3,2,1,0:T(8,128)(2,1)}, u32[]{:S(2)}, u32[]{:S(2)}) collective-permute-start(bf16[4,2,32,16,128]{4,3,2,1,0:T(8,128)(2,1)} %copy-done.12), channel_id=1, source_target_pairs={{0,1},{1,0},{2,3},{3,2},{4,5},{5,4},{6,7},{7,6},{8,9},{9,8},{10,11... | collective-permute-start | bytes 3145736 | tf_op jit(solution)/shard_map/ppermute | solution.py:363
  146.8 8.1 %collective-permute-start.23 = (bf16[4,2,32,16,128]{4,3,2,1,0:T(8,128)(2,1)}, bf16[4,2,32,16,128]{4,3,2,1,0:T(8,128)(2,1)}, u32[]{:S(2)}, u32[]{:S(2)}) collective-permute-start(bf16[4,2,32,16,128]{4,3,2,1,0:T(8,128)(2,1)} %copy-done.14), channel_id=1, source_target_pairs={{0,1},{1,0},{2,3},{3,2},{4,5},{5,4},{6,7},{7,6},{8,9},{9,8},{10,11... | collective-permute-start | bytes 3145736 | tf_op jit(solution)/shard_map/ppermute | solution.py:363
  146.9 9.9 %collective-permute-start.24 = (bf16[4,2,32,16,128]{4,3,2,1,0:T(8,128)(2,1)}, bf16[4,2,32,16,128]{4,3,2,1,0:T(8,128)(2,1)}, u32[]{:S(2)}, u32[]{:S(2)}) collective-permute-start(bf16[4,2,32,16,128]{4,3,2,1,0:T(8,128)(2,1)} %collective-permute-done.9.refs_3_), channel_id=1, source_target_pairs={{0,1},{1,0},{2,3},{3,2},{4,5},{5,4},{6,7},{7,6},{8,9},{9,8},{10,11... | collective-permute-start | bytes 3145736 | tf_op jit(solution)/shard_map/ppermute | solution.py:363
  147.4 11.2 %collective-permute-start.25 = (bf16[4,2,32,16,128]{4,3,2,1,0:T(8,128)(2,1)S(1)}, bf16[4,2,32,16,128]{4,3,2,1,0:T(8,128)(2,1)}, u32[]{:S(2)}, u32[]{:S(2)}) collective-permute-start(bf16[4,2,32,16,128]{4,3,2,1,0:T(8,128)(2,1)S(1)} %copy-done.4), channel_id=1, source_target_pairs={{0,1},{1,0},{2,3},{3,2},{4,5},{5,4},{6,7},{7,6},{8,9},{9,8},{10,11... | collective-permute-start | bytes 3145736 | tf_op jit(solution)/shard_map/ppermute | solution.py:363
  150.7 8.2 %collective-permute-start.26 = (bf16[4,2,32,16,128]{4,3,2,1,0:T(8,128)(2,1)}, bf16[4,2,32,16,128]{4,3,2,1,0:T(8,128)(2,1)S(1)}, u32[]{:S(2)}, u32[]{:S(2)}) collective-permute-start(bf16[4,2,32,16,128]{4,3,2,1,0:T(8,128)(2,1)} %copy-done.13), channel_id=1, source_target_pairs={{0,1},{1,0},{2,3},{3,2},{4,5},{5,4},{6,7},{7,6},{8,9},{9,8},{10,11... | collective-permute-start | bytes 3145736 | tf_op jit(solution)/shard_map/ppermute | solution.py:363
  152.0 8.7 %collective-permute-start.27 = (bf16[4,2,32,16,128]{4,3,2,1,0:T(8,128)(2,1)}, bf16[4,2,32,16,128]{4,3,2,1,0:T(8,128)(2,1)}, u32[]{:S(2)}, u32[]{:S(2)}) collective-permute-start(bf16[4,2,32,16,128]{4,3,2,1,0:T(8,128)(2,1)} %copy-done.11), channel_id=1, source_target_pairs={{0,1},{1,0},{2,3},{3,2},{4,5},{5,4},{6,7},{7,6},{8,9},{9,8},{10,11... | collective-permute-start | bytes 3145736 | tf_op jit(solution)/shard_map/ppermute | solution.py:363
  155.0 5.9 %collective-permute-start.28 = (bf16[4,2,32,16,128]{4,3,2,1,0:T(8,128)(2,1)}, bf16[4,2,32,16,128]{4,3,2,1,0:T(8,128)(2,1)}, u32[]{:S(2)}, u32[]{:S(2)}) collective-permute-start(bf16[4,2,32,16,128]{4,3,2,1,0:T(8,128)(2,1)} %copy-done.15), channel_id=1, source_target_pairs={{0,1},{1,0},{2,3},{3,2},{4,5},{5,4},{6,7},{7,6},{8,9},{9,8},{10,11... | collective-permute-start | bytes 3145736 | tf_op jit(solution)/shard_map/ppermute | solution.py:363
  156.8 37.1 %collective-permute-start.29 = (bf16[4,576,128]{2,1,0:T(8,128)(2,1)}, bf16[4,576,128]{2,1,0:T(8,128)(2,1)S(1)}, u32[]{:S(2)}, u32[]{:S(2)}) collective-permute-start(bf16[4,576,128]{2,1,0:T(8,128)(2,1)} %copy-done.6), channel_id=1, source_target_pairs={{0,4},{2,6},{4,0},{6,2},{8,12},{10,14},{12,8},{14,10},{16,20},{18,... | collective-permute-start | bytes 1769480 | tf_op jit(solution)/shard_map/ppermute | solution.py:351
  158.6 45.5 %collective-permute-start.30 = (bf16[4,576,128]{2,1,0:T(8,128)(2,1)}, bf16[4,576,128]{2,1,0:T(8,128)(2,1)S(1)}, u32[]{:S(2)}, u32[]{:S(2)}) collective-permute-start(bf16[4,576,128]{2,1,0:T(8,128)(2,1)} %copy-done.20), channel_id=1, source_target_pairs={{0,4},{2,6},{4,0},{6,2},{8,12},{10,14},{12,8},{14,10},{16,20},{18,... | collective-permute-start | bytes 1769480 | tf_op jit(solution)/shard_map/ppermute | solution.py:351
  158.9 45.2 %collective-permute-start.31 = (bf16[4,576,128]{2,1,0:T(8,128)(2,1)S(1)}, bf16[4,576,128]{2,1,0:T(8,128)(2,1)S(1)}, u32[]{:S(2)}, u32[]{:S(2)}) collective-permute-start(bf16[4,576,128]{2,1,0:T(8,128)(2,1)S(1)} %pad_maximum_fusion.3.refs_8_), channel_id=1, source_target_pairs={{0,2},{2,0},{4,6},{6,4},{8,10},{10,8},{12,14},{14,12},{16,18},{18,... | collective-permute-start | bytes 1769480 | tf_op jit(solution)/shard_map/ppermute | solution.py:351
  160.6 51.2 %collective-permute-start.32 = (bf16[4,576,128]{2,1,0:T(8,128)(2,1)}, bf16[4,576,128]{2,1,0:T(8,128)(2,1)}, u32[]{:S(2)}, u32[]{:S(2)}) collective-permute-start(bf16[4,576,128]{2,1,0:T(8,128)(2,1)} %copy-done.18), channel_id=1, source_target_pairs={{0,2},{2,0},{4,6},{6,4},{8,10},{10,8},{12,14},{14,12},{16,18},{18,... | collective-permute-start | bytes 1769480 | tf_op jit(solution)/shard_map/ppermute | solution.py:351
  211.8 66.3 %all-to-all-start.1 = ((bf16[16,96,1024]{2,1,0:T(8,128)(2,1)}), bf16[16,96,1024]{2,1,0:T(8,128)(2,1)}, u32[]{:S(2)}, u32[]{:S(2)}) async-start(bf16[16,96,1024]{2,1,0:T(8,128)(2,1)} %hphi.1), calls=%async_computation.1 | async-start | bytes 6291456 | tf_op jit(solution)/shard_map/all_to_all | solution.py:377
  217.8 2.1 collective-permute-start.33
  217.9 2.8 collective-permute-start.34
  218.4 3.2 collective-permute-start.37
  218.5 4.8 %collective-permute-start.39 = (bf16[4,576,128]{2,1,0:T(8,128)(2,1)S(1)}, bf16[4,576,128]{2,1,0:T(8,128)(2,1)S(1)}, u32[]{:S(2)}, u32[]{:S(2)}) collective-permute-start(bf16[4,576,128]{2,1,0:T(8,128)(2,1)S(1)} %copy-done.19), channel_id=1, source_target_pairs={{0,1},{1,0},{2,3},{3,2},{4,5},{5,4},{6,7},{7,6},{8,9},{9,8},{10,11... | collective-permute-start | bytes 1769480 | tf_op jit(solution)/shard_map/ppermute | solution.py:363
  218.9 6.0 %collective-permute-start.35 = (bf16[4,576,128]{2,1,0:T(8,128)(2,1)S(1)}, bf16[4,576,128]{2,1,0:T(8,128)(2,1)S(1)}, u32[]{:S(2)}, u32[]{:S(2)}) collective-permute-start(bf16[4,576,128]{2,1,0:T(8,128)(2,1)S(1)} %copy-done.23), channel_id=1, source_target_pairs={{0,1},{1,0},{2,3},{3,2},{4,5},{5,4},{6,7},{7,6},{8,9},{9,8},{10,11... | collective-permute-start | bytes 1769480 | tf_op jit(solution)/shard_map/ppermute | solution.py:363
  219.9 5.1 %collective-permute-start.36 = (bf16[4,576,128]{2,1,0:T(8,128)(2,1)}, bf16[4,576,128]{2,1,0:T(8,128)(2,1)S(1)}, u32[]{:S(2)}, u32[]{:S(2)}) collective-permute-start(bf16[4,576,128]{2,1,0:T(8,128)(2,1)} %copy-done.24), channel_id=1, source_target_pairs={{0,1},{1,0},{2,3},{3,2},{4,5},{5,4},{6,7},{7,6},{8,9},{9,8},{10,11... | collective-permute-start | bytes 1769480 | tf_op jit(solution)/shard_map/ppermute | solution.py:363
  220.7 4.4 %collective-permute-start.38 = (bf16[4,576,128]{2,1,0:T(8,128)(2,1)}, bf16[4,576,128]{2,1,0:T(8,128)(2,1)S(1)}, u32[]{:S(2)}, u32[]{:S(2)}) collective-permute-start(bf16[4,576,128]{2,1,0:T(8,128)(2,1)} %copy-done.25), channel_id=1, source_target_pairs={{0,1},{1,0},{2,3},{3,2},{4,5},{5,4},{6,7},{7,6},{8,9},{9,8},{10,11... | collective-permute-start | bytes 1769480 | tf_op jit(solution)/shard_map/ppermute | solution.py:363
  221.6 4.4 %collective-permute-start.40 = (bf16[4,576,128]{2,1,0:T(8,128)(2,1)}, bf16[4,576,128]{2,1,0:T(8,128)(2,1)S(1)}, u32[]{:S(2)}, u32[]{:S(2)}) collective-permute-start(bf16[4,576,128]{2,1,0:T(8,128)(2,1)} %collective-permute-done.32.refs_11_), channel_id=1, source_target_pairs={{0,1},{1,0},{2,3},{3,2},{4,5},{5,4},{6,7},{7,6},{8,9},{9,8},{10,11... | collective-permute-start | bytes 1769480 | tf_op jit(solution)/shard_map/ppermute | solution.py:363
  (30 other events, 346.0 us)

commit v8 on v3

--- a/solution.py
+++ b/solution.py
@@ -388,6 +388,7 @@
     halo = lax.ppermute(edge, "rep", [(0, 1), (1, 0)])
     info = jnp.concatenate([centres[:, :1] + planes * rep, centres[:, 1:]], axis=1)
     info = info.astype(jnp.int32)
+    band = planar_band()
 
     resident = n_func == SIDES[0] * SIDES[1] * SIDES[2]
     if resident:
@@ -395,7 +396,9 @@
         here = jnp.stack([rep, y, x]).astype(jnp.int32)
         per = x_blocks // PIECES
         lines = [along_z(half[p * per : (p + 1) * per]) for p in range(PIECES)]
-        lines, kernel, hamiltonian = lax.optimization_barrier((lines, kernel, hamiltonian))
+        lines, kernel, hamiltonian, halo, band, info, phi_cut = lax.optimization_barrier(
+            (lines, kernel, hamiltonian, halo, band, info, phi_cut)
+        )
         near = [swapped(lines[p], 1 + p) for p in range(PIECES)]
         matrix_lines = [along_z(stored[0]) for stored in (kernel, hamiltonian)]
         far = [(swapped(lines[p], 2 - p), swapped(near[p], 2 - p)) for p in range(PIECES)]
@@ -423,12 +426,15 @@
         jnp.pad(halo, ((0, 0), (0, extra), (0, 0))),
     ]
     info, phi_planes, halo = padded
-    hphi = make_hphi(info, here, phi_planes, halo, planar_band(), pot, resident)[:, :owned]
+    hphi = make_hphi(info, here, phi_planes, halo, band, pot, resident)[:, :owned]
     if resident:
         hphi, matrix_near = lax.optimization_barrier((hphi, matrix_near))
         matrix_far = [
             (swapped(matrix_lines[p], 2 - p), swapped(matrix_near[p], 2 - p)) for p in range(2)
         ]
+        sides = [pair[0] for pair in matrix_far]
+        hphi, sides = lax.optimization_barrier((hphi, sides))
+        matrix_far = [(side, pair[1]) for side, pair in zip(sides, matrix_far)]
         k_parts, h_parts = (
             ordered(matrix_lines[p : p + 1], matrix_near[p : p + 1], matrix_far[p : p + 1], p)
             for p in range(2)

time: 402 us -> 369 us (0.918)
  waiting for transfers between devices: 155 us -> 139 us
  starting transfers between devices: 68.7 us -> 57.4 us
  blocking collectives: 83.7 us -> 79.2 us
    all_to_all x2, waiting for transfers between devices: 11.8 us -> 0.01 us  [exchange(): return lax.all_to_all(rows, 'func', split_axis=0, concat_axis=0, tiled=True)]
    ppermute x12, waiting for transfers between devices: 88.6 us -> 80.5 us  [swapped(): return lax.ppermute(block, 'func', [(i, i ^ bit) for i in range(n)])]
    ppermute x12, starting transfers between devices: 30.3 us -> 24 us  [along_z(): lax.ppermute(part, 'func', [(i, (i + 4 * k) % n) for i in range(n)])]
    ppermute x16, waiting for transfers between devices: 3.44 us -> 8.54 us  [other_core(): return lax.ppermute(block, 'rep', [(0, 1), (1, 0)])]
    all_to_all x1, blocking collectives: 83.7 us -> 79.2 us  [exchange(): return lax.all_to_all(rows, 'func', split_axis=0, concat_axis=0, tiled=True)]
    all_to_all x2, starting transfers between devices: 19.6 us -> 15.1 us  [exchange(): return lax.all_to_all(rows, 'func', split_axis=0, concat_axis=0, tiled=True)]
    unnamed x57 -> x65, local copies, waits for them, and re-layouts: 10.2 us -> 9.97 us
  transfers between devices with their start and end apart: 43 -> 43, of which waited for: 20 -> 18; matrix products, arithmetic and copies ran while one was open for 2% -> 3% of each run, Pallas kernels for 16% -> 17%
where the time goes in v8:
time: 369 us
  waiting for transfers between devices  139 us (38%)
  blocking collectives  79.2 us (21%)
  Pallas kernels  73.1 us (20%)
  starting transfers between devices  57.4 us (16%)
  local copies, waits for them, and re-layouts  14.2 us (4%)
  other arithmetic  5.04 us (1%)
    ppermute x12, waiting for transfers between devices, swapped(): return lax.ppermute(block, 'func', [(i, i ^ bit) for i in range(n)])  80.5 us
    all_to_all x1, blocking collectives, exchange(): return lax.all_to_all(rows, 'func', split_axis=0, concat_axis=0, tiled=True)  79.2 us
    ppermute x12, waiting for transfers between devices, along_z(): lax.ppermute(part, 'func', [(i, (i + 4 * k) % n) for i in range(n)])  50.2 us
    pallas_call x1, Pallas kernels, make_hphi(): pl.pallas_call(functools.partial(hphi_kernel, resident=resident), out_sha...  32.9 us
    pallas_call x1, Pallas kernels, first_products(): pl.pallas_call(first_kernel, out_shape=[jax.ShapeDtypeStruct((NF, NF), jn...  29.9 us
    ppermute x12, starting transfers between devices, along_z(): lax.ppermute(part, 'func', [(i, (i + 4 * k) % n) for i in range(n)])  24 us
    all_to_all x2, starting transfers between devices, exchange(): return lax.all_to_all(rows, 'func', split_axis=0, concat_axis=0, tiled=True)  15.1 us
    ppermute x12, starting transfers between devices, swapped(): return lax.ppermute(block, 'func', [(i, i ^ bit) for i in range(n)])  14.5 us
  transfers between devices with their start and end apart: 43, of which 18 were waited for; matrix products, arithmetic and copies ran while one was open for 3% of the time, Pallas kernels for 17%

profile of v8, /device:TPU:0, one launch (start us, length us, event | category | flops | bytes accessed | tf_op | source)
XLA Modules:
  0.0 368.7 jit_solution(12684276403055582046)
XLA Ops:
  0.0 1.6 copy-done
  1.8 5.1 %collective-permute-start.3 = (bf16[2,32,16,128]{3,2,1,0:T(8,128)(2,1)S(1)}, bf16[2,32,16,128]{3,2,1,0:T(8,128)(2,1)S(1)}, u32[]{:S(2)}, u32[]{:S(2)}) collective-permute-start(bf16[2,32,16,128]{3,2,1,0:T(8,128)(2,1)S(1)} %get-tuple-element.75), channel_id=1, source_target_pairs={{0,24},{2,26},{4,28},{6,30},{8,0},{10,2},{12,4},{14,6},{16,8},{18,... | collective-permute-start | bytes 786440 | tf_op jit(solution)/shard_map/ppermute | solution.py:338
  6.9 1.0 collective-permute-start.5
  7.9 2.8 collective-permute-start
  10.7 1.1 collective-permute-start.1
  11.9 1.6 select_convert_fusion.band
  13.5 5.3 %copy.25 = bf16[96,16,1024]{2,0,1:T(8,128)(2,1)} copy(bf16[96,16,1024]{2,1,0:T(8,128)(2,1)} %param.7) | data formatting | bytes 6291456 | tf_op args[0]
  18.8 1.2 slice_select_fusion
  20.0 4.3 %collective-permute-start.2 = (bf16[2,32,16,128]{3,2,1,0:T(8,128)(2,1)S(1)}, bf16[2,32,16,128]{3,2,1,0:T(8,128)(2,1)S(1)}, u32[]{:S(2)}, u32[]{:S(2)}) collective-permute-start(bf16[2,32,16,128]{3,2,1,0:T(8,128)(2,1)S(1)} %get-tuple-element.76), channel_id=1, source_target_pairs={{0,8},{2,10},{4,12},{6,14},{8,16},{10,18},{12,20},{14,22},{16,24},... | collective-permute-start | bytes 786440 | tf_op jit(solution)/shard_map/ppermute | solution.py:338
  24.2 7.3 %collective-permute-done.4 = bf16[2,32,16,128]{3,2,1,0:T(8,128)(2,1)S(1)} collective-permute-done((bf16[2,32,16,128]{3,2,1,0:T(8,128)(2,1)S(1)}, bf16[2,32,16,128]{3,2,1,0:T(8,128)(2,1)S(1)}, u32[]{:S(2)}, u32[]{:S(2)}) %collective-permute-start.4) | collective-permute-done | bytes 262176 | tf_op jit(solution)/shard_map/ppermute | solution.py:338
  31.7 20.0 %collective-permute-done.1 = bf16[2,32,16,128]{3,2,1,0:T(8,128)(2,1)S(1)} collective-permute-done((bf16[2,32,16,128]{3,2,1,0:T(8,128)(2,1)S(1)}, bf16[2,32,16,128]{3,2,1,0:T(8,128)(2,1)S(1)}, u32[]{:S(2)}, u32[]{:S(2)}) %collective-permute-start.1) | collective-permute-done | bytes 262176 | tf_op jit(solution)/shard_map/ppermute | solution.py:338
  52.1 1.6 collective-permute-start.11
  53.7 1.5 collective-permute-start.7
  55.2 2.8 collective-permute-start.17
  58.0 2.0 collective-permute-start.18
  60.0 1.8 collective-permute-done.16
  61.8 2.0 collective-permute-start.13
  63.8 8.0 %collective-permute-done.17 = bf16[576,128]{1,0:T(8,128)(2,1)S(1)} collective-permute-done((bf16[576,128]{1,0:T(8,128)(2,1)S(1)}, bf16[576,128]{1,0:T(8,128)(2,1)S(1)}, u32[]{:S(2)}, u32[]{:S(2)}) %collective-permute-start.17) | collective-permute-done | bytes 147488 | tf_op jit(solution)/shard_map/ppermute | solution.py:338
  72.9 5.4 %collective-permute-done.11.refs_6_ = bf16[4,2,32,16,128]{4,3,2,1,0:T(8,128)(2,1)S(1)} collective-permute-done((bf16[4,2,32,16,128]{4,3,2,1,0:T(8,128)(2,1)S(1)}, bf16[4,2,32,16,128]{4,3,2,1,0:T(8,128)(2,1)S(1)}, u32[]{:S(2)}, u32[]{:S(2)}) %collective-permute-start.11) | collective-permute-done | bytes 1048608 | tf_op jit(solution)/shard_map/ppermute | solution.py:351
  78.3 1.5 collective-permute-start.12
  79.8 1.5 collective-permute-start.9
  81.3 2.8 collective-permute-start.14
  84.1 6.4 %collective-permute-done.14 = bf16[576,128]{1,0:T(8,128)(2,1)S(1)} collective-permute-done((bf16[576,128]{1,0:T(8,128)(2,1)S(1)}, bf16[576,128]{1,0:T(8,128)(2,1)S(1)}, u32[]{:S(2)}, u32[]{:S(2)}) %collective-permute-start.14) | collective-permute-done | bytes 147488 | tf_op jit(solution)/shard_map/ppermute | solution.py:338
  90.7 6.8 %collective-permute-done.15 = bf16[576,128]{1,0:T(8,128)(2,1)S(1)} collective-permute-done((bf16[576,128]{1,0:T(8,128)(2,1)S(1)}, bf16[576,128]{1,0:T(8,128)(2,1)S(1)}, u32[]{:S(2)}, u32[]{:S(2)}) %collective-permute-start.15) | collective-permute-done | bytes 147488 | tf_op jit(solution)/shard_map/ppermute | solution.py:338
  97.5 0.9 pad_maximum_fusion.2.refs_0_
  98.4 3.8 %collective-permute-done.10.refs_5_ = bf16[4,2,32,16,128]{4,3,2,1,0:T(8,128)(2,1)S(1)} collective-permute-done((bf16[4,2,32,16,128]{4,3,2,1,0:T(8,128)(2,1)S(1)}, bf16[4,2,32,16,128]{4,3,2,1,0:T(8,128)(2,1)S(1)}, u32[]{:S(2)}, u32[]{:S(2)}) %collective-permute-start.10) | collective-permute-done | bytes 1048608 | tf_op jit(solution)/shard_map/ppermute | solution.py:351
  102.3 20.1 %collective-permute-done.12.refs_7_ = bf16[4,2,32,16,128]{4,3,2,1,0:T(8,128)(2,1)S(1)} collective-permute-done((bf16[4,2,32,16,128]{4,3,2,1,0:T(8,128)(2,1)S(1)}, bf16[4,2,32,16,128]{4,3,2,1,0:T(8,128)(2,1)S(1)}, u32[]{:S(2)}, u32[]{:S(2)}) %collective-permute-start.12) | collective-permute-done | bytes 1048608 | tf_op jit(solution)/shard_map/ppermute | solution.py:351
  122.4 1.0 copy-done.14
  123.4 5.6 %all-to-all-start = ((bf16[16,96,1024]{2,1,0:T(8,128)(2,1)}), bf16[16,96,1024]{2,1,0:T(8,128)(2,1)}, u32[]{:S(2)}, u32[]{:S(2)}) async-start(bf16[16,96,1024]{2,1,0:T(8,128)(2,1)} %bitcast.58.phi), calls=%async_computation | async-start | bytes 6291456 | tf_op jit(solution)/shard_map/all_to_all | solution.py:377
  130.2 2.3 collective-permute-done.19.refs_8_
  132.5 1.0 copy-done.15
  133.6 1.1 collective-permute-done.20.refs_9_
  135.1 2.6 collective-permute-done.21.refs_10_
  139.6 1.9 collective-permute-start.27
  141.5 1.5 collective-permute-start.29
  143.9 32.9 %hphi.1 = bf16[16,96,1024]{2,1,0:T(8,128)(2,1)} custom-call(s32[96,3]{1,0:T(8,128)} %copy.21.info, s32[3]{0:T(128)} %pad_add_fusion.1.here, bf16[16,96,1024]{2,1,0:T(8,128)(2,1)} %bitcast.58.phi, bf16[2,96,1024]{2,1,0:T(8,128)(2,1)} %copy-done.31, bf16[512,256]{1,0:T(8,128)(2,1)} %select_convert_fusion.band, bf16[4,2,32,16,128]{4,3,2,1,0:T(8,128)(2,1)} %copy-done.2, ...), custom_call_target="tpu_custom_call" | custom-call | flops 12884901888 | bytes 62914560 | tf_op jit(solution)/shard_map/hphi/pallas_call | solution.py:204
  176.8 12.6 %collective-permute-done.28.refs_10_ = bf16[4,576,128]{2,1,0:T(8,128)(2,1)S(1)} collective-permute-done((bf16[4,576,128]{2,1,0:T(8,128)(2,1)S(1)}, bf16[4,576,128]{2,1,0:T(8,128)(2,1)S(1)}, u32[]{:S(2)}, u32[]{:S(2)}) %collective-permute-start.28) | collective-permute-done | bytes 589856 | tf_op jit(solution)/shard_map/ppermute | solution.py:351
  189.5 3.9 %collective-permute-done.30.refs_9_ = bf16[4,576,128]{2,1,0:T(8,128)(2,1)} collective-permute-done((bf16[4,576,128]{2,1,0:T(8,128)(2,1)S(1)}, bf16[4,576,128]{2,1,0:T(8,128)(2,1)}, u32[]{:S(2)}, u32[]{:S(2)}) %collective-permute-start.30) | collective-permute-done | bytes 589856 | tf_op jit(solution)/shard_map/ppermute | solution.py:351
  193.3 9.5 %all-to-all-start.1 = ((bf16[16,96,1024]{2,1,0:T(8,128)(2,1)}), bf16[16,96,1024]{2,1,0:T(8,128)(2,1)}, u32[]{:S(2)}, u32[]{:S(2)}) async-start(bf16[16,96,1024]{2,1,0:T(8,128)(2,1)} %hphi.1), calls=%async_computation.1 | async-start | bytes 6291456 | tf_op jit(solution)/shard_map/all_to_all | solution.py:377
  203.6 1.9 collective-permute-start.31
  205.4 1.5 collective-permute-start.36
  207.6 34.6 %collective-permute-done.31.refs_3_ = bf16[4,576,128]{2,1,0:T(8,128)(2,1)S(1)} collective-permute-done((bf16[4,576,128]{2,1,0:T(8,128)(2,1)S(1)}, bf16[4,576,128]{2,1,0:T(8,128)(2,1)S(1)}, u32[]{:S(2)}, u32[]{:S(2)}) %collective-permute-start.31) | collective-permute-done | bytes 589856 | tf_op jit(solution)/shard_map/ppermute | solution.py:351
  242.8 1.4 collective-permute-done.35.refs_7_
  244.2 0.8 collective-permute-done.40.refs_15_
  245.9 29.9 %products.1 = (bf16[1536,1536]{1,0:T(8,128)(2,1)}, f32[1536,1024]{1,0:T(8,128)}) custom-call(s32[3]{0:T(128)} %pad_add_fusion.1.here, s32[12,12]{1,0:T(8,128)} %k_cols.1, s32[12,12]{1,0:T(8,128)} %h_cols.1, bf16[4,576,128]{2,1,0:T(8,128)(2,1)} %pad_maximum_fusion.2.refs_0_, bf16[4,576,128]{2,1,0:T(8,128)(2,1)} %copy-done.17, ...), custom_call_target="tpu_custom_call" | custom-call | flops 9663676416 | bytes 25165824 | tf_op jit(solution)/shard_map/products/pallas_call | solution.py:290
  275.8 10.3 %gradient.1 = bf16[1536,1024]{1,0:T(8,128)(2,1)} custom-call(bf16[1536,1536]{1,0:T(8,128)(2,1)} %get-tuple-element.56.dense_k, bf16[1536,1024]{1,0:T(8,128)(2,1)} %bitcast.25.hphi, f32[1536,1024]{1,0:T(8,128)} %get-tuple-element.58.product), custom_call_target="tpu_custom_call" | custom-call | flops 4831838208 | bytes 17825792 | tf_op jit(solution)/shard_map/gradient/pallas_call | solution.py:314
  286.1 79.2 %all_to_all.15 = bf16[16,96,1024]{2,1,0:T(8,128)(2,1)S(1)} all-to-all(bf16[16,96,1024]{2,1,0:T(8,128)(2,1)} %bitcast.64), channel_id=1, replica_groups=mesh['func'=16,'rep'=2] {'func'}, dimensions={0} | all-to-all | bytes 6291456 | tf_op jit(solution)/shard_map/all_to_all | solution.py:377
  365.3 3.4 copy.22
  (131 shorter events, 9.2 us)
Async XLA Ops:
  1.8 18.2 %collective-permute-start.3 = (bf16[2,32,16,128]{3,2,1,0:T(8,128)(2,1)S(1)}, bf16[2,32,16,128]{3,2,1,0:T(8,128)(2,1)S(1)}, u32[]{:S(2)}, u32[]{:S(2)}) collective-permute-start(bf16[2,32,16,128]{3,2,1,0:T(8,128)(2,1)S(1)} %get-tuple-element.75), channel_id=1, source_target_pairs={{0,24},{2,26},{4,28},{6,30},{8,0},{10,2},{12,4},{14,6},{16,8},{18,... | collective-permute-start | bytes 786440 | tf_op jit(solution)/shard_map/ppermute | solution.py:338
  6.9 24.6 %collective-permute-start.4 = (bf16[2,32,16,128]{3,2,1,0:T(8,128)(2,1)S(1)}, bf16[2,32,16,128]{3,2,1,0:T(8,128)(2,1)S(1)}, u32[]{:S(2)}, u32[]{:S(2)}) collective-permute-start(bf16[2,32,16,128]{3,2,1,0:T(8,128)(2,1)S(1)} %get-tuple-element.75), channel_id=1, source_target_pairs={{0,16},{2,18},{4,20},{6,22},{8,24},{10,26},{12,28},{14,30},{16,0},... | collective-permute-start | bytes 786440 | tf_op jit(solution)/shard_map/ppermute | solution.py:338
  6.9 24.6 %collective-permute-start.5 = (bf16[2,32,16,128]{3,2,1,0:T(8,128)(2,1)S(1)}, bf16[2,32,16,128]{3,2,1,0:T(8,128)(2,1)S(1)}, u32[]{:S(2)}, u32[]{:S(2)}) collective-permute-start(bf16[2,32,16,128]{3,2,1,0:T(8,128)(2,1)S(1)} %get-tuple-element.75), channel_id=1, source_target_pairs={{0,8},{2,10},{4,12},{6,14},{8,16},{10,18},{12,20},{14,22},{16,24},... | collective-permute-start | bytes 786440 | tf_op jit(solution)/shard_map/ppermute | solution.py:338
  7.9 23.8 %collective-permute-start = (bf16[2,32,16,128]{3,2,1,0:T(8,128)(2,1)S(1)}, bf16[2,32,16,128]{3,2,1,0:T(8,128)(2,1)S(1)}, u32[]{:S(2)}, u32[]{:S(2)}) collective-permute-start(bf16[2,32,16,128]{3,2,1,0:T(8,128)(2,1)S(1)} %get-tuple-element.76), channel_id=1, source_target_pairs={{0,24},{2,26},{4,28},{6,30},{8,0},{10,2},{12,4},{14,6},{16,8},{18,... | collective-permute-start | bytes 786440 | tf_op jit(solution)/shard_map/ppermute | solution.py:338
  10.7 41.0 %collective-permute-start.1 = (bf16[2,32,16,128]{3,2,1,0:T(8,128)(2,1)S(1)}, bf16[2,32,16,128]{3,2,1,0:T(8,128)(2,1)S(1)}, u32[]{:S(2)}, u32[]{:S(2)}) collective-permute-start(bf16[2,32,16,128]{3,2,1,0:T(8,128)(2,1)S(1)} %get-tuple-element.76), channel_id=1, source_target_pairs={{0,16},{2,18},{4,20},{6,22},{8,24},{10,26},{12,28},{14,30},{16,0},... | collective-permute-start | bytes 786440 | tf_op jit(solution)/shard_map/ppermute | solution.py:338
  20.0 31.7 %collective-permute-start.2 = (bf16[2,32,16,128]{3,2,1,0:T(8,128)(2,1)S(1)}, bf16[2,32,16,128]{3,2,1,0:T(8,128)(2,1)S(1)}, u32[]{:S(2)}, u32[]{:S(2)}) collective-permute-start(bf16[2,32,16,128]{3,2,1,0:T(8,128)(2,1)S(1)} %get-tuple-element.76), channel_id=1, source_target_pairs={{0,8},{2,10},{4,12},{6,14},{8,16},{10,18},{12,20},{14,22},{16,24},... | collective-permute-start | bytes 786440 | tf_op jit(solution)/shard_map/ppermute | solution.py:338
  31.5 20.6 %collective-permute-start.6 = (bf16[2,96,1024]{2,1,0:T(8,128)(2,1)S(1)}, bf16[2,96,1024]{2,1,0:T(8,128)(2,1)S(1)}, u32[]{:S(2)}, u32[]{:S(2)}) collective-permute-start(bf16[2,96,1024]{2,1,0:T(8,128)(2,1)S(1)} %slice_select_fusion), channel_id=1, source_target_pairs={{0,1},{1,0},{2,3},{3,2},{4,5},{5,4},{6,7},{7,6},{8,9},{9,8},{10,11... | collective-permute-start | bytes 1179656 | tf_op jit(solution)/shard_map/ppermute | solution.py:388
  52.1 50.2 %copy-start.3 = (bf16[4,2,32,16,128]{4,3,2,1,0:T(8,128)(2,1)}, bf16[4,2,32,16,128]{4,3,2,1,0:T(8,128)(2,1)S(1)}, u32[]{:S(2)}) copy-start(bf16[4,2,32,16,128]{4,3,2,1,0:T(8,128)(2,1)S(1)} %get-tuple-element.45.refs_4_) | copy-start | bytes 3145732
  52.1 77.0 %copy-start.2 = (bf16[4,2,32,16,128]{4,3,2,1,0:T(8,128)(2,1)}, bf16[4,2,32,16,128]{4,3,2,1,0:T(8,128)(2,1)S(1)}, u32[]{:S(2)}) copy-start(bf16[4,2,32,16,128]{4,3,2,1,0:T(8,128)(2,1)S(1)} %get-tuple-element.41.refs_0_) | copy-start | bytes 3145732
  52.1 70.3 %copy-start.31 = (bf16[2,96,1024]{2,1,0:T(8,128)(2,1)}, bf16[2,96,1024]{2,1,0:T(8,128)(2,1)S(1)}, u32[]{:S(2)}) copy-start(bf16[2,96,1024]{2,1,0:T(8,128)(2,1)S(1)} %collective-permute-done.6.halo) | copy-start | bytes 1179652
  52.1 26.2 %collective-permute-start.11 = (bf16[4,2,32,16,128]{4,3,2,1,0:T(8,128)(2,1)S(1)}, bf16[4,2,32,16,128]{4,3,2,1,0:T(8,128)(2,1)S(1)}, u32[]{:S(2)}, u32[]{:S(2)}) collective-permute-start(bf16[4,2,32,16,128]{4,3,2,1,0:T(8,128)(2,1)S(1)} %get-tuple-element.45.refs_4_), channel_id=1, source_target_pairs={{0,4},{2,6},{4,0},{6,2},{8,12},{10,14},{12,8},{14,10},{16,20},{18,... | collective-permute-start | bytes 3145736 | tf_op jit(solution)/shard_map/ppermute | solution.py:351
  53.7 26.1 %collective-permute-start.7 = (bf16[4,2,32,16,128]{4,3,2,1,0:T(8,128)(2,1)S(1)}, bf16[4,2,32,16,128]{4,3,2,1,0:T(8,128)(2,1)S(1)}, u32[]{:S(2)}, u32[]{:S(2)}) collective-permute-start(bf16[4,2,32,16,128]{4,3,2,1,0:T(8,128)(2,1)S(1)} %get-tuple-element.41.refs_0_), channel_id=1, source_target_pairs={{0,2},{2,0},{4,6},{6,4},{8,10},{10,8},{12,14},{14,12},{16,18},{18,... | collective-permute-start | bytes 3145736 | tf_op jit(solution)/shard_map/ppermute | solution.py:351
  55.2 6.7 %collective-permute-start.16 = (bf16[576,128]{1,0:T(8,128)(2,1)S(1)}, bf16[576,128]{1,0:T(8,128)(2,1)S(1)}, u32[]{:S(2)}, u32[]{:S(2)}) collective-permute-start(bf16[576,128]{1,0:T(8,128)(2,1)S(1)} %bitcast.66), channel_id=1, source_target_pairs={{0,24},{2,26},{4,28},{6,30},{8,0},{10,2},{12,4},{14,6},{16,8},{18,... | collective-permute-start | bytes 442376 | tf_op jit(solution)/shard_map/ppermute | solution.py:338
  55.2 16.6 %collective-permute-start.17 = (bf16[576,128]{1,0:T(8,128)(2,1)S(1)}, bf16[576,128]{1,0:T(8,128)(2,1)S(1)}, u32[]{:S(2)}, u32[]{:S(2)}) collective-permute-start(bf16[576,128]{1,0:T(8,128)(2,1)S(1)} %bitcast.67), channel_id=1, source_target_pairs={{0,16},{2,18},{4,20},{6,22},{8,24},{10,26},{12,28},{14,30},{16,0},... | collective-permute-start | bytes 442376 | tf_op jit(solution)/shard_map/ppermute | solution.py:338
  58.0 14.3 %collective-permute-start.18 = (bf16[576,128]{1,0:T(8,128)(2,1)S(1)}, bf16[576,128]{1,0:T(8,128)(2,1)S(1)}, u32[]{:S(2)}, u32[]{:S(2)}) collective-permute-start(bf16[576,128]{1,0:T(8,128)(2,1)S(1)} %bitcast.68), channel_id=1, source_target_pairs={{0,8},{2,10},{4,12},{6,14},{8,16},{10,18},{12,20},{14,22},{16,24},... | collective-permute-start | bytes 442376 | tf_op jit(solution)/shard_map/ppermute | solution.py:338
  61.8 19.4 %collective-permute-start.13 = (bf16[576,128]{1,0:T(8,128)(2,1)S(1)}, bf16[576,128]{1,0:T(8,128)(2,1)S(1)}, u32[]{:S(2)}, u32[]{:S(2)}) collective-permute-start(bf16[576,128]{1,0:T(8,128)(2,1)S(1)} %bitcast.69), channel_id=1, source_target_pairs={{0,24},{2,26},{4,28},{6,30},{8,0},{10,2},{12,4},{14,6},{16,8},{18,... | collective-permute-start | bytes 442376 | tf_op jit(solution)/shard_map/ppermute | solution.py:338
  71.8 30.4 %collective-permute-start.10 = (bf16[4,2,32,16,128]{4,3,2,1,0:T(8,128)(2,1)S(1)}, bf16[4,2,32,16,128]{4,3,2,1,0:T(8,128)(2,1)S(1)}, u32[]{:S(2)}, u32[]{:S(2)}) collective-permute-start(bf16[4,2,32,16,128]{4,3,2,1,0:T(8,128)(2,1)S(1)} %get-tuple-element.45.refs_4_), channel_id=1, source_target_pairs={{0,2},{2,0},{4,6},{6,4},{8,10},{10,8},{12,14},{14,12},{16,18},{18,... | collective-permute-start | bytes 3145736 | tf_op jit(solution)/shard_map/ppermute | solution.py:351
  72.4 29.9 %collective-permute-start.8 = (bf16[4,2,32,16,128]{4,3,2,1,0:T(8,128)(2,1)S(1)}, bf16[4,2,32,16,128]{4,3,2,1,0:T(8,128)(2,1)S(1)}, u32[]{:S(2)}, u32[]{:S(2)}) collective-permute-start(bf16[4,2,32,16,128]{4,3,2,1,0:T(8,128)(2,1)S(1)} %get-tuple-element.41.refs_0_), channel_id=1, source_target_pairs={{0,4},{2,6},{4,0},{6,2},{8,12},{10,14},{12,8},{14,10},{16,20},{18,... | collective-permute-start | bytes 3145736 | tf_op jit(solution)/shard_map/ppermute | solution.py:351
  78.3 44.1 %copy-start.10 = (bf16[4,2,32,16,128]{4,3,2,1,0:T(8,128)(2,1)}, bf16[4,2,32,16,128]{4,3,2,1,0:T(8,128)(2,1)S(1)}, u32[]{:S(2)}) copy-start(bf16[4,2,32,16,128]{4,3,2,1,0:T(8,128)(2,1)S(1)} %collective-permute-done.11.refs_6_) | copy-start | bytes 3145732
  78.3 44.1 %collective-permute-start.12 = (bf16[4,2,32,16,128]{4,3,2,1,0:T(8,128)(2,1)S(1)}, bf16[4,2,32,16,128]{4,3,2,1,0:T(8,128)(2,1)S(1)}, u32[]{:S(2)}, u32[]{:S(2)}) collective-permute-start(bf16[4,2,32,16,128]{4,3,2,1,0:T(8,128)(2,1)S(1)} %collective-permute-done.11.refs_6_), channel_id=1, source_target_pairs={{0,2},{2,0},{4,6},{6,4},{8,10},{10,8},{12,14},{14,12},{16,18},{18,... | collective-permute-start | bytes 3145736 | tf_op jit(solution)/shard_map/ppermute | solution.py:351
  79.8 43.6 %collective-permute-start.9 = (bf16[4,2,32,16,128]{4,3,2,1,0:T(8,128)(2,1)S(1)}, bf16[4,2,32,16,128]{4,3,2,1,0:T(8,128)(2,1)}, u32[]{:S(2)}, u32[]{:S(2)}) collective-permute-start(bf16[4,2,32,16,128]{4,3,2,1,0:T(8,128)(2,1)S(1)} %collective-permute-done.7.refs_1_), channel_id=1, source_target_pairs={{0,4},{2,6},{4,0},{6,2},{8,12},{10,14},{12,8},{14,10},{16,20},{18,... | collective-permute-start | bytes 3145736 | tf_op jit(solution)/shard_map/ppermute | solution.py:351
  81.3 9.2 %collective-permute-start.14 = (bf16[576,128]{1,0:T(8,128)(2,1)S(1)}, bf16[576,128]{1,0:T(8,128)(2,1)S(1)}, u32[]{:S(2)}, u32[]{:S(2)}) collective-permute-start(bf16[576,128]{1,0:T(8,128)(2,1)S(1)} %bitcast.70), channel_id=1, source_target_pairs={{0,16},{2,18},{4,20},{6,22},{8,24},{10,26},{12,28},{14,30},{16,0},... | collective-permute-start | bytes 442376 | tf_op jit(solution)/shard_map/ppermute | solution.py:338
  90.5 6.9 %collective-permute-start.15 = (bf16[576,128]{1,0:T(8,128)(2,1)S(1)}, bf16[576,128]{1,0:T(8,128)(2,1)S(1)}, u32[]{:S(2)}, u32[]{:S(2)}) collective-permute-start(bf16[576,128]{1,0:T(8,128)(2,1)S(1)} %bitcast.71), channel_id=1, source_target_pairs={{0,8},{2,10},{4,12},{6,14},{8,16},{10,18},{12,20},{14,22},{16,24},... | collective-permute-start | bytes 442376 | tf_op jit(solution)/shard_map/ppermute | solution.py:338
  90.7 112.3 %copy-start.5 = (bf16[4,576,128]{2,1,0:T(8,128)(2,1)}, bf16[4,576,128]{2,1,0:T(8,128)(2,1)S(1)}, u32[]{:S(2)}) copy-start(bf16[4,576,128]{2,1,0:T(8,128)(2,1)S(1)} %pad_maximum_fusion.3.refs_8_) | copy-start | bytes 1769476
  123.4 69.9 %all-to-all-start = ((bf16[16,96,1024]{2,1,0:T(8,128)(2,1)}), bf16[16,96,1024]{2,1,0:T(8,128)(2,1)}, u32[]{:S(2)}, u32[]{:S(2)}) async-start(bf16[16,96,1024]{2,1,0:T(8,128)(2,1)} %bitcast.58.phi), calls=%async_computation | async-start | bytes 6291456 | tf_op jit(solution)/shard_map/all_to_all | solution.py:377
  129.0 3.4 collective-permute-start.19
  129.1 5.6 %collective-permute-start.20 = (bf16[4,2,32,16,128]{4,3,2,1,0:T(8,128)(2,1)}, bf16[4,2,32,16,128]{4,3,2,1,0:T(8,128)(2,1)}, u32[]{:S(2)}, u32[]{:S(2)}) collective-permute-start(bf16[4,2,32,16,128]{4,3,2,1,0:T(8,128)(2,1)} %copy-done.11), channel_id=1, source_target_pairs={{0,1},{1,0},{2,3},{3,2},{4,5},{5,4},{6,7},{7,6},{8,9},{9,8},{10,11... | collective-permute-start | bytes 3145736 | tf_op jit(solution)/shard_map/ppermute | solution.py:363
  129.6 8.1 %collective-permute-start.21 = (bf16[4,2,32,16,128]{4,3,2,1,0:T(8,128)(2,1)}, bf16[4,2,32,16,128]{4,3,2,1,0:T(8,128)(2,1)}, u32[]{:S(2)}, u32[]{:S(2)}) collective-permute-start(bf16[4,2,32,16,128]{4,3,2,1,0:T(8,128)(2,1)} %copy-done.13), channel_id=1, source_target_pairs={{0,1},{1,0},{2,3},{3,2},{4,5},{5,4},{6,7},{7,6},{8,9},{9,8},{10,11... | collective-permute-start | bytes 3145736 | tf_op jit(solution)/shard_map/ppermute | solution.py:363
  129.7 9.9 %collective-permute-start.22 = (bf16[4,2,32,16,128]{4,3,2,1,0:T(8,128)(2,1)}, bf16[4,2,32,16,128]{4,3,2,1,0:T(8,128)(2,1)}, u32[]{:S(2)}, u32[]{:S(2)}) collective-permute-start(bf16[4,2,32,16,128]{4,3,2,1,0:T(8,128)(2,1)} %collective-permute-done.9.refs_3_), channel_id=1, source_target_pairs={{0,1},{1,0},{2,3},{3,2},{4,5},{5,4},{6,7},{7,6},{8,9},{9,8},{10,11... | collective-permute-start | bytes 3145736 | tf_op jit(solution)/shard_map/ppermute | solution.py:363
  130.1 11.4 %collective-permute-start.23 = (bf16[4,2,32,16,128]{4,3,2,1,0:T(8,128)(2,1)S(1)}, bf16[4,2,32,16,128]{4,3,2,1,0:T(8,128)(2,1)}, u32[]{:S(2)}, u32[]{:S(2)}) collective-permute-start(bf16[4,2,32,16,128]{4,3,2,1,0:T(8,128)(2,1)S(1)} %copy-done.4), channel_id=1, source_target_pairs={{0,1},{1,0},{2,3},{3,2},{4,5},{5,4},{6,7},{7,6},{8,9},{9,8},{10,11... | collective-permute-start | bytes 3145736 | tf_op jit(solution)/shard_map/ppermute | solution.py:363
  133.4 9.5 %collective-permute-start.24 = (bf16[4,2,32,16,128]{4,3,2,1,0:T(8,128)(2,1)}, bf16[4,2,32,16,128]{4,3,2,1,0:T(8,128)(2,1)S(1)}, u32[]{:S(2)}, u32[]{:S(2)}) collective-permute-start(bf16[4,2,32,16,128]{4,3,2,1,0:T(8,128)(2,1)} %copy-done.12), channel_id=1, source_target_pairs={{0,1},{1,0},{2,3},{3,2},{4,5},{5,4},{6,7},{7,6},{8,9},{9,8},{10,11... | collective-permute-start | bytes 3145736 | tf_op jit(solution)/shard_map/ppermute | solution.py:363
  134.7 8.8 %collective-permute-start.25 = (bf16[4,2,32,16,128]{4,3,2,1,0:T(8,128)(2,1)}, bf16[4,2,32,16,128]{4,3,2,1,0:T(8,128)(2,1)}, u32[]{:S(2)}, u32[]{:S(2)}) collective-permute-start(bf16[4,2,32,16,128]{4,3,2,1,0:T(8,128)(2,1)} %copy-done.10), channel_id=1, source_target_pairs={{0,1},{1,0},{2,3},{3,2},{4,5},{5,4},{6,7},{7,6},{8,9},{9,8},{10,11... | collective-permute-start | bytes 3145736 | tf_op jit(solution)/shard_map/ppermute | solution.py:363
  137.7 5.9 %collective-permute-start.26 = (bf16[4,2,32,16,128]{4,3,2,1,0:T(8,128)(2,1)}, bf16[4,2,32,16,128]{4,3,2,1,0:T(8,128)(2,1)}, u32[]{:S(2)}, u32[]{:S(2)}) collective-permute-start(bf16[4,2,32,16,128]{4,3,2,1,0:T(8,128)(2,1)} %copy-done.14), channel_id=1, source_target_pairs={{0,1},{1,0},{2,3},{3,2},{4,5},{5,4},{6,7},{7,6},{8,9},{9,8},{10,11... | collective-permute-start | bytes 3145736 | tf_op jit(solution)/shard_map/ppermute | solution.py:363
  139.6 37.2 %collective-permute-start.27 = (bf16[4,576,128]{2,1,0:T(8,128)(2,1)}, bf16[4,576,128]{2,1,0:T(8,128)(2,1)S(1)}, u32[]{:S(2)}, u32[]{:S(2)}) collective-permute-start(bf16[4,576,128]{2,1,0:T(8,128)(2,1)} %pad_maximum_fusion.2.refs_0_), channel_id=1, source_target_pairs={{0,2},{2,0},{4,6},{6,4},{8,10},{10,8},{12,14},{14,12},{16,18},{18,... | collective-permute-start | bytes 1769480 | tf_op jit(solution)/shard_map/ppermute | solution.py:351
  141.5 48.0 %collective-permute-start.29 = (bf16[4,576,128]{2,1,0:T(8,128)(2,1)}, bf16[4,576,128]{2,1,0:T(8,128)(2,1)S(1)}, u32[]{:S(2)}, u32[]{:S(2)}) collective-permute-start(bf16[4,576,128]{2,1,0:T(8,128)(2,1)} %pad_maximum_fusion.2.refs_0_), channel_id=1, source_target_pairs={{0,4},{2,6},{4,0},{6,2},{8,12},{10,14},{12,8},{14,10},{16,20},{18,... | collective-permute-start | bytes 1769480 | tf_op jit(solution)/shard_map/ppermute | solution.py:351
  143.0 46.5 %collective-permute-start.28 = (bf16[4,576,128]{2,1,0:T(8,128)(2,1)S(1)}, bf16[4,576,128]{2,1,0:T(8,128)(2,1)S(1)}, u32[]{:S(2)}, u32[]{:S(2)}) collective-permute-start(bf16[4,576,128]{2,1,0:T(8,128)(2,1)S(1)} %pad_maximum_fusion.3.refs_8_), channel_id=1, source_target_pairs={{0,4},{2,6},{4,0},{6,2},{8,12},{10,14},{12,8},{14,10},{16,20},{18,... | collective-permute-start | bytes 1769480 | tf_op jit(solution)/shard_map/ppermute | solution.py:351
  143.5 49.8 %collective-permute-start.30 = (bf16[4,576,128]{2,1,0:T(8,128)(2,1)S(1)}, bf16[4,576,128]{2,1,0:T(8,128)(2,1)}, u32[]{:S(2)}, u32[]{:S(2)}) collective-permute-start(bf16[4,576,128]{2,1,0:T(8,128)(2,1)S(1)} %pad_maximum_fusion.3.refs_8_), channel_id=1, source_target_pairs={{0,2},{2,0},{4,6},{6,4},{8,10},{10,8},{12,14},{14,12},{16,18},{18,... | collective-permute-start | bytes 1769480 | tf_op jit(solution)/shard_map/ppermute | solution.py:351
  193.3 82.4 %all-to-all-start.1 = ((bf16[16,96,1024]{2,1,0:T(8,128)(2,1)}), bf16[16,96,1024]{2,1,0:T(8,128)(2,1)}, u32[]{:S(2)}, u32[]{:S(2)}) async-start(bf16[16,96,1024]{2,1,0:T(8,128)(2,1)} %hphi.1), calls=%async_computation.1 | async-start | bytes 6291456 | tf_op jit(solution)/shard_map/all_to_all | solution.py:377
  202.9 4.0 %collective-permute-start.32 = (bf16[4,576,128]{2,1,0:T(8,128)(2,1)S(1)}, bf16[4,576,128]{2,1,0:T(8,128)(2,1)S(1)}, u32[]{:S(2)}, u32[]{:S(2)}) collective-permute-start(bf16[4,576,128]{2,1,0:T(8,128)(2,1)S(1)} %copy-done.6), channel_id=1, source_target_pairs={{0,1},{1,0},{2,3},{3,2},{4,5},{5,4},{6,7},{7,6},{8,9},{9,8},{10,11... | collective-permute-start | bytes 1769480 | tf_op jit(solution)/shard_map/ppermute | solution.py:363
  203.0 3.9 %collective-permute-start.37 = (bf16[4,576,128]{2,1,0:T(8,128)(2,1)S(1)}, bf16[4,576,128]{2,1,0:T(8,128)(2,1)S(1)}, u32[]{:S(2)}, u32[]{:S(2)}) collective-permute-start(bf16[4,576,128]{2,1,0:T(8,128)(2,1)S(1)} %pad_maximum_fusion.3.refs_8_), channel_id=1, source_target_pairs={{0,1},{1,0},{2,3},{3,2},{4,5},{5,4},{6,7},{7,6},{8,9},{9,8},{10,11... | collective-permute-start | bytes 1769480 | tf_op jit(solution)/shard_map/ppermute | solution.py:363
  203.5 4.0 %collective-permute-start.34 = (bf16[4,576,128]{2,1,0:T(8,128)(2,1)S(1)}, bf16[4,576,128]{2,1,0:T(8,128)(2,1)S(1)}, u32[]{:S(2)}, u32[]{:S(2)}) collective-permute-start(bf16[4,576,128]{2,1,0:T(8,128)(2,1)S(1)} %collective-permute-done.29.refs_2_), channel_id=1, source_target_pairs={{0,1},{1,0},{2,3},{3,2},{4,5},{5,4},{6,7},{7,6},{8,9},{9,8},{10,11... | collective-permute-start | bytes 1769480 | tf_op jit(solution)/shard_map/ppermute | solution.py:363
  203.6 38.6 %collective-permute-start.31 = (bf16[4,576,128]{2,1,0:T(8,128)(2,1)S(1)}, bf16[4,576,128]{2,1,0:T(8,128)(2,1)S(1)}, u32[]{:S(2)}, u32[]{:S(2)}) collective-permute-start(bf16[4,576,128]{2,1,0:T(8,128)(2,1)S(1)} %copy-done.18), channel_id=1, source_target_pairs={{0,4},{2,6},{4,0},{6,2},{8,12},{10,14},{12,8},{14,10},{16,20},{18,... | collective-permute-start | bytes 1769480 | tf_op jit(solution)/shard_map/ppermute | solution.py:351
  205.4 36.8 %collective-permute-start.36 = (bf16[4,576,128]{2,1,0:T(8,128)(2,1)S(1)}, bf16[4,576,128]{2,1,0:T(8,128)(2,1)S(1)}, u32[]{:S(2)}, u32[]{:S(2)}) collective-permute-start(bf16[4,576,128]{2,1,0:T(8,128)(2,1)S(1)} %collective-permute-done.28.refs_10_), channel_id=1, source_target_pairs={{0,2},{2,0},{4,6},{6,4},{8,10},{10,8},{12,14},{14,12},{16,18},{18,... | collective-permute-start | bytes 1769480 | tf_op jit(solution)/shard_map/ppermute | solution.py:351
  206.9 35.8 %collective-permute-start.33 = (bf16[4,576,128]{2,1,0:T(8,128)(2,1)S(1)}, bf16[4,576,128]{2,1,0:T(8,128)(2,1)S(1)}, u32[]{:S(2)}, u32[]{:S(2)}) collective-permute-start(bf16[4,576,128]{2,1,0:T(8,128)(2,1)S(1)} %copy-done.18), channel_id=1, source_target_pairs={{0,1},{1,0},{2,3},{3,2},{4,5},{5,4},{6,7},{7,6},{8,9},{9,8},{10,11... | collective-permute-start | bytes 1769480 | tf_op jit(solution)/shard_map/ppermute | solution.py:363
  207.0 35.8 %collective-permute-start.39 = (bf16[4,576,128]{2,1,0:T(8,128)(2,1)S(1)}, bf16[4,576,128]{2,1,0:T(8,128)(2,1)S(1)}, u32[]{:S(2)}, u32[]{:S(2)}) collective-permute-start(bf16[4,576,128]{2,1,0:T(8,128)(2,1)S(1)} %collective-permute-done.28.refs_10_), channel_id=1, source_target_pairs={{0,1},{1,0},{2,3},{3,2},{4,5},{5,4},{6,7},{7,6},{8,9},{9,8},{10,11... | collective-permute-start | bytes 1769480 | tf_op jit(solution)/shard_map/ppermute | solution.py:363
  207.5 35.2 %collective-permute-start.38 = (bf16[4,576,128]{2,1,0:T(8,128)(2,1)}, bf16[4,576,128]{2,1,0:T(8,128)(2,1)S(1)}, u32[]{:S(2)}, u32[]{:S(2)}) collective-permute-start(bf16[4,576,128]{2,1,0:T(8,128)(2,1)} %collective-permute-done.30.refs_9_), channel_id=1, source_target_pairs={{0,1},{1,0},{2,3},{3,2},{4,5},{5,4},{6,7},{7,6},{8,9},{9,8},{10,11... | collective-permute-start | bytes 1769480 | tf_op jit(solution)/shard_map/ppermute | solution.py:363
  242.2 2.0 collective-permute-start.35
  242.2 2.8 collective-permute-start.40
  (27 other events, 375.9 us)
